TPU v7x, 32 devices: a whole 2x2x4 slice. The times are simulated.
32 devices in a mesh: dp: 8 (over y, x, core), feat: 4 (over z).
Axes of the slice: x: 2, y: 2, z: 4, core: 2. Of those that a mesh axis runs over, the one named last changes fastest.
Arguments:
- view_features: bfloat16 [2, 1024, 8192], P(None, 'dp', 'feat'), may hold values from 0 to 55, as said below
- weight: float32 [8192, 8192], P('dp', 'feat'), may hold values from -64 to 64
- velocity: float32 [8192, 8192], P('dp', 'feat'), may hold values from -6 to 6
Outputs:
- new_weight: float32 [8192, 8192], P('dp', 'feat')
- new_velocity: float32 [8192, 8192], P('dp', 'feat')
Inputs may be any that keep to these rules, and one draw needn't show every extreme that they name: `view_features`: nonnegative features.
All inputs are finite; a program needn't handle non-finite values.
Results may differ from a plain program's by a relative error of at most 0.039.
Values may be sent and summed in bfloat16 or wider, within the bound.
No kernel may reach another device: no remote copies, remote signals or barrier semaphores. Data moves between devices by JAX's collectives and lax.ppermute only.
A program may use at most 128 MiB of HBM per device.

v0:
```python
import jax
import jax.numpy as jnp
from jax import lax
from jax.sharding import PartitionSpec as P

EPSILON = 1e-05
NORM_EPSILON = 1e-06
REDUNDANCY = 0.0051
MOMENTUM = 0.9
LEARN_RATE = 0.2


def per_device(view_features, weight, velocity):
    images_dev = view_features.shape[1]
    feat_width = view_features.shape[2]
    dp_width = weight.shape[0]
    batch_total = images_dev * lax.axis_size("dp")
    dp_index = lax.axis_index("dp")
    feat_index = lax.axis_index("feat")
    view_rows = lax.all_gather(view_features, "feat", axis=2, tiled=True)
    columns = lax.all_to_all(view_rows, "dp", split_axis=2, concat_axis=1, tiled=True)
    weight_half = weight.astype(jnp.bfloat16)
    block_rows = columns
    outputs = lax.psum_scatter(
        jnp.einsum(
            "vnk,kf->nvf", block_rows, weight_half, preferred_element_type=jnp.float32
        ).astype(jnp.bfloat16),
        "dp",
        scatter_dimension=0,
        tiled=True,
    ).astype(jnp.float32)
    average = lax.psum(jnp.sum(outputs, 0), "dp") / batch_total
    centered = outputs - average
    variance = lax.psum(jnp.sum(centered * centered, 0), "dp") / batch_total
    inverse = lax.rsqrt(variance + EPSILON)
    normed = centered * inverse
    normed_half = normed.astype(jnp.bfloat16)
    first_rows = normed_half[:, 0]
    second_all = lax.all_gather(normed_half[:, 1], "dp", axis=0, tiled=True)
    first_wide = lax.all_gather(first_rows, "feat", axis=1, tiled=True)
    first_cols = lax.all_to_all(first_wide, "dp", split_axis=1, concat_axis=0, tiled=True)
    correlation = (
        jnp.einsum("nk,nf->kf", first_cols, second_all, preferred_element_type=jnp.float32)
        / batch_total
    )
    row_ids = dp_index * dp_width + lax.broadcasted_iota(jnp.int32, (dp_width, feat_width), 0)
    col_ids = feat_index * feat_width + lax.broadcasted_iota(jnp.int32, (dp_width, feat_width), 1)
    diagonal = row_ids == col_ids
    scaled = (
        jnp.where(diagonal, -2.0 * (1.0 - correlation), 2.0 * REDUNDANCY * correlation)
        / batch_total
    ).astype(jnp.bfloat16)
    first_part = jnp.einsum(
        "nf,kf->nk", second_all, scaled, preferred_element_type=jnp.float32
    ).astype(jnp.bfloat16)
    exchanged = lax.all_to_all(first_part, "dp", split_axis=0, concat_axis=1, tiled=True)
    first_grad = lax.psum_scatter(exchanged, "feat", scatter_dimension=1, tiled=True).astype(
        jnp.float32
    )
    block_rows = first_cols
    second_grad = lax.psum_scatter(
        jnp.dot(block_rows, scaled, preferred_element_type=jnp.float32).astype(jnp.bfloat16),
        "dp",
        scatter_dimension=0,
        tiled=True,
    ).astype(jnp.float32)
    feature_grads = jnp.stack([first_grad, second_grad], 1)
    grad_sum, grad_cross = lax.psum(
        (jnp.sum(feature_grads, 0), jnp.sum(feature_grads * normed, 0)), "dp"
    )
    out_grad = (
        inverse * (feature_grads - grad_sum / batch_total - normed * (grad_cross / batch_total))
    ).astype(jnp.bfloat16)
    weight_grad = jnp.einsum(
        "vnk,nvf->kf",
        columns,
        lax.all_gather(out_grad, "dp", axis=0, tiled=True),
        preferred_element_type=jnp.float32,
    )
    weight_local = jnp.sum(weight * weight)
    grad_local = jnp.sum(weight_grad * weight_grad)
    weight_sq, grad_sq = lax.psum((weight_local, grad_local), ("dp", "feat"))
    trust = jnp.sqrt(weight_sq) / (jnp.sqrt(grad_sq) + NORM_EPSILON)
    new_velocity = MOMENTUM * velocity + trust * weight_grad
    new_weight = weight - LEARN_RATE * new_velocity
    return (new_weight, new_velocity)


def solution(mesh):
    in_specs = (P(None, "dp", "feat"), P("dp", "feat"), P("dp", "feat"))
    out_specs = (P("dp", "feat"), P("dp", "feat"))
    return jax.shard_map(
        per_device, mesh=mesh, in_specs=in_specs, out_specs=out_specs, check_vma=False
    )
```

profile of v0, /device:TPU:0, one launch (start us, length us, event | category | flops | bytes accessed | tf_op | source)
XLA Modules:
  0.0 711.9 jit_solution(18370969267367403777)
XLA Ops:
  7.2 0.0 all-gather.7.cloned.1.call-start
  7.2 3.7 copy.33
  10.9 0.0 reduce-scatter.10.cloned.1.call-start
  11.0 83.6 %all-gather.7.cloned.1.call-done = bf16[2,128,8192]{1,0,2:T(2,128)(2,1)} async-done(((bf16[2,128,2048]{1,0,2:T(2,128)(2,1)}), bf16[2,128,8192]{1,0,2:T(2,128)(2,1)}) %all-gather.7.cloned.1.call-update) | async-done | bytes 4194320 | tf_op jit(solution)/shard_map/all_gather | solution.py:20
  94.5 53.5 %all_to_all.56 = bf16[2,128,8192]{1,0,2:T(2,128)(2,1)} all-to-all(bf16[2,128,8192]{1,0,2:T(2,128)(2,1)} %all-gather.7.cloned.1.call-done), channel_id=1, replica_groups=mesh['dp'=8,'feat'=4] {'dp'}, dimensions={2} | all-to-all | bytes 8388608 | tf_op jit(solution)/shard_map/all_to_all | solution.py:21
  148.1 11.1 %copy.34 = bf16[2,128,8,1024]{3,1,2,0:T(8,128)(2,1)} copy(bf16[2,128,8,1024]{1,0,3,2:T(2,128)(2,1)} %bitcast.54) | data formatting | bytes 8388608 | tf_op jit(solution)/shard_map/all_to_all | solution.py:21
  159.2 15.2 %convolution_convert_fusion = bf16[2048,2,1024]{2,0,1:T(8,128)(2,1)} fusion(bf16[2,1024,1024]{2,1,0:T(8,128)(2,1)} %bitcast.60, f32[1024,2048]{1,0:T(8,128)} %param.4), kind=kOutput, calls=%fused_computation.7 | convolution fusion | flops 8596226048 | bytes 20971520 | tf_op jit(solution)/shard_map/vnk,kf->nvf/dot_general | solution.py:25
  174.4 11.9 %copy.48 = bf16[1024,4096]{1,0:T(8,128)(2,1)} copy(bf16[1024,4096]{0,1:T(8,128)(2,1)} %bitcast.55) | data formatting | bytes 16777216
  186.4 0.0 all-gather.13.cloned.1.call-start
  186.4 68.1 %reduce-scatter.10.cloned.1.call-done = bf16[128,4096]{1,0:T(8,128)(2,1)} async-done(((bf16[1024,4096]{1,0:T(8,128)(2,1)}), bf16[128,4096]{1,0:T(8,128)(2,1)}) %reduce-scatter.10.cloned.1.call-update) | async-done | bytes 1048592
  254.5 1.6 copy.49
  256.1 0.4 convert_reduce_fusion.1
  256.5 23.1 %psum.43 = f32[2,2048]{1,0:T(2,128)S(1)} all-reduce(f32[2,2048]{1,0:T(2,128)S(1)} %convert_reduce_fusion.1), channel_id=1, replica_groups=mesh['dp'=8,'feat'=4] {'dp'}, use_global_device_ids=true, to_apply=%region_4.0 | all-reduce | flops 4096 | bytes 32768 | tf_op jit(solution)/shard_map/psum | solution.py:32
  279.6 1.3 fusion.16
  280.9 22.3 %psum.44 = f32[2,2048]{1,0:T(2,128)S(1)} all-reduce(f32[2,2048]{1,0:T(2,128)S(1)} %fusion.16), channel_id=1, replica_groups=mesh['dp'=8,'feat'=4] {'dp'}, use_global_device_ids=true, to_apply=%region_6.7 | all-reduce | flops 4096 | bytes 32768 | tf_op jit(solution)/shard_map/psum | solution.py:34
  303.2 1.3 fusion.12
  304.6 1.0 fusion.21
  305.6 0.0 all-gather.11.cloned.1.call-start
  305.7 0.5 all-gather.11.cloned.1.call-update
  306.2 45.5 %all-gather.13.cloned.1.call-done = bf16[128,1,8192]{0,2,1:T(8,128)(2,1)} async-done(((bf16[128,1,2048]{0,2,1:T(8,128)(2,1)}), bf16[128,1,8192]{0,2,1:T(8,128)(2,1)}) %all-gather.13.cloned.1.call-update) | async-done | bytes 2097168 | tf_op jit(solution)/shard_map/all_gather | solution.py:40
  351.7 3.9 copy.36
  355.6 3.6 all-to-all-start.1
  359.2 0.2 reduce-scatter.12.cloned.1.call-start
  359.5 33.0 %all-to-all-done.1 = bf16[128,8,1024]{2,0,1:T(8,128)(2,1)S(1)} async-done(((bf16[128,8,1024]{2,0,1:T(8,128)(2,1)}), bf16[128,8,1024]{2,0,1:T(8,128)(2,1)S(1)}, u32[]{:S(2)}, u32[]{:S(2)}) %all-to-all-start.1) | async-done | bytes 2097184 | tf_op jit(solution)/shard_map/all_to_all | solution.py:41
  392.4 12.8 %all-gather.11.cloned.1.call-done = bf16[1024,1,2048]{0,2,1:T(8,128)(2,1)} async-done(((bf16[128,1,2048]{0,2,1:T(8,128)(2,1)}), bf16[1024,1,2048]{0,2,1:T(8,128)(2,1)}) %all-gather.11.cloned.1.call-update) | async-done | bytes 4194320 | tf_op jit(solution)/shard_map/all_gather | solution.py:39
  405.2 8.5 %multiply_convert_fusion = bf16[1024,2048]{1,0:T(8,128)(2,1)S(1)} fusion(bf16[1024,1024]{1,0:T(8,128)(2,1)S(1)} %bitcast.62, bf16[1024,1,2048]{0,2,1:T(8,128)(2,1)} %all-gather.11.cloned.1.call-done, s32[2048]{0:T(1024)S(1)} %iota_add_fusion, s32[1024]{0:T(1024)S(1)} %iota_add_fusion.1), kind=kOutput, calls=%fused_computation.5 | convolution fusion | flops 4311744512 | bytes 10498048 | tf_op jit(solution)/shard_map/nk,nf->kf/dot_general | solution.py:43
  413.7 2.0 copy-done
  415.7 6.1 convolution_convert_fusion.1
  421.8 0.0 reduce-scatter.8.cloned.1.call-start
  421.8 8.0 %fusion.18 = bf16[1024,1024]{1,0:T(8,128)(2,1)S(1)} fusion(bf16[1024,2048]{1,0:T(8,128)(2,1)} %copy-done, bf16[1024,1,2048]{0,2,1:T(8,128)(2,1)} %all-gather.11.cloned.1.call-done), kind=kOutput, calls=%fused_computation.29 | convolution fusion | flops 4296015872 | bytes 10485760 | tf_op jit(solution)/shard_map/nf,kf->nk/dot_general | solution.py:53
  429.9 40.3 %all_to_all.57 = bf16[8,128,1024]{2,1,0:T(8,128)(2,1)S(1)} all-to-all(bf16[8,128,1024]{2,1,0:T(8,128)(2,1)S(1)} %bitcast.65), channel_id=1, replica_groups=mesh['dp'=8,'feat'=4] {'dp'}, dimensions={0} | all-to-all | bytes 4194304 | tf_op jit(solution)/shard_map/all_to_all | solution.py:56
  470.1 2.4 copy.37
  472.5 0.0 all-gather.9.cloned.1.call-start
  472.6 10.8 %reduce-scatter.12.cloned.1.call-done = bf16[128,2048]{1,0:T(8,128)(2,1)} async-done(((bf16[1024,2048]{1,0:T(8,128)(2,1)}), bf16[128,2048]{1,0:T(8,128)(2,1)}) %reduce-scatter.12.cloned.1.call-update) | async-done | bytes 524304
  483.4 1.3 copy.47
  484.7 45.3 %reduce-scatter.8.cloned.1.call-done = bf16[128,2048]{0,1:T(8,128)(2,1)} async-done(((bf16[128,8192]{0,1:T(8,128)(2,1)}), bf16[128,2048]{0,1:T(8,128)(2,1)}) %reduce-scatter.8.cloned.1.call-update) | async-done | bytes 524304 | tf_op jit(solution)/shard_map/reduce_scatter | solution.py:57
  530.0 3.1 convert_reduce_fusion
  533.1 23.9 %all-reduce.1 = (f32[2,2048]{1,0:T(2,128)S(1)}, f32[2,2048]{1,0:T(2,128)S(1)}) all-reduce(f32[2,2048]{1,0:T(2,128)S(1)} %get-tuple-element.11, f32[2,2048]{1,0:T(2,128)S(1)} %get-tuple-element.10), channel_id=1, replica_groups=mesh['dp'=8,'feat'=4] {'dp'}, use_global_device_ids=true, to_apply=%region_12.13 | all-reduce | flops 8192 | bytes 65536 | tf_op jit(solution)/shard_map/psum | solution.py:68
  557.1 5.4 fusion.15
  562.5 9.4 %copy.39 = f32[1024,2048]{0,1:T(8,128)} copy(f32[1024,2048]{1,0:T(8,128)} %param.4) | data formatting | bytes 16777216 | tf_op args[1]
  571.9 9.3 %copy.32 = f32[1024,2048]{0,1:T(8,128)} copy(f32[1024,2048]{1,0:T(8,128)} %param.5) | data formatting | bytes 16777216 | tf_op args[2]
  581.2 6.1 multiply_reduce_fusion
  587.3 29.0 %all-gather.9.cloned.1.call-done = bf16[1024,2,2048]{0,2,1:T(8,128)(2,1)} async-done(((bf16[128,2,2048]{0,2,1:T(8,128)(2,1)}), bf16[1024,2,2048]{0,2,1:T(8,128)(2,1)}) %all-gather.9.cloned.1.call-update) | async-done | bytes 8388624 | tf_op jit(solution)/shard_map/all_gather | solution.py:77
  616.3 15.4 %fusion = (f32[]{:T(128)}, f32[2048,1024,1]{1,0,2:T(8,128)}) fusion(bf16[1024,2,2048]{0,2,1:T(8,128)(2,1)} %all-gather.9.cloned.1.call-done, bf16[2,1024,1024]{2,1,0:T(8,128)(2,1)} %bitcast.61), kind=kOutput, calls=%fused_computation.3 | convolution fusion | flops 8594128896 | bytes 20971524 | tf_op jit(solution)/shard_map/vnk,nvf->kf/dot_general | solution.py:74
  631.7 39.5 %all-reduce = (f32[]{:T(128)}, f32[]{:T(128)}) all-reduce(f32[]{:T(128)} %multiply_reduce_fusion, f32[]{:T(128)} %get-tuple-element.20), channel_id=1, replica_groups=mesh['dp'=8,'feat'=4] {'dp','feat'}, use_global_device_ids=true, to_apply=%region_1.0 | all-reduce | flops 2 | bytes 16 | tf_op jit(solution)/shard_map/psum | solution.py:82
  672.6 14.2 %multiply_subtract_fusion = (f32[1024,2048]{0,1:T(8,128)}, f32[1024,2048]{0,1:T(8,128)}) fusion(f32[1024,2048]{0,1:T(8,128)} %copy.39, f32[2048,1024,1]{1,0,2:T(8,128)} %get-tuple-element.21, f32[]{:T(128)S(6)} %div.27, f32[1024,2048]{0,1:T(8,128)} %copy.32), kind=kLoop, calls=%fused_computation.4 | loop fusion | flops 10485760 | bytes 41943044 | tf_op jit(solution)/shard_map/sub | solution.py:85
  686.8 9.1 %copy.40 = f32[1024,2048]{1,0:T(8,128)} copy(f32[1024,2048]{0,1:T(8,128)} %get-tuple-element.16) | data formatting | bytes 16777216
  695.9 9.1 %copy.41 = f32[1024,2048]{1,0:T(8,128)} copy(f32[1024,2048]{0,1:T(8,128)} %get-tuple-element.17) | data formatting | bytes 16777216
  (12 shorter events, 0.2 us)
Async XLA Ops:
  7.2 87.4 %all-gather.7.cloned.1.call-start = ((), (), s32[]{:S(2)}) async-start(), calls=%async_computation.6 | async-start | bytes 5242880 | tf_op jit(solution)/shard_map/all_gather | solution.py:20
  10.9 243.6 %reduce-scatter.10.cloned.1.call-start = ((), (), s32[]{:S(2)}) async-start(), calls=%async_computation.11 | async-start | bytes 9437184
  186.4 165.3 %all-gather.13.cloned.1.call-start = ((), (), s32[]{:S(2)}) async-start(), calls=%async_computation.10 | async-start | bytes 2621440 | tf_op jit(solution)/shard_map/all_gather | solution.py:40
  305.6 99.6 %all-gather.11.cloned.1.call-start = ((), (), s32[]{:S(2)}) async-start(), calls=%async_computation.9 | async-start | bytes 4718592 | tf_op jit(solution)/shard_map/all_gather | solution.py:39
  355.6 36.9 %all-to-all-start.1 = ((bf16[128,8,1024]{2,0,1:T(8,128)(2,1)}), bf16[128,8,1024]{2,0,1:T(8,128)(2,1)S(1)}, u32[]{:S(2)}, u32[]{:S(2)}) async-start(bf16[128,8,1024]{2,0,1:T(8,128)(2,1)} %copy.36), calls=%async_computation.1 | async-start | bytes 4194304 | tf_op jit(solution)/shard_map/all_to_all | solution.py:41
  359.2 124.1 %reduce-scatter.12.cloned.1.call-start = ((), (), s32[]{:S(2)}) async-start(), calls=%async_computation.12 | async-start | bytes 4718592
  413.7 2.0 copy-start
  421.8 108.2 %reduce-scatter.8.cloned.1.call-start = ((), (), s32[]{:S(2)}) async-start(), calls=%async_computation.7 | async-start | bytes 2621440 | tf_op jit(solution)/shard_map/reduce_scatter | solution.py:57
  472.5 143.8 %all-gather.9.cloned.1.call-start = ((), (), s32[]{:S(2)}) async-start(), calls=%async_computation.8 | async-start | bytes 9437184 | tf_op jit(solution)/shard_map/all_gather | solution.py:77
Sparse Core Ops, SparseCore 0:
  11.0 83.4 all-gather.6
  186.5 67.9 reduce-scatter.9
  305.8 45.8 all-gather.12
  354.1 51.0 all-gather.10
  421.9 61.3 reduce-scatter.11
  486.1 43.8 reduce-scatter.7
  562.6 53.6 all-gather.8
where the time goes:
time: 714 us; the launch traced here: 712 us
  waiting for transfers between devices  329 us (46%)
  blocking collectives  203 us (28%)
  local copies, waits for them, and re-layouts  75.9 us (11%)
  matrix products  53.2 us (7%)
  other arithmetic  32 us (4%)
  between operations  15.5 us (2%)
    all_gather x1, waiting for transfers between devices, per_device(): view_rows = lax.all_gather(view_features, 'feat', axis=2, tiled=True)  83.6 us
    unnamed x9, waiting for transfers between devices  79.5 us
    unnamed x10, local copies, waits for them, and re-layouts  57.4 us
    all_to_all x1, blocking collectives, per_device(): lax.all_to_all(view_rows, 'dp', split_axis=2, concat_axis=1, tiled=True)  53.5 us
    all_gather x1, waiting for transfers between devices, per_device(): first_wide = lax.all_gather(first_rows, 'feat', axis=1, tiled=True)  45.5 us
    reduce_scatter x1, waiting for transfers between devices, per_device(): lax.psum_scatter(exchanged, 'feat', scatter_dimension=1, tiled=True)  45.3 us
    all_to_all x1, blocking collectives, per_device(): lax.all_to_all(first_part, 'dp', split_axis=0, concat_axis=1, tiled=True)  40.3 us
    psum x1, blocking collectives, per_device(): weight_sq, grad_sq = lax.psum((weight_local, grad_local), ('dp', 'feat'))  39.5 us
  transfers between devices with their start and end apart: 8, of which 8 were waited for; matrix products, arithmetic and copies ran while one was open for 6% of the time, Pallas kernels for 0%

commit v1 on v0

v1 whole, which is shorter than its diff:
```python
import jax
import jax.numpy as jnp
from jax import lax
from jax.sharding import PartitionSpec as P

EPSILON = 1e-05
NORM_EPSILON = 1e-06
REDUNDANCY = 0.0051
MOMENTUM = 0.9
LEARN_RATE = 0.2


def per_device(view_features, weight, velocity):
    n_dp = lax.axis_size("dp")
    n_feat = lax.axis_size("feat")
    images_dev = view_features.shape[1]
    dp_width = weight.shape[0]
    batch = images_dev * n_dp
    per_feat = n_dp // n_feat
    weight_half = weight.astype(jnp.bfloat16)

    columns, normed, half, inverse, gram = [None] * 2, [None] * 2, [None] * 2, [None] * 2, [None] * 2
    for v in (1, 0):
        pieces = view_features[v].reshape(images_dev, per_feat, dp_width).transpose(1, 0, 2)
        rows = lax.all_gather(pieces, "feat", axis=0, tiled=True)
        columns[v] = lax.all_to_all(rows, "dp", split_axis=0, concat_axis=0, tiled=True).reshape(
            batch, dp_width
        )
        local_mean = jnp.mean(columns[v].astype(jnp.float32), 0).astype(jnp.bfloat16)
        offset = jnp.einsum("kf,k->f", weight_half, local_mean, preferred_element_type=jnp.float32)
        block = jnp.einsum(
            "kf,nk->fn", weight_half, columns[v], preferred_element_type=jnp.float32
        )
        block = (block - offset[:, None]).astype(jnp.bfloat16)
        outputs = lax.psum_scatter(block, "dp", scatter_dimension=0, tiled=True).astype(jnp.float32)
        centered = outputs - jnp.mean(outputs, 1, keepdims=True)
        variance = jnp.mean(centered * centered, 1, keepdims=True)
        inverse[v] = lax.rsqrt(variance + EPSILON)
        normed[v] = centered * inverse[v]
        half[v] = normed[v].astype(jnp.bfloat16)
        partial = jnp.einsum("fn,fm->nm", half[v], half[v], preferred_element_type=jnp.float32)
        gram[v] = lax.psum(partial.astype(jnp.bfloat16), ("dp", "feat"))

    first, second = half[0].astype(jnp.float32), half[1].astype(jnp.float32)
    diagonal = jnp.sum(first * second, 1, keepdims=True) / batch
    extra = (-2.0 * (1.0 - diagonal) - 2.0 * REDUNDANCY * diagonal) / batch
    weight_grad = 0.0
    for v in (0, 1):
        grads = jnp.einsum("nm,fm->fn", gram[1 - v], half[v], preferred_element_type=jnp.float32)
        grads = grads * (2.0 * REDUNDANCY / (batch * batch)) + extra * (second, first)[v]
        grad_mean = jnp.mean(grads, 1, keepdims=True)
        grad_cross = jnp.mean(grads * normed[v], 1, keepdims=True)
        out_grad = (inverse[v] * (grads - grad_mean - normed[v] * grad_cross)).astype(jnp.bfloat16)
        gathered = lax.all_gather(out_grad, "dp", axis=0, tiled=True)
        weight_grad += jnp.einsum(
            "nk,fn->kf", columns[v], gathered, preferred_element_type=jnp.float32
        )
    weight_local = jnp.sum(weight * weight)
    grad_local = jnp.sum(weight_grad * weight_grad)
    weight_sq, grad_sq = lax.psum((weight_local, grad_local), ("dp", "feat"))
    trust = jnp.sqrt(weight_sq) / (jnp.sqrt(grad_sq) + NORM_EPSILON)
    new_velocity = MOMENTUM * velocity + trust * weight_grad
    new_weight = weight - LEARN_RATE * new_velocity
    return (new_weight, new_velocity)


def solution(mesh):
    in_specs = (P(None, "dp", "feat"), P("dp", "feat"), P("dp", "feat"))
    out_specs = (P("dp", "feat"), P("dp", "feat"))
    return jax.shard_map(
        per_device, mesh=mesh, in_specs=in_specs, out_specs=out_specs, check_vma=False
    )
```

time: 714 us -> 544 us (0.76)
  blocking collectives: 203 us -> 73.2 us
  local copies, waits for them, and re-layouts: 75.9 us -> 41 us
    psum x0 -> x1, waiting for transfers between devices: none -> 142 us  [per_device(): gram[v] = lax.psum(partial.astype(jnp.bfloat16), ('dp', 'feat'))]
    unnamed x9 -> x7, waiting for transfers between devices: 79.5 us -> 0.11 us
    psum x3 -> x0, blocking collectives: 69.3 us -> none  [the longest x1 23.9 us: per_device(): lax.psum((jnp.sum(feature_grads, 0), jnp.sum(feature_grads * normed, 0)),...]
    all_gather x4, waiting for transfers between devices: 171 us -> 103 us  [the longest x2 59.7 us: per_device(): rows = lax.all_gather(pieces, 'feat', axis=0, tiled=True)]
    all_to_all x2 -> x1, blocking collectives: 93.8 us -> 33.4 us  [per_device(): lax.all_to_all(rows, 'dp', split_axis=0, concat_axis=0, tiled=True)]
    reduce_scatter x1 -> x2, waiting for transfers between devices: 45.3 us -> 65.4 us  [per_device(): lax.psum_scatter(block, 'dp', scatter_dimension=0, tiled=True)]
    unnamed x10 -> x16, local copies, waits for them, and re-layouts: 57.4 us -> 37.7 us
    all_to_all x1, waiting for transfers between devices: 33 us -> 14.7 us  [per_device(): lax.all_to_all(rows, 'dp', split_axis=0, concat_axis=0, tiled=True)]
  transfers between devices with their start and end apart: 8 -> 8, of which waited for: 8 -> 8; matrix products, arithmetic and copies ran while one was open for 6% -> 12% of each run, Pallas kernels for 0% -> 0%
where the time goes in v1:
time: 544 us; the launch traced here: 543 us
  waiting for transfers between devices  324 us (60%)
  blocking collectives  73.2 us (13%)
  matrix products  51 us (9%)
  local copies, waits for them, and re-layouts  41 us (8%)
  other arithmetic  33.4 us (6%)
  between operations  15.5 us (3%)
    psum x1, waiting for transfers between devices, per_device(): gram[v] = lax.psum(partial.astype(jnp.bfloat16), ('dp', 'feat'))  142 us
    reduce_scatter x2, waiting for transfers between devices, per_device(): lax.psum_scatter(block, 'dp', scatter_dimension=0, tiled=True)  65.4 us
    all_gather x2, waiting for transfers between devices, per_device(): rows = lax.all_gather(pieces, 'feat', axis=0, tiled=True)  59.7 us
    all_gather x2, waiting for transfers between devices, per_device(): gathered = lax.all_gather(out_grad, 'dp', axis=0, tiled=True)  42.9 us
    psum x1, blocking collectives, per_device(): weight_sq, grad_sq = lax.psum((weight_local, grad_local), ('dp', 'feat'))  39.8 us
    unnamed x16, local copies, waits for them, and re-layouts  37.7 us
    all_to_all x1, blocking collectives, per_device(): lax.all_to_all(rows, 'dp', split_axis=0, concat_axis=0, tiled=True)  33.4 us
    dot_general x2, matrix products, per_device(): jnp.einsum('nk,fn->kf', columns[v], gathered, preferred_element_type=jnp....  22.7 us
  transfers between devices with their start and end apart: 8, of which 8 were waited for; matrix products, arithmetic and copies ran while one was open for 12% of the time, Pallas kernels for 0%

profile of v1, /device:TPU:0, one launch (start us, length us, event | category | flops | bytes accessed | tf_op | source)
XLA Modules:
  0.0 542.7 jit_solution(2108882633843963132)
XLA Ops:
  7.2 1.3 fusion.29
  8.5 0.3 copy.29
  8.8 1.0 copy.23
  9.8 49.0 %all-gather.5.cloned.1.call-done = bf16[8,128,1024]{2,1,0:T(8,128)(2,1)} async-done(((bf16[2,128,1024]{2,1,0:T(8,128)(2,1)}), bf16[8,128,1024]{2,1,0:T(8,128)(2,1)}) %all-gather.5.cloned.1.call-update) | async-done | bytes 2097168 | tf_op jit(solution)/shard_map/all_gather | solution.py:25
  58.8 3.6 all-to-all-start
  62.5 0.3 copy.30
  62.8 1.0 copy.25
  63.8 0.0 reduce-scatter.3.cloned.1.call-start
  63.9 10.6 %multiply_reduce_fusion.1 = (f32[]{:T(128)}, bf16[1024,2048]{1,0:T(8,128)(2,1)}) fusion(f32[1024,2048]{1,0:T(8,128)} %param.4), kind=kLoop, calls=%fused_computation.5 | loop fusion | flops 6291455 | bytes 12582916 | tf_op jit(solution)/shard_map/reduce_sum | solution.py:58
  74.4 14.7 %all-to-all-done = bf16[8,128,1024]{2,1,0:T(8,128)(2,1)S(1)} async-done(((bf16[8,128,1024]{2,1,0:T(8,128)(2,1)}), bf16[8,128,1024]{2,1,0:T(8,128)(2,1)S(1)}, u32[]{:S(2)}, u32[]{:S(2)}) %all-to-all-start) | async-done | bytes 2097184 | tf_op jit(solution)/shard_map/all_to_all | solution.py:26
  89.1 0.4 convert_reduce_fusion.1
  89.5 3.0 fusion.30
  92.5 0.0 copy-done
  92.6 6.8 %subtract_convert_fusion.1 = bf16[2048,1024]{1,0:T(8,128)(2,1)} fusion(f32[2048]{0:T(1024)S(1)} %bitcast.34, bf16[1024,2048]{1,0:T(8,128)(2,1)S(1)} %copy-done, bf16[1024,1024]{1,0:T(8,128)(2,1)S(1)} %bitcast.27), kind=kOutput, calls=%fused_computation.4 | convolution fusion | flops 4299161600 | bytes 10493952 | tf_op jit(solution)/shard_map/kf,nk->fn/dot_general | solution.py:31
  99.4 0.0 reduce-scatter.5.cloned.1.call-start
  99.4 10.7 %all-gather.7.cloned.1.call-done = bf16[8,128,1024]{2,1,0:T(8,128)(2,1)} async-done(((bf16[2,128,1024]{2,1,0:T(8,128)(2,1)}), bf16[8,128,1024]{2,1,0:T(8,128)(2,1)}) %all-gather.7.cloned.1.call-update) | async-done | bytes 2097168 | tf_op jit(solution)/shard_map/all_gather | solution.py:25
  110.1 33.4 %all_to_all.10 = bf16[8,128,1024]{2,1,0:T(8,128)(2,1)S(1)} all-to-all(bf16[8,128,1024]{2,1,0:T(8,128)(2,1)} %all-gather.7.cloned.1.call-done), channel_id=1, replica_groups=mesh['dp'=8,'feat'=4] {'dp'}, dimensions={0} | all-to-all | bytes 4194304 | tf_op jit(solution)/shard_map/all_to_all | solution.py:26
  143.5 0.4 convert_reduce_fusion
  143.9 0.7 fusion.31
  144.5 0.3 copy-done.2
  144.8 6.8 %subtract_convert_fusion = bf16[2048,1024]{1,0:T(8,128)(2,1)} fusion(f32[2048]{0:T(1024)S(1)} %bitcast.33, bf16[1024,2048]{1,0:T(8,128)(2,1)S(1)} %copy-done.1, bf16[1024,1024]{1,0:T(8,128)(2,1)S(1)} %bitcast.29), kind=kOutput, calls=%fused_computation.3 | convolution fusion | flops 4299161600 | bytes 10493952 | tf_op jit(solution)/shard_map/kf,nk->fn/dot_general | solution.py:31
  151.6 0.2 all-reduce.4.cloned.1.call-start
  151.9 12.6 %reduce-scatter.3.cloned.1.call-done = bf16[256,1024]{1,0:T(8,128)(2,1)} async-done(((bf16[2048,1024]{1,0:T(8,128)(2,1)}), bf16[256,1024]{1,0:T(8,128)(2,1)}) %reduce-scatter.3.cloned.1.call-update) | async-done | bytes 524304 | tf_op jit(solution)/shard_map/reduce_scatter | solution.py:35
  164.4 1.3 convert_reduce_fusion.3
  165.7 1.3 fusion.21
  167.0 52.9 %reduce-scatter.5.cloned.1.call-done = bf16[256,1024]{1,0:T(8,128)(2,1)} async-done(((bf16[2048,1024]{1,0:T(8,128)(2,1)}), bf16[256,1024]{1,0:T(8,128)(2,1)}) %reduce-scatter.5.cloned.1.call-update) | async-done | bytes 524304 | tf_op jit(solution)/shard_map/reduce_scatter | solution.py:35
  219.9 1.2 convert_reduce_fusion.2
  221.1 1.3 fusion.16
  222.4 3.5 convolution_convert_fusion.1
  226.0 2.3 convolution_convert_fusion
  228.2 0.0 all-gather.9.cloned.1.call-start
  228.3 0.4 fusion.22
  228.7 141.6 %all-reduce.4.cloned.1.call-done = (bf16[1024,1024]{1,0:T(8,128)(2,1)}, bf16[1024,1024]{1,0:T(8,128)(2,1)}) async-done(((bf16[1024,1024]{1,0:T(8,128)(2,1)}, bf16[1024,1024]{1,0:T(8,128)(2,1)}), (bf16[1024,1024]{1,0:T(8,128)(2,1)}, bf16[1024,1024]{1,0:T(8,128)(2,1)})) %all-reduce.4.cloned.1.call-update) | async-done | bytes 4194320 | tf_op jit(solution)/shard_map/psum | solution.py:42
  370.3 2.7 fusion.28
  373.0 1.1 fusion.20
  374.2 0.0 all-gather.11.cloned.1.call-start
  374.2 2.7 fusion.27
  376.9 1.1 fusion.15
  378.1 9.3 %copy.26 = f32[1024,2048]{0,1:T(8,128)} copy(f32[1024,2048]{1,0:T(8,128)} %param.4) | data formatting | bytes 16777216 | tf_op args[1]
  387.4 9.3 %copy.21 = f32[1024,2048]{0,1:T(8,128)} copy(f32[1024,2048]{1,0:T(8,128)} %param.5) | data formatting | bytes 16777216 | tf_op args[2]
  396.7 13.2 %all-gather.9.cloned.1.call-done = bf16[2048,1024]{1,0:T(8,128)(2,1)} async-done(((bf16[256,1024]{1,0:T(8,128)(2,1)}), bf16[2048,1024]{1,0:T(8,128)(2,1)}) %all-gather.9.cloned.1.call-update) | async-done | bytes 4194320 | tf_op jit(solution)/shard_map/all_gather | solution.py:54
  409.9 8.9 %fusion.32 = f32[2048,1024]{1,0:T(8,128)} fusion(bf16[2048,1024]{1,0:T(8,128)(2,1)} %all-gather.9.cloned.1.call-done, bf16[1024,1024]{1,0:T(8,128)(2,1)S(1)} %bitcast.28), kind=kOutput, calls=%fused_computation.59 | convolution fusion | flops 4294967296 | bytes 14680064 | tf_op jit(solution)/shard_map/nk,fn->kf/dot_general | solution.py:55
  418.8 29.7 %all-gather.11.cloned.1.call-done = bf16[2048,1024]{1,0:T(8,128)(2,1)} async-done(((bf16[256,1024]{1,0:T(8,128)(2,1)}), bf16[2048,1024]{1,0:T(8,128)(2,1)}) %all-gather.11.cloned.1.call-update) | async-done | bytes 4194320 | tf_op jit(solution)/shard_map/all_gather | solution.py:54
  448.5 13.8 %multiply_reduce_fusion = (f32[]{:T(128)}, f32[2048,1024]{1,0:T(8,128)}) fusion(f32[2048,1024]{1,0:T(8,128)} %fusion.32, bf16[2048,1024]{1,0:T(8,128)(2,1)} %all-gather.11.cloned.1.call-done, bf16[1024,1024]{1,0:T(8,128)(2,1)} %bitcast.30), kind=kOutput, calls=%fused_computation.2 | convolution fusion | flops 4301258752 | bytes 23068676 | tf_op jit(solution)/shard_map/nk,fn->kf/dot_general | solution.py:55
  462.3 39.8 %all-reduce = (f32[]{:T(128)}, f32[]{:T(128)}) all-reduce(f32[]{:T(128)} %get-tuple-element.20, f32[]{:T(128)} %get-tuple-element.26), channel_id=1, replica_groups=mesh['dp'=8,'feat'=4] {'dp','feat'}, use_global_device_ids=true, to_apply=%region_1.0 | all-reduce | flops 2 | bytes 16 | tf_op jit(solution)/shard_map/psum | solution.py:60
  503.4 14.2 %multiply_subtract_fusion = (f32[1024,2048]{0,1:T(8,128)}, f32[1024,2048]{0,1:T(8,128)}) fusion(f32[1024,2048]{0,1:T(8,128)} %copy.26, f32[2048,1024]{1,0:T(8,128)} %get-tuple-element.27, f32[]{:T(128)S(6)} %div.51, f32[1024,2048]{0,1:T(8,128)} %copy.21), kind=kLoop, calls=%fused_computation.1 | loop fusion | flops 10485760 | bytes 41943044 | tf_op jit(solution)/shard_map/sub | solution.py:63
  517.6 9.1 %copy.27 = f32[1024,2048]{1,0:T(8,128)} copy(f32[1024,2048]{0,1:T(8,128)} %get-tuple-element.18) | data formatting | bytes 16777216
  526.7 9.1 %copy.28 = f32[1024,2048]{1,0:T(8,128)} copy(f32[1024,2048]{0,1:T(8,128)} %get-tuple-element.19) | data formatting | bytes 16777216
  (28 shorter events, 0.3 us)
Async XLA Ops:
  7.2 51.6 %all-gather.5.cloned.1.call-start = ((), (), s32[]{:S(2)}) async-start(), calls=%async_computation.4 | async-start | bytes 2621440 | tf_op jit(solution)/shard_map/all_gather | solution.py:25
  58.8 30.3 %all-to-all-start = ((bf16[8,128,1024]{2,1,0:T(8,128)(2,1)}), bf16[8,128,1024]{2,1,0:T(8,128)(2,1)S(1)}, u32[]{:S(2)}, u32[]{:S(2)}) async-start(bf16[8,128,1024]{2,1,0:T(8,128)(2,1)} %all-gather.5.cloned.1.call-done), calls=%async_computation | async-start | bytes 4194304 | tf_op jit(solution)/shard_map/all_to_all | solution.py:26
  62.4 47.7 %all-gather.7.cloned.1.call-start = ((), (), s32[]{:S(2)}) async-start(), calls=%async_computation.6 | async-start | bytes 2621440 | tf_op jit(solution)/shard_map/all_gather | solution.py:25
  63.8 100.6 %reduce-scatter.3.cloned.1.call-start = ((), (), s32[]{:S(2)}) async-start(), calls=%async_computation.5 | async-start | bytes 4718592 | tf_op jit(solution)/shard_map/reduce_scatter | solution.py:35
  89.1 3.5 copy-start
  99.4 120.5 %reduce-scatter.5.cloned.1.call-start = ((), (), s32[]{:S(2)}) async-start(), calls=%async_computation.7 | async-start | bytes 4718592 | tf_op jit(solution)/shard_map/reduce_scatter | solution.py:35
  110.1 33.8 %copy-start.1 = (bf16[1024,2048]{1,0:T(8,128)(2,1)S(1)}, bf16[1024,2048]{1,0:T(8,128)(2,1)}, u32[]{:S(2)}) copy-start(bf16[1024,2048]{1,0:T(8,128)(2,1)} %get-tuple-element.21) | copy-start | bytes 12582916
  143.5 1.4 copy-start.2
  151.6 218.7 %all-reduce.4.cloned.1.call-start = ((), (), s32[]{:S(2)}) async-start(), calls=%async_computation.10 | async-start | bytes 8388608 | tf_op jit(solution)/shard_map/psum | solution.py:42
  164.4 61.6 %copy-start.3 = (bf16[256,1024]{1,0:T(8,128)(2,1)S(1)}, bf16[256,1024]{1,0:T(8,128)(2,1)}, u32[]{:S(2)}) copy-start(bf16[256,1024]{1,0:T(8,128)(2,1)} %reduce-scatter.3.cloned.1.call-done) | copy-start | bytes 1572868
  222.4 5.9 %copy-start.4 = (bf16[256,1024]{1,0:T(8,128)(2,1)S(1)}, bf16[256,1024]{1,0:T(8,128)(2,1)}, u32[]{:S(2)}) copy-start(bf16[256,1024]{1,0:T(8,128)(2,1)} %reduce-scatter.5.cloned.1.call-done) | copy-start | bytes 1572868
  228.2 181.6 %all-gather.9.cloned.1.call-start = ((), (), s32[]{:S(2)}) async-start(), calls=%async_computation.8 | async-start | bytes 4718592 | tf_op jit(solution)/shard_map/all_gather | solution.py:54
  374.2 74.3 %all-gather.11.cloned.1.call-start = ((), (), s32[]{:S(2)}) async-start(), calls=%async_computation.9 | async-start | bytes 4718592 | tf_op jit(solution)/shard_map/all_gather | solution.py:54
Sparse Core Ops, SparseCore 0:
  10.1 48.6 all-gather.4
  64.9 45.1 all-gather.6
  114.0 50.3 reduce-scatter.2
  168.6 51.2 reduce-scatter.4
  228.4 141.9 all-reduce.3
  374.3 35.5 all-gather.8
  411.8 36.7 all-gather.10

commit v2 on v1

v2 whole, which is shorter than its diff:
```python
import jax
import jax.numpy as jnp
from jax import lax
from jax.experimental import pallas as pl
from jax.experimental.pallas import tpu as pltpu
from jax.sharding import PartitionSpec as P

EPSILON = 1e-05
NORM_EPSILON = 1e-06
REDUNDANCY = 0.0051
MOMENTUM = 0.9
LEARN_RATE = 0.2
ROWS_BY_ROWS = (((1,), (1,)), ((), ()))
MIB = 1024 * 1024
F32, BF16 = jnp.float32, jnp.bfloat16


def swap(value, axis, mask):
    return lax.ppermute(value, axis, [(i, i ^ mask) for i in range(lax.axis_size(axis))])


def bit_value(axis, bit):
    return (lax.axis_index(axis) >> bit) & 1


def join(mine, other, bit):
    return jnp.where(
        bit == 0, jnp.concatenate([mine, other], 0), jnp.concatenate([other, mine], 0)
    )


def sum_everywhere(value):
    for axis in ("dp", "feat"):
        others = [swap(value, axis, mask) for mask in range(1, lax.axis_size(axis))]
        for other in others:
            value = value + other
    return value


def whole(array):
    zeros = (0,) * array.ndim
    return pl.BlockSpec(array.shape, lambda *_: zeros, pipeline_mode=pl.Buffered(1))


def like(shape, kind):
    return jax.ShapeDtypeStruct(shape, kind)


def run(body, scalars, operands, in_specs, outs, out_specs, grid=(1,), scratch=(), after=(),
        flops=0, moved=0, limit=32):
    n_in, n_after = len(operands), len(after)

    def kernel(scalars_ref, *refs):
        body(scalars_ref, *refs[:n_in], *refs[n_in + n_after :])

    return pl.pallas_call(
        kernel,
        grid_spec=pltpu.PrefetchScalarGridSpec(
            num_scalar_prefetch=1,
            grid=grid,
            in_specs=list(in_specs) + [pl.BlockSpec(memory_space=pl.ANY)] * n_after,
            out_specs=list(out_specs),
            scratch_shapes=list(scratch),
        ),
        out_shape=list(outs),
        compiler_params=pltpu.CompilerParams(vmem_limit_bytes=limit * MIB),
        cost_estimate=pl.CostEstimate(flops=flops, bytes_accessed=moved, transcendentals=0),
    )(scalars, *operands, *after)


def fold(square):
    part = jnp.sum(square.reshape(-1, 8, square.shape[1]), 0)
    return sum(part[:, start : start + 128] for start in range(0, part.shape[1], 128))


def turn_weight(weight, half):
    depth, width = weight.shape
    quarter = width // 4
    step = min(256, quarter)
    steps = quarter // step

    def body(half_ref, weight_ref, turned_ref, square_ref):
        block = weight_ref[...]
        turned_ref[...] = block.T.astype(BF16)

        @pl.when((pl.program_id(0) == 0) & (pl.program_id(1) == 0))
        def _():
            square_ref[...] = jnp.zeros_like(square_ref)

        square_ref[...] += fold(block * block)

    return run(
        body, half.reshape(1), [weight],
        [pl.BlockSpec((depth, step), lambda p, i, h: (0, (2 * p + h[0]) * steps + i))],
        [like((2 * quarter, depth), BF16), like((8, 128), F32)],
        [
            pl.BlockSpec((step, depth), lambda p, i, h: (p * steps + i, 0)),
            pl.BlockSpec((8, 128), lambda p, i, h: (0, 0)),
        ],
        grid=(2, steps), flops=depth * width, moved=3 * depth * width, limit=16,
    )


def share_of(view_features, view, after=()):
    _, count, width = view_features.shape

    def body(_, rows_ref, out_ref):
        out_ref[...] = rows_ref[...]

    (out,) = run(
        body, jnp.zeros((1,), jnp.int32), [view_features],
        [pl.BlockSpec((None, count, width), lambda i, s: (view, 0, 0))],
        [like((count, width), BF16)], [pl.BlockSpec((count, width), lambda i, s: (0, 0))],
        after=after, moved=4 * count * width, limit=8,
    )
    return out


def go_round(share):
    n_feat = lax.axis_size("feat")
    shares = [share]
    for _ in range(1, n_feat):
        ring = [(i, (i + 1) % n_feat) for i in range(n_feat)]
        shares.append(lax.ppermute(shares[-1], "feat", ring))
    return shares


def choose(shares, n_chip, after=()):
    n_feat = len(shares)
    chip = lax.axis_index("dp") >> 1
    back = [lax.rem(lax.axis_index("feat") - (chip ^ mask) + n_feat, n_feat) for mask in range(n_chip)]

    def body(back_ref, *refs):
        for mask in range(n_chip):
            for place in range(n_feat):

                @pl.when(back_ref[mask] == place)
                def _():
                    refs[n_feat + mask][...] = refs[place][...]

    shape = shares[0].shape
    return run(
        body, jnp.stack(back), shares, [whole(share) for share in shares],
        [like(shape, BF16)] * n_chip, [whole(shares[0])] * n_chip,
        after=after, moved=4 * n_chip * shape[0] * shape[1], limit=16,
    )


def assemble(place, own, other, after=()):
    n_chip = len(own)
    count, width = own[0].shape
    half = width // 2

    def body(place_ref, *refs):
        chip, core = place_ref[0], place_ref[1]
        out_ref = refs[-1]
        for mask in range(n_chip):
            for flip in range(2):
                piece_ref = refs[flip * n_chip + mask]
                row = pl.multiple_of(((chip ^ mask) * 2 + (core ^ flip)) * count, count)
                for side in range(2):
                    lane = pl.multiple_of((core ^ side) * half, half)
                    out_ref[pl.ds(row, count), side * half : (side + 1) * half] = piece_ref[
                        :, pl.ds(lane, half)
                    ]

    out = like((2 * n_chip * count, width), BF16)
    (columns,) = run(
        body, place, [*own, *other], [whole(piece) for piece in [*own, *other]],
        [out], [whole(out)], after=after, moved=8 * n_chip * count * width, limit=24,
    )
    return columns


def turn_columns(columns):
    batch, width = columns.shape
    depth = width // 2
    step = 256

    def body(_, columns_ref, out_ref):
        out_ref[...] = columns_ref[...].astype(F32).T.astype(BF16)

    (turned,) = run(
        body, jnp.zeros((1,), jnp.int32), [columns],
        [pl.BlockSpec((step, depth), lambda i, s: (i, 0))],
        [like((depth, batch), BF16)], [pl.BlockSpec((depth, step), lambda i, s: (0, i))],
        grid=(batch // step,), moved=4 * batch * depth, limit=8,
    )
    return turned


def forward(bits, turned_own, turned_other, columns, after=()):
    rows, depth = turned_own.shape
    batch = columns.shape[0]
    out_rows = rows // 4
    step = min(256, out_rows)
    steps = out_rows // step

    def body(bits_ref, own_a, other_a, own_b, other_b, columns_ref, out_a, out_b):
        for own_ref, other_ref, out_ref in ((own_a, other_a, out_a), (own_b, other_b, out_b)):
            block = lax.dot_general(
                own_ref[...], columns_ref[:, :depth], ROWS_BY_ROWS, preferred_element_type=F32
            )
            block += lax.dot_general(
                other_ref[...], columns_ref[:, depth:], ROWS_BY_ROWS, preferred_element_type=F32
            )
            out_ref[...] = (block - jnp.mean(block, 1, keepdims=True)).astype(BF16)

    def of_path(path):
        return pl.BlockSpec((step, depth), lambda i, b: ((2 * path + b[path]) * steps + i, 0))

    out_spec = pl.BlockSpec((step, batch), lambda i, b: (i, 0))
    return run(
        body, bits, [turned_own, turned_other, turned_own, turned_other, columns],
        [of_path(0), of_path(0), of_path(1), of_path(1), whole(columns)],
        [like((out_rows, batch), BF16)] * 2, [out_spec] * 2, grid=(steps,), after=after,
        flops=8 * out_rows * depth * batch, moved=8 * out_rows * depth + 4 * batch * depth,
    )


def add_halves(bits, kept, got, after=()):
    rows, batch = kept[0].shape
    half = rows // 2

    def body(bits_ref, kept_a, got_a, kept_b, got_b, send_a, send_b, keep_a, keep_b):
        for path, (kept_ref, got_ref, send_ref, keep_ref) in enumerate(
            ((kept_a, got_a, send_a, keep_a), (kept_b, got_b, send_b, keep_b))
        ):
            for flip, out_ref in ((1, send_ref), (0, keep_ref)):
                rows_of = pl.ds(pl.multiple_of((bits_ref[path] ^ flip) * half, half), half)
                total = kept_ref[rows_of, :].astype(F32) + got_ref[rows_of, :].astype(F32)
                out_ref[...] = total.astype(BF16)

    operands = [kept[0], got[0], kept[1], got[1]]
    out = like((half, batch), BF16)
    outs = run(
        body, bits, operands, [whole(one) for one in operands],
        [out] * 4, [whole(out)] * 4, after=after, moved=12 * rows * batch, limit=16,
    )
    return outs[:2], outs[2:]


def normalise(kept, got, after=()):
    rows, batch = kept[0].shape

    def body(_, kept_a, got_a, kept_b, got_b, normed_ref, half_ref, inverse_ref):
        for path, (kept_ref, got_ref) in enumerate(((kept_a, got_a), (kept_b, got_b))):
            total = kept_ref[...].astype(F32) + got_ref[...].astype(F32)
            total -= jnp.mean(total, 1, keepdims=True)
            inverse = lax.rsqrt(jnp.mean(total * total, 1, keepdims=True) + EPSILON)
            normed = total * inverse
            place = slice(path * rows, (path + 1) * rows)
            normed_ref[place, :] = normed
            half_ref[place, :] = normed.astype(BF16)
            inverse_ref[place, :] = jnp.broadcast_to(inverse, (rows, 128))

    operands = [kept[0], got[0], kept[1], got[1]]
    outs = [like((2 * rows, width), kind) for width, kind in ((batch, F32), (batch, BF16), (128, F32))]
    return run(
        body, jnp.zeros((1,), jnp.int32), operands, [whole(one) for one in operands],
        outs, [whole(out) for out in outs], after=after, moved=20 * rows * batch, limit=16,
    )


def gram_rows(place, own, other, n_chip, after=()):
    rows, batch = own.shape
    blocks = 2 * n_chip
    size = batch // blocks
    width = (blocks // 2 + 1) * size

    def body(place_ref, own_ref, other_ref, *refs):
        twice_ref = refs[-1]
        for start, ref in ((0, own_ref), (rows, other_ref)):
            twice_ref[start : start + rows, :batch] = ref[...]
            twice_ref[start : start + rows, batch:] = ref[...]
        for mask in range(n_chip):
            row = pl.multiple_of(((place_ref[0] ^ mask) * 2 + place_ref[1]) * size, size)
            left = twice_ref[:, pl.ds(row, size)].astype(F32).T.astype(BF16)
            right = twice_ref[:, pl.ds(row, width)]
            refs[mask][...] = jnp.dot(left, right, preferred_element_type=F32).astype(BF16)

    out = like((size, width), BF16)
    return run(
        body, place, [own, other], [whole(own), whole(other)],
        [out] * n_chip, [whole(out)] * n_chip,
        scratch=[pltpu.VMEM((2 * rows, 2 * batch), BF16)], after=after,
        flops=4 * rows * width * batch // 2, moved=8 * rows * batch, limit=24,
    )


def out_grad_of(place, gram_own, gram_other, normed, half, half_other, inverse, after=()):
    rows, batch = half.shape
    n_chip = gram_own.shape[0]
    blocks = 2 * n_chip
    size = batch // blocks

    def body(place_ref, own_ref, other_ref, normed_ref, half_ref, half_other_ref, inverse_ref,
             out_ref, gram_ref):
        for flip, ref in ((0, own_ref), (1, other_ref)):
            for mask in range(n_chip):
                row = (place_ref[0] ^ mask) * 2 + (place_ref[1] ^ flip)
                down = pl.ds(pl.multiple_of(row * size, size), size)
                for ahead in range(blocks // 2 + 1):
                    col = lax.rem(row + ahead, blocks)
                    along = pl.ds(pl.multiple_of(col * size, size), size)
                    tile = ref[mask, :, ahead * size : (ahead + 1) * size]
                    gram_ref[down, along] = tile
                    if 0 < ahead < blocks // 2:
                        gram_ref[along, down] = tile.astype(F32).T.astype(BF16)
        normed = normed_ref[...]
        other = half_other_ref[...].astype(F32)
        diagonal = jnp.mean(half_ref[...].astype(F32) * other, 1, keepdims=True)
        extra = (-2.0 * (1.0 - diagonal) - 2.0 * REDUNDANCY * diagonal) / batch
        grads = lax.dot_general(
            half_ref[...], gram_ref[...], ROWS_BY_ROWS, preferred_element_type=F32
        )
        grads = grads * (2.0 * REDUNDANCY / (batch * batch)) + extra * other
        grad_mean = jnp.mean(grads, 1, keepdims=True)
        grad_cross = jnp.mean(grads * normed, 1, keepdims=True)
        out_ref[...] = (
            inverse_ref[:, :1] * (grads - grad_mean - normed * grad_cross)
        ).astype(BF16)

    operands = [gram_own, gram_other, normed, half, half_other, inverse]
    out = like((rows, batch), BF16)
    (out_grad,) = run(
        body, place, operands, [whole(one) for one in operands], [out], [whole(out)],
        scratch=[pltpu.VMEM((batch, batch), BF16)], after=after,
        flops=2 * rows * batch * batch, moved=12 * rows * batch + 2 * batch * batch, limit=24,
    )
    return out_grad


def weight_grad_of(place, turned, pieces, base=None, after=()):
    depth, batch = turned.shape
    cols = pieces[0].shape[0]
    last = base is not None

    def body(place_ref, turned_ref, *refs):
        if last:
            base_ref, out_ref, square_ref = refs[4:]
        else:
            (out_ref,) = refs[4:]
        for index in range(4):

            @pl.when(pl.program_id(0) == index)
            def _():
                total = lax.dot_general(
                    turned_ref[...], refs[index][...], ROWS_BY_ROWS, preferred_element_type=F32
                )
                if last:
                    total += base_ref[...]
                    square = fold(total * total)
                    square_ref[...] = square if index == 0 else square_ref[...] + square
                out_ref[...] = total

    tile = pl.BlockSpec((depth, cols), lambda j, s: (0, (j >> 1) * 2 + ((j & 1) ^ s[1])))
    square = pl.BlockSpec((8, 128), lambda j, s: (0, 0))
    operands = [turned, *pieces]
    return run(
        body, place, operands + ([base] if last else []),
        [whole(one) for one in operands] + ([tile] if last else []),
        [like((depth, 4 * cols), F32)] + ([like((8, 128), F32)] if last else []),
        [tile] + ([square] if last else []), grid=(4,), after=after,
        flops=8 * cols * batch * depth, moved=16 * depth * cols * (2 if last else 1), limit=32,
    )


def per_device(view_features, weight, velocity):
    n_dp, n_feat = lax.axis_size("dp"), lax.axis_size("feat")
    n_chip = n_dp // 2
    assert n_chip == n_feat and view_features.shape[2] == 2 * weight.shape[0]
    high = list(range(1, n_dp.bit_length() - 1))
    orders = (high, high[::-1])
    chip, core = lax.axis_index("dp") >> 1, bit_value("dp", 0)
    place = jnp.stack([chip, core])

    def bits_at(level):
        return jnp.stack([bit_value("dp", order[level]) for order in orders])

    shares = [None] * 2
    shares[1] = go_round(share_of(view_features, 1))
    shares[0] = go_round(share_of(view_features, 0, after=[shares[1][-2]]))
    sent, sent_squares = turn_weight(weight, 1 - core)
    turned_other = swap(sent, "dp", 1)
    turned_own, own_squares = turn_weight(weight, core)
    weight_squares = sent_squares + own_squares

    turned, gram, normed, half, inverse = ([None] * 2 for _ in range(5))
    ahead = ()
    for v in (1, 0):
        own = list(choose(shares[v], n_chip, after=ahead[:1]))
        for mask in range(1, n_chip):
            own[mask] = swap(own[mask], "dp", 2 * mask)
        other = [swap(piece, "dp", 1) for piece in own]
        columns = assemble(place, own, other, after=ahead)
        turned[v] = turn_columns(columns)
        bits = bits_at(0)
        send = forward(1 - bits, turned_own, turned_other, columns)
        ahead = [send[0]]
        got = [swap(send[p], "dp", 1 << orders[p][0]) for p in range(2)]
        keep = forward(bits, turned_own, turned_other, columns)
        for level in range(1, len(high)):
            send, keep = add_halves(bits_at(level), keep, got)
            got = [swap(send[p], "dp", 1 << orders[p][level]) for p in range(2)]
        normed[v], half[v], inverse[v] = normalise(keep, got)
        rows = list(gram_rows(place, half[v], swap(half[v], "dp", 1), n_chip))
        ahead.append(rows[0])
        total = rows[0].astype(F32)
        for mask in range(1, n_chip):
            total += swap(rows[mask], "dp", 2 * mask).astype(F32)
        total = total.astype(BF16)
        for bit in range(n_feat.bit_length() - 1):
            total = (total.astype(F32) + swap(total, "feat", 1 << bit).astype(F32)).astype(BF16)
        gram_own = jnp.stack(
            [total] + [swap(total, "dp", 2 * mask) for mask in range(1, n_chip)]
        )
        gram[v] = (gram_own, swap(gram_own, "dp", 1))

    result = []
    for v in (0, 1):
        out_grad = out_grad_of(place, *gram[1 - v], normed[v], half[v], half[1 - v], inverse[v])
        share = out_grad.shape[0] // 2
        pieces = []
        for path in range(2):
            own = out_grad[path * share : (path + 1) * share]
            for bit in reversed(orders[path]):
                own = join(own, swap(own, "dp", 1 << bit), bit_value("dp", bit))
            pieces += [own, swap(own, "dp", 1)]
        result = weight_grad_of(place, turned[v], pieces, *result)
    weight_grad, squares = result
    sums = sum_everywhere(jnp.stack([jnp.sum(weight_squares), jnp.sum(squares)]))
    trust = jnp.sqrt(sums[0]) / (jnp.sqrt(sums[1]) + NORM_EPSILON)
    new_velocity = MOMENTUM * velocity + trust * weight_grad
    new_weight = weight - LEARN_RATE * new_velocity
    return (new_weight, new_velocity)


def solution(mesh):
    in_specs = (P(None, "dp", "feat"), P("dp", "feat"), P("dp", "feat"))
    out_specs = (P("dp", "feat"), P("dp", "feat"))
    return jax.shard_map(
        per_device, mesh=mesh, in_specs=in_specs, out_specs=out_specs, check_vma=False
    )
```

time: 544 us -> 332 us (0.61)
  waiting for transfers between devices: 324 us -> 165 us
  blocking collectives: 73.2 us -> 0 us
  starting transfers between devices: 4.1 us -> 62.7 us
  Pallas kernels: 0 us -> 52.6 us
  matrix products: 51 us -> 0 us
  local copies, waits for them, and re-layouts: 41 us -> 19 us
  between operations: 15.5 us -> 2.92 us
  other arithmetic: 33.4 us -> 25 us
    ppermute x0 -> x71, waiting for transfers between devices: none -> 165 us  [the longest x65 103 us: swap(): lax.ppermute(value, axis, [(i, i ^ mask) for i in range(lax.axis_size(axi...]
    psum x1 -> x0, waiting for transfers between devices: 142 us -> none  [per_device(): gram[v] = lax.psum(partial.astype(jnp.bfloat16), ('dp', 'feat'))]
    all_gather x4 -> x0, waiting for transfers between devices: 103 us -> none  [the longest x2 59.7 us: per_device(): rows = lax.all_gather(pieces, 'feat', axis=0, tiled=True)]
    reduce_scatter x2 -> x0, waiting for transfers between devices: 65.4 us -> none  [per_device(): lax.psum_scatter(block, 'dp', scatter_dimension=0, tiled=True)]
    ppermute x0 -> x71, starting transfers between devices: none -> 62.7 us  [the longest x65 59.5 us: swap(): lax.ppermute(value, axis, [(i, i ^ mask) for i in range(lax.axis_size(axi...]
    pallas_call x0 -> x24, Pallas kernels: none -> 52.6 us  [run(): pl.pallas_call(kernel, grid_spec=pltpu.PrefetchScalarGridSpec(num_scalar_...]
    dot_general x10 -> x0, matrix products: 51 us -> none  [the longest x2 22.7 us: per_device(): jnp.einsum('nk,fn->kf', columns[v], gathered, preferred_element_type=jnp....]
    psum x1 -> x0, blocking collectives: 39.8 us -> none  [per_device(): weight_sq, grad_sq = lax.psum((weight_local, grad_local), ('dp', 'feat'))]
  transfers between devices with their start and end apart: 8 -> 71, of which waited for: 8 -> 38; matrix products, arithmetic and copies ran while one was open for 12% -> 3% of each run, Pallas kernels for 0% -> 12%
where the time goes in v2:
time: 332 us; the launch traced here: 327 us
  waiting for transfers between devices  165 us (50%)
  starting transfers between devices  62.7 us (19%)
  Pallas kernels  52.6 us (16%)
  other arithmetic  25 us (8%)
  local copies, waits for them, and re-layouts  19 us (6%)
    ppermute x65, waiting for transfers between devices, swap(): lax.ppermute(value, axis, [(i, i ^ mask) for i in range(lax.axis_size(axi...  103 us
    ppermute x6, waiting for transfers between devices, go_round(): shares.append(lax.ppermute(shares[-1], 'feat', ring))  61.3 us
    ppermute x65, starting transfers between devices, swap(): lax.ppermute(value, axis, [(i, i ^ mask) for i in range(lax.axis_size(axi...  59.5 us
    pallas_call x24, Pallas kernels, run(): pl.pallas_call(kernel, grid_spec=pltpu.PrefetchScalarGridSpec(num_scalar_...  52.6 us
    unnamed x30, local copies, waits for them, and re-layouts  17.7 us
    sub x1, other arithmetic, per_device(): new_weight = weight - LEARN_RATE * new_velocity  14.4 us
  transfers between devices with their start and end apart: 71, of which 38 were waited for; matrix products, arithmetic and copies ran while one was open for 3% of the time, Pallas kernels for 12%

profile of v2, /device:TPU:0, one launch (start us, length us, event | category | flops | bytes accessed | tf_op | source)
XLA Modules:
  0.0 326.9 jit_solution(16691333837604827076)
XLA Ops:
  1.9 3.1 collective-permute-start
  5.0 14.1 %collective-permute-done.refs_1_ = bf16[128,2048]{1,0:T(8,128)(2,1)} collective-permute-done((bf16[128,2048]{1,0:T(8,128)(2,1)S(1)}, bf16[128,2048]{1,0:T(8,128)(2,1)}, u32[]{:S(2)}, u32[]{:S(2)}) %collective-permute-start) | collective-permute-done | bytes 524320 | tf_op jit(solution)/shard_map/ppermute | solution.py:124
  19.0 3.4 %copy-done = f32[1024,2048]{1,0:T(8,128)S(1)} copy-done((f32[1024,2048]{1,0:T(8,128)S(1)}, f32[1024,2048]{1,0:T(8,128)}, u32[]{:S(2)}) %copy-start) | copy-done | bytes 8388632
  22.4 2.6 shard_map.50
  25.1 9.1 %collective-permute-done.1.refs_2_.refs_1_ = bf16[128,2048]{1,0:T(8,128)(2,1)S(1)} collective-permute-done((bf16[128,2048]{1,0:T(8,128)(2,1)}, bf16[128,2048]{1,0:T(8,128)(2,1)S(1)}, u32[]{:S(2)}, u32[]{:S(2)}) %collective-permute-start.1) | collective-permute-done | bytes 524320 | tf_op jit(solution)/shard_map/ppermute | solution.py:124
  35.0 17.0 %collective-permute-done.11.refs_1_ = bf16[128,2048]{1,0:T(8,128)(2,1)} collective-permute-done((bf16[128,2048]{1,0:T(8,128)(2,1)}, bf16[128,2048]{1,0:T(8,128)(2,1)}, u32[]{:S(2)}, u32[]{:S(2)}) %collective-permute-start.11) | collective-permute-done | bytes 524320 | tf_op jit(solution)/shard_map/ppermute | solution.py:124
  52.0 11.2 %collective-permute-done.2.refs_3_ = bf16[128,2048]{1,0:T(8,128)(2,1)} collective-permute-done((bf16[128,2048]{1,0:T(8,128)(2,1)S(1)}, bf16[128,2048]{1,0:T(8,128)(2,1)}, u32[]{:S(2)}, u32[]{:S(2)}) %collective-permute-start.2) | collective-permute-done | bytes 524320 | tf_op jit(solution)/shard_map/ppermute | solution.py:124
  63.2 2.8 shard_map.53
  69.4 2.2 collective-permute-done.12.refs_2_
  71.6 8.5 %collective-permute-done.3.refs_1_ = bf16[128,2048]{1,0:T(8,128)(2,1)S(1)} collective-permute-done((bf16[128,2048]{1,0:T(8,128)(2,1)S(1)}, bf16[128,2048]{1,0:T(8,128)(2,1)S(1)}, u32[]{:S(2)}, u32[]{:S(2)}) %collective-permute-start.3) | collective-permute-done | bytes 524320 | tf_op jit(solution)/shard_map/ppermute | solution.py:19
  80.2 6.1 %collective-permute-done.4.refs_2_ = bf16[128,2048]{1,0:T(8,128)(2,1)S(1)} collective-permute-done((bf16[128,2048]{1,0:T(8,128)(2,1)S(1)}, bf16[128,2048]{1,0:T(8,128)(2,1)S(1)}, u32[]{:S(2)}, u32[]{:S(2)}) %collective-permute-start.4) | collective-permute-done | bytes 524320 | tf_op jit(solution)/shard_map/ppermute | solution.py:19
  86.8 3.4 %copy-done.1 = f32[1024,2048]{1,0:T(8,128)S(1)} copy-done((f32[1024,2048]{1,0:T(8,128)S(1)}, f32[1024,2048]{1,0:T(8,128)}, u32[]{:S(2)}) %copy-start.1) | copy-done | bytes 8388632
  90.2 1.8 shard_map.51
  92.1 2.6 shard_map.54.refs_0_.refs_4_
  94.8 3.0 shard_map.57
  97.8 1.7 collective-permute-start.22
  99.9 7.8 %collective-permute-done.13.refs_3_ = bf16[128,2048]{1,0:T(8,128)(2,1)S(1)} collective-permute-done((bf16[128,2048]{1,0:T(8,128)(2,1)S(1)}, bf16[128,2048]{1,0:T(8,128)(2,1)S(1)}, u32[]{:S(2)}, u32[]{:S(2)}) %collective-permute-start.13) | collective-permute-done | bytes 524320 | tf_op jit(solution)/shard_map/ppermute | solution.py:124
  107.7 2.1 shard_map.58
  113.5 3.0 shard_map.59
  119.4 21.9 %collective-permute-done.23.refs_1_ = bf16[128,1024]{1,0:T(8,128)(2,1)S(1)} collective-permute-done((bf16[128,1024]{1,0:T(8,128)(2,1)S(1)}, bf16[128,1024]{1,0:T(8,128)(2,1)S(1)}, u32[]{:S(2)}, u32[]{:S(2)}) %collective-permute-start.23) | collective-permute-done | bytes 262176 | tf_op jit(solution)/shard_map/ppermute | solution.py:19
  148.5 3.0 shard_map.65
  153.4 3.0 shard_map.64
  156.4 9.1 %collective-permute-done.26.refs_1_ = bf16[256,1024]{1,0:T(8,128)(2,1)S(1)} collective-permute-done((bf16[256,1024]{1,0:T(8,128)(2,1)S(1)}, bf16[256,1024]{1,0:T(8,128)(2,1)S(1)}, u32[]{:S(2)}, u32[]{:S(2)}) %collective-permute-start.26) | collective-permute-done | bytes 524320 | tf_op jit(solution)/shard_map/ppermute | solution.py:19
  171.9 3.7 %collective-permute-done.28.refs_1_ = bf16[128,1024]{1,0:T(8,128)(2,1)S(1)} collective-permute-done((bf16[128,1024]{1,0:T(8,128)(2,1)S(1)}, bf16[128,1024]{1,0:T(8,128)(2,1)S(1)}, u32[]{:S(2)}, u32[]{:S(2)}) %collective-permute-start.28) | collective-permute-done | bytes 262176 | tf_op jit(solution)/shard_map/ppermute | solution.py:19
  177.6 2.5 collective-permute-done.46
  180.1 2.0 collective-permute-done.48
  185.5 1.7 collective-permute-start.33
  187.6 3.6 %collective-permute-start.50 = (bf16[128,640]{1,0:T(8,128)(2,1)S(1)}, bf16[128,640]{1,0:T(8,128)(2,1)S(1)}, u32[]{:S(2)}, u32[]{:S(2)}) collective-permute-start(bf16[128,640]{1,0:T(8,128)(2,1)S(1)} %add_convert_fusion.1), channel_id=1, source_target_pairs={{0,2},{1,3},{2,0},{3,1},{4,6},{5,7},{6,4},{7,5},{8,10},{9,11},{10,... | collective-permute-start | bytes 491528 | tf_op jit(solution)/shard_map/ppermute | solution.py:19
  192.2 2.1 collective-permute-start.34
  194.3 2.0 collective-permute-done.50
  200.0 2.8 collective-permute-start.35
  204.9 2.9 collective-permute-done.35
  211.5 2.9 collective-permute-done.38
  216.4 2.3 shard_map.71
  221.2 7.3 %collective-permute-done.58 = bf16[128,1024]{1,0:T(8,128)(2,1)} collective-permute-done((bf16[128,1024]{1,0:T(8,128)(2,1)}, bf16[128,1024]{1,0:T(8,128)(2,1)}, u32[]{:S(2)}, u32[]{:S(2)}) %collective-permute-start.58) | collective-permute-done | bytes 262176 | tf_op jit(solution)/shard_map/ppermute | solution.py:19
  232.1 2.3 shard_map.69
  239.0 4.7 %collective-permute-done.43 = bf16[128,1024]{1,0:T(8,128)(2,1)S(1)} collective-permute-done((bf16[128,1024]{1,0:T(8,128)(2,1)S(1)}, bf16[128,1024]{1,0:T(8,128)(2,1)S(1)}, u32[]{:S(2)}, u32[]{:S(2)}) %collective-permute-start.43) | collective-permute-done | bytes 262176 | tf_op jit(solution)/shard_map/ppermute | solution.py:19
  245.0 5.3 %collective-permute-done.40 = bf16[128,1024]{1,0:T(8,128)(2,1)S(1)} collective-permute-done((bf16[128,1024]{1,0:T(8,128)(2,1)S(1)}, bf16[128,1024]{1,0:T(8,128)(2,1)S(1)}, u32[]{:S(2)}, u32[]{:S(2)}) %collective-permute-start.40) | collective-permute-done | bytes 262176 | tf_op jit(solution)/shard_map/ppermute | solution.py:19
  255.5 4.8 %collective-permute-done.44 = bf16[256,1024]{1,0:T(8,128)(2,1)S(1)} collective-permute-done((bf16[256,1024]{1,0:T(8,128)(2,1)S(1)}, bf16[256,1024]{1,0:T(8,128)(2,1)S(1)}, u32[]{:S(2)}, u32[]{:S(2)}) %collective-permute-start.44) | collective-permute-done | bytes 524320 | tf_op jit(solution)/shard_map/ppermute | solution.py:19
  260.8 3.7 %collective-permute-done.41 = bf16[256,1024]{1,0:T(8,128)(2,1)S(1)} collective-permute-done((bf16[256,1024]{1,0:T(8,128)(2,1)S(1)}, bf16[256,1024]{1,0:T(8,128)(2,1)S(1)}, u32[]{:S(2)}, u32[]{:S(2)}) %collective-permute-start.41) | collective-permute-done | bytes 524320 | tf_op jit(solution)/shard_map/ppermute | solution.py:19
  269.2 6.4 %shard_map.72.refs_5_ = f32[1024,2048]{1,0:T(8,128)S(1)} custom-call(s32[2]{0:T(128)S(1)} %pad_add_fusion.scalars_ref, bf16[1024,1024]{1,0:T(8,128)(2,1)S(1)} %shard_map.70.refs_0_, bf16[512,1024]{1,0:T(8,128)(2,1)S(1)} %maximum_select_fusion.2.refs_1_, bf16[512,1024]{1,0:T(8,128)(2,1)S(1)} %collective-permute-done.57.refs_2_, ...), custom_call_target="tpu_custom_call" | custom-call | flops 4294967296 | bytes 8388608 | tf_op jit(solution)/shard_map/pallas_call | solution.py:56
  275.6 3.4 %copy-done.13 = f32[1024,2048]{1,0:T(8,128)} copy-done((f32[1024,2048]{1,0:T(8,128)}, f32[1024,2048]{1,0:T(8,128)S(1)}, u32[]{:S(2)}) %copy-start.13) | copy-done | bytes 8388632
  279.0 8.2 %shard_map.73 = (f32[1024,2048]{1,0:T(8,128)S(1)}, f32[8,128]{1,0:T(8,128)S(1)}) custom-call(s32[2]{0:T(128)S(1)} %pad_add_fusion.scalars_ref, bf16[1024,1024]{1,0:T(8,128)(2,1)S(1)} %shard_map.55.refs_0_, bf16[512,1024]{1,0:T(8,128)(2,1)S(1)} %maximum_select_fusion.refs_1_, bf16[512,1024]{1,0:T(8,128)(2,1)S(1)} %collective-permute-done.42.refs_2_, ...), custom_call_target="tpu_custom_call" | custom-call | flops 4294967296 | bytes 16777216 | tf_op jit(solution)/shard_map/pallas_call | solution.py:56
  287.2 3.4 %copy-done.6 = f32[1024,2048]{1,0:T(8,128)} copy-done((f32[1024,2048]{1,0:T(8,128)}, f32[1024,2048]{1,0:T(8,128)S(1)}, u32[]{:S(2)}) %copy-start.6) | copy-done | bytes 8388632
  292.4 1.7 collective-permute-start.66
  302.8 2.9 collective-permute-start.70
  308.1 2.0 collective-permute-done.69
  312.1 14.4 %multiply_subtract_fusion = (f32[1024,2048]{1,0:T(8,128)}, f32[1024,2048]{1,0:T(8,128)}) fusion(f32[1024,2048]{1,0:T(8,128)} %refs_0_.5, f32[1024,2048]{1,0:T(8,128)} %copy-done.6, f32[]{:T(128)} %bitcast.19, f32[1024,2048]{1,0:T(8,128)} %param.5), kind=kLoop, calls=%fused_computation | loop fusion | flops 10485760 | bytes 41943044 | tf_op jit(solution)/shard_map/sub | solution.py:435
  (177 shorter events, 82.6 us)
Async XLA Ops:
  1.9 17.1 %collective-permute-start = (bf16[128,2048]{1,0:T(8,128)(2,1)S(1)}, bf16[128,2048]{1,0:T(8,128)(2,1)}, u32[]{:S(2)}, u32[]{:S(2)}) collective-permute-start(bf16[128,2048]{1,0:T(8,128)(2,1)S(1)} %shard_map.52.refs_0_), channel_id=1, source_target_pairs={{0,1},{1,2},{2,3},{3,0},{4,5},{5,6},{6,7},{7,4},{8,9},{9,10},{10,1... | collective-permute-start | bytes 1572872 | tf_op jit(solution)/shard_map/ppermute | solution.py:124
  19.0 15.1 %collective-permute-start.1 = (bf16[128,2048]{1,0:T(8,128)(2,1)}, bf16[128,2048]{1,0:T(8,128)(2,1)S(1)}, u32[]{:S(2)}, u32[]{:S(2)}) collective-permute-start(bf16[128,2048]{1,0:T(8,128)(2,1)} %collective-permute-done.refs_1_), channel_id=1, source_target_pairs={{0,1},{1,2},{2,3},{3,0},{4,5},{5,6},{6,7},{7,4},{8,9},{9,10},{10,1... | collective-permute-start | bytes 1572872 | tf_op jit(solution)/shard_map/ppermute | solution.py:124
  25.1 69.7 %collective-permute-start.10 = (bf16[1024,1024]{1,0:T(8,128)(2,1)}, bf16[1024,1024]{1,0:T(8,128)(2,1)S(1)}, u32[]{:S(2)}, u32[]{:S(2)}) collective-permute-start(bf16[1024,1024]{1,0:T(8,128)(2,1)} %get-tuple-element.53), channel_id=1, source_target_pairs={{0,4},{4,0},{8,12},{12,8},{16,20},{20,16},{24,28},{28,24},{1,5},{5... | collective-permute-start | bytes 6291464 | tf_op jit(solution)/shard_map/ppermute | solution.py:19
  35.0 17.0 %collective-permute-start.11 = (bf16[128,2048]{1,0:T(8,128)(2,1)}, bf16[128,2048]{1,0:T(8,128)(2,1)}, u32[]{:S(2)}, u32[]{:S(2)}) collective-permute-start(bf16[128,2048]{1,0:T(8,128)(2,1)} %shard_map.56.refs_0_), channel_id=1, source_target_pairs={{0,1},{1,2},{2,3},{3,0},{4,5},{5,6},{6,7},{7,4},{8,9},{9,10},{10,1... | collective-permute-start | bytes 1572872 | tf_op jit(solution)/shard_map/ppermute | solution.py:124
  35.0 28.2 %collective-permute-start.2 = (bf16[128,2048]{1,0:T(8,128)(2,1)S(1)}, bf16[128,2048]{1,0:T(8,128)(2,1)}, u32[]{:S(2)}, u32[]{:S(2)}) collective-permute-start(bf16[128,2048]{1,0:T(8,128)(2,1)S(1)} %collective-permute-done.1.refs_2_.refs_1_), channel_id=1, source_target_pairs={{0,1},{1,2},{2,3},{3,0},{4,5},{5,6},{6,7},{7,4},{8,9},{9,10},{10,1... | collective-permute-start | bytes 1572872 | tf_op jit(solution)/shard_map/ppermute | solution.py:124
  51.9 19.7 %collective-permute-start.12 = (bf16[128,2048]{1,0:T(8,128)(2,1)}, bf16[128,2048]{1,0:T(8,128)(2,1)S(1)}, u32[]{:S(2)}, u32[]{:S(2)}) collective-permute-start(bf16[128,2048]{1,0:T(8,128)(2,1)} %collective-permute-done.11.refs_1_), channel_id=1, source_target_pairs={{0,1},{1,2},{2,3},{3,0},{4,5},{5,6},{6,7},{7,4},{8,9},{9,10},{10,1... | collective-permute-start | bytes 1572872 | tf_op jit(solution)/shard_map/ppermute | solution.py:124
  66.0 14.2 %collective-permute-start.3 = (bf16[128,2048]{1,0:T(8,128)(2,1)S(1)}, bf16[128,2048]{1,0:T(8,128)(2,1)S(1)}, u32[]{:S(2)}, u32[]{:S(2)}) collective-permute-start(bf16[128,2048]{1,0:T(8,128)(2,1)S(1)} %get-tuple-element.49), channel_id=1, source_target_pairs={{0,8},{4,12},{8,0},{12,4},{16,24},{20,28},{24,16},{28,20},{1,9},{5... | collective-permute-start | bytes 1572872 | tf_op jit(solution)/shard_map/ppermute | solution.py:19
  67.2 19.1 %collective-permute-start.4 = (bf16[128,2048]{1,0:T(8,128)(2,1)S(1)}, bf16[128,2048]{1,0:T(8,128)(2,1)S(1)}, u32[]{:S(2)}, u32[]{:S(2)}) collective-permute-start(bf16[128,2048]{1,0:T(8,128)(2,1)S(1)} %get-tuple-element.50), channel_id=1, source_target_pairs={{0,16},{4,20},{8,24},{12,28},{16,0},{20,4},{24,8},{28,12},{1,17},{... | collective-permute-start | bytes 1572872 | tf_op jit(solution)/shard_map/ppermute | solution.py:19
  68.7 17.6 %collective-permute-start.5 = (bf16[128,2048]{1,0:T(8,128)(2,1)S(1)}, bf16[128,2048]{1,0:T(8,128)(2,1)}, u32[]{:S(2)}, u32[]{:S(2)}) collective-permute-start(bf16[128,2048]{1,0:T(8,128)(2,1)S(1)} %get-tuple-element.51), channel_id=1, source_target_pairs={{0,24},{4,28},{8,16},{12,20},{16,8},{20,12},{24,0},{28,4},{1,25},{... | collective-permute-start | bytes 1572872 | tf_op jit(solution)/shard_map/ppermute | solution.py:19
  71.6 20.4 %collective-permute-start.6 = (bf16[128,2048]{1,0:T(8,128)(2,1)}, bf16[128,2048]{1,0:T(8,128)(2,1)}, u32[]{:S(2)}, u32[]{:S(2)}) collective-permute-start(bf16[128,2048]{1,0:T(8,128)(2,1)} %get-tuple-element.48.refs_0_), channel_id=1, source_target_pairs={{0,4},{4,0},{8,12},{12,8},{16,20},{20,16},{24,28},{28,24},{1,5},{5... | collective-permute-start | bytes 1572872 | tf_op jit(solution)/shard_map/ppermute | solution.py:19
  80.2 12.0 %collective-permute-start.7 = (bf16[128,2048]{1,0:T(8,128)(2,1)S(1)}, bf16[128,2048]{1,0:T(8,128)(2,1)}, u32[]{:S(2)}, u32[]{:S(2)}) collective-permute-start(bf16[128,2048]{1,0:T(8,128)(2,1)S(1)} %collective-permute-done.3.refs_1_), channel_id=1, source_target_pairs={{0,4},{4,0},{8,12},{12,8},{16,20},{20,16},{24,28},{28,24},{1,5},{5... | collective-permute-start | bytes 1572872 | tf_op jit(solution)/shard_map/ppermute | solution.py:19
  92.0 15.7 %collective-permute-start.13 = (bf16[128,2048]{1,0:T(8,128)(2,1)S(1)}, bf16[128,2048]{1,0:T(8,128)(2,1)S(1)}, u32[]{:S(2)}, u32[]{:S(2)}) collective-permute-start(bf16[128,2048]{1,0:T(8,128)(2,1)S(1)} %copy-done.12), channel_id=1, source_target_pairs={{0,1},{1,2},{2,3},{3,0},{4,5},{5,6},{6,7},{7,4},{8,9},{9,10},{10,1... | collective-permute-start | bytes 1572872 | tf_op jit(solution)/shard_map/ppermute | solution.py:124
  97.8 18.7 %collective-permute-start.22 = (bf16[256,1024]{1,0:T(8,128)(2,1)S(1)}, bf16[256,1024]{1,0:T(8,128)(2,1)S(1)}, u32[]{:S(2)}, u32[]{:S(2)}) collective-permute-start(bf16[256,1024]{1,0:T(8,128)(2,1)S(1)} %get-tuple-element.61), channel_id=1, source_target_pairs={{0,16},{4,20},{8,24},{12,28},{16,0},{20,4},{24,8},{28,12},{1,17},{... | collective-permute-start | bytes 1572872 | tf_op jit(solution)/shard_map/ppermute | solution.py:19
  99.5 17.1 %collective-permute-start.21 = (bf16[256,1024]{1,0:T(8,128)(2,1)S(1)}, bf16[256,1024]{1,0:T(8,128)(2,1)S(1)}, u32[]{:S(2)}, u32[]{:S(2)}) collective-permute-start(bf16[256,1024]{1,0:T(8,128)(2,1)S(1)} %get-tuple-element.54.refs_4_.refs_8_), channel_id=1, source_target_pairs={{0,8},{4,12},{8,0},{12,4},{16,24},{20,28},{24,16},{28,20},{1,9},{5... | collective-permute-start | bytes 1572872 | tf_op jit(solution)/shard_map/ppermute | solution.py:19
  109.9 33.3 %collective-permute-start.14 = (bf16[128,2048]{1,0:T(8,128)(2,1)S(1)}, bf16[128,2048]{1,0:T(8,128)(2,1)S(1)}, u32[]{:S(2)}, u32[]{:S(2)}) collective-permute-start(bf16[128,2048]{1,0:T(8,128)(2,1)S(1)} %get-tuple-element.56), channel_id=1, source_target_pairs={{0,8},{4,12},{8,0},{12,4},{16,24},{20,28},{24,16},{28,20},{1,9},{5... | collective-permute-start | bytes 1572872 | tf_op jit(solution)/shard_map/ppermute | solution.py:19
  111.2 32.0 %collective-permute-start.15 = (bf16[128,2048]{1,0:T(8,128)(2,1)S(1)}, bf16[128,2048]{1,0:T(8,128)(2,1)S(1)}, u32[]{:S(2)}, u32[]{:S(2)}) collective-permute-start(bf16[128,2048]{1,0:T(8,128)(2,1)S(1)} %get-tuple-element.57), channel_id=1, source_target_pairs={{0,16},{4,20},{8,24},{12,28},{16,0},{20,4},{24,8},{28,12},{1,17},{... | collective-permute-start | bytes 1572872 | tf_op jit(solution)/shard_map/ppermute | solution.py:19
  112.0 31.8 %collective-permute-start.16 = (bf16[128,2048]{1,0:T(8,128)(2,1)S(1)}, bf16[128,2048]{1,0:T(8,128)(2,1)S(1)}, u32[]{:S(2)}, u32[]{:S(2)}) collective-permute-start(bf16[128,2048]{1,0:T(8,128)(2,1)S(1)} %get-tuple-element.58), channel_id=1, source_target_pairs={{0,24},{4,28},{8,16},{12,20},{16,8},{20,12},{24,0},{28,4},{1,25},{... | collective-permute-start | bytes 1572872 | tf_op jit(solution)/shard_map/ppermute | solution.py:19
  117.3 24.0 %collective-permute-start.23 = (bf16[128,1024]{1,0:T(8,128)(2,1)S(1)}, bf16[128,1024]{1,0:T(8,128)(2,1)S(1)}, u32[]{:S(2)}, u32[]{:S(2)}) collective-permute-start(bf16[128,1024]{1,0:T(8,128)(2,1)S(1)} %get-tuple-element.63), channel_id=1, source_target_pairs={{0,16},{4,20},{8,24},{12,28},{16,0},{20,4},{24,8},{28,12},{1,17},{... | collective-permute-start | bytes 786440 | tf_op jit(solution)/shard_map/ppermute | solution.py:19
  119.0 22.4 %collective-permute-start.24 = (bf16[128,1024]{1,0:T(8,128)(2,1)S(1)}, bf16[128,1024]{1,0:T(8,128)(2,1)S(1)}, u32[]{:S(2)}, u32[]{:S(2)}) collective-permute-start(bf16[128,1024]{1,0:T(8,128)(2,1)S(1)} %get-tuple-element.65), channel_id=1, source_target_pairs={{0,8},{4,12},{8,0},{12,4},{16,24},{20,28},{24,16},{28,20},{1,9},{5... | collective-permute-start | bytes 786440 | tf_op jit(solution)/shard_map/ppermute | solution.py:19
  151.5 14.0 %collective-permute-start.26 = (bf16[256,1024]{1,0:T(8,128)(2,1)S(1)}, bf16[256,1024]{1,0:T(8,128)(2,1)S(1)}, u32[]{:S(2)}, u32[]{:S(2)}) collective-permute-start(bf16[256,1024]{1,0:T(8,128)(2,1)S(1)} %get-tuple-element.69), channel_id=1, source_target_pairs={{0,8},{4,12},{8,0},{12,4},{16,24},{20,28},{24,16},{28,20},{1,9},{5... | collective-permute-start | bytes 1572872 | tf_op jit(solution)/shard_map/ppermute | solution.py:19
  151.9 13.7 %collective-permute-start.27 = (bf16[256,1024]{1,0:T(8,128)(2,1)S(1)}, bf16[256,1024]{1,0:T(8,128)(2,1)S(1)}, u32[]{:S(2)}, u32[]{:S(2)}) collective-permute-start(bf16[256,1024]{1,0:T(8,128)(2,1)S(1)} %get-tuple-element.71), channel_id=1, source_target_pairs={{0,16},{4,20},{8,24},{12,28},{16,0},{20,4},{24,8},{28,12},{1,17},{... | collective-permute-start | bytes 1572872 | tf_op jit(solution)/shard_map/ppermute | solution.py:19
  166.4 9.3 %collective-permute-start.28 = (bf16[128,1024]{1,0:T(8,128)(2,1)S(1)}, bf16[128,1024]{1,0:T(8,128)(2,1)S(1)}, u32[]{:S(2)}, u32[]{:S(2)}) collective-permute-start(bf16[128,1024]{1,0:T(8,128)(2,1)S(1)} %get-tuple-element.73), channel_id=1, source_target_pairs={{0,16},{4,20},{8,24},{12,28},{16,0},{20,4},{24,8},{28,12},{1,17},{... | collective-permute-start | bytes 786440 | tf_op jit(solution)/shard_map/ppermute | solution.py:19
  167.9 9.2 %collective-permute-start.29 = (bf16[128,1024]{1,0:T(8,128)(2,1)S(1)}, bf16[128,1024]{1,0:T(8,128)(2,1)S(1)}, u32[]{:S(2)}, u32[]{:S(2)}) collective-permute-start(bf16[128,1024]{1,0:T(8,128)(2,1)S(1)} %get-tuple-element.75), channel_id=1, source_target_pairs={{0,8},{4,12},{8,0},{12,4},{16,24},{20,28},{24,16},{28,20},{1,9},{5... | collective-permute-start | bytes 786440 | tf_op jit(solution)/shard_map/ppermute | solution.py:19
  168.4 11.7 %collective-permute-start.46 = (bf16[128,640]{1,0:T(8,128)(2,1)S(1)}, bf16[128,640]{1,0:T(8,128)(2,1)S(1)}, u32[]{:S(2)}, u32[]{:S(2)}) collective-permute-start(bf16[128,640]{1,0:T(8,128)(2,1)S(1)} %get-tuple-element.83), channel_id=1, source_target_pairs={{0,8},{4,12},{8,0},{12,4},{16,24},{20,28},{24,16},{28,20},{1,9},{5... | collective-permute-start | bytes 491528 | tf_op jit(solution)/shard_map/ppermute | solution.py:19
  169.9 10.2 %collective-permute-start.47 = (bf16[128,640]{1,0:T(8,128)(2,1)S(1)}, bf16[128,640]{1,0:T(8,128)(2,1)S(1)}, u32[]{:S(2)}, u32[]{:S(2)}) collective-permute-start(bf16[128,640]{1,0:T(8,128)(2,1)S(1)} %get-tuple-element.84), channel_id=1, source_target_pairs={{0,16},{4,20},{8,24},{12,28},{16,0},{20,4},{24,8},{28,12},{1,17},{... | collective-permute-start | bytes 491528 | tf_op jit(solution)/shard_map/ppermute | solution.py:19
  170.5 11.6 %collective-permute-start.48 = (bf16[128,640]{1,0:T(8,128)(2,1)S(1)}, bf16[128,640]{1,0:T(8,128)(2,1)S(1)}, u32[]{:S(2)}, u32[]{:S(2)}) collective-permute-start(bf16[128,640]{1,0:T(8,128)(2,1)S(1)} %get-tuple-element.85), channel_id=1, source_target_pairs={{0,24},{4,28},{8,16},{12,20},{16,8},{20,12},{24,0},{28,4},{1,25},{... | collective-permute-start | bytes 491528 | tf_op jit(solution)/shard_map/ppermute | solution.py:19
  183.6 7.6 %collective-permute-start.31 = (bf16[128,640]{1,0:T(8,128)(2,1)S(1)}, bf16[128,640]{1,0:T(8,128)(2,1)S(1)}, u32[]{:S(2)}, u32[]{:S(2)}) collective-permute-start(bf16[128,640]{1,0:T(8,128)(2,1)S(1)} %get-tuple-element.78), channel_id=1, source_target_pairs={{0,8},{4,12},{8,0},{12,4},{16,24},{20,28},{24,16},{28,20},{1,9},{5... | collective-permute-start | bytes 491528 | tf_op jit(solution)/shard_map/ppermute | solution.py:19
  185.1 7.1 %collective-permute-start.32 = (bf16[128,640]{1,0:T(8,128)(2,1)S(1)}, bf16[128,640]{1,0:T(8,128)(2,1)S(1)}, u32[]{:S(2)}, u32[]{:S(2)}) collective-permute-start(bf16[128,640]{1,0:T(8,128)(2,1)S(1)} %get-tuple-element.79), channel_id=1, source_target_pairs={{0,16},{4,20},{8,24},{12,28},{16,0},{20,4},{24,8},{28,12},{1,17},{... | collective-permute-start | bytes 491528 | tf_op jit(solution)/shard_map/ppermute | solution.py:19
  185.5 6.7 %collective-permute-start.33 = (bf16[128,640]{1,0:T(8,128)(2,1)S(1)}, bf16[128,640]{1,0:T(8,128)(2,1)S(1)}, u32[]{:S(2)}, u32[]{:S(2)}) collective-permute-start(bf16[128,640]{1,0:T(8,128)(2,1)S(1)} %get-tuple-element.80), channel_id=1, source_target_pairs={{0,24},{4,28},{8,16},{12,20},{16,8},{20,12},{24,0},{28,4},{1,25},{... | collective-permute-start | bytes 491528 | tf_op jit(solution)/shard_map/ppermute | solution.py:19
  187.6 8.7 %collective-permute-start.50 = (bf16[128,640]{1,0:T(8,128)(2,1)S(1)}, bf16[128,640]{1,0:T(8,128)(2,1)S(1)}, u32[]{:S(2)}, u32[]{:S(2)}) collective-permute-start(bf16[128,640]{1,0:T(8,128)(2,1)S(1)} %add_convert_fusion.1), channel_id=1, source_target_pairs={{0,2},{1,3},{2,0},{3,1},{4,6},{5,7},{6,4},{7,5},{8,10},{9,11},{10,... | collective-permute-start | bytes 491528 | tf_op jit(solution)/shard_map/ppermute | solution.py:19
  192.2 7.7 %collective-permute-start.34 = (bf16[128,640]{1,0:T(8,128)(2,1)S(1)}, bf16[128,640]{1,0:T(8,128)(2,1)S(1)}, u32[]{:S(2)}, u32[]{:S(2)}) collective-permute-start(bf16[128,640]{1,0:T(8,128)(2,1)S(1)} %add_convert_fusion.5), channel_id=1, source_target_pairs={{0,1},{1,0},{2,3},{3,2},{4,5},{5,4},{6,7},{7,6},{8,9},{9,8},{10,11... | collective-permute-start | bytes 491528 | tf_op jit(solution)/shard_map/ppermute | solution.py:19
  197.7 6.7 %collective-permute-start.52 = (bf16[128,640]{1,0:T(8,128)(2,1)S(1)}, bf16[128,640]{1,0:T(8,128)(2,1)S(1)}, u32[]{:S(2)}, u32[]{:S(2)}) collective-permute-start(bf16[128,640]{1,0:T(8,128)(2,1)S(1)} %add_convert_fusion), channel_id=1, source_target_pairs={{0,16},{4,20},{8,24},{12,28},{16,0},{20,4},{24,8},{28,12},{1,17},{... | collective-permute-start | bytes 491528 | tf_op jit(solution)/shard_map/ppermute | solution.py:19
  200.0 7.9 %collective-permute-start.35 = (bf16[128,640]{1,0:T(8,128)(2,1)S(1)}, bf16[128,640]{1,0:T(8,128)(2,1)S(1)}, u32[]{:S(2)}, u32[]{:S(2)}) collective-permute-start(bf16[128,640]{1,0:T(8,128)(2,1)S(1)} %add_convert_fusion.4), channel_id=1, source_target_pairs={{0,2},{1,3},{2,0},{3,1},{4,6},{5,7},{6,4},{7,5},{8,10},{9,11},{10,... | collective-permute-start | bytes 491528 | tf_op jit(solution)/shard_map/ppermute | solution.py:19
  204.6 11.8 %collective-permute-start.54 = (bf16[4,128,640]{2,1,0:T(8,128)(2,1)S(1)}, bf16[4,128,640]{2,1,0:T(8,128)(2,1)S(1)}, u32[]{:S(2)}, u32[]{:S(2)}) collective-permute-start(bf16[4,128,640]{2,1,0:T(8,128)(2,1)S(1)} %pad_maximum_fusion.1.refs_0_), channel_id=1, source_target_pairs={{0,4},{4,0},{8,12},{12,8},{16,20},{20,16},{24,28},{28,24},{1,5},{5... | collective-permute-start | bytes 1966088 | tf_op jit(solution)/shard_map/ppermute | solution.py:19
  209.2 6.8 %collective-permute-start.37 = (bf16[128,640]{1,0:T(8,128)(2,1)S(1)}, bf16[128,640]{1,0:T(8,128)(2,1)S(1)}, u32[]{:S(2)}, u32[]{:S(2)}) collective-permute-start(bf16[128,640]{1,0:T(8,128)(2,1)S(1)} %add_convert_fusion.3), channel_id=1, source_target_pairs={{0,16},{4,20},{8,24},{12,28},{16,0},{20,4},{24,8},{28,12},{1,17},{... | collective-permute-start | bytes 491528 | tf_op jit(solution)/shard_map/ppermute | solution.py:19
  216.3 14.5 %collective-permute-start.39 = (bf16[4,128,640]{2,1,0:T(8,128)(2,1)S(1)}, bf16[4,128,640]{2,1,0:T(8,128)(2,1)S(1)}, u32[]{:S(2)}, u32[]{:S(2)}) collective-permute-start(bf16[4,128,640]{2,1,0:T(8,128)(2,1)S(1)} %pad_maximum_fusion.refs_0_), channel_id=1, source_target_pairs={{0,4},{4,0},{8,12},{12,8},{16,20},{20,16},{24,28},{28,24},{1,5},{5... | collective-permute-start | bytes 1966088 | tf_op jit(solution)/shard_map/ppermute | solution.py:19
  219.4 9.0 %collective-permute-start.58 = (bf16[128,1024]{1,0:T(8,128)(2,1)}, bf16[128,1024]{1,0:T(8,128)(2,1)}, u32[]{:S(2)}, u32[]{:S(2)}) collective-permute-start(bf16[128,1024]{1,0:T(8,128)(2,1)} %get-tuple-element.94), channel_id=1, source_target_pairs={{0,8},{4,12},{8,0},{12,4},{16,24},{20,28},{24,16},{28,20},{1,9},{5... | collective-permute-start | bytes 786440 | tf_op jit(solution)/shard_map/ppermute | solution.py:19
  220.6 16.1 %collective-permute-start.55 = (bf16[128,1024]{1,0:T(8,128)(2,1)S(1)}, bf16[128,1024]{1,0:T(8,128)(2,1)}, u32[]{:S(2)}, u32[]{:S(2)}) collective-permute-start(bf16[128,1024]{1,0:T(8,128)(2,1)S(1)} %get-tuple-element.95), channel_id=1, source_target_pairs={{0,16},{4,20},{8,24},{12,28},{16,0},{20,4},{24,8},{28,12},{1,17},{... | collective-permute-start | bytes 786440 | tf_op jit(solution)/shard_map/ppermute | solution.py:19
  229.8 21.9 %collective-permute-start.59 = (bf16[256,1024]{1,0:T(8,128)(2,1)S(1)}, bf16[256,1024]{1,0:T(8,128)(2,1)}, u32[]{:S(2)}, u32[]{:S(2)}) collective-permute-start(bf16[256,1024]{1,0:T(8,128)(2,1)S(1)} %maximum_select_fusion.7), channel_id=1, source_target_pairs={{0,16},{4,20},{8,24},{12,28},{16,0},{20,4},{24,8},{28,12},{1,17},{... | collective-permute-start | bytes 1572872 | tf_op jit(solution)/shard_map/ppermute | solution.py:19
  234.4 9.3 %collective-permute-start.43 = (bf16[128,1024]{1,0:T(8,128)(2,1)S(1)}, bf16[128,1024]{1,0:T(8,128)(2,1)S(1)}, u32[]{:S(2)}, u32[]{:S(2)}) collective-permute-start(bf16[128,1024]{1,0:T(8,128)(2,1)S(1)} %get-tuple-element.96), channel_id=1, source_target_pairs={{0,8},{4,12},{8,0},{12,4},{16,24},{20,28},{24,16},{28,20},{1,9},{5... | collective-permute-start | bytes 786440 | tf_op jit(solution)/shard_map/ppermute | solution.py:19
  235.3 15.1 %collective-permute-start.40 = (bf16[128,1024]{1,0:T(8,128)(2,1)S(1)}, bf16[128,1024]{1,0:T(8,128)(2,1)S(1)}, u32[]{:S(2)}, u32[]{:S(2)}) collective-permute-start(bf16[128,1024]{1,0:T(8,128)(2,1)S(1)} %get-tuple-element.97), channel_id=1, source_target_pairs={{0,16},{4,20},{8,24},{12,28},{16,0},{20,4},{24,8},{28,12},{1,17},{... | collective-permute-start | bytes 786440 | tf_op jit(solution)/shard_map/ppermute | solution.py:19
  238.1 16.8 %collective-permute-start.56 = (bf16[256,1024]{1,0:T(8,128)(2,1)S(1)}, bf16[256,1024]{1,0:T(8,128)(2,1)S(1)}, u32[]{:S(2)}, u32[]{:S(2)}) collective-permute-start(bf16[256,1024]{1,0:T(8,128)(2,1)S(1)} %maximum_select_fusion.6), channel_id=1, source_target_pairs={{0,8},{4,12},{8,0},{12,4},{16,24},{20,28},{24,16},{28,20},{1,9},{5... | collective-permute-start | bytes 1572872 | tf_op jit(solution)/shard_map/ppermute | solution.py:19
  243.8 16.5 %collective-permute-start.44 = (bf16[256,1024]{1,0:T(8,128)(2,1)S(1)}, bf16[256,1024]{1,0:T(8,128)(2,1)S(1)}, u32[]{:S(2)}, u32[]{:S(2)}) collective-permute-start(bf16[256,1024]{1,0:T(8,128)(2,1)S(1)} %maximum_select_fusion.5), channel_id=1, source_target_pairs={{0,16},{4,20},{8,24},{12,28},{16,0},{20,4},{24,8},{28,12},{1,17},{... | collective-permute-start | bytes 1572872 | tf_op jit(solution)/shard_map/ppermute | solution.py:19
  250.5 14.1 %collective-permute-start.41 = (bf16[256,1024]{1,0:T(8,128)(2,1)S(1)}, bf16[256,1024]{1,0:T(8,128)(2,1)S(1)}, u32[]{:S(2)}, u32[]{:S(2)}) collective-permute-start(bf16[256,1024]{1,0:T(8,128)(2,1)S(1)} %maximum_select_fusion.4), channel_id=1, source_target_pairs={{0,8},{4,12},{8,0},{12,4},{16,24},{20,28},{24,16},{28,20},{1,9},{5... | collective-permute-start | bytes 1572872 | tf_op jit(solution)/shard_map/ppermute | solution.py:19
  253.4 15.8 %collective-permute-start.60 = (bf16[512,1024]{1,0:T(8,128)(2,1)S(1)}, bf16[512,1024]{1,0:T(8,128)(2,1)S(1)}, u32[]{:S(2)}, u32[]{:S(2)}) collective-permute-start(bf16[512,1024]{1,0:T(8,128)(2,1)S(1)} %maximum_select_fusion.3.refs_3_), channel_id=1, source_target_pairs={{0,4},{4,0},{8,12},{12,8},{16,20},{20,16},{24,28},{28,24},{1,5},{5... | collective-permute-start | bytes 3145736 | tf_op jit(solution)/shard_map/ppermute | solution.py:19
  255.4 13.7 %collective-permute-start.57 = (bf16[512,1024]{1,0:T(8,128)(2,1)S(1)}, bf16[512,1024]{1,0:T(8,128)(2,1)S(1)}, u32[]{:S(2)}, u32[]{:S(2)}) collective-permute-start(bf16[512,1024]{1,0:T(8,128)(2,1)S(1)} %maximum_select_fusion.2.refs_1_), channel_id=1, source_target_pairs={{0,4},{4,0},{8,12},{12,8},{16,20},{20,16},{24,28},{28,24},{1,5},{5... | collective-permute-start | bytes 3145736 | tf_op jit(solution)/shard_map/ppermute | solution.py:19
  260.8 18.2 %collective-permute-start.45 = (bf16[512,1024]{1,0:T(8,128)(2,1)S(1)}, bf16[512,1024]{1,0:T(8,128)(2,1)S(1)}, u32[]{:S(2)}, u32[]{:S(2)}) collective-permute-start(bf16[512,1024]{1,0:T(8,128)(2,1)S(1)} %maximum_select_fusion.1.refs_3_), channel_id=1, source_target_pairs={{0,4},{4,0},{8,12},{12,8},{16,20},{20,16},{24,28},{28,24},{1,5},{5... | collective-permute-start | bytes 3145736 | tf_op jit(solution)/shard_map/ppermute | solution.py:19
  265.1 13.9 %collective-permute-start.42 = (bf16[512,1024]{1,0:T(8,128)(2,1)S(1)}, bf16[512,1024]{1,0:T(8,128)(2,1)S(1)}, u32[]{:S(2)}, u32[]{:S(2)}) collective-permute-start(bf16[512,1024]{1,0:T(8,128)(2,1)S(1)} %maximum_select_fusion.refs_1_), channel_id=1, source_target_pairs={{0,4},{4,0},{8,12},{12,8},{16,20},{20,16},{24,28},{28,24},{1,5},{5... | collective-permute-start | bytes 3145736 | tf_op jit(solution)/shard_map/ppermute | solution.py:19
  (38 other events, 201.2 us)

commit v3 on v2

--- a/solution.py
+++ b/solution.py
@@ -30,11 +30,16 @@
 
 
 def sum_everywhere(value):
-    for axis in ("dp", "feat"):
-        others = [swap(value, axis, mask) for mask in range(1, lax.axis_size(axis))]
-        for other in others:
-            value = value + other
-    return value
+    axes = ("dp", "feat")
+    count = lax.axis_size(axes)
+    parts = [value]
+    for low in range(0, count.bit_length() - 1, 2):
+        masks = [mask << low for mask in range(1, 4) if mask << low < count]
+        value = sum(parts[1:], parts[0])
+        parts = [value] + [
+            lax.ppermute(value, axes, [(i, i ^ mask) for i in range(count)]) for mask in masks
+        ]
+    return parts
 
 
 def whole(array):
@@ -73,56 +78,77 @@
     return sum(part[:, start : start + 128] for start in range(0, part.shape[1], 128))
 
 
-def turn_weight(weight, half):
+def turn_weight(weight, core, after=()):
     depth, width = weight.shape
     quarter = width // 4
     step = min(256, quarter)
     steps = quarter // step
 
-    def body(half_ref, weight_ref, turned_ref, square_ref):
+    def body(core_ref, weight_ref, sent_ref, kept_ref, square_ref):
         block = weight_ref[...]
-        turned_ref[...] = block.T.astype(BF16)
-
-        @pl.when((pl.program_id(0) == 0) & (pl.program_id(1) == 0))
+        block_turned = block.T.astype(BF16)
+        square = fold(block * block)
+        first = (pl.program_id(0) == 0) & (pl.program_id(1) == 0)
+
+        @pl.when(pl.program_id(0) == 0)
         def _():
-            square_ref[...] = jnp.zeros_like(square_ref)
-
-        square_ref[...] += fold(block * block)
-
-    return run(
-        body, half.reshape(1), [weight],
-        [pl.BlockSpec((depth, step), lambda p, i, h: (0, (2 * p + h[0]) * steps + i))],
-        [like((2 * quarter, depth), BF16), like((8, 128), F32)],
+            sent_ref[...] = block_turned
+
+        @pl.when(pl.program_id(0) == 1)
+        def _():
+            kept_ref[...] = block_turned
+
+        @pl.when(first)
+        def _():
+            square_ref[...] = square
+
+        @pl.when(jnp.logical_not(first))
+        def _():
+            square_ref[...] += square
+
+    out = like((2 * quarter, depth), BF16)
+    return run(
+        body, core.reshape(1), [weight],
         [
-            pl.BlockSpec((step, depth), lambda p, i, h: (p * steps + i, 0)),
-            pl.BlockSpec((8, 128), lambda p, i, h: (0, 0)),
+            pl.BlockSpec(
+                (depth, step),
+                lambda k, j, c: (0, (2 * (j // steps) + (c[0] ^ (1 - k))) * steps + j % steps),
+            )
         ],
-        grid=(2, steps), flops=depth * width, moved=3 * depth * width, limit=16,
-    )
-
-
-def share_of(view_features, view, after=()):
+        [out, out, like((8, 128), F32)],
+        [
+            pl.BlockSpec((step, depth), lambda k, j, c: (jnp.where(k == 0, j, 2 * steps - 1), 0)),
+            pl.BlockSpec((step, depth), lambda k, j, c: (jnp.where(k == 1, j, 0), 0)),
+            pl.BlockSpec((8, 128), lambda k, j, c: (0, 0)),
+        ],
+        grid=(2, 2 * steps), after=after, flops=2 * depth * width, moved=6 * depth * width, limit=16,
+    )
+
+
+def shares_of(view_features, view, after=()):
     _, count, width = view_features.shape
-
-    def body(_, rows_ref, out_ref):
-        out_ref[...] = rows_ref[...]
-
-    (out,) = run(
+    half = count // 2
+
+    def body(_, rows_ref, low_ref, high_ref):
+        low_ref[...] = rows_ref[:half, :]
+        high_ref[...] = rows_ref[half:, :]
+
+    out = like((half, width), BF16)
+    return run(
         body, jnp.zeros((1,), jnp.int32), [view_features],
         [pl.BlockSpec((None, count, width), lambda i, s: (view, 0, 0))],
-        [like((count, width), BF16)], [pl.BlockSpec((count, width), lambda i, s: (0, 0))],
-        after=after, moved=4 * count * width, limit=8,
-    )
-    return out
-
-
-def go_round(share):
+        [out, out], [whole(out), whole(out)], after=after, moved=4 * count * width, limit=8,
+    )
+
+
+def go_round(parts):
     n_feat = lax.axis_size("feat")
-    shares = [share]
+    ring = [(i, (i + 1) % n_feat) for i in range(n_feat)]
+    lists = [[part] for part in parts]
     for _ in range(1, n_feat):
-        ring = [(i, (i + 1) % n_feat) for i in range(n_feat)]
-        shares.append(lax.ppermute(shares[-1], "feat", ring))
-    return shares
+        for shares in lists:
+            shares.append(lax.ppermute(shares[-1], "feat", ring))
+    return lists
 
 
 def choose(shares, n_chip, after=()):
@@ -147,27 +173,30 @@
 
 
 def assemble(place, own, other, after=()):
-    n_chip = len(own)
-    count, width = own[0].shape
+    n_part, n_chip = len(own), len(own[0])
+    count, width = own[0][0].shape
     half = width // 2
+    operands = [piece for pieces in (*own, *other) for piece in pieces]
 
     def body(place_ref, *refs):
         chip, core = place_ref[0], place_ref[1]
         out_ref = refs[-1]
-        for mask in range(n_chip):
-            for flip in range(2):
-                piece_ref = refs[flip * n_chip + mask]
-                row = pl.multiple_of(((chip ^ mask) * 2 + (core ^ flip)) * count, count)
-                for side in range(2):
-                    lane = pl.multiple_of((core ^ side) * half, half)
-                    out_ref[pl.ds(row, count), side * half : (side + 1) * half] = piece_ref[
-                        :, pl.ds(lane, half)
-                    ]
-
-    out = like((2 * n_chip * count, width), BF16)
+        for flip in range(2):
+            for part in range(n_part):
+                for mask in range(n_chip):
+                    piece_ref = refs[(flip * n_part + part) * n_chip + mask]
+                    row = (((chip ^ mask) * 2 + (core ^ flip)) * n_part + part) * count
+                    rows = pl.ds(pl.multiple_of(row, count), count)
+                    for side in range(2):
+                        lane = pl.multiple_of((core ^ side) * half, half)
+                        out_ref[rows, side * half : (side + 1) * half] = piece_ref[
+                            :, pl.ds(lane, half)
+                        ]
+
+    out = like((len(operands) * count, width), BF16)
     (columns,) = run(
-        body, place, [*own, *other], [whole(piece) for piece in [*own, *other]],
-        [out], [whole(out)], after=after, moved=8 * n_chip * count * width, limit=24,
+        body, place, operands, [whole(piece) for piece in operands],
+        [out], [whole(out)], after=after, moved=4 * len(operands) * count * width, limit=24,
     )
     return columns
 
@@ -331,14 +360,14 @@
     return out_grad
 
 
-def weight_grad_of(place, turned, pieces, base=None, after=()):
+def weight_grad_of(place, turned, pieces, base=None, weight_squares=None, after=()):
     depth, batch = turned.shape
     cols = pieces[0].shape[0]
     last = base is not None
 
     def body(place_ref, turned_ref, *refs):
         if last:
-            base_ref, out_ref, square_ref = refs[4:]
+            base_ref, weight_squares_ref, out_ref, square_ref = refs[4:]
         else:
             (out_ref,) = refs[4:]
         for index in range(4):
@@ -351,18 +380,48 @@
                 if last:
                     total += base_ref[...]
                     square = fold(total * total)
-                    square_ref[...] = square if index == 0 else square_ref[...] + square
+                    if index == 0:
+                        square_ref[:8, :] = square
+                        square_ref[8:, :] = weight_squares_ref[...]
+                    else:
+                        square_ref[:8, :] += square
                 out_ref[...] = total
 
     tile = pl.BlockSpec((depth, cols), lambda j, s: (0, (j >> 1) * 2 + ((j & 1) ^ s[1])))
-    square = pl.BlockSpec((8, 128), lambda j, s: (0, 0))
+    square = pl.BlockSpec((16, 128), lambda j, s: (0, 0))
     operands = [turned, *pieces]
     return run(
-        body, place, operands + ([base] if last else []),
-        [whole(one) for one in operands] + ([tile] if last else []),
-        [like((depth, 4 * cols), F32)] + ([like((8, 128), F32)] if last else []),
+        body, place, operands + ([base, weight_squares] if last else []),
+        [whole(one) for one in operands] + ([tile, whole(weight_squares)] if last else []),
+        [like((depth, 4 * cols), F32)] + ([like((16, 128), F32)] if last else []),
         [tile] + ([square] if last else []), grid=(4,), after=after,
         flops=8 * cols * batch * depth, moved=16 * depth * cols * (2 if last else 1), limit=32,
+    )
+
+
+def update(sums, weight, velocity, weight_grad):
+    depth, width = weight.shape
+    step = min(128, depth)
+    n_sum = len(sums)
+
+    def body(_, *refs):
+        weight_ref, velocity_ref, grad_ref, new_weight_ref, new_velocity_ref = refs[n_sum:]
+        total = refs[0][...]
+        for ref in refs[1:n_sum]:
+            total += ref[...]
+        grad_norm = jnp.sqrt(jnp.sum(total[:8], keepdims=True))
+        weight_norm = jnp.sqrt(jnp.sum(total[8:], keepdims=True))
+        trust = weight_norm / (grad_norm + NORM_EPSILON)
+        new_velocity = MOMENTUM * velocity_ref[...] + trust * grad_ref[...]
+        new_velocity_ref[...] = new_velocity
+        new_weight_ref[...] = weight_ref[...] - LEARN_RATE * new_velocity
+
+    tile = pl.BlockSpec((step, width), lambda i, s: (i, 0))
+    out = like((depth, width), F32)
+    return run(
+        body, jnp.zeros((1,), jnp.int32), [*sums, weight, velocity, weight_grad],
+        [whole(one) for one in sums] + [tile] * 3, [out, out], [tile, tile],
+        grid=(depth // step,), flops=4 * depth * width, moved=20 * depth * width, limit=16,
     )
 
 
@@ -379,20 +438,19 @@
         return jnp.stack([bit_value("dp", order[level]) for order in orders])
 
     shares = [None] * 2
-    shares[1] = go_round(share_of(view_features, 1))
-    shares[0] = go_round(share_of(view_features, 0, after=[shares[1][-2]]))
-    sent, sent_squares = turn_weight(weight, 1 - core)
+    shares[1] = go_round(shares_of(view_features, 1))
+    sent, turned_own, weight_squares = turn_weight(weight, core, after=[shares[1][-1][-2]])
     turned_other = swap(sent, "dp", 1)
-    turned_own, own_squares = turn_weight(weight, core)
-    weight_squares = sent_squares + own_squares
+    shares[0] = go_round(shares_of(view_features, 0, after=[turned_own]))
 
     turned, gram, normed, half, inverse = ([None] * 2 for _ in range(5))
     ahead = ()
     for v in (1, 0):
-        own = list(choose(shares[v], n_chip, after=ahead[:1]))
-        for mask in range(1, n_chip):
-            own[mask] = swap(own[mask], "dp", 2 * mask)
-        other = [swap(piece, "dp", 1) for piece in own]
+        own = [list(choose(part, n_chip, after=ahead[:1])) for part in shares[v]]
+        for pieces in own:
+            for mask in range(1, n_chip):
+                pieces[mask] = swap(pieces[mask], "dp", 2 * mask)
+        other = [[swap(piece, "dp", 1) for piece in pieces] for pieces in own]
         columns = assemble(place, own, other, after=ahead)
         turned[v] = turn_columns(columns)
         bits = bits_at(0)
@@ -417,7 +475,6 @@
         )
         gram[v] = (gram_own, swap(gram_own, "dp", 1))
 
-    result = []
     for v in (0, 1):
         out_grad = out_grad_of(place, *gram[1 - v], normed[v], half[v], half[1 - v], inverse[v])
         share = out_grad.shape[0] // 2
@@ -427,13 +484,10 @@
             for bit in reversed(orders[path]):
                 own = join(own, swap(own, "dp", 1 << bit), bit_value("dp", bit))
             pieces += [own, swap(own, "dp", 1)]
-        result = weight_grad_of(place, turned[v], pieces, *result)
-    weight_grad, squares = result
-    sums = sum_everywhere(jnp.stack([jnp.sum(weight_squares), jnp.sum(squares)]))
-    trust = jnp.sqrt(sums[0]) / (jnp.sqrt(sums[1]) + NORM_EPSILON)
-    new_velocity = MOMENTUM * velocity + trust * weight_grad
-    new_weight = weight - LEARN_RATE * new_velocity
-    return (new_weight, new_velocity)
+        if v == 0:
+            (base,) = weight_grad_of(place, turned[v], pieces)
+    weight_grad, squares = weight_grad_of(place, turned[1], pieces, base, weight_squares)
+    return update(sum_everywhere(squares), weight, velocity, weight_grad)
 
 
 def solution(mesh):

time: 332 us -> 339 us (1.021)
  local copies, waits for them, and re-layouts: 19 us -> 38.1 us
  other arithmetic: 25 us -> 6.82 us
  Pallas kernels: 52.6 us -> 65.8 us
  waiting for transfers between devices: 165 us -> 156 us
  starting transfers between devices: 62.7 us -> 68.4 us
    sub x1 -> x0, other arithmetic: 14.4 us -> none  [per_device(): new_weight = weight - LEARN_RATE * new_velocity]
    pallas_call x24 -> x26, Pallas kernels: 52.6 us -> 65.8 us  [run(): pl.pallas_call(kernel, grid_spec=pltpu.PrefetchScalarGridSpec(num_scalar_...]
    ppermute x65 -> x69, waiting for transfers between devices: 103 us -> 91.7 us  [swap(): lax.ppermute(value, axis, [(i, i ^ mask) for i in range(lax.axis_size(axi...]
    slice x2, local copies, waits for them, and re-layouts: 0.77 us -> 11.2 us  [per_device(): own = out_grad[path * share:(path + 1) * share]]
    unnamed x30 -> x82, local copies, waits for them, and re-layouts: 17.7 us -> 26.9 us
    ppermute x0 -> x7, starting transfers between devices: none -> 7.64 us  [sum_everywhere(): lax.ppermute(value, axes, [(i, i ^ mask) for i in range(count)])]
    ppermute x0 -> x7, waiting for transfers between devices: none -> 7.41 us  [sum_everywhere(): lax.ppermute(value, axes, [(i, i ^ mask) for i in range(count)])]
    ppermute x65 -> x69, starting transfers between devices: 59.5 us -> 55 us  [swap(): lax.ppermute(value, axis, [(i, i ^ mask) for i in range(lax.axis_size(axi...]
  transfers between devices with their start and end apart: 71 -> 88, of which waited for: 38 -> 48; matrix products, arithmetic and copies ran while one was open for 3% -> 5% of each run, Pallas kernels for 12% -> 11%
where the time goes in v3:
time: 339 us; the launch traced here: 336 us
  waiting for transfers between devices  156 us (46%)
  starting transfers between devices  68.4 us (20%)
  Pallas kernels  65.8 us (19%)
  local copies, waits for them, and re-layouts  38.1 us (11%)
  other arithmetic  6.82 us (2%)
    ppermute x69, waiting for transfers between devices, swap(): lax.ppermute(value, axis, [(i, i ^ mask) for i in range(lax.axis_size(axi...  91.7 us
    pallas_call x26, Pallas kernels, run(): pl.pallas_call(kernel, grid_spec=pltpu.PrefetchScalarGridSpec(num_scalar_...  65.8 us
    ppermute x12, waiting for transfers between devices, go_round(): shares.append(lax.ppermute(shares[-1], 'feat', ring))  56.7 us
    ppermute x69, starting transfers between devices, swap(): lax.ppermute(value, axis, [(i, i ^ mask) for i in range(lax.axis_size(axi...  55 us
    unnamed x82, local copies, waits for them, and re-layouts  26.9 us
    slice x2, local copies, waits for them, and re-layouts, per_device(): own = out_grad[path * share:(path + 1) * share]  11.2 us
    ppermute x7, starting transfers between devices, sum_everywhere(): lax.ppermute(value, axes, [(i, i ^ mask) for i in range(count)])  7.64 us
    ppermute x7, waiting for transfers between devices, sum_everywhere(): lax.ppermute(value, axes, [(i, i ^ mask) for i in range(count)])  7.41 us
  transfers between devices with their start and end apart: 88, of which 48 were waited for; matrix products, arithmetic and copies ran while one was open for 5% of the time, Pallas kernels for 11%

profile of v3, /device:TPU:0, one launch (start us, length us, event | category | flops | bytes accessed | tf_op | source)
XLA Modules:
  0.0 336.5 jit_solution(15460478284635289120)
XLA Ops:
  2.6 3.0 collective-permute-start.6
  6.3 7.6 %collective-permute-done.6.refs_1_ = bf16[64,2048]{1,0:T(8,128)(2,1)S(1)} collective-permute-done((bf16[64,2048]{1,0:T(8,128)(2,1)S(1)}, bf16[64,2048]{1,0:T(8,128)(2,1)S(1)}, u32[]{:S(2)}, u32[]{:S(2)}) %collective-permute-start.6) | collective-permute-done | bytes 262176 | tf_op jit(solution)/shard_map/ppermute | solution.py:150
  14.7 8.6 %collective-permute-done.7.refs_2_.refs_1_ = bf16[64,2048]{1,0:T(8,128)(2,1)S(1)} collective-permute-done((bf16[64,2048]{1,0:T(8,128)(2,1)S(1)}, bf16[64,2048]{1,0:T(8,128)(2,1)S(1)}, u32[]{:S(2)}, u32[]{:S(2)}) %collective-permute-start.7) | collective-permute-done | bytes 262176 | tf_op jit(solution)/shard_map/ppermute | solution.py:150
  23.2 3.4 %copy-done.4 = f32[1024,2048]{1,0:T(8,128)S(1)} copy-done((f32[1024,2048]{1,0:T(8,128)S(1)}, f32[1024,2048]{1,0:T(8,128)}, u32[]{:S(2)}) %copy-start.4) | copy-done | bytes 8388632
  26.6 4.6 %shard_map.55 = (bf16[1024,1024]{1,0:T(8,128)(2,1)}, bf16[1024,1024]{1,0:T(8,128)(2,1)S(1)}, f32[8,128]{1,0:T(8,128)S(1)}) custom-call(s32[1]{0:T(128)} %bitcast.1.scalars_ref, f32[1024,2048]{1,0:T(8,128)S(1)} %copy-done.4, bf16[64,2048]{1,0:T(8,128)(2,1)S(1)} %collective-permute-done.7.refs_2_.refs_1_), custom_call_target="tpu_custom_call" | custom-call | flops 4194304 | bytes 12582912 | tf_op jit(solution)/shard_map/pallas_call | solution.py:61
  31.3 10.5 %collective-permute-done.refs_1_ = bf16[64,2048]{1,0:T(8,128)(2,1)S(1)} collective-permute-done((bf16[64,2048]{1,0:T(8,128)(2,1)S(1)}, bf16[64,2048]{1,0:T(8,128)(2,1)S(1)}, u32[]{:S(2)}, u32[]{:S(2)}) %collective-permute-start) | collective-permute-done | bytes 262176 | tf_op jit(solution)/shard_map/ppermute | solution.py:150
  42.5 9.1 %collective-permute-done.1.refs_2_ = bf16[64,2048]{1,0:T(8,128)(2,1)} collective-permute-done((bf16[64,2048]{1,0:T(8,128)(2,1)S(1)}, bf16[64,2048]{1,0:T(8,128)(2,1)}, u32[]{:S(2)}, u32[]{:S(2)}) %collective-permute-start.1) | collective-permute-done | bytes 262176 | tf_op jit(solution)/shard_map/ppermute | solution.py:150
  52.5 10.5 %collective-permute-done.2.refs_3_ = bf16[64,2048]{1,0:T(8,128)(2,1)} collective-permute-done((bf16[64,2048]{1,0:T(8,128)(2,1)}, bf16[64,2048]{1,0:T(8,128)(2,1)}, u32[]{:S(2)}, u32[]{:S(2)}) %collective-permute-start.2) | collective-permute-done | bytes 262176 | tf_op jit(solution)/shard_map/ppermute | solution.py:150
  68.5 2.2 collective-permute-start.5
  80.1 2.4 collective-permute-done.9.refs_5_
  82.5 6.0 %collective-permute-done.10.refs_6_ = bf16[64,2048]{1,0:T(8,128)(2,1)} collective-permute-done((bf16[64,2048]{1,0:T(8,128)(2,1)S(1)}, bf16[64,2048]{1,0:T(8,128)(2,1)}, u32[]{:S(2)}, u32[]{:S(2)}) %collective-permute-start.10) | collective-permute-done | bytes 262176 | tf_op jit(solution)/shard_map/ppermute | solution.py:19
  97.3 2.2 shard_map.53.refs_0_.refs_4_
  99.5 5.0 %shard_map.57 = (bf16[256,1024]{1,0:T(8,128)(2,1)S(1)}, bf16[256,1024]{1,0:T(8,128)(2,1)S(1)}) custom-call(s32[2]{0:T(128)S(1)} %get-tuple-element.112.scalars_ref, bf16[1024,1024]{1,0:T(8,128)(2,1)S(1)} %get-tuple-element.67.refs_1_.refs_0_.refs_2_, bf16[1024,1024]{1,0:T(8,128)(2,1)} %collective-permute-done.20.refs_1_.refs_3_, ...), custom_call_target="tpu_custom_call" | custom-call | flops 2147483648 | bytes 6291456 | tf_op jit(solution)/shard_map/pallas_call | solution.py:61
  108.1 2.1 collective-permute-start.29
  110.3 7.7 %collective-permute-done.22.refs_2_ = bf16[64,2048]{1,0:T(8,128)(2,1)S(1)} collective-permute-done((bf16[64,2048]{1,0:T(8,128)(2,1)S(1)}, bf16[64,2048]{1,0:T(8,128)(2,1)S(1)}, u32[]{:S(2)}, u32[]{:S(2)}) %collective-permute-start.22) | collective-permute-done | bytes 262176 | tf_op jit(solution)/shard_map/ppermute | solution.py:150
  118.0 4.2 %shard_map.60 = (bf16[256,1024]{1,0:T(8,128)(2,1)S(1)}, bf16[256,1024]{1,0:T(8,128)(2,1)S(1)}) custom-call(s32[2]{0:T(128)S(1)} %get-tuple-element.113.scalars_ref, bf16[1024,1024]{1,0:T(8,128)(2,1)S(1)} %get-tuple-element.67.refs_1_.refs_0_.refs_2_, bf16[1024,1024]{1,0:T(8,128)(2,1)} %collective-permute-done.20.refs_1_.refs_3_, ...), custom_call_target="tpu_custom_call" | custom-call | flops 2147483648 | bytes 6291456 | tf_op jit(solution)/shard_map/pallas_call | solution.py:61
  131.1 2.2 collective-permute-done.43.refs_1_
  135.9 2.1 collective-permute-done.30.refs_5_
  138.0 3.6 %collective-permute-done.31.refs_6_ = bf16[64,2048]{1,0:T(8,128)(2,1)S(1)} collective-permute-done((bf16[64,2048]{1,0:T(8,128)(2,1)S(1)}, bf16[64,2048]{1,0:T(8,128)(2,1)S(1)}, u32[]{:S(2)}, u32[]{:S(2)}) %collective-permute-start.31) | collective-permute-done | bytes 262176 | tf_op jit(solution)/shard_map/ppermute | solution.py:19
  142.0 3.1 collective-permute-done.32.refs_7_
  145.1 3.5 %collective-permute-done.24.refs_1_ = bf16[64,2048]{1,0:T(8,128)(2,1)S(1)} collective-permute-done((bf16[64,2048]{1,0:T(8,128)(2,1)S(1)}, bf16[64,2048]{1,0:T(8,128)(2,1)S(1)}, u32[]{:S(2)}, u32[]{:S(2)}) %collective-permute-start.24) | collective-permute-done | bytes 262176 | tf_op jit(solution)/shard_map/ppermute | solution.py:19
  149.1 3.1 collective-permute-done.26.refs_3_
  156.1 5.0 %shard_map.66 = (bf16[256,1024]{1,0:T(8,128)(2,1)S(1)}, bf16[256,1024]{1,0:T(8,128)(2,1)S(1)}) custom-call(s32[2]{0:T(128)S(1)} %get-tuple-element.112.scalars_ref, bf16[1024,1024]{1,0:T(8,128)(2,1)S(1)} %get-tuple-element.67.refs_1_.refs_0_.refs_2_, bf16[1024,1024]{1,0:T(8,128)(2,1)} %collective-permute-done.20.refs_1_.refs_3_, ...), custom_call_target="tpu_custom_call" | custom-call | flops 2147483648 | bytes 6291456 | tf_op jit(solution)/shard_map/pallas_call | solution.py:61
  162.9 4.2 %shard_map.65 = (bf16[256,1024]{1,0:T(8,128)(2,1)S(1)}, bf16[256,1024]{1,0:T(8,128)(2,1)S(1)}) custom-call(s32[2]{0:T(128)S(1)} %get-tuple-element.113.scalars_ref, bf16[1024,1024]{1,0:T(8,128)(2,1)S(1)} %get-tuple-element.67.refs_1_.refs_0_.refs_2_, bf16[1024,1024]{1,0:T(8,128)(2,1)} %collective-permute-done.20.refs_1_.refs_3_, ...), custom_call_target="tpu_custom_call" | custom-call | flops 2147483648 | bytes 6291456 | tf_op jit(solution)/shard_map/pallas_call | solution.py:61
  167.1 8.0 %collective-permute-done.46.refs_1_ = bf16[256,1024]{1,0:T(8,128)(2,1)S(1)} collective-permute-done((bf16[256,1024]{1,0:T(8,128)(2,1)S(1)}, bf16[256,1024]{1,0:T(8,128)(2,1)S(1)}, u32[]{:S(2)}, u32[]{:S(2)}) %collective-permute-start.46) | collective-permute-done | bytes 524320 | tf_op jit(solution)/shard_map/ppermute | solution.py:19
  181.9 4.2 %collective-permute-done.48.refs_1_ = bf16[128,1024]{1,0:T(8,128)(2,1)S(1)} collective-permute-done((bf16[128,1024]{1,0:T(8,128)(2,1)S(1)}, bf16[128,1024]{1,0:T(8,128)(2,1)S(1)}, u32[]{:S(2)}, u32[]{:S(2)}) %collective-permute-start.48) | collective-permute-done | bytes 262176 | tf_op jit(solution)/shard_map/ppermute | solution.py:19
  187.2 2.5 collective-permute-done.66
  189.7 2.8 collective-permute-done.68
  198.4 3.4 %collective-permute-start.70 = (bf16[128,640]{1,0:T(8,128)(2,1)S(1)}, bf16[128,640]{1,0:T(8,128)(2,1)S(1)}, u32[]{:S(2)}, u32[]{:S(2)}) collective-permute-start(bf16[128,640]{1,0:T(8,128)(2,1)S(1)} %add_convert_fusion.1), channel_id=1, source_target_pairs={{0,2},{1,3},{2,0},{3,1},{4,6},{5,7},{6,4},{7,5},{8,10},{9,11},{10,... | collective-permute-start | bytes 491528 | tf_op jit(solution)/shard_map/ppermute | solution.py:19
  204.0 3.0 collective-permute-done.70
  210.6 2.5 collective-permute-start.55
  215.0 3.5 %collective-permute-done.55 = bf16[128,640]{1,0:T(8,128)(2,1)S(1)} collective-permute-done((bf16[128,640]{1,0:T(8,128)(2,1)S(1)}, bf16[128,640]{1,0:T(8,128)(2,1)S(1)}, u32[]{:S(2)}, u32[]{:S(2)}) %collective-permute-start.55) | collective-permute-done | bytes 163872 | tf_op jit(solution)/shard_map/ppermute | solution.py:19
  222.1 2.8 collective-permute-done.58
  226.6 2.3 shard_map.72
  228.9 11.2 %fusion = (bf16[128,1024]{1,0:T(8,128)(2,1)}, bf16[128,1024]{1,0:T(8,128)(2,1)S(1)}) fusion(bf16[256,1024]{1,0:T(8,128)(2,1)S(1)} %shard_map.72), kind=kLoop, calls=%fused_computation.23 | loop fusion | bytes 1048576 | tf_op jit(solution)/shard_map/slice | solution.py:483
  241.6 7.5 %collective-permute-done.78 = bf16[128,1024]{1,0:T(8,128)(2,1)} collective-permute-done((bf16[128,1024]{1,0:T(8,128)(2,1)}, bf16[128,1024]{1,0:T(8,128)(2,1)}, u32[]{:S(2)}, u32[]{:S(2)}) %collective-permute-start.78) | collective-permute-done | bytes 262176 | tf_op jit(solution)/shard_map/ppermute | solution.py:19
  252.6 2.3 shard_map.70
  259.6 4.7 %collective-permute-done.63 = bf16[128,1024]{1,0:T(8,128)(2,1)S(1)} collective-permute-done((bf16[128,1024]{1,0:T(8,128)(2,1)S(1)}, bf16[128,1024]{1,0:T(8,128)(2,1)S(1)}, u32[]{:S(2)}, u32[]{:S(2)}) %collective-permute-start.63) | collective-permute-done | bytes 262176 | tf_op jit(solution)/shard_map/ppermute | solution.py:19
  265.7 5.3 %collective-permute-done.60 = bf16[128,1024]{1,0:T(8,128)(2,1)S(1)} collective-permute-done((bf16[128,1024]{1,0:T(8,128)(2,1)S(1)}, bf16[128,1024]{1,0:T(8,128)(2,1)S(1)}, u32[]{:S(2)}, u32[]{:S(2)}) %collective-permute-start.60) | collective-permute-done | bytes 262176 | tf_op jit(solution)/shard_map/ppermute | solution.py:19
  276.1 4.9 %collective-permute-done.64 = bf16[256,1024]{1,0:T(8,128)(2,1)S(1)} collective-permute-done((bf16[256,1024]{1,0:T(8,128)(2,1)S(1)}, bf16[256,1024]{1,0:T(8,128)(2,1)S(1)}, u32[]{:S(2)}, u32[]{:S(2)}) %collective-permute-start.64) | collective-permute-done | bytes 524320 | tf_op jit(solution)/shard_map/ppermute | solution.py:19
  281.5 3.6 %collective-permute-done.61 = bf16[256,1024]{1,0:T(8,128)(2,1)S(1)} collective-permute-done((bf16[256,1024]{1,0:T(8,128)(2,1)S(1)}, bf16[256,1024]{1,0:T(8,128)(2,1)S(1)}, u32[]{:S(2)}, u32[]{:S(2)}) %collective-permute-start.61) | collective-permute-done | bytes 524320 | tf_op jit(solution)/shard_map/ppermute | solution.py:19
  290.1 6.4 %shard_map.73.refs_5_ = f32[1024,2048]{1,0:T(8,128)S(1)} custom-call(s32[2]{0:T(128)S(1)} %pad_add_fusion.scalars_ref, bf16[1024,1024]{1,0:T(8,128)(2,1)S(1)} %shard_map.71.refs_0_, bf16[512,1024]{1,0:T(8,128)(2,1)S(1)} %maximum_select_fusion.2.refs_1_, bf16[512,1024]{1,0:T(8,128)(2,1)S(1)} %collective-permute-done.77.refs_2_, ...), custom_call_target="tpu_custom_call" | custom-call | flops 4294967296 | bytes 8388608 | tf_op jit(solution)/shard_map/pallas_call | solution.py:61
  296.5 3.4 %copy-done.36 = f32[1024,2048]{1,0:T(8,128)} copy-done((f32[1024,2048]{1,0:T(8,128)}, f32[1024,2048]{1,0:T(8,128)S(1)}, u32[]{:S(2)}) %copy-start.36) | copy-done | bytes 8388632
  305.2 8.5 %shard_map.74 = (f32[1024,2048]{1,0:T(8,128)S(1)}, f32[16,128]{1,0:T(8,128)S(1)}) custom-call(s32[2]{0:T(128)S(1)} %pad_add_fusion.scalars_ref, bf16[1024,1024]{1,0:T(8,128)(2,1)S(1)} %copy-done.8, bf16[512,1024]{1,0:T(8,128)(2,1)S(1)} %copy-done.10, bf16[512,1024]{1,0:T(8,128)(2,1)S(1)} %copy-done.35, bf16[512,1024]{1,0:T(8,128)(2,1)S(1)} %maximum_select_fusion.1.refs_3_, ...), custom_call_target="tpu_custom_call" | custom-call | flops 4294967296 | bytes 16777216 | tf_op jit(solution)/shard_map/pallas_call | solution.py:61
  313.7 3.0 collective-permute-start.83
  319.2 2.0 collective-permute-done.82
  326.3 2.5 collective-permute-done.87.refs_1_
  328.8 7.5 %shard_map.75 = (f32[1024,2048]{1,0:T(8,128)}, f32[1024,2048]{1,0:T(8,128)}) custom-call(s32[1]{0:T(128)} %constant.21.clone.1.scalars_ref, f32[16,128]{1,0:T(8,128)S(1)} %add_add_fusion.refs_0_, f32[16,128]{1,0:T(8,128)S(1)} %collective-permute-done.87.refs_1_, f32[1024,2048]{1,0:T(8,128)S(1)} %bitcast.17, f32[1024,2048]{1,0:T(8,128)S(1)} %bitcast.19, ...), custom_call_target="tpu_custom_call" | custom-call | flops 8388608 | bytes 41943040 | tf_op jit(solution)/shard_map/pallas_call | solution.py:61
  (262 shorter events, 111.3 us)
Async XLA Ops:
  2.6 11.4 %collective-permute-start.6 = (bf16[64,2048]{1,0:T(8,128)(2,1)S(1)}, bf16[64,2048]{1,0:T(8,128)(2,1)S(1)}, u32[]{:S(2)}, u32[]{:S(2)}) collective-permute-start(bf16[64,2048]{1,0:T(8,128)(2,1)S(1)} %get-tuple-element.62.refs_0_), channel_id=1, source_target_pairs={{0,1},{1,2},{2,3},{3,0},{4,5},{5,6},{6,7},{7,4},{8,9},{9,10},{10,1... | collective-permute-start | bytes 786440 | tf_op jit(solution)/shard_map/ppermute | solution.py:150
  14.0 9.3 %collective-permute-start.7 = (bf16[64,2048]{1,0:T(8,128)(2,1)S(1)}, bf16[64,2048]{1,0:T(8,128)(2,1)S(1)}, u32[]{:S(2)}, u32[]{:S(2)}) collective-permute-start(bf16[64,2048]{1,0:T(8,128)(2,1)S(1)} %collective-permute-done.6.refs_1_), channel_id=1, source_target_pairs={{0,1},{1,2},{2,3},{3,0},{4,5},{5,6},{6,7},{7,4},{8,9},{9,10},{10,1... | collective-permute-start | bytes 786440 | tf_op jit(solution)/shard_map/ppermute | solution.py:150
  31.3 68.3 %collective-permute-start.20 = (bf16[1024,1024]{1,0:T(8,128)(2,1)}, bf16[1024,1024]{1,0:T(8,128)(2,1)}, u32[]{:S(2)}, u32[]{:S(2)}) collective-permute-start(bf16[1024,1024]{1,0:T(8,128)(2,1)} %get-tuple-element.68), channel_id=1, source_target_pairs={{0,4},{4,0},{8,12},{12,8},{16,20},{20,16},{24,28},{28,24},{1,5},{5... | collective-permute-start | bytes 6291464 | tf_op jit(solution)/shard_map/ppermute | solution.py:19
  31.3 10.5 %collective-permute-start = (bf16[64,2048]{1,0:T(8,128)(2,1)S(1)}, bf16[64,2048]{1,0:T(8,128)(2,1)S(1)}, u32[]{:S(2)}, u32[]{:S(2)}) collective-permute-start(bf16[64,2048]{1,0:T(8,128)(2,1)S(1)} %copy-done.30), channel_id=1, source_target_pairs={{0,1},{1,2},{2,3},{3,0},{4,5},{5,6},{6,7},{7,4},{8,9},{9,10},{10,1... | collective-permute-start | bytes 786440 | tf_op jit(solution)/shard_map/ppermute | solution.py:150
  41.8 9.8 %collective-permute-start.1 = (bf16[64,2048]{1,0:T(8,128)(2,1)S(1)}, bf16[64,2048]{1,0:T(8,128)(2,1)}, u32[]{:S(2)}, u32[]{:S(2)}) collective-permute-start(bf16[64,2048]{1,0:T(8,128)(2,1)S(1)} %collective-permute-done.refs_1_), channel_id=1, source_target_pairs={{0,1},{1,2},{2,3},{3,0},{4,5},{5,6},{6,7},{7,4},{8,9},{9,10},{10,1... | collective-permute-start | bytes 786440 | tf_op jit(solution)/shard_map/ppermute | solution.py:150
  51.6 11.4 %collective-permute-start.2 = (bf16[64,2048]{1,0:T(8,128)(2,1)}, bf16[64,2048]{1,0:T(8,128)(2,1)}, u32[]{:S(2)}, u32[]{:S(2)}) collective-permute-start(bf16[64,2048]{1,0:T(8,128)(2,1)} %collective-permute-done.1.refs_2_), channel_id=1, source_target_pairs={{0,1},{1,2},{2,3},{3,0},{4,5},{5,6},{6,7},{7,4},{8,9},{9,10},{10,1... | collective-permute-start | bytes 786440 | tf_op jit(solution)/shard_map/ppermute | solution.py:150
  51.7 16.8 %collective-permute-start.8 = (bf16[64,2048]{1,0:T(8,128)(2,1)S(1)}, bf16[64,2048]{1,0:T(8,128)(2,1)S(1)}, u32[]{:S(2)}, u32[]{:S(2)}) collective-permute-start(bf16[64,2048]{1,0:T(8,128)(2,1)S(1)} %collective-permute-done.7.refs_2_.refs_1_), channel_id=1, source_target_pairs={{0,1},{1,2},{2,3},{3,0},{4,5},{5,6},{6,7},{7,4},{8,9},{9,10},{10,1... | collective-permute-start | bytes 786440 | tf_op jit(solution)/shard_map/ppermute | solution.py:150
  51.8 20.2 %collective-permute-start.27 = (bf16[64,2048]{1,0:T(8,128)(2,1)S(1)}, bf16[64,2048]{1,0:T(8,128)(2,1)}, u32[]{:S(2)}, u32[]{:S(2)}) collective-permute-start(bf16[64,2048]{1,0:T(8,128)(2,1)S(1)} %get-tuple-element.75.refs_0_), channel_id=1, source_target_pairs={{0,1},{1,2},{2,3},{3,0},{4,5},{5,6},{6,7},{7,4},{8,9},{9,10},{10,1... | collective-permute-start | bytes 786440 | tf_op jit(solution)/shard_map/ppermute | solution.py:150
  66.0 10.3 %collective-permute-start.4 = (bf16[64,2048]{1,0:T(8,128)(2,1)S(1)}, bf16[64,2048]{1,0:T(8,128)(2,1)S(1)}, u32[]{:S(2)}, u32[]{:S(2)}) collective-permute-start(bf16[64,2048]{1,0:T(8,128)(2,1)S(1)} %get-tuple-element.60), channel_id=1, source_target_pairs={{0,16},{4,20},{8,24},{12,28},{16,0},{20,4},{24,8},{28,12},{1,17},{... | collective-permute-start | bytes 786440 | tf_op jit(solution)/shard_map/ppermute | solution.py:19
  68.5 9.5 %collective-permute-start.5 = (bf16[64,2048]{1,0:T(8,128)(2,1)S(1)}, bf16[64,2048]{1,0:T(8,128)(2,1)S(1)}, u32[]{:S(2)}, u32[]{:S(2)}) collective-permute-start(bf16[64,2048]{1,0:T(8,128)(2,1)S(1)} %get-tuple-element.61), channel_id=1, source_target_pairs={{0,24},{4,28},{8,16},{12,20},{16,8},{20,12},{24,0},{28,4},{1,25},{... | collective-permute-start | bytes 786440 | tf_op jit(solution)/shard_map/ppermute | solution.py:19
  73.1 9.4 %collective-permute-start.9 = (bf16[64,2048]{1,0:T(8,128)(2,1)S(1)}, bf16[64,2048]{1,0:T(8,128)(2,1)}, u32[]{:S(2)}, u32[]{:S(2)}) collective-permute-start(bf16[64,2048]{1,0:T(8,128)(2,1)S(1)} %get-tuple-element.64), channel_id=1, source_target_pairs={{0,8},{4,12},{8,0},{12,4},{16,24},{20,28},{24,16},{28,20},{1,9},{5... | collective-permute-start | bytes 786440 | tf_op jit(solution)/shard_map/ppermute | solution.py:19
  76.4 12.1 %collective-permute-start.10 = (bf16[64,2048]{1,0:T(8,128)(2,1)S(1)}, bf16[64,2048]{1,0:T(8,128)(2,1)}, u32[]{:S(2)}, u32[]{:S(2)}) collective-permute-start(bf16[64,2048]{1,0:T(8,128)(2,1)S(1)} %get-tuple-element.65), channel_id=1, source_target_pairs={{0,16},{4,20},{8,24},{12,28},{16,0},{20,4},{24,8},{28,12},{1,17},{... | collective-permute-start | bytes 786440 | tf_op jit(solution)/shard_map/ppermute | solution.py:19
  78.0 10.4 %collective-permute-start.11 = (bf16[64,2048]{1,0:T(8,128)(2,1)S(1)}, bf16[64,2048]{1,0:T(8,128)(2,1)}, u32[]{:S(2)}, u32[]{:S(2)}) collective-permute-start(bf16[64,2048]{1,0:T(8,128)(2,1)S(1)} %get-tuple-element.66), channel_id=1, source_target_pairs={{0,24},{4,28},{8,16},{12,20},{16,8},{20,12},{24,0},{28,4},{1,25},{... | collective-permute-start | bytes 786440 | tf_op jit(solution)/shard_map/ppermute | solution.py:19
  79.4 9.6 %collective-permute-start.16 = (bf16[64,2048]{1,0:T(8,128)(2,1)S(1)}, bf16[64,2048]{1,0:T(8,128)(2,1)S(1)}, u32[]{:S(2)}, u32[]{:S(2)}) collective-permute-start(bf16[64,2048]{1,0:T(8,128)(2,1)S(1)} %get-tuple-element.63.refs_4_), channel_id=1, source_target_pairs={{0,4},{4,0},{8,12},{12,8},{16,20},{20,16},{24,28},{28,24},{1,5},{5... | collective-permute-start | bytes 786440 | tf_op jit(solution)/shard_map/ppermute | solution.py:19
  91.8 15.2 %collective-permute-start.21 = (bf16[64,2048]{1,0:T(8,128)(2,1)}, bf16[64,2048]{1,0:T(8,128)(2,1)S(1)}, u32[]{:S(2)}, u32[]{:S(2)}) collective-permute-start(bf16[64,2048]{1,0:T(8,128)(2,1)} %copy-done.21), channel_id=1, source_target_pairs={{0,1},{1,2},{2,3},{3,0},{4,5},{5,6},{6,7},{7,4},{8,9},{9,10},{10,1... | collective-permute-start | bytes 786440 | tf_op jit(solution)/shard_map/ppermute | solution.py:150
  91.8 16.3 %collective-permute-start.28 = (bf16[64,2048]{1,0:T(8,128)(2,1)}, bf16[64,2048]{1,0:T(8,128)(2,1)S(1)}, u32[]{:S(2)}, u32[]{:S(2)}) collective-permute-start(bf16[64,2048]{1,0:T(8,128)(2,1)} %collective-permute-done.27.refs_1_), channel_id=1, source_target_pairs={{0,1},{1,2},{2,3},{3,0},{4,5},{5,6},{6,7},{7,4},{8,9},{9,10},{10,1... | collective-permute-start | bytes 786440 | tf_op jit(solution)/shard_map/ppermute | solution.py:150
  104.6 17.6 %collective-permute-start.42 = (bf16[256,1024]{1,0:T(8,128)(2,1)S(1)}, bf16[256,1024]{1,0:T(8,128)(2,1)S(1)}, u32[]{:S(2)}, u32[]{:S(2)}) collective-permute-start(bf16[256,1024]{1,0:T(8,128)(2,1)S(1)} %get-tuple-element.82), channel_id=1, source_target_pairs={{0,16},{4,20},{8,24},{12,28},{16,0},{20,4},{24,8},{28,12},{1,17},{... | collective-permute-start | bytes 1572872 | tf_op jit(solution)/shard_map/ppermute | solution.py:19
  106.3 15.9 %collective-permute-start.41 = (bf16[256,1024]{1,0:T(8,128)(2,1)S(1)}, bf16[256,1024]{1,0:T(8,128)(2,1)S(1)}, u32[]{:S(2)}, u32[]{:S(2)}) collective-permute-start(bf16[256,1024]{1,0:T(8,128)(2,1)S(1)} %get-tuple-element.70.refs_4_.refs_16_), channel_id=1, source_target_pairs={{0,8},{4,12},{8,0},{12,4},{16,24},{20,28},{24,16},{28,20},{1,9},{5... | collective-permute-start | bytes 1572872 | tf_op jit(solution)/shard_map/ppermute | solution.py:19
  106.9 11.0 %collective-permute-start.22 = (bf16[64,2048]{1,0:T(8,128)(2,1)S(1)}, bf16[64,2048]{1,0:T(8,128)(2,1)S(1)}, u32[]{:S(2)}, u32[]{:S(2)}) collective-permute-start(bf16[64,2048]{1,0:T(8,128)(2,1)S(1)} %collective-permute-done.21.refs_1_), channel_id=1, source_target_pairs={{0,1},{1,2},{2,3},{3,0},{4,5},{5,6},{6,7},{7,4},{8,9},{9,10},{10,1... | collective-permute-start | bytes 786440 | tf_op jit(solution)/shard_map/ppermute | solution.py:150
  108.1 16.7 %collective-permute-start.29 = (bf16[64,2048]{1,0:T(8,128)(2,1)S(1)}, bf16[64,2048]{1,0:T(8,128)(2,1)S(1)}, u32[]{:S(2)}, u32[]{:S(2)}) collective-permute-start(bf16[64,2048]{1,0:T(8,128)(2,1)S(1)} %collective-permute-done.28.refs_2_), channel_id=1, source_target_pairs={{0,1},{1,2},{2,3},{3,0},{4,5},{5,6},{6,7},{7,4},{8,9},{9,10},{10,1... | collective-permute-start | bytes 786440 | tf_op jit(solution)/shard_map/ppermute | solution.py:150
  118.0 10.9 %collective-permute-start.23 = (bf16[64,2048]{1,0:T(8,128)(2,1)S(1)}, bf16[64,2048]{1,0:T(8,128)(2,1)S(1)}, u32[]{:S(2)}, u32[]{:S(2)}) collective-permute-start(bf16[64,2048]{1,0:T(8,128)(2,1)S(1)} %collective-permute-done.22.refs_2_), channel_id=1, source_target_pairs={{0,1},{1,2},{2,3},{3,0},{4,5},{5,6},{6,7},{7,4},{8,9},{9,10},{10,1... | collective-permute-start | bytes 786440 | tf_op jit(solution)/shard_map/ppermute | solution.py:150
  123.0 10.2 %collective-permute-start.43 = (bf16[128,1024]{1,0:T(8,128)(2,1)S(1)}, bf16[128,1024]{1,0:T(8,128)(2,1)S(1)}, u32[]{:S(2)}, u32[]{:S(2)}) collective-permute-start(bf16[128,1024]{1,0:T(8,128)(2,1)S(1)} %get-tuple-element.84), channel_id=1, source_target_pairs={{0,16},{4,20},{8,24},{12,28},{16,0},{20,4},{24,8},{28,12},{1,17},{... | collective-permute-start | bytes 786440 | tf_op jit(solution)/shard_map/ppermute | solution.py:19
  123.1 11.4 %collective-permute-start.44 = (bf16[128,1024]{1,0:T(8,128)(2,1)S(1)}, bf16[128,1024]{1,0:T(8,128)(2,1)S(1)}, u32[]{:S(2)}, u32[]{:S(2)}) collective-permute-start(bf16[128,1024]{1,0:T(8,128)(2,1)S(1)} %get-tuple-element.86), channel_id=1, source_target_pairs={{0,8},{4,12},{8,0},{12,4},{16,24},{20,28},{24,16},{28,20},{1,9},{5... | collective-permute-start | bytes 786440 | tf_op jit(solution)/shard_map/ppermute | solution.py:19
  126.5 11.5 %collective-permute-start.30 = (bf16[64,2048]{1,0:T(8,128)(2,1)S(1)}, bf16[64,2048]{1,0:T(8,128)(2,1)S(1)}, u32[]{:S(2)}, u32[]{:S(2)}) collective-permute-start(bf16[64,2048]{1,0:T(8,128)(2,1)S(1)} %get-tuple-element.77), channel_id=1, source_target_pairs={{0,8},{4,12},{8,0},{12,4},{16,24},{20,28},{24,16},{28,20},{1,9},{5... | collective-permute-start | bytes 786440 | tf_op jit(solution)/shard_map/ppermute | solution.py:19
  126.9 14.8 %collective-permute-start.31 = (bf16[64,2048]{1,0:T(8,128)(2,1)S(1)}, bf16[64,2048]{1,0:T(8,128)(2,1)S(1)}, u32[]{:S(2)}, u32[]{:S(2)}) collective-permute-start(bf16[64,2048]{1,0:T(8,128)(2,1)S(1)} %get-tuple-element.78), channel_id=1, source_target_pairs={{0,16},{4,20},{8,24},{12,28},{16,0},{20,4},{24,8},{28,12},{1,17},{... | collective-permute-start | bytes 786440 | tf_op jit(solution)/shard_map/ppermute | solution.py:19
  128.9 16.2 %collective-permute-start.32 = (bf16[64,2048]{1,0:T(8,128)(2,1)S(1)}, bf16[64,2048]{1,0:T(8,128)(2,1)S(1)}, u32[]{:S(2)}, u32[]{:S(2)}) collective-permute-start(bf16[64,2048]{1,0:T(8,128)(2,1)S(1)} %get-tuple-element.79), channel_id=1, source_target_pairs={{0,24},{4,28},{8,16},{12,20},{16,8},{20,12},{24,0},{28,4},{1,25},{... | collective-permute-start | bytes 786440 | tf_op jit(solution)/shard_map/ppermute | solution.py:19
  133.2 15.4 %collective-permute-start.24 = (bf16[64,2048]{1,0:T(8,128)(2,1)S(1)}, bf16[64,2048]{1,0:T(8,128)(2,1)S(1)}, u32[]{:S(2)}, u32[]{:S(2)}) collective-permute-start(bf16[64,2048]{1,0:T(8,128)(2,1)S(1)} %get-tuple-element.72), channel_id=1, source_target_pairs={{0,8},{4,12},{8,0},{12,4},{16,24},{20,28},{24,16},{28,20},{1,9},{5... | collective-permute-start | bytes 786440 | tf_op jit(solution)/shard_map/ppermute | solution.py:19
  134.5 14.4 %collective-permute-start.25 = (bf16[64,2048]{1,0:T(8,128)(2,1)S(1)}, bf16[64,2048]{1,0:T(8,128)(2,1)S(1)}, u32[]{:S(2)}, u32[]{:S(2)}) collective-permute-start(bf16[64,2048]{1,0:T(8,128)(2,1)S(1)} %get-tuple-element.73), channel_id=1, source_target_pairs={{0,16},{4,20},{8,24},{12,28},{16,0},{20,4},{24,8},{28,12},{1,17},{... | collective-permute-start | bytes 786440 | tf_op jit(solution)/shard_map/ppermute | solution.py:19
  138.0 15.2 %collective-permute-start.45 = (bf16[256,1024]{1,0:T(8,128)(2,1)S(1)}, bf16[256,1024]{1,0:T(8,128)(2,1)S(1)}, u32[]{:S(2)}, u32[]{:S(2)}) collective-permute-start(bf16[256,1024]{1,0:T(8,128)(2,1)S(1)} %get-tuple-element.87.refs_0_.refs_3_.refs_4_), channel_id=1, source_target_pairs={{0,4},{4,0},{8,12},{12,8},{16,20},{20,16},{24,28},{28,24},{1,5},{5... | collective-permute-start | bytes 1572872 | tf_op jit(solution)/shard_map/ppermute | solution.py:19
  141.7 10.6 %collective-permute-start.26 = (bf16[64,2048]{1,0:T(8,128)(2,1)S(1)}, bf16[64,2048]{1,0:T(8,128)(2,1)S(1)}, u32[]{:S(2)}, u32[]{:S(2)}) collective-permute-start(bf16[64,2048]{1,0:T(8,128)(2,1)S(1)} %get-tuple-element.74), channel_id=1, source_target_pairs={{0,24},{4,28},{8,16},{12,20},{16,8},{20,12},{24,0},{28,4},{1,25},{... | collective-permute-start | bytes 786440 | tf_op jit(solution)/shard_map/ppermute | solution.py:19
  161.1 14.0 %collective-permute-start.46 = (bf16[256,1024]{1,0:T(8,128)(2,1)S(1)}, bf16[256,1024]{1,0:T(8,128)(2,1)S(1)}, u32[]{:S(2)}, u32[]{:S(2)}) collective-permute-start(bf16[256,1024]{1,0:T(8,128)(2,1)S(1)} %get-tuple-element.90), channel_id=1, source_target_pairs={{0,8},{4,12},{8,0},{12,4},{16,24},{20,28},{24,16},{28,20},{1,9},{5... | collective-permute-start | bytes 1572872 | tf_op jit(solution)/shard_map/ppermute | solution.py:19
  162.6 13.7 %collective-permute-start.47 = (bf16[256,1024]{1,0:T(8,128)(2,1)S(1)}, bf16[256,1024]{1,0:T(8,128)(2,1)S(1)}, u32[]{:S(2)}, u32[]{:S(2)}) collective-permute-start(bf16[256,1024]{1,0:T(8,128)(2,1)S(1)} %get-tuple-element.92), channel_id=1, source_target_pairs={{0,16},{4,20},{8,24},{12,28},{16,0},{20,4},{24,8},{28,12},{1,17},{... | collective-permute-start | bytes 1572872 | tf_op jit(solution)/shard_map/ppermute | solution.py:19
  178.4 11.2 %collective-permute-start.66 = (bf16[128,640]{1,0:T(8,128)(2,1)S(1)}, bf16[128,640]{1,0:T(8,128)(2,1)S(1)}, u32[]{:S(2)}, u32[]{:S(2)}) collective-permute-start(bf16[128,640]{1,0:T(8,128)(2,1)S(1)} %get-tuple-element.104), channel_id=1, source_target_pairs={{0,8},{4,12},{8,0},{12,4},{16,24},{20,28},{24,16},{28,20},{1,9},{5... | collective-permute-start | bytes 491528 | tf_op jit(solution)/shard_map/ppermute | solution.py:19
  179.5 10.2 %collective-permute-start.67 = (bf16[128,640]{1,0:T(8,128)(2,1)S(1)}, bf16[128,640]{1,0:T(8,128)(2,1)S(1)}, u32[]{:S(2)}, u32[]{:S(2)}) collective-permute-start(bf16[128,640]{1,0:T(8,128)(2,1)S(1)} %get-tuple-element.105), channel_id=1, source_target_pairs={{0,16},{4,20},{8,24},{12,28},{16,0},{20,4},{24,8},{28,12},{1,17},{... | collective-permute-start | bytes 491528 | tf_op jit(solution)/shard_map/ppermute | solution.py:19
  181.1 11.4 %collective-permute-start.68 = (bf16[128,640]{1,0:T(8,128)(2,1)S(1)}, bf16[128,640]{1,0:T(8,128)(2,1)S(1)}, u32[]{:S(2)}, u32[]{:S(2)}) collective-permute-start(bf16[128,640]{1,0:T(8,128)(2,1)S(1)} %get-tuple-element.106), channel_id=1, source_target_pairs={{0,24},{4,28},{8,16},{12,20},{16,8},{20,12},{24,0},{28,4},{1,25},{... | collective-permute-start | bytes 491528 | tf_op jit(solution)/shard_map/ppermute | solution.py:19
  214.9 11.6 %collective-permute-start.74 = (bf16[4,128,640]{2,1,0:T(8,128)(2,1)S(1)}, bf16[4,128,640]{2,1,0:T(8,128)(2,1)S(1)}, u32[]{:S(2)}, u32[]{:S(2)}) collective-permute-start(bf16[4,128,640]{2,1,0:T(8,128)(2,1)S(1)} %pad_maximum_fusion.1.refs_0_), channel_id=1, source_target_pairs={{0,4},{4,0},{8,12},{12,8},{16,20},{20,16},{24,28},{28,24},{1,5},{5... | collective-permute-start | bytes 1966088 | tf_op jit(solution)/shard_map/ppermute | solution.py:19
  226.5 24.9 %collective-permute-start.59 = (bf16[4,128,640]{2,1,0:T(8,128)(2,1)S(1)}, bf16[4,128,640]{2,1,0:T(8,128)(2,1)S(1)}, u32[]{:S(2)}, u32[]{:S(2)}) collective-permute-start(bf16[4,128,640]{2,1,0:T(8,128)(2,1)S(1)} %pad_maximum_fusion.refs_0_), channel_id=1, source_target_pairs={{0,4},{4,0},{8,12},{12,8},{16,20},{20,16},{24,28},{28,24},{1,5},{5... | collective-permute-start | bytes 1966088 | tf_op jit(solution)/shard_map/ppermute | solution.py:19
  241.1 16.2 %collective-permute-start.75 = (bf16[128,1024]{1,0:T(8,128)(2,1)S(1)}, bf16[128,1024]{1,0:T(8,128)(2,1)}, u32[]{:S(2)}, u32[]{:S(2)}) collective-permute-start(bf16[128,1024]{1,0:T(8,128)(2,1)S(1)} %get-tuple-element.115), channel_id=1, source_target_pairs={{0,16},{4,20},{8,24},{12,28},{16,0},{20,4},{24,8},{28,12},{1,17},{... | collective-permute-start | bytes 786440 | tf_op jit(solution)/shard_map/ppermute | solution.py:19
  250.5 21.8 %collective-permute-start.79 = (bf16[256,1024]{1,0:T(8,128)(2,1)S(1)}, bf16[256,1024]{1,0:T(8,128)(2,1)}, u32[]{:S(2)}, u32[]{:S(2)}) collective-permute-start(bf16[256,1024]{1,0:T(8,128)(2,1)S(1)} %maximum_select_fusion.7), channel_id=1, source_target_pairs={{0,16},{4,20},{8,24},{12,28},{16,0},{20,4},{24,8},{28,12},{1,17},{... | collective-permute-start | bytes 1572872 | tf_op jit(solution)/shard_map/ppermute | solution.py:19
  255.0 9.3 %collective-permute-start.63 = (bf16[128,1024]{1,0:T(8,128)(2,1)S(1)}, bf16[128,1024]{1,0:T(8,128)(2,1)S(1)}, u32[]{:S(2)}, u32[]{:S(2)}) collective-permute-start(bf16[128,1024]{1,0:T(8,128)(2,1)S(1)} %get-tuple-element.116), channel_id=1, source_target_pairs={{0,8},{4,12},{8,0},{12,4},{16,24},{20,28},{24,16},{28,20},{1,9},{5... | collective-permute-start | bytes 786440 | tf_op jit(solution)/shard_map/ppermute | solution.py:19
  255.7 15.3 %collective-permute-start.60 = (bf16[128,1024]{1,0:T(8,128)(2,1)S(1)}, bf16[128,1024]{1,0:T(8,128)(2,1)S(1)}, u32[]{:S(2)}, u32[]{:S(2)}) collective-permute-start(bf16[128,1024]{1,0:T(8,128)(2,1)S(1)} %get-tuple-element.117), channel_id=1, source_target_pairs={{0,16},{4,20},{8,24},{12,28},{16,0},{20,4},{24,8},{28,12},{1,17},{... | collective-permute-start | bytes 786440 | tf_op jit(solution)/shard_map/ppermute | solution.py:19
  258.5 17.0 %collective-permute-start.76 = (bf16[256,1024]{1,0:T(8,128)(2,1)S(1)}, bf16[256,1024]{1,0:T(8,128)(2,1)S(1)}, u32[]{:S(2)}, u32[]{:S(2)}) collective-permute-start(bf16[256,1024]{1,0:T(8,128)(2,1)S(1)} %maximum_select_fusion.6), channel_id=1, source_target_pairs={{0,8},{4,12},{8,0},{12,4},{16,24},{20,28},{24,16},{28,20},{1,9},{5... | collective-permute-start | bytes 1572872 | tf_op jit(solution)/shard_map/ppermute | solution.py:19
  264.4 16.5 %collective-permute-start.64 = (bf16[256,1024]{1,0:T(8,128)(2,1)S(1)}, bf16[256,1024]{1,0:T(8,128)(2,1)S(1)}, u32[]{:S(2)}, u32[]{:S(2)}) collective-permute-start(bf16[256,1024]{1,0:T(8,128)(2,1)S(1)} %maximum_select_fusion.5), channel_id=1, source_target_pairs={{0,16},{4,20},{8,24},{12,28},{16,0},{20,4},{24,8},{28,12},{1,17},{... | collective-permute-start | bytes 1572872 | tf_op jit(solution)/shard_map/ppermute | solution.py:19
  271.2 14.0 %collective-permute-start.61 = (bf16[256,1024]{1,0:T(8,128)(2,1)S(1)}, bf16[256,1024]{1,0:T(8,128)(2,1)S(1)}, u32[]{:S(2)}, u32[]{:S(2)}) collective-permute-start(bf16[256,1024]{1,0:T(8,128)(2,1)S(1)} %maximum_select_fusion.4), channel_id=1, source_target_pairs={{0,8},{4,12},{8,0},{12,4},{16,24},{20,28},{24,16},{28,20},{1,9},{5... | collective-permute-start | bytes 1572872 | tf_op jit(solution)/shard_map/ppermute | solution.py:19
  273.9 16.1 %collective-permute-start.80 = (bf16[512,1024]{1,0:T(8,128)(2,1)S(1)}, bf16[512,1024]{1,0:T(8,128)(2,1)S(1)}, u32[]{:S(2)}, u32[]{:S(2)}) collective-permute-start(bf16[512,1024]{1,0:T(8,128)(2,1)S(1)} %maximum_select_fusion.3.refs_3_), channel_id=1, source_target_pairs={{0,4},{4,0},{8,12},{12,8},{16,20},{20,16},{24,28},{28,24},{1,5},{5... | collective-permute-start | bytes 3145736 | tf_op jit(solution)/shard_map/ppermute | solution.py:19
  276.0 14.1 %collective-permute-start.77 = (bf16[512,1024]{1,0:T(8,128)(2,1)S(1)}, bf16[512,1024]{1,0:T(8,128)(2,1)S(1)}, u32[]{:S(2)}, u32[]{:S(2)}) collective-permute-start(bf16[512,1024]{1,0:T(8,128)(2,1)S(1)} %maximum_select_fusion.2.refs_1_), channel_id=1, source_target_pairs={{0,4},{4,0},{8,12},{12,8},{16,20},{20,16},{24,28},{28,24},{1,5},{5... | collective-permute-start | bytes 3145736 | tf_op jit(solution)/shard_map/ppermute | solution.py:19
  281.4 18.5 %collective-permute-start.65 = (bf16[512,1024]{1,0:T(8,128)(2,1)S(1)}, bf16[512,1024]{1,0:T(8,128)(2,1)S(1)}, u32[]{:S(2)}, u32[]{:S(2)}) collective-permute-start(bf16[512,1024]{1,0:T(8,128)(2,1)S(1)} %maximum_select_fusion.1.refs_3_), channel_id=1, source_target_pairs={{0,4},{4,0},{8,12},{12,8},{16,20},{20,16},{24,28},{28,24},{1,5},{5... | collective-permute-start | bytes 3145736 | tf_op jit(solution)/shard_map/ppermute | solution.py:19
  285.7 14.2 %collective-permute-start.62 = (bf16[512,1024]{1,0:T(8,128)(2,1)S(1)}, bf16[512,1024]{1,0:T(8,128)(2,1)S(1)}, u32[]{:S(2)}, u32[]{:S(2)}) collective-permute-start(bf16[512,1024]{1,0:T(8,128)(2,1)S(1)} %maximum_select_fusion.refs_1_), channel_id=1, source_target_pairs={{0,4},{4,0},{8,12},{12,8},{16,20},{20,16},{24,28},{28,24},{1,5},{5... | collective-permute-start | bytes 3145736 | tf_op jit(solution)/shard_map/ppermute | solution.py:19
  (81 other events, 530.8 us)

commit v4 on v3

--- a/solution.py
+++ b/solution.py
@@ -125,19 +125,17 @@
     )
 
 
-def shares_of(view_features, view, after=()):
+def share_of(view_features, view):
     _, count, width = view_features.shape
-    half = count // 2
-
-    def body(_, rows_ref, low_ref, high_ref):
-        low_ref[...] = rows_ref[:half, :]
-        high_ref[...] = rows_ref[half:, :]
-
-    out = like((half, width), BF16)
+
+    def body(_, rows_ref, out_ref):
+        out_ref[...] = rows_ref[...]
+
+    out = like((count, width), BF16)
     return run(
         body, jnp.zeros((1,), jnp.int32), [view_features],
         [pl.BlockSpec((None, count, width), lambda i, s: (view, 0, 0))],
-        [out, out], [whole(out), whole(out)], after=after, moved=4 * count * width, limit=8,
+        [out], [whole(out)], moved=4 * count * width, limit=8,
     )
 
 
@@ -395,7 +393,7 @@
         [whole(one) for one in operands] + ([tile, whole(weight_squares)] if last else []),
         [like((depth, 4 * cols), F32)] + ([like((16, 128), F32)] if last else []),
         [tile] + ([square] if last else []), grid=(4,), after=after,
-        flops=8 * cols * batch * depth, moved=16 * depth * cols * (2 if last else 1), limit=32,
+        flops=8 * cols * batch * depth, moved=16 * depth * cols * (2 if last else 1), limit=20,
     )
 
 
@@ -437,29 +435,27 @@
     def bits_at(level):
         return jnp.stack([bit_value("dp", order[level]) for order in orders])
 
-    shares = [None] * 2
-    shares[1] = go_round(shares_of(view_features, 1))
-    sent, turned_own, weight_squares = turn_weight(weight, core, after=[shares[1][-1][-2]])
+    shares = [go_round(share_of(view_features, v)) for v in (0, 1)]
+    sent, turned_own, weight_squares = turn_weight(weight, core)
     turned_other = swap(sent, "dp", 1)
-    shares[0] = go_round(shares_of(view_features, 0, after=[turned_own]))
 
     turned, gram, normed, half, inverse = ([None] * 2 for _ in range(5))
     ahead = ()
     for v in (1, 0):
-        own = [list(choose(part, n_chip, after=ahead[:1])) for part in shares[v]]
+        own = [list(choose(part, n_chip)) for part in shares[v]]
         for pieces in own:
             for mask in range(1, n_chip):
                 pieces[mask] = swap(pieces[mask], "dp", 2 * mask)
         other = [[swap(piece, "dp", 1) for piece in pieces] for pieces in own]
-        columns = assemble(place, own, other, after=ahead)
+        columns = assemble(place, own, other, after=ahead[:1])
         turned[v] = turn_columns(columns)
         bits = bits_at(0)
         send = forward(1 - bits, turned_own, turned_other, columns)
-        ahead = [send[0]]
         got = [swap(send[p], "dp", 1 << orders[p][0]) for p in range(2)]
-        keep = forward(bits, turned_own, turned_other, columns)
+        keep = forward(bits, turned_own, turned_other, columns, after=[turned[v]])
         for level in range(1, len(high)):
-            send, keep = add_halves(bits_at(level), keep, got)
+            send, keep = add_halves(bits_at(level), keep, got, after=ahead[1:])
+            ahead = [send[0]]
             got = [swap(send[p], "dp", 1 << orders[p][level]) for p in range(2)]
         normed[v], half[v], inverse[v] = normalise(keep, got)
         rows = list(gram_rows(place, half[v], swap(half[v], "dp", 1), n_chip))

time: 339 us -> 306 us (0.903)
  local copies, waits for them, and re-layouts: 38.1 us -> 11.2 us
  starting transfers between devices: 68.4 us -> 58.1 us
  waiting for transfers between devices: 156 us -> 164 us
    unnamed x82 -> x32, local copies, waits for them, and re-layouts: 26.9 us -> 11.1 us
    ppermute x69 -> x55, waiting for transfers between devices: 91.7 us -> 103 us  [swap(): lax.ppermute(value, axis, [(i, i ^ mask) for i in range(lax.axis_size(axi...]
    slice x2, local copies, waits for them, and re-layouts: 11.2 us -> 0.07 us  [per_device(): own = out_grad[path * share:(path + 1) * share]]
    ppermute x69 -> x55, starting transfers between devices: 55 us -> 45.9 us  [swap(): lax.ppermute(value, axis, [(i, i ^ mask) for i in range(lax.axis_size(axi...]
    ppermute x12 -> x6, waiting for transfers between devices: 56.7 us -> 53.8 us  [go_round(): shares.append(lax.ppermute(shares[-1], 'feat', ring))]
    pallas_call x26 -> x24, Pallas kernels: 65.8 us -> 63.9 us  [run(): pl.pallas_call(kernel, grid_spec=pltpu.PrefetchScalarGridSpec(num_scalar_...]
  transfers between devices with their start and end apart: 88 -> 68, of which waited for: 48 -> 43; matrix products, arithmetic and copies ran while one was open for 5% -> 2% of each run, Pallas kernels for 11% -> 16%
where the time goes in v4:
time: 306 us; the launch traced here: 305 us
  waiting for transfers between devices  164 us (54%)
  Pallas kernels  63.9 us (21%)
  starting transfers between devices  58.1 us (19%)
  local copies, waits for them, and re-layouts  11.2 us (4%)
  other arithmetic  6.92 us (2%)
    ppermute x55, waiting for transfers between devices, swap(): lax.ppermute(value, axis, [(i, i ^ mask) for i in range(lax.axis_size(axi...  103 us
    pallas_call x24, Pallas kernels, run(): pl.pallas_call(kernel, grid_spec=pltpu.PrefetchScalarGridSpec(num_scalar_...  63.9 us
    ppermute x6, waiting for transfers between devices, go_round(): shares.append(lax.ppermute(shares[-1], 'feat', ring))  53.8 us
    ppermute x55, starting transfers between devices, swap(): lax.ppermute(value, axis, [(i, i ^ mask) for i in range(lax.axis_size(axi...  45.9 us
    unnamed x32, local copies, waits for them, and re-layouts  11.1 us
    ppermute x7, starting transfers between devices, sum_everywhere(): lax.ppermute(value, axes, [(i, i ^ mask) for i in range(count)])  7.37 us
    ppermute x7, waiting for transfers between devices, sum_everywhere(): lax.ppermute(value, axes, [(i, i ^ mask) for i in range(count)])  7.11 us
  transfers between devices with their start and end apart: 68, of which 43 were waited for; matrix products, arithmetic and copies ran while one was open for 2% of the time, Pallas kernels for 16%

profile of v4, /device:TPU:0, one launch (start us, length us, event | category | flops | bytes accessed | tf_op | source)
XLA Modules:
  0.0 305.2 jit_solution(7133208916483025987)
XLA Ops:
  1.9 3.1 %collective-permute-start = (bf16[128,2048]{1,0:T(8,128)(2,1)S(1)}, bf16[128,2048]{1,0:T(8,128)(2,1)}, u32[]{:S(2)}, u32[]{:S(2)}) collective-permute-start(bf16[128,2048]{1,0:T(8,128)(2,1)S(1)} %shard_map.50.refs_0_), channel_id=1, source_target_pairs={{0,1},{1,2},{2,3},{3,0},{4,5},{5,6},{6,7},{7,4},{8,9},{9,10},{10,1... | collective-permute-start | bytes 1572872 | tf_op jit(solution)/shard_map/ppermute | solution.py:148
  6.6 13.2 %collective-permute-done.refs_1_ = bf16[128,2048]{1,0:T(8,128)(2,1)} collective-permute-done((bf16[128,2048]{1,0:T(8,128)(2,1)S(1)}, bf16[128,2048]{1,0:T(8,128)(2,1)}, u32[]{:S(2)}, u32[]{:S(2)}) %collective-permute-start) | collective-permute-done | bytes 524320 | tf_op jit(solution)/shard_map/ppermute | solution.py:148
  19.9 3.4 %copy-done = f32[1024,2048]{1,0:T(8,128)S(1)} copy-done((f32[1024,2048]{1,0:T(8,128)S(1)}, f32[1024,2048]{1,0:T(8,128)}, u32[]{:S(2)}) %copy-start) | copy-done | bytes 8388632
  23.3 4.6 %shard_map.54 = (bf16[1024,1024]{1,0:T(8,128)(2,1)}, bf16[1024,1024]{1,0:T(8,128)(2,1)S(1)}, f32[8,128]{1,0:T(8,128)S(1)}) custom-call(s32[1]{0:T(128)} %bitcast.1.scalars_ref, f32[1024,2048]{1,0:T(8,128)S(1)} %copy-done), custom_call_target="tpu_custom_call" | custom-call | flops 4194304 | bytes 12582912 | tf_op jit(solution)/shard_map/pallas_call | solution.py:61
  27.9 3.2 %collective-permute-done.11.refs_1_ = bf16[128,2048]{1,0:T(8,128)(2,1)} collective-permute-done((bf16[128,2048]{1,0:T(8,128)(2,1)S(1)}, bf16[128,2048]{1,0:T(8,128)(2,1)}, u32[]{:S(2)}, u32[]{:S(2)}) %collective-permute-start.11) | collective-permute-done | bytes 524320 | tf_op jit(solution)/shard_map/ppermute | solution.py:148
  31.1 11.2 %collective-permute-done.1.refs_2_ = bf16[128,2048]{1,0:T(8,128)(2,1)} collective-permute-done((bf16[128,2048]{1,0:T(8,128)(2,1)}, bf16[128,2048]{1,0:T(8,128)(2,1)}, u32[]{:S(2)}, u32[]{:S(2)}) %collective-permute-start.1) | collective-permute-done | bytes 524320 | tf_op jit(solution)/shard_map/ppermute | solution.py:148
  42.4 11.2 %collective-permute-done.12.refs_2_ = bf16[128,2048]{1,0:T(8,128)(2,1)} collective-permute-done((bf16[128,2048]{1,0:T(8,128)(2,1)}, bf16[128,2048]{1,0:T(8,128)(2,1)}, u32[]{:S(2)}, u32[]{:S(2)}) %collective-permute-start.12) | collective-permute-done | bytes 524320 | tf_op jit(solution)/shard_map/ppermute | solution.py:148
  53.7 11.1 %collective-permute-done.2.refs_3_ = bf16[128,2048]{1,0:T(8,128)(2,1)} collective-permute-done((bf16[128,2048]{1,0:T(8,128)(2,1)}, bf16[128,2048]{1,0:T(8,128)(2,1)}, u32[]{:S(2)}, u32[]{:S(2)}) %collective-permute-start.2) | collective-permute-done | bytes 524320 | tf_op jit(solution)/shard_map/ppermute | solution.py:148
  64.8 2.9 shard_map.51
  67.7 1.7 collective-permute-start.3
  71.2 3.9 %collective-permute-done.13.refs_3_ = bf16[128,2048]{1,0:T(8,128)(2,1)S(1)} collective-permute-done((bf16[128,2048]{1,0:T(8,128)(2,1)}, bf16[128,2048]{1,0:T(8,128)(2,1)S(1)}, u32[]{:S(2)}, u32[]{:S(2)}) %collective-permute-start.13) | collective-permute-done | bytes 524320 | tf_op jit(solution)/shard_map/ppermute | solution.py:148
  76.0 6.6 %collective-permute-done.3.refs_1_ = bf16[128,2048]{1,0:T(8,128)(2,1)S(1)} collective-permute-done((bf16[128,2048]{1,0:T(8,128)(2,1)S(1)}, bf16[128,2048]{1,0:T(8,128)(2,1)S(1)}, u32[]{:S(2)}, u32[]{:S(2)}) %collective-permute-start.3) | collective-permute-done | bytes 524320 | tf_op jit(solution)/shard_map/ppermute | solution.py:19
  82.6 9.7 %collective-permute-done.4.refs_2_ = bf16[128,2048]{1,0:T(8,128)(2,1)} collective-permute-done((bf16[128,2048]{1,0:T(8,128)(2,1)S(1)}, bf16[128,2048]{1,0:T(8,128)(2,1)}, u32[]{:S(2)}, u32[]{:S(2)}) %collective-permute-start.4) | collective-permute-done | bytes 524320 | tf_op jit(solution)/shard_map/ppermute | solution.py:19
  93.9 2.2 shard_map.56
  99.7 2.8 shard_map.52.refs_0_.refs_4_
  102.6 4.2 %shard_map.58 = (bf16[256,1024]{1,0:T(8,128)(2,1)S(1)}, bf16[256,1024]{1,0:T(8,128)(2,1)S(1)}) custom-call(s32[2]{0:T(128)S(1)} %get-tuple-element.88.scalars_ref, bf16[1024,1024]{1,0:T(8,128)(2,1)S(1)} %get-tuple-element.49.refs_0_.refs_2_, bf16[1024,1024]{1,0:T(8,128)(2,1)} %collective-permute-done.10.refs_1_.refs_3_, ...), custom_call_target="tpu_custom_call" | custom-call | flops 2147483648 | bytes 6291456 | tf_op jit(solution)/shard_map/pallas_call | solution.py:61
  108.9 2.1 collective-permute-done.14.refs_1_
  111.0 11.7 %collective-permute-done.15.refs_2_ = bf16[128,2048]{1,0:T(8,128)(2,1)S(1)} collective-permute-done((bf16[128,2048]{1,0:T(8,128)(2,1)S(1)}, bf16[128,2048]{1,0:T(8,128)(2,1)S(1)}, u32[]{:S(2)}, u32[]{:S(2)}) %collective-permute-start.15) | collective-permute-done | bytes 524320 | tf_op jit(solution)/shard_map/ppermute | solution.py:19
  123.2 9.3 %collective-permute-done.21.refs_1_ = bf16[256,1024]{1,0:T(8,128)(2,1)S(1)} collective-permute-done((bf16[256,1024]{1,0:T(8,128)(2,1)S(1)}, bf16[256,1024]{1,0:T(8,128)(2,1)S(1)}, u32[]{:S(2)}, u32[]{:S(2)}) %collective-permute-start.21) | collective-permute-done | bytes 524320 | tf_op jit(solution)/shard_map/ppermute | solution.py:19
  133.9 4.4 %shard_map.57 = (bf16[256,1024]{1,0:T(8,128)(2,1)S(1)}, bf16[256,1024]{1,0:T(8,128)(2,1)S(1)}) custom-call(s32[2]{0:T(128)S(1)} %get-tuple-element.89.scalars_ref, bf16[1024,1024]{1,0:T(8,128)(2,1)S(1)} %get-tuple-element.49.refs_0_.refs_2_, bf16[1024,1024]{1,0:T(8,128)(2,1)} %collective-permute-done.10.refs_1_.refs_3_, ...), custom_call_target="tpu_custom_call" | custom-call | flops 2147483648 | bytes 6291456 | tf_op jit(solution)/shard_map/pallas_call | solution.py:61
  142.1 5.8 %collective-permute-done.26.refs_3_ = bf16[128,1024]{1,0:T(8,128)(2,1)S(1)} collective-permute-done((bf16[128,1024]{1,0:T(8,128)(2,1)S(1)}, bf16[128,1024]{1,0:T(8,128)(2,1)S(1)}, u32[]{:S(2)}, u32[]{:S(2)}) %collective-permute-start.26) | collective-permute-done | bytes 262176 | tf_op jit(solution)/shard_map/ppermute | solution.py:19
  150.2 4.2 %shard_map.63 = (bf16[256,1024]{1,0:T(8,128)(2,1)S(1)}, bf16[256,1024]{1,0:T(8,128)(2,1)S(1)}) custom-call(s32[2]{0:T(128)S(1)} %get-tuple-element.88.scalars_ref, bf16[1024,1024]{1,0:T(8,128)(2,1)S(1)} %get-tuple-element.49.refs_0_.refs_2_, bf16[1024,1024]{1,0:T(8,128)(2,1)} %collective-permute-done.10.refs_1_.refs_3_, ...), custom_call_target="tpu_custom_call" | custom-call | flops 2147483648 | bytes 6291456 | tf_op jit(solution)/shard_map/pallas_call | solution.py:61
  158.3 4.4 %shard_map.62 = (bf16[256,1024]{1,0:T(8,128)(2,1)S(1)}, bf16[256,1024]{1,0:T(8,128)(2,1)S(1)}) custom-call(s32[2]{0:T(128)S(1)} %get-tuple-element.89.scalars_ref, bf16[1024,1024]{1,0:T(8,128)(2,1)S(1)} %get-tuple-element.49.refs_0_.refs_2_, bf16[1024,1024]{1,0:T(8,128)(2,1)} %collective-permute-done.10.refs_1_.refs_3_, ...), custom_call_target="tpu_custom_call" | custom-call | flops 2147483648 | bytes 6291456 | tf_op jit(solution)/shard_map/pallas_call | solution.py:61
  164.1 4.7 %collective-permute-done.23.refs_1_ = bf16[256,1024]{1,0:T(8,128)(2,1)S(1)} collective-permute-done((bf16[256,1024]{1,0:T(8,128)(2,1)S(1)}, bf16[256,1024]{1,0:T(8,128)(2,1)S(1)}, u32[]{:S(2)}, u32[]{:S(2)}) %collective-permute-start.23) | collective-permute-done | bytes 524320 | tf_op jit(solution)/shard_map/ppermute | solution.py:19
  175.8 3.7 %collective-permute-done.28.refs_1_ = bf16[128,1024]{1,0:T(8,128)(2,1)S(1)} collective-permute-done((bf16[128,1024]{1,0:T(8,128)(2,1)S(1)}, bf16[128,1024]{1,0:T(8,128)(2,1)S(1)}, u32[]{:S(2)}, u32[]{:S(2)}) %collective-permute-start.28) | collective-permute-done | bytes 262176 | tf_op jit(solution)/shard_map/ppermute | solution.py:19
  181.4 2.9 collective-permute-done.46
  184.3 1.7 collective-permute-done.48
  191.6 1.9 collective-permute-start.50
  194.5 1.7 collective-permute-done.33
  196.3 1.8 collective-permute-start.34
  202.4 2.8 collective-permute-start.35
  207.0 3.4 %collective-permute-done.35 = bf16[128,640]{1,0:T(8,128)(2,1)S(1)} collective-permute-done((bf16[128,640]{1,0:T(8,128)(2,1)S(1)}, bf16[128,640]{1,0:T(8,128)(2,1)S(1)}, u32[]{:S(2)}, u32[]{:S(2)}) %collective-permute-start.35) | collective-permute-done | bytes 163872 | tf_op jit(solution)/shard_map/ppermute | solution.py:19
  212.1 1.9 collective-permute-start.36
  214.0 2.8 collective-permute-done.38
  218.7 2.3 shard_map.70
  223.4 6.6 %collective-permute-done.58 = bf16[128,1024]{1,0:T(8,128)(2,1)} collective-permute-done((bf16[128,1024]{1,0:T(8,128)(2,1)S(1)}, bf16[128,1024]{1,0:T(8,128)(2,1)}, u32[]{:S(2)}, u32[]{:S(2)}) %collective-permute-start.58) | collective-permute-done | bytes 262176 | tf_op jit(solution)/shard_map/ppermute | solution.py:19
  230.0 2.0 maximum_select_fusion.7
  234.3 2.3 shard_map.69
  239.9 6.0 %collective-permute-done.43 = bf16[128,1024]{1,0:T(8,128)(2,1)S(1)} collective-permute-done((bf16[128,1024]{1,0:T(8,128)(2,1)S(1)}, bf16[128,1024]{1,0:T(8,128)(2,1)S(1)}, u32[]{:S(2)}, u32[]{:S(2)}) %collective-permute-start.43) | collective-permute-done | bytes 262176 | tf_op jit(solution)/shard_map/ppermute | solution.py:19
  247.1 5.5 %collective-permute-done.40 = bf16[128,1024]{1,0:T(8,128)(2,1)S(1)} collective-permute-done((bf16[128,1024]{1,0:T(8,128)(2,1)S(1)}, bf16[128,1024]{1,0:T(8,128)(2,1)S(1)}, u32[]{:S(2)}, u32[]{:S(2)}) %collective-permute-start.40) | collective-permute-done | bytes 262176 | tf_op jit(solution)/shard_map/ppermute | solution.py:19
  253.7 2.0 maximum_select_fusion.3.refs_3_
  257.8 4.8 %collective-permute-done.44 = bf16[256,1024]{1,0:T(8,128)(2,1)S(1)} collective-permute-done((bf16[256,1024]{1,0:T(8,128)(2,1)S(1)}, bf16[256,1024]{1,0:T(8,128)(2,1)S(1)}, u32[]{:S(2)}, u32[]{:S(2)}) %collective-permute-start.44) | collective-permute-done | bytes 524320 | tf_op jit(solution)/shard_map/ppermute | solution.py:19
  263.4 3.4 %collective-permute-done.41 = bf16[256,1024]{1,0:T(8,128)(2,1)S(1)} collective-permute-done((bf16[256,1024]{1,0:T(8,128)(2,1)S(1)}, bf16[256,1024]{1,0:T(8,128)(2,1)S(1)}, u32[]{:S(2)}, u32[]{:S(2)}) %collective-permute-start.41) | collective-permute-done | bytes 524320 | tf_op jit(solution)/shard_map/ppermute | solution.py:19
  267.4 6.4 %shard_map.71.refs_5_ = f32[1024,2048]{1,0:T(8,128)S(1)} custom-call(s32[2]{0:T(128)S(1)} %pad_add_fusion.scalars_ref, bf16[1024,1024]{1,0:T(8,128)(2,1)S(1)} %copy-done.4, bf16[512,1024]{1,0:T(8,128)(2,1)S(1)} %maximum_select_fusion.2.refs_1_, bf16[512,1024]{1,0:T(8,128)(2,1)S(1)} %collective-permute-done.57.refs_2_, ...), custom_call_target="tpu_custom_call" | custom-call | flops 4294967296 | bytes 8388608 | tf_op jit(solution)/shard_map/pallas_call | solution.py:61
  276.2 7.0 %shard_map.72 = (f32[1024,2048]{1,0:T(8,128)S(1)}, f32[16,128]{1,0:T(8,128)S(1)}) custom-call(s32[2]{0:T(128)S(1)} %pad_add_fusion.scalars_ref, bf16[1024,1024]{1,0:T(8,128)(2,1)S(1)} %copy-done.2, bf16[512,1024]{1,0:T(8,128)(2,1)S(1)} %maximum_select_fusion.refs_1_, bf16[512,1024]{1,0:T(8,128)(2,1)S(1)} %copy-done.11, ...), custom_call_target="tpu_custom_call" | custom-call | flops 4294967296 | bytes 16777216 | tf_op jit(solution)/shard_map/pallas_call | solution.py:61
  283.2 1.8 collective-permute-start.63
  295.0 2.7 collective-permute-done.67.refs_1_
  297.7 7.5 %shard_map.73 = (f32[1024,2048]{1,0:T(8,128)}, f32[1024,2048]{1,0:T(8,128)}) custom-call(s32[1]{0:T(128)} %constant.21.clone.1.scalars_ref, f32[16,128]{1,0:T(8,128)S(1)} %add_add_fusion.refs_0_, f32[16,128]{1,0:T(8,128)S(1)} %collective-permute-done.67.refs_1_, f32[1024,2048]{1,0:T(8,128)S(1)} %bitcast.17, f32[1024,2048]{1,0:T(8,128)S(1)} %bitcast.19, ...), custom_call_target="tpu_custom_call" | custom-call | flops 8388608 | bytes 41943040 | tf_op jit(solution)/shard_map/pallas_call | solution.py:61
  (170 shorter events, 77.4 us)
Async XLA Ops:
  1.9 18.0 %collective-permute-start = (bf16[128,2048]{1,0:T(8,128)(2,1)S(1)}, bf16[128,2048]{1,0:T(8,128)(2,1)}, u32[]{:S(2)}, u32[]{:S(2)}) collective-permute-start(bf16[128,2048]{1,0:T(8,128)(2,1)S(1)} %shard_map.50.refs_0_), channel_id=1, source_target_pairs={{0,1},{1,2},{2,3},{3,0},{4,5},{5,6},{6,7},{7,4},{8,9},{9,10},{10,1... | collective-permute-start | bytes 1572872 | tf_op jit(solution)/shard_map/ppermute | solution.py:148
  5.0 26.1 %collective-permute-start.11 = (bf16[128,2048]{1,0:T(8,128)(2,1)S(1)}, bf16[128,2048]{1,0:T(8,128)(2,1)}, u32[]{:S(2)}, u32[]{:S(2)}) collective-permute-start(bf16[128,2048]{1,0:T(8,128)(2,1)S(1)} %shard_map.55.refs_0_), channel_id=1, source_target_pairs={{0,1},{1,2},{2,3},{3,0},{4,5},{5,6},{6,7},{7,4},{8,9},{9,10},{10,1... | collective-permute-start | bytes 1572872 | tf_op jit(solution)/shard_map/ppermute | solution.py:148
  19.9 22.5 %collective-permute-start.1 = (bf16[128,2048]{1,0:T(8,128)(2,1)}, bf16[128,2048]{1,0:T(8,128)(2,1)}, u32[]{:S(2)}, u32[]{:S(2)}) collective-permute-start(bf16[128,2048]{1,0:T(8,128)(2,1)} %collective-permute-done.refs_1_), channel_id=1, source_target_pairs={{0,1},{1,2},{2,3},{3,0},{4,5},{5,6},{6,7},{7,4},{8,9},{9,10},{10,1... | collective-permute-start | bytes 1572872 | tf_op jit(solution)/shard_map/ppermute | solution.py:148
  27.9 74.7 %collective-permute-start.10 = (bf16[1024,1024]{1,0:T(8,128)(2,1)}, bf16[1024,1024]{1,0:T(8,128)(2,1)}, u32[]{:S(2)}, u32[]{:S(2)}) collective-permute-start(bf16[1024,1024]{1,0:T(8,128)(2,1)} %get-tuple-element.50), channel_id=1, source_target_pairs={{0,4},{4,0},{8,12},{12,8},{16,20},{20,16},{24,28},{28,24},{1,5},{5... | collective-permute-start | bytes 6291464 | tf_op jit(solution)/shard_map/ppermute | solution.py:19
  31.1 22.5 %collective-permute-start.12 = (bf16[128,2048]{1,0:T(8,128)(2,1)}, bf16[128,2048]{1,0:T(8,128)(2,1)}, u32[]{:S(2)}, u32[]{:S(2)}) collective-permute-start(bf16[128,2048]{1,0:T(8,128)(2,1)} %collective-permute-done.11.refs_1_), channel_id=1, source_target_pairs={{0,1},{1,2},{2,3},{3,0},{4,5},{5,6},{6,7},{7,4},{8,9},{9,10},{10,1... | collective-permute-start | bytes 1572872 | tf_op jit(solution)/shard_map/ppermute | solution.py:148
  42.3 22.5 %collective-permute-start.2 = (bf16[128,2048]{1,0:T(8,128)(2,1)}, bf16[128,2048]{1,0:T(8,128)(2,1)}, u32[]{:S(2)}, u32[]{:S(2)}) collective-permute-start(bf16[128,2048]{1,0:T(8,128)(2,1)} %collective-permute-done.1.refs_2_), channel_id=1, source_target_pairs={{0,1},{1,2},{2,3},{3,0},{4,5},{5,6},{6,7},{7,4},{8,9},{9,10},{10,1... | collective-permute-start | bytes 1572872 | tf_op jit(solution)/shard_map/ppermute | solution.py:148
  53.6 21.5 %collective-permute-start.13 = (bf16[128,2048]{1,0:T(8,128)(2,1)}, bf16[128,2048]{1,0:T(8,128)(2,1)S(1)}, u32[]{:S(2)}, u32[]{:S(2)}) collective-permute-start(bf16[128,2048]{1,0:T(8,128)(2,1)} %collective-permute-done.12.refs_2_), channel_id=1, source_target_pairs={{0,1},{1,2},{2,3},{3,0},{4,5},{5,6},{6,7},{7,4},{8,9},{9,10},{10,1... | collective-permute-start | bytes 1572872 | tf_op jit(solution)/shard_map/ppermute | solution.py:148
  67.7 14.9 %collective-permute-start.3 = (bf16[128,2048]{1,0:T(8,128)(2,1)S(1)}, bf16[128,2048]{1,0:T(8,128)(2,1)S(1)}, u32[]{:S(2)}, u32[]{:S(2)}) collective-permute-start(bf16[128,2048]{1,0:T(8,128)(2,1)S(1)} %get-tuple-element.46), channel_id=1, source_target_pairs={{0,8},{4,12},{8,0},{12,4},{16,24},{20,28},{24,16},{28,20},{1,9},{5... | collective-permute-start | bytes 1572872 | tf_op jit(solution)/shard_map/ppermute | solution.py:19
  69.4 22.8 %collective-permute-start.4 = (bf16[128,2048]{1,0:T(8,128)(2,1)S(1)}, bf16[128,2048]{1,0:T(8,128)(2,1)}, u32[]{:S(2)}, u32[]{:S(2)}) collective-permute-start(bf16[128,2048]{1,0:T(8,128)(2,1)S(1)} %get-tuple-element.47), channel_id=1, source_target_pairs={{0,16},{4,20},{8,24},{12,28},{16,0},{20,4},{24,8},{28,12},{1,17},{... | collective-permute-start | bytes 1572872 | tf_op jit(solution)/shard_map/ppermute | solution.py:19
  71.0 21.3 %collective-permute-start.5 = (bf16[128,2048]{1,0:T(8,128)(2,1)S(1)}, bf16[128,2048]{1,0:T(8,128)(2,1)}, u32[]{:S(2)}, u32[]{:S(2)}) collective-permute-start(bf16[128,2048]{1,0:T(8,128)(2,1)S(1)} %get-tuple-element.48), channel_id=1, source_target_pairs={{0,24},{4,28},{8,16},{12,20},{16,8},{20,12},{24,0},{28,4},{1,25},{... | collective-permute-start | bytes 1572872 | tf_op jit(solution)/shard_map/ppermute | solution.py:19
  75.9 20.1 %collective-permute-start.6 = (bf16[128,2048]{1,0:T(8,128)(2,1)}, bf16[128,2048]{1,0:T(8,128)(2,1)}, u32[]{:S(2)}, u32[]{:S(2)}) collective-permute-start(bf16[128,2048]{1,0:T(8,128)(2,1)} %get-tuple-element.45.refs_0_), channel_id=1, source_target_pairs={{0,4},{4,0},{8,12},{12,8},{16,20},{20,16},{24,28},{28,24},{1,5},{5... | collective-permute-start | bytes 1572872 | tf_op jit(solution)/shard_map/ppermute | solution.py:19
  82.6 14.4 %collective-permute-start.7 = (bf16[128,2048]{1,0:T(8,128)(2,1)S(1)}, bf16[128,2048]{1,0:T(8,128)(2,1)}, u32[]{:S(2)}, u32[]{:S(2)}) collective-permute-start(bf16[128,2048]{1,0:T(8,128)(2,1)S(1)} %collective-permute-done.3.refs_1_), channel_id=1, source_target_pairs={{0,4},{4,0},{8,12},{12,8},{16,20},{20,16},{24,28},{28,24},{1,5},{5... | collective-permute-start | bytes 1572872 | tf_op jit(solution)/shard_map/ppermute | solution.py:19
  92.3 7.4 %collective-permute-start.9 = (bf16[128,2048]{1,0:T(8,128)(2,1)}, bf16[128,2048]{1,0:T(8,128)(2,1)}, u32[]{:S(2)}, u32[]{:S(2)}) collective-permute-start(bf16[128,2048]{1,0:T(8,128)(2,1)} %collective-permute-done.5.refs_3_), channel_id=1, source_target_pairs={{0,4},{4,0},{8,12},{12,8},{16,20},{20,16},{24,28},{28,24},{1,5},{5... | collective-permute-start | bytes 1572872 | tf_op jit(solution)/shard_map/ppermute | solution.py:19
  96.1 14.9 %collective-permute-start.14 = (bf16[128,2048]{1,0:T(8,128)(2,1)S(1)}, bf16[128,2048]{1,0:T(8,128)(2,1)S(1)}, u32[]{:S(2)}, u32[]{:S(2)}) collective-permute-start(bf16[128,2048]{1,0:T(8,128)(2,1)S(1)} %get-tuple-element.52), channel_id=1, source_target_pairs={{0,8},{4,12},{8,0},{12,4},{16,24},{20,28},{24,16},{28,20},{1,9},{5... | collective-permute-start | bytes 1572872 | tf_op jit(solution)/shard_map/ppermute | solution.py:19
  97.0 25.7 %collective-permute-start.15 = (bf16[128,2048]{1,0:T(8,128)(2,1)S(1)}, bf16[128,2048]{1,0:T(8,128)(2,1)S(1)}, u32[]{:S(2)}, u32[]{:S(2)}) collective-permute-start(bf16[128,2048]{1,0:T(8,128)(2,1)S(1)} %get-tuple-element.53), channel_id=1, source_target_pairs={{0,16},{4,20},{8,24},{12,28},{16,0},{20,4},{24,8},{28,12},{1,17},{... | collective-permute-start | bytes 1572872 | tf_op jit(solution)/shard_map/ppermute | solution.py:19
  98.3 24.9 %collective-permute-start.16 = (bf16[128,2048]{1,0:T(8,128)(2,1)S(1)}, bf16[128,2048]{1,0:T(8,128)(2,1)S(1)}, u32[]{:S(2)}, u32[]{:S(2)}) collective-permute-start(bf16[128,2048]{1,0:T(8,128)(2,1)S(1)} %get-tuple-element.54), channel_id=1, source_target_pairs={{0,24},{4,28},{8,16},{12,20},{16,8},{20,12},{24,0},{28,4},{1,25},{... | collective-permute-start | bytes 1572872 | tf_op jit(solution)/shard_map/ppermute | solution.py:19
  106.8 25.7 %collective-permute-start.21 = (bf16[256,1024]{1,0:T(8,128)(2,1)S(1)}, bf16[256,1024]{1,0:T(8,128)(2,1)S(1)}, u32[]{:S(2)}, u32[]{:S(2)}) collective-permute-start(bf16[256,1024]{1,0:T(8,128)(2,1)S(1)} %get-tuple-element.56), channel_id=1, source_target_pairs={{0,8},{4,12},{8,0},{12,4},{16,24},{20,28},{24,16},{28,20},{1,9},{5... | collective-permute-start | bytes 1572872 | tf_op jit(solution)/shard_map/ppermute | solution.py:19
  107.6 30.7 %collective-permute-start.22 = (bf16[256,1024]{1,0:T(8,128)(2,1)S(1)}, bf16[256,1024]{1,0:T(8,128)(2,1)S(1)}, u32[]{:S(2)}, u32[]{:S(2)}) collective-permute-start(bf16[256,1024]{1,0:T(8,128)(2,1)S(1)} %get-tuple-element.58), channel_id=1, source_target_pairs={{0,16},{4,20},{8,24},{12,28},{16,0},{20,4},{24,8},{28,12},{1,17},{... | collective-permute-start | bytes 1572872 | tf_op jit(solution)/shard_map/ppermute | solution.py:19
  111.0 29.4 %collective-permute-start.17 = (bf16[128,2048]{1,0:T(8,128)(2,1)S(1)}, bf16[128,2048]{1,0:T(8,128)(2,1)S(1)}, u32[]{:S(2)}, u32[]{:S(2)}) collective-permute-start(bf16[128,2048]{1,0:T(8,128)(2,1)S(1)} %get-tuple-element.51.refs_0_), channel_id=1, source_target_pairs={{0,4},{4,0},{8,12},{12,8},{16,20},{20,16},{24,28},{28,24},{1,5},{5... | collective-permute-start | bytes 1572872 | tf_op jit(solution)/shard_map/ppermute | solution.py:19
  122.7 18.5 %collective-permute-start.18 = (bf16[128,2048]{1,0:T(8,128)(2,1)S(1)}, bf16[128,2048]{1,0:T(8,128)(2,1)S(1)}, u32[]{:S(2)}, u32[]{:S(2)}) collective-permute-start(bf16[128,2048]{1,0:T(8,128)(2,1)S(1)} %collective-permute-done.14.refs_1_), channel_id=1, source_target_pairs={{0,4},{4,0},{8,12},{12,8},{16,20},{20,16},{24,28},{28,24},{1,5},{5... | collective-permute-start | bytes 1572872 | tf_op jit(solution)/shard_map/ppermute | solution.py:19
  123.2 18.0 %collective-permute-start.19 = (bf16[128,2048]{1,0:T(8,128)(2,1)S(1)}, bf16[128,2048]{1,0:T(8,128)(2,1)S(1)}, u32[]{:S(2)}, u32[]{:S(2)}) collective-permute-start(bf16[128,2048]{1,0:T(8,128)(2,1)S(1)} %collective-permute-done.15.refs_2_), channel_id=1, source_target_pairs={{0,4},{4,0},{8,12},{12,8},{16,20},{20,16},{24,28},{28,24},{1,5},{5... | collective-permute-start | bytes 1572872 | tf_op jit(solution)/shard_map/ppermute | solution.py:19
  132.5 8.7 %collective-permute-start.20 = (bf16[128,2048]{1,0:T(8,128)(2,1)S(1)}, bf16[128,2048]{1,0:T(8,128)(2,1)S(1)}, u32[]{:S(2)}, u32[]{:S(2)}) collective-permute-start(bf16[128,2048]{1,0:T(8,128)(2,1)S(1)} %collective-permute-done.16.refs_3_), channel_id=1, source_target_pairs={{0,4},{4,0},{8,12},{12,8},{16,20},{20,16},{24,28},{28,24},{1,5},{5... | collective-permute-start | bytes 1572872 | tf_op jit(solution)/shard_map/ppermute | solution.py:19
  139.1 8.8 %collective-permute-start.26 = (bf16[128,1024]{1,0:T(8,128)(2,1)S(1)}, bf16[128,1024]{1,0:T(8,128)(2,1)S(1)}, u32[]{:S(2)}, u32[]{:S(2)}) collective-permute-start(bf16[128,1024]{1,0:T(8,128)(2,1)S(1)} %get-tuple-element.66), channel_id=1, source_target_pairs={{0,8},{4,12},{8,0},{12,4},{16,24},{20,28},{24,16},{28,20},{1,9},{5... | collective-permute-start | bytes 786440 | tf_op jit(solution)/shard_map/ppermute | solution.py:19
  140.4 8.4 %collective-permute-start.25 = (bf16[128,1024]{1,0:T(8,128)(2,1)S(1)}, bf16[128,1024]{1,0:T(8,128)(2,1)S(1)}, u32[]{:S(2)}, u32[]{:S(2)}) collective-permute-start(bf16[128,1024]{1,0:T(8,128)(2,1)S(1)} %get-tuple-element.59.refs_8_), channel_id=1, source_target_pairs={{0,16},{4,20},{8,24},{12,28},{16,0},{20,4},{24,8},{28,12},{1,17},{... | collective-permute-start | bytes 786440 | tf_op jit(solution)/shard_map/ppermute | solution.py:19
  150.2 12.5 %collective-permute-start.27 = (bf16[256,1024]{1,0:T(8,128)(2,1)S(1)}, bf16[256,1024]{1,0:T(8,128)(2,1)S(1)}, u32[]{:S(2)}, u32[]{:S(2)}) collective-permute-start(bf16[256,1024]{1,0:T(8,128)(2,1)S(1)} %get-tuple-element.67.refs_0_.refs_3_.refs_4_), channel_id=1, source_target_pairs={{0,4},{4,0},{8,12},{12,8},{16,20},{20,16},{24,28},{28,24},{1,5},{5... | collective-permute-start | bytes 1572872 | tf_op jit(solution)/shard_map/ppermute | solution.py:19
  154.4 14.4 %collective-permute-start.23 = (bf16[256,1024]{1,0:T(8,128)(2,1)S(1)}, bf16[256,1024]{1,0:T(8,128)(2,1)S(1)}, u32[]{:S(2)}, u32[]{:S(2)}) collective-permute-start(bf16[256,1024]{1,0:T(8,128)(2,1)S(1)} %get-tuple-element.61), channel_id=1, source_target_pairs={{0,8},{4,12},{8,0},{12,4},{16,24},{20,28},{24,16},{28,20},{1,9},{5... | collective-permute-start | bytes 1572872 | tf_op jit(solution)/shard_map/ppermute | solution.py:19
  155.3 14.1 %collective-permute-start.24 = (bf16[256,1024]{1,0:T(8,128)(2,1)S(1)}, bf16[256,1024]{1,0:T(8,128)(2,1)S(1)}, u32[]{:S(2)}, u32[]{:S(2)}) collective-permute-start(bf16[256,1024]{1,0:T(8,128)(2,1)S(1)} %get-tuple-element.63), channel_id=1, source_target_pairs={{0,16},{4,20},{8,24},{12,28},{16,0},{20,4},{24,8},{28,12},{1,17},{... | collective-permute-start | bytes 1572872 | tf_op jit(solution)/shard_map/ppermute | solution.py:19
  170.1 9.3 %collective-permute-start.28 = (bf16[128,1024]{1,0:T(8,128)(2,1)S(1)}, bf16[128,1024]{1,0:T(8,128)(2,1)S(1)}, u32[]{:S(2)}, u32[]{:S(2)}) collective-permute-start(bf16[128,1024]{1,0:T(8,128)(2,1)S(1)} %get-tuple-element.70), channel_id=1, source_target_pairs={{0,16},{4,20},{8,24},{12,28},{16,0},{20,4},{24,8},{28,12},{1,17},{... | collective-permute-start | bytes 786440 | tf_op jit(solution)/shard_map/ppermute | solution.py:19
  171.7 9.2 %collective-permute-start.29 = (bf16[128,1024]{1,0:T(8,128)(2,1)S(1)}, bf16[128,1024]{1,0:T(8,128)(2,1)S(1)}, u32[]{:S(2)}, u32[]{:S(2)}) collective-permute-start(bf16[128,1024]{1,0:T(8,128)(2,1)S(1)} %get-tuple-element.72), channel_id=1, source_target_pairs={{0,8},{4,12},{8,0},{12,4},{16,24},{20,28},{24,16},{28,20},{1,9},{5... | collective-permute-start | bytes 786440 | tf_op jit(solution)/shard_map/ppermute | solution.py:19
  172.3 12.1 %collective-permute-start.46 = (bf16[128,640]{1,0:T(8,128)(2,1)S(1)}, bf16[128,640]{1,0:T(8,128)(2,1)S(1)}, u32[]{:S(2)}, u32[]{:S(2)}) collective-permute-start(bf16[128,640]{1,0:T(8,128)(2,1)S(1)} %get-tuple-element.80), channel_id=1, source_target_pairs={{0,8},{4,12},{8,0},{12,4},{16,24},{20,28},{24,16},{28,20},{1,9},{5... | collective-permute-start | bytes 491528 | tf_op jit(solution)/shard_map/ppermute | solution.py:19
  173.8 10.6 %collective-permute-start.47 = (bf16[128,640]{1,0:T(8,128)(2,1)S(1)}, bf16[128,640]{1,0:T(8,128)(2,1)S(1)}, u32[]{:S(2)}, u32[]{:S(2)}) collective-permute-start(bf16[128,640]{1,0:T(8,128)(2,1)S(1)} %get-tuple-element.81), channel_id=1, source_target_pairs={{0,16},{4,20},{8,24},{12,28},{16,0},{20,4},{24,8},{28,12},{1,17},{... | collective-permute-start | bytes 491528 | tf_op jit(solution)/shard_map/ppermute | solution.py:19
  174.3 11.8 %collective-permute-start.48 = (bf16[128,640]{1,0:T(8,128)(2,1)S(1)}, bf16[128,640]{1,0:T(8,128)(2,1)S(1)}, u32[]{:S(2)}, u32[]{:S(2)}) collective-permute-start(bf16[128,640]{1,0:T(8,128)(2,1)S(1)} %get-tuple-element.82), channel_id=1, source_target_pairs={{0,24},{4,28},{8,16},{12,20},{16,8},{20,12},{24,0},{28,4},{1,25},{... | collective-permute-start | bytes 491528 | tf_op jit(solution)/shard_map/ppermute | solution.py:19
  191.6 7.1 %collective-permute-start.50 = (bf16[128,640]{1,0:T(8,128)(2,1)S(1)}, bf16[128,640]{1,0:T(8,128)(2,1)S(1)}, u32[]{:S(2)}, u32[]{:S(2)}) collective-permute-start(bf16[128,640]{1,0:T(8,128)(2,1)S(1)} %add_convert_fusion.1), channel_id=1, source_target_pairs={{0,2},{1,3},{2,0},{3,1},{4,6},{5,7},{6,4},{7,5},{8,10},{9,11},{10,... | collective-permute-start | bytes 491528 | tf_op jit(solution)/shard_map/ppermute | solution.py:19
  202.4 8.0 %collective-permute-start.35 = (bf16[128,640]{1,0:T(8,128)(2,1)S(1)}, bf16[128,640]{1,0:T(8,128)(2,1)S(1)}, u32[]{:S(2)}, u32[]{:S(2)}) collective-permute-start(bf16[128,640]{1,0:T(8,128)(2,1)S(1)} %add_convert_fusion.4), channel_id=1, source_target_pairs={{0,2},{1,3},{2,0},{3,1},{4,6},{5,7},{6,4},{7,5},{8,10},{9,11},{10,... | collective-permute-start | bytes 491528 | tf_op jit(solution)/shard_map/ppermute | solution.py:19
  207.0 11.8 %collective-permute-start.54 = (bf16[4,128,640]{2,1,0:T(8,128)(2,1)S(1)}, bf16[4,128,640]{2,1,0:T(8,128)(2,1)S(1)}, u32[]{:S(2)}, u32[]{:S(2)}) collective-permute-start(bf16[4,128,640]{2,1,0:T(8,128)(2,1)S(1)} %pad_maximum_fusion.1.refs_0_), channel_id=1, source_target_pairs={{0,4},{4,0},{8,12},{12,8},{16,20},{20,16},{24,28},{28,24},{1,5},{5... | collective-permute-start | bytes 1966088 | tf_op jit(solution)/shard_map/ppermute | solution.py:19
  210.5 7.7 %collective-permute-start.37 = (bf16[128,640]{1,0:T(8,128)(2,1)S(1)}, bf16[128,640]{1,0:T(8,128)(2,1)S(1)}, u32[]{:S(2)}, u32[]{:S(2)}) collective-permute-start(bf16[128,640]{1,0:T(8,128)(2,1)S(1)} %add_convert_fusion.3), channel_id=1, source_target_pairs={{0,16},{4,20},{8,24},{12,28},{16,0},{20,4},{24,8},{28,12},{1,17},{... | collective-permute-start | bytes 491528 | tf_op jit(solution)/shard_map/ppermute | solution.py:19
  218.7 14.4 %collective-permute-start.39 = (bf16[4,128,640]{2,1,0:T(8,128)(2,1)S(1)}, bf16[4,128,640]{2,1,0:T(8,128)(2,1)S(1)}, u32[]{:S(2)}, u32[]{:S(2)}) collective-permute-start(bf16[4,128,640]{2,1,0:T(8,128)(2,1)S(1)} %pad_maximum_fusion.refs_0_), channel_id=1, source_target_pairs={{0,4},{4,0},{8,12},{12,8},{16,20},{20,16},{24,28},{28,24},{1,5},{5... | collective-permute-start | bytes 1966088 | tf_op jit(solution)/shard_map/ppermute | solution.py:19
  221.1 8.9 %collective-permute-start.58 = (bf16[128,1024]{1,0:T(8,128)(2,1)S(1)}, bf16[128,1024]{1,0:T(8,128)(2,1)}, u32[]{:S(2)}, u32[]{:S(2)}) collective-permute-start(bf16[128,1024]{1,0:T(8,128)(2,1)S(1)} %get-tuple-element.90), channel_id=1, source_target_pairs={{0,8},{4,12},{8,0},{12,4},{16,24},{20,28},{24,16},{28,20},{1,9},{5... | collective-permute-start | bytes 786440 | tf_op jit(solution)/shard_map/ppermute | solution.py:19
  222.0 16.5 %collective-permute-start.55 = (bf16[128,1024]{1,0:T(8,128)(2,1)S(1)}, bf16[128,1024]{1,0:T(8,128)(2,1)S(1)}, u32[]{:S(2)}, u32[]{:S(2)}) collective-permute-start(bf16[128,1024]{1,0:T(8,128)(2,1)S(1)} %get-tuple-element.91), channel_id=1, source_target_pairs={{0,16},{4,20},{8,24},{12,28},{16,0},{20,4},{24,8},{28,12},{1,17},{... | collective-permute-start | bytes 786440 | tf_op jit(solution)/shard_map/ppermute | solution.py:19
  232.0 21.7 %collective-permute-start.59 = (bf16[256,1024]{1,0:T(8,128)(2,1)}, bf16[256,1024]{1,0:T(8,128)(2,1)}, u32[]{:S(2)}, u32[]{:S(2)}) collective-permute-start(bf16[256,1024]{1,0:T(8,128)(2,1)} %maximum_select_fusion.7), channel_id=1, source_target_pairs={{0,16},{4,20},{8,24},{12,28},{16,0},{20,4},{24,8},{28,12},{1,17},{... | collective-permute-start | bytes 1572872 | tf_op jit(solution)/shard_map/ppermute | solution.py:19
  236.6 9.3 %collective-permute-start.43 = (bf16[128,1024]{1,0:T(8,128)(2,1)S(1)}, bf16[128,1024]{1,0:T(8,128)(2,1)S(1)}, u32[]{:S(2)}, u32[]{:S(2)}) collective-permute-start(bf16[128,1024]{1,0:T(8,128)(2,1)S(1)} %get-tuple-element.92), channel_id=1, source_target_pairs={{0,8},{4,12},{8,0},{12,4},{16,24},{20,28},{24,16},{28,20},{1,9},{5... | collective-permute-start | bytes 786440 | tf_op jit(solution)/shard_map/ppermute | solution.py:19
  237.9 14.8 %collective-permute-start.40 = (bf16[128,1024]{1,0:T(8,128)(2,1)S(1)}, bf16[128,1024]{1,0:T(8,128)(2,1)S(1)}, u32[]{:S(2)}, u32[]{:S(2)}) collective-permute-start(bf16[128,1024]{1,0:T(8,128)(2,1)S(1)} %get-tuple-element.93), channel_id=1, source_target_pairs={{0,16},{4,20},{8,24},{12,28},{16,0},{20,4},{24,8},{28,12},{1,17},{... | collective-permute-start | bytes 786440 | tf_op jit(solution)/shard_map/ppermute | solution.py:19
  238.6 18.5 %collective-permute-start.56 = (bf16[256,1024]{1,0:T(8,128)(2,1)S(1)}, bf16[256,1024]{1,0:T(8,128)(2,1)S(1)}, u32[]{:S(2)}, u32[]{:S(2)}) collective-permute-start(bf16[256,1024]{1,0:T(8,128)(2,1)S(1)} %maximum_select_fusion.6), channel_id=1, source_target_pairs={{0,8},{4,12},{8,0},{12,4},{16,24},{20,28},{24,16},{28,20},{1,9},{5... | collective-permute-start | bytes 1572872 | tf_op jit(solution)/shard_map/ppermute | solution.py:19
  246.1 16.5 %collective-permute-start.44 = (bf16[256,1024]{1,0:T(8,128)(2,1)S(1)}, bf16[256,1024]{1,0:T(8,128)(2,1)S(1)}, u32[]{:S(2)}, u32[]{:S(2)}) collective-permute-start(bf16[256,1024]{1,0:T(8,128)(2,1)S(1)} %maximum_select_fusion.5), channel_id=1, source_target_pairs={{0,16},{4,20},{8,24},{12,28},{16,0},{20,4},{24,8},{28,12},{1,17},{... | collective-permute-start | bytes 1572872 | tf_op jit(solution)/shard_map/ppermute | solution.py:19
  252.8 14.0 %collective-permute-start.41 = (bf16[256,1024]{1,0:T(8,128)(2,1)S(1)}, bf16[256,1024]{1,0:T(8,128)(2,1)S(1)}, u32[]{:S(2)}, u32[]{:S(2)}) collective-permute-start(bf16[256,1024]{1,0:T(8,128)(2,1)S(1)} %maximum_select_fusion.4), channel_id=1, source_target_pairs={{0,8},{4,12},{8,0},{12,4},{16,24},{20,28},{24,16},{28,20},{1,9},{5... | collective-permute-start | bytes 1572872 | tf_op jit(solution)/shard_map/ppermute | solution.py:19
  255.7 11.7 %collective-permute-start.60 = (bf16[512,1024]{1,0:T(8,128)(2,1)S(1)}, bf16[512,1024]{1,0:T(8,128)(2,1)S(1)}, u32[]{:S(2)}, u32[]{:S(2)}) collective-permute-start(bf16[512,1024]{1,0:T(8,128)(2,1)S(1)} %maximum_select_fusion.3.refs_3_), channel_id=1, source_target_pairs={{0,4},{4,0},{8,12},{12,8},{16,20},{20,16},{24,28},{28,24},{1,5},{5... | collective-permute-start | bytes 3145736 | tf_op jit(solution)/shard_map/ppermute | solution.py:19
  257.7 9.7 %collective-permute-start.57 = (bf16[512,1024]{1,0:T(8,128)(2,1)S(1)}, bf16[512,1024]{1,0:T(8,128)(2,1)S(1)}, u32[]{:S(2)}, u32[]{:S(2)}) collective-permute-start(bf16[512,1024]{1,0:T(8,128)(2,1)S(1)} %maximum_select_fusion.2.refs_1_), channel_id=1, source_target_pairs={{0,4},{4,0},{8,12},{12,8},{16,20},{20,16},{24,28},{28,24},{1,5},{5... | collective-permute-start | bytes 3145736 | tf_op jit(solution)/shard_map/ppermute | solution.py:19
  263.3 10.5 %collective-permute-start.45 = (bf16[512,1024]{1,0:T(8,128)(2,1)S(1)}, bf16[512,1024]{1,0:T(8,128)(2,1)S(1)}, u32[]{:S(2)}, u32[]{:S(2)}) collective-permute-start(bf16[512,1024]{1,0:T(8,128)(2,1)S(1)} %maximum_select_fusion.1.refs_3_), channel_id=1, source_target_pairs={{0,4},{4,0},{8,12},{12,8},{16,20},{20,16},{24,28},{28,24},{1,5},{5... | collective-permute-start | bytes 3145736 | tf_op jit(solution)/shard_map/ppermute | solution.py:19
  (36 other events, 238.2 us)

commit v5 on v4

--- a/solution.py
+++ b/solution.py
@@ -52,7 +52,7 @@
 
 
 def run(body, scalars, operands, in_specs, outs, out_specs, grid=(1,), scratch=(), after=(),
-        flops=0, moved=0, limit=32):
+        flops=0, moved=0, limit=32, name=None):
     n_in, n_after = len(operands), len(after)
 
     def kernel(scalars_ref, *refs):
@@ -70,6 +70,7 @@
         out_shape=list(outs),
         compiler_params=pltpu.CompilerParams(vmem_limit_bytes=limit * MIB),
         cost_estimate=pl.CostEstimate(flops=flops, bytes_accessed=moved, transcendentals=0),
+        name=name,
     )(scalars, *operands, *after)
 
 
@@ -121,22 +122,25 @@
             pl.BlockSpec((step, depth), lambda k, j, c: (jnp.where(k == 1, j, 0), 0)),
             pl.BlockSpec((8, 128), lambda k, j, c: (0, 0)),
         ],
-        grid=(2, 2 * steps), after=after, flops=2 * depth * width, moved=6 * depth * width, limit=16,
-    )
-
-
-def share_of(view_features, view):
+        grid=(2, 2 * steps), after=after, flops=2 * depth * width, moved=6 * depth * width, limit=16, name="turn_weight",
+    )
+
+
+def shares_of(view_features):
     _, count, width = view_features.shape
-
-    def body(_, rows_ref, out_ref):
-        out_ref[...] = rows_ref[...]
-
-    out = like((count, width), BF16)
-    return run(
-        body, jnp.zeros((1,), jnp.int32), [view_features],
-        [pl.BlockSpec((None, count, width), lambda i, s: (view, 0, 0))],
-        [out], [whole(out)], moved=4 * count * width, limit=8,
-    )
+    half = count // 2
+
+    def body(_, rows_ref, first_ref, low_ref, high_ref):
+        low_ref[...] = rows_ref[1, :half, :]
+        high_ref[...] = rows_ref[1, half:, :]
+        first_ref[...] = rows_ref[0]
+
+    outs = [like((rows, width), BF16) for rows in (count, half, half)]
+    first, low, high = run(
+        body, jnp.zeros((1,), jnp.int32), [view_features], [whole(view_features)],
+        outs, [whole(out) for out in outs], moved=8 * count * width, limit=8, name="shares_of",
+    )
+    return [first], [low, high]
 
 
 def go_round(parts):
@@ -166,35 +170,50 @@
     return run(
         body, jnp.stack(back), shares, [whole(share) for share in shares],
         [like(shape, BF16)] * n_chip, [whole(shares[0])] * n_chip,
-        after=after, moved=4 * n_chip * shape[0] * shape[1], limit=16,
-    )
-
-
-def assemble(place, own, other, after=()):
+        after=after, moved=4 * n_chip * shape[0] * shape[1], limit=16, name="choose",
+    )
+
+
+def collect(place, own, after=()):
     n_part, n_chip = len(own), len(own[0])
     count, width = own[0][0].shape
+    operands = [piece for pieces in own for piece in pieces]
+
+    def body(place_ref, *refs):
+        for part in range(n_part):
+            for mask in range(n_chip):
+                row = ((place_ref[0] ^ mask) * n_part + part) * count
+                rows = pl.ds(pl.multiple_of(row, count), count)
+                refs[-1][rows, :] = refs[part * n_chip + mask][...]
+
+    out = like((len(operands) * count, width), BF16)
+    (images,) = run(
+        body, place, operands, [whole(piece) for piece in operands], [out], [whole(out)],
+        after=after, moved=4 * len(operands) * count * width, limit=16, name="collect",
+    )
+    return images
+
+
+def assemble(place, own, other, count, after=()):
+    n_chip = own.shape[0] // count
+    width = own.shape[1]
     half = width // 2
-    operands = [piece for pieces in (*own, *other) for piece in pieces]
-
-    def body(place_ref, *refs):
-        chip, core = place_ref[0], place_ref[1]
-        out_ref = refs[-1]
-        for flip in range(2):
-            for part in range(n_part):
-                for mask in range(n_chip):
-                    piece_ref = refs[(flip * n_part + part) * n_chip + mask]
-                    row = (((chip ^ mask) * 2 + (core ^ flip)) * n_part + part) * count
-                    rows = pl.ds(pl.multiple_of(row, count), count)
-                    for side in range(2):
-                        lane = pl.multiple_of((core ^ side) * half, half)
-                        out_ref[rows, side * half : (side + 1) * half] = piece_ref[
-                            :, pl.ds(lane, half)
-                        ]
-
-    out = like((len(operands) * count, width), BF16)
+
+    def body(place_ref, own_ref, other_ref, out_ref):
+        core = place_ref[1]
+        for flip, ref in ((0, own_ref), (1, other_ref)):
+            for chip in range(n_chip):
+                rows = pl.ds(pl.multiple_of((chip * 2 + (core ^ flip)) * count, count), count)
+                for side in range(2):
+                    lane = pl.multiple_of((core ^ side) * half, half)
+                    out_ref[rows, side * half : (side + 1) * half] = ref[
+                        chip * count : (chip + 1) * count, pl.ds(lane, half)
+                    ]
+
+    out = like((2 * n_chip * count, width), BF16)
     (columns,) = run(
-        body, place, operands, [whole(piece) for piece in operands],
-        [out], [whole(out)], after=after, moved=4 * len(operands) * count * width, limit=24,
+        body, place, [own, other], [whole(own), whole(other)], [out], [whole(out)], after=after,
+        moved=8 * n_chip * count * width, limit=24, name="assemble",
     )
     return columns
 
@@ -211,7 +230,7 @@
         body, jnp.zeros((1,), jnp.int32), [columns],
         [pl.BlockSpec((step, depth), lambda i, s: (i, 0))],
         [like((depth, batch), BF16)], [pl.BlockSpec((depth, step), lambda i, s: (0, i))],
-        grid=(batch // step,), moved=4 * batch * depth, limit=8,
+        grid=(batch // step,), moved=4 * batch * depth, limit=8, name="turn_columns",
     )
     return turned
 
@@ -241,7 +260,7 @@
         body, bits, [turned_own, turned_other, turned_own, turned_other, columns],
         [of_path(0), of_path(0), of_path(1), of_path(1), whole(columns)],
         [like((out_rows, batch), BF16)] * 2, [out_spec] * 2, grid=(steps,), after=after,
-        flops=8 * out_rows * depth * batch, moved=8 * out_rows * depth + 4 * batch * depth,
+        flops=8 * out_rows * depth * batch, moved=8 * out_rows * depth + 4 * batch * depth, name="forward",
     )
 
 
@@ -262,7 +281,7 @@
     out = like((half, batch), BF16)
     outs = run(
         body, bits, operands, [whole(one) for one in operands],
-        [out] * 4, [whole(out)] * 4, after=after, moved=12 * rows * batch, limit=16,
+        [out] * 4, [whole(out)] * 4, after=after, moved=12 * rows * batch, limit=16, name="add_halves",
     )
     return outs[:2], outs[2:]
 
@@ -285,7 +304,7 @@
     outs = [like((2 * rows, width), kind) for width, kind in ((batch, F32), (batch, BF16), (128, F32))]
     return run(
         body, jnp.zeros((1,), jnp.int32), operands, [whole(one) for one in operands],
-        outs, [whole(out) for out in outs], after=after, moved=20 * rows * batch, limit=16,
+        outs, [whole(out) for out in outs], after=after, moved=20 * rows * batch, limit=16, name="normalise",
     )
 
 
@@ -311,8 +330,23 @@
         body, place, [own, other], [whole(own), whole(other)],
         [out] * n_chip, [whole(out)] * n_chip,
         scratch=[pltpu.VMEM((2 * rows, 2 * batch), BF16)], after=after,
-        flops=4 * rows * width * batch // 2, moved=8 * rows * batch, limit=24,
-    )
+        flops=4 * rows * width * batch // 2, moved=8 * rows * batch, limit=24, name="gram_rows",
+    )
+
+
+def pile(parts, after=()):
+    rows, width = parts[0].shape
+
+    def body(_, *refs):
+        for index in range(len(parts)):
+            refs[-1][index] = refs[index][...]
+
+    out = like((len(parts), rows, width), BF16)
+    (stack,) = run(
+        body, jnp.zeros((1,), jnp.int32), parts, [whole(part) for part in parts],
+        [out], [whole(out)], after=after, moved=4 * len(parts) * rows * width, limit=8, name="pile",
+    )
+    return stack
 
 
 def out_grad_of(place, gram_own, gram_other, normed, half, half_other, inverse, after=()):
@@ -353,7 +387,7 @@
     (out_grad,) = run(
         body, place, operands, [whole(one) for one in operands], [out], [whole(out)],
         scratch=[pltpu.VMEM((batch, batch), BF16)], after=after,
-        flops=2 * rows * batch * batch, moved=12 * rows * batch + 2 * batch * batch, limit=24,
+        flops=2 * rows * batch * batch, moved=12 * rows * batch + 2 * batch * batch, limit=24, name="out_grad_of",
     )
     return out_grad
 
@@ -393,7 +427,7 @@
         [whole(one) for one in operands] + ([tile, whole(weight_squares)] if last else []),
         [like((depth, 4 * cols), F32)] + ([like((16, 128), F32)] if last else []),
         [tile] + ([square] if last else []), grid=(4,), after=after,
-        flops=8 * cols * batch * depth, moved=16 * depth * cols * (2 if last else 1), limit=20,
+        flops=8 * cols * batch * depth, moved=16 * depth * cols * (2 if last else 1), limit=20, name="weight_grad_of",
     )
 
 
@@ -419,7 +453,7 @@
     return run(
         body, jnp.zeros((1,), jnp.int32), [*sums, weight, velocity, weight_grad],
         [whole(one) for one in sums] + [tile] * 3, [out, out], [tile, tile],
-        grid=(depth // step,), flops=4 * depth * width, moved=20 * depth * width, limit=16,
+        grid=(depth // step,), flops=4 * depth * width, moved=20 * depth * width, limit=16, name="update",
     )
 
 
@@ -435,54 +469,96 @@
     def bits_at(level):
         return jnp.stack([bit_value("dp", order[level]) for order in orders])
 
-    shares = [go_round(share_of(view_features, v)) for v in (0, 1)]
-    sent, turned_own, weight_squares = turn_weight(weight, core)
-    turned_other = swap(sent, "dp", 1)
-
-    turned, gram, normed, half, inverse = ([None] * 2 for _ in range(5))
-    ahead = ()
-    for v in (1, 0):
-        own = [list(choose(part, n_chip)) for part in shares[v]]
-        for pieces in own:
-            for mask in range(1, n_chip):
-                pieces[mask] = swap(pieces[mask], "dp", 2 * mask)
-        other = [[swap(piece, "dp", 1) for piece in pieces] for pieces in own]
-        columns = assemble(place, own, other, after=ahead[:1])
-        turned[v] = turn_columns(columns)
-        bits = bits_at(0)
-        send = forward(1 - bits, turned_own, turned_other, columns)
-        got = [swap(send[p], "dp", 1 << orders[p][0]) for p in range(2)]
-        keep = forward(bits, turned_own, turned_other, columns, after=[turned[v]])
-        for level in range(1, len(high)):
-            send, keep = add_halves(bits_at(level), keep, got, after=ahead[1:])
-            ahead = [send[0]]
-            got = [swap(send[p], "dp", 1 << orders[p][level]) for p in range(2)]
-        normed[v], half[v], inverse[v] = normalise(keep, got)
-        rows = list(gram_rows(place, half[v], swap(half[v], "dp", 1), n_chip))
-        ahead.append(rows[0])
+    shares = [go_round(parts) for parts in shares_of(view_features)]
+    def cross_plane(part, after=()):
+        own = list(choose(part, n_chip, after=after))
+        for mask in range(1, n_chip):
+            own[mask] = swap(own[mask], "dp", 2 * mask)
+        return own
+
+    def both_cores(own, collect_after=(), after=()):
+        images = collect(place, own, after=collect_after)
+        other = swap(images, "dp", 1)
+        return assemble(place, images, other, view_features.shape[1], after=after)
+
+    def send_on(v, level, send):
+        return [swap(send[p], "dp", 1 << orders[p][level]) for p in range(2)]
+
+    def sum_plane(rows):
         total = rows[0].astype(F32)
         for mask in range(1, n_chip):
             total += swap(rows[mask], "dp", 2 * mask).astype(F32)
-        total = total.astype(BF16)
-        for bit in range(n_feat.bit_length() - 1):
-            total = (total.astype(F32) + swap(total, "feat", 1 << bit).astype(F32)).astype(BF16)
-        gram_own = jnp.stack(
-            [total] + [swap(total, "dp", 2 * mask) for mask in range(1, n_chip)]
-        )
-        gram[v] = (gram_own, swap(gram_own, "dp", 1))
-
-    for v in (0, 1):
-        out_grad = out_grad_of(place, *gram[1 - v], normed[v], half[v], half[1 - v], inverse[v])
-        share = out_grad.shape[0] // 2
-        pieces = []
-        for path in range(2):
-            own = out_grad[path * share : (path + 1) * share]
-            for bit in reversed(orders[path]):
-                own = join(own, swap(own, "dp", 1 << bit), bit_value("dp", bit))
-            pieces += [own, swap(own, "dp", 1)]
-        if v == 0:
-            (base,) = weight_grad_of(place, turned[v], pieces)
-    weight_grad, squares = weight_grad_of(place, turned[1], pieces, base, weight_squares)
+        return total.astype(BF16)
+
+    def sum_line(total, bit):
+        return (total.astype(F32) + swap(total, "feat", 1 << bit).astype(F32)).astype(BF16)
+
+    def spread_gram(total, after=()):
+        parts = [total] + [swap(total, "dp", 2 * mask) for mask in range(1, n_chip)]
+        own = pile(parts, after=after)
+        return own, swap(own, "dp", 1)
+
+    def gather_step(parts, step):
+        bits_of = [order[len(order) - 1 - step] for order in orders]
+        return [
+            join(part, swap(part, "dp", 1 << bit), bit_value("dp", bit))
+            for part, bit in zip(parts, bits_of)
+        ]
+
+    columns, turned, send, keep, got, gram, normed, half, inverse, rows = (
+        [None] * 2 for _ in range(10)
+    )
+    bits = bits_at(0)
+    line_bits = range(n_feat.bit_length() - 1)
+    pieces = [cross_plane(part) for part in shares[1]]
+    sent, turned_own, weight_squares = turn_weight(weight, core, after=[pieces[1][0]])
+    turned_other = swap(sent, "dp", 1)
+    columns[1] = both_cores(pieces, collect_after=[turned_own, shares[0][0][-2]])
+    turned[1] = turn_columns(columns[1])
+    send[1] = forward(1 - bits, turned_own, turned_other, columns[1])
+    got[1] = send_on(1, 0, send[1])
+    pieces = [cross_plane(part, [send[1][0]]) for part in shares[0]]
+    keep[1] = forward(bits, turned_own, turned_other, columns[1], after=[turned[1], send[1][0]])
+    for level in range(1, len(high)):
+        send[1], keep[1] = add_halves(bits_at(level), keep[1], got[1])
+        got[1] = send_on(1, level, send[1])
+    columns[0] = both_cores(pieces, [send[1][0]])
+    turned[0] = turn_columns(columns[0])
+    send[0] = forward(1 - bits, turned_own, turned_other, columns[0])
+    ahead = [send[0][0]]
+    got[0] = send_on(0, 0, send[0])
+    normed[1], half[1], inverse[1] = normalise(keep[1], got[1], after=ahead)
+    rows[1] = list(gram_rows(place, half[1], swap(half[1], "dp", 1), n_chip))
+    gram[1] = sum_plane(rows[1])
+    keep[0] = forward(bits, turned_own, turned_other, columns[0], after=[turned[0], send[1][0]])
+    for level in range(1, len(high)):
+        send[0], keep[0] = add_halves(bits_at(level), keep[0], got[0], after=[rows[1][0]])
+        got[0] = send_on(0, level, send[0])
+    normed[0], half[0], inverse[0] = normalise(keep[0], got[0], after=[gram[1]])
+    rows[0] = list(gram_rows(place, half[0], swap(half[0], "dp", 1), n_chip))
+    for bit in line_bits:
+        gram[1] = sum_line(gram[1], bit)
+    gram[1] = spread_gram(gram[1])
+    out_grad = [None] * 2
+    out_grad[0] = out_grad_of(place, *gram[1], normed[0], half[0], half[1], inverse[0])
+    gram[0] = sum_plane(rows[0])
+    for bit in line_bits:
+        gram[0] = sum_line(gram[0], bit)
+    gram[0] = spread_gram(gram[0], after=[out_grad[0]])
+    share = out_grad[0].shape[0] // 2
+    parts = [None] * 2
+    parts[0] = gather_step([out_grad[0][:share], out_grad[0][share:]], 0)
+    out_grad[1] = out_grad_of(
+        place, *gram[0], normed[1], half[1], half[0], inverse[1], after=[parts[0][0]]
+    )
+    parts[1] = gather_step([out_grad[1][:share], out_grad[1][share:]], 0)
+    for step in range(1, len(high)):
+        parts = [gather_step(part, step) for part in parts]
+    gathered = [[one for own in part for one in (own, swap(own, "dp", 1))] for part in parts]
+    (base,) = weight_grad_of(place, turned[0], gathered[0])
+    weight_grad, squares = weight_grad_of(
+        place, turned[1], gathered[1], base, weight_squares
+    )
     return update(sum_everywhere(squares), weight, velocity, weight_grad)
 
 

time: 306 us -> 292 us (0.954)
  waiting for transfers between devices: 164 us -> 146 us
  starting transfers between devices: 58.1 us -> 62.6 us
  Pallas kernels: 63.9 us -> 68.1 us
  other arithmetic: 6.92 us -> 3.32 us
    ppermute x6 -> x9, waiting for transfers between devices: 53.8 us -> 41.9 us  [go_round(): shares.append(lax.ppermute(shares[-1], 'feat', ring))]
    ppermute x55 -> x52, waiting for transfers between devices: 103 us -> 97.9 us  [swap(): lax.ppermute(value, axis, [(i, i ^ mask) for i in range(lax.axis_size(axi...]
    pallas_call x24 -> x28, Pallas kernels: 63.9 us -> 68.1 us  [run(): pl.pallas_call(kernel, grid_spec=pltpu.PrefetchScalarGridSpec(num_scalar_...]
    select_n x8, other arithmetic: 6.06 us -> 2.67 us  [join(): jnp.where(bit == 0, jnp.concatenate([mine, other], 0), jnp.concatenate([o...]
    ppermute x55 -> x52, starting transfers between devices: 45.9 us -> 48.5 us  [swap(): lax.ppermute(value, axis, [(i, i ^ mask) for i in range(lax.axis_size(axi...]
    ppermute x6 -> x9, starting transfers between devices: 4.83 us -> 6.63 us  [go_round(): shares.append(lax.ppermute(shares[-1], 'feat', ring))]
    unnamed x32 -> x40, local copies, waits for them, and re-layouts: 11.1 us -> 10.3 us
  transfers between devices with their start and end apart: 68 -> 68, of which waited for: 43 -> 40; matrix products, arithmetic and copies ran while one was open for 2% -> 1% of each run, Pallas kernels for 16% -> 17%
where the time goes in v5:
time: 292 us
  waiting for transfers between devices  146 us (50%)
  Pallas kernels  68.1 us (23%)
  starting transfers between devices  62.6 us (21%)
  local copies, waits for them, and re-layouts  10.4 us (4%)
  other arithmetic  3.32 us (1%)
    ppermute x52, waiting for transfers between devices, swap(): lax.ppermute(value, axis, [(i, i ^ mask) for i in range(lax.axis_size(axi...  97.9 us
    pallas_call x28, Pallas kernels, run(): pl.pallas_call(kernel, grid_spec=pltpu.PrefetchScalarGridSpec(num_scalar_...  68.1 us
    ppermute x52, starting transfers between devices, swap(): lax.ppermute(value, axis, [(i, i ^ mask) for i in range(lax.axis_size(axi...  48.5 us
    ppermute x9, waiting for transfers between devices, go_round(): shares.append(lax.ppermute(shares[-1], 'feat', ring))  41.9 us
    unnamed x40, local copies, waits for them, and re-layouts  10.3 us
    ppermute x7, starting transfers between devices, sum_everywhere(): lax.ppermute(value, axes, [(i, i ^ mask) for i in range(count)])  7.47 us
    ppermute x9, starting transfers between devices, go_round(): shares.append(lax.ppermute(shares[-1], 'feat', ring))  6.63 us
    ppermute x7, waiting for transfers between devices, sum_everywhere(): lax.ppermute(value, axes, [(i, i ^ mask) for i in range(count)])  6.51 us
  transfers between devices with their start and end apart: 68, of which 40 were waited for; matrix products, arithmetic and copies ran while one was open for 1% of the time, Pallas kernels for 17%

profile of v5, /device:TPU:0, one launch (start us, length us, event | category | flops | bytes accessed | tf_op | source)
XLA Modules:
  0.0 292.0 jit_solution(5241543921232902998)
XLA Ops:
  1.9 3.1 %collective-permute-start = (bf16[64,2048]{1,0:T(8,128)(2,1)S(1)}, bf16[64,2048]{1,0:T(8,128)(2,1)S(1)}, u32[]{:S(2)}, u32[]{:S(2)}) collective-permute-start(bf16[64,2048]{1,0:T(8,128)(2,1)S(1)} %get-tuple-element.52.refs_0_), channel_id=1, source_target_pairs={{0,1},{1,2},{2,3},{3,0},{4,5},{5,6},{6,7},{7,4},{8,9},{9,10},{10,1... | collective-permute-start | bytes 786440 | tf_op jit(solution)/shard_map/ppermute | solution.py:152
  6.6 7.6 %collective-permute-done.refs_1_ = bf16[64,2048]{1,0:T(8,128)(2,1)S(1)} collective-permute-done((bf16[64,2048]{1,0:T(8,128)(2,1)S(1)}, bf16[64,2048]{1,0:T(8,128)(2,1)S(1)}, u32[]{:S(2)}, u32[]{:S(2)}) %collective-permute-start) | collective-permute-done | bytes 262176 | tf_op jit(solution)/shard_map/ppermute | solution.py:152
  15.8 4.0 %collective-permute-done.6.refs_1_ = bf16[64,2048]{1,0:T(8,128)(2,1)S(1)} collective-permute-done((bf16[64,2048]{1,0:T(8,128)(2,1)S(1)}, bf16[64,2048]{1,0:T(8,128)(2,1)S(1)}, u32[]{:S(2)}, u32[]{:S(2)}) %collective-permute-start.6) | collective-permute-done | bytes 262176 | tf_op jit(solution)/shard_map/ppermute | solution.py:152
  19.8 5.6 %collective-permute-done.1.refs_2_ = bf16[64,2048]{1,0:T(8,128)(2,1)S(1)} collective-permute-done((bf16[64,2048]{1,0:T(8,128)(2,1)S(1)}, bf16[64,2048]{1,0:T(8,128)(2,1)S(1)}, u32[]{:S(2)}, u32[]{:S(2)}) %collective-permute-start.1) | collective-permute-done | bytes 262176 | tf_op jit(solution)/shard_map/ppermute | solution.py:152
  25.5 16.7 %collective-permute-done.7.refs_2_ = bf16[64,2048]{1,0:T(8,128)(2,1)S(1)} collective-permute-done((bf16[64,2048]{1,0:T(8,128)(2,1)S(1)}, bf16[64,2048]{1,0:T(8,128)(2,1)S(1)}, u32[]{:S(2)}, u32[]{:S(2)}) %collective-permute-start.7) | collective-permute-done | bytes 262176 | tf_op jit(solution)/shard_map/ppermute | solution.py:152
  42.3 5.6 %collective-permute-done.2.refs_3_ = bf16[64,2048]{1,0:T(8,128)(2,1)S(1)} collective-permute-done((bf16[64,2048]{1,0:T(8,128)(2,1)S(1)}, bf16[64,2048]{1,0:T(8,128)(2,1)S(1)}, u32[]{:S(2)}, u32[]{:S(2)}) %collective-permute-start.2) | collective-permute-done | bytes 262176 | tf_op jit(solution)/shard_map/ppermute | solution.py:152
  56.9 2.4 collective-permute-done.3.refs_1_
  60.0 1.8 collective-permute-start.10
  65.6 3.4 %copy-done = f32[1024,2048]{1,0:T(8,128)S(1)} copy-done((f32[1024,2048]{1,0:T(8,128)S(1)}, f32[1024,2048]{1,0:T(8,128)}, u32[]{:S(2)}) %copy-start) | copy-done | bytes 8388632
  69.0 4.6 %turn_weight.1 = (bf16[1024,1024]{1,0:T(8,128)(2,1)}, bf16[1024,1024]{1,0:T(8,128)(2,1)S(1)}, f32[8,128]{1,0:T(8,128)S(1)}) custom-call(s32[1]{0:T(128)} %bitcast.1.scalars_ref, f32[1024,2048]{1,0:T(8,128)S(1)} %copy-done, bf16[64,2048]{1,0:T(8,128)(2,1)S(1)} %get-tuple-element.58.refs_1_.refs_4_), custom_call_target="tpu_custom_call" | custom-call | flops 4194304 | bytes 12582912 | tf_op jit(solution)/shard_map/turn_weight/pallas_call | solution.py:61
  74.6 3.2 %collect.2.refs_0_ = bf16[512,2048]{1,0:T(8,128)(2,1)} custom-call(s32[2]{0:T(128)S(1)} %pad_add_fusion.scalars_ref, bf16[64,2048]{1,0:T(8,128)(2,1)S(1)} %copy-done.9, bf16[64,2048]{1,0:T(8,128)(2,1)S(1)} %copy-done.11, bf16[64,2048]{1,0:T(8,128)(2,1)S(1)} %copy-done.13, bf16[64,2048]{1,0:T(8,128)(2,1)} %collective-permute-done.5.refs_3_, ...), custom_call_target="tpu_custom_call" | custom-call | bytes 4194304 | tf_op jit(solution)/shard_map/collect/pallas_call | solution.py:61
  78.7 3.6 %collective-permute-done.14.refs_1_ = bf16[512,2048]{1,0:T(8,128)(2,1)} collective-permute-done((bf16[512,2048]{1,0:T(8,128)(2,1)}, bf16[512,2048]{1,0:T(8,128)(2,1)}, u32[]{:S(2)}, u32[]{:S(2)}) %collective-permute-start.14) | collective-permute-done | bytes 2097184 | tf_op jit(solution)/shard_map/ppermute | solution.py:19
  82.3 3.0 %assemble.2.refs_0_.refs_4_ = bf16[1024,2048]{1,0:T(8,128)(2,1)S(1)} custom-call(s32[2]{0:T(128)S(1)} %pad_add_fusion.scalars_ref, bf16[512,2048]{1,0:T(8,128)(2,1)} %collect.2.refs_0_, bf16[512,2048]{1,0:T(8,128)(2,1)} %collective-permute-done.14.refs_1_), custom_call_target="tpu_custom_call" | custom-call | bytes 8388608 | tf_op jit(solution)/shard_map/assemble/pallas_call | solution.py:61
  85.4 4.2 %forward.4 = (bf16[256,1024]{1,0:T(8,128)(2,1)S(1)}, bf16[256,1024]{1,0:T(8,128)(2,1)S(1)}) custom-call(s32[2]{0:T(128)S(1)} %get-tuple-element.102.scalars_ref, bf16[1024,1024]{1,0:T(8,128)(2,1)S(1)} %get-tuple-element.62.refs_8_.refs_0_.refs_2_, bf16[1024,1024]{1,0:T(8,128)(2,1)} %collective-permute-done.15.refs_1_.refs_3_, ...), custom_call_target="tpu_custom_call" | custom-call | flops 2147483648 | bytes 6291456 | tf_op jit(solution)/shard_map/forward/pallas_call | solution.py:61
  91.7 2.4 collective-permute-done.16.refs_3_
  94.1 2.2 choose.5
  96.2 2.0 collective-permute-start.17
  101.2 4.4 %forward.5 = (bf16[256,1024]{1,0:T(8,128)(2,1)S(1)}, bf16[256,1024]{1,0:T(8,128)(2,1)S(1)}) custom-call(s32[2]{0:T(128)S(1)} %get-tuple-element.103.scalars_ref, bf16[1024,1024]{1,0:T(8,128)(2,1)S(1)} %get-tuple-element.62.refs_8_.refs_0_.refs_2_, bf16[1024,1024]{1,0:T(8,128)(2,1)} %collective-permute-done.15.refs_1_.refs_3_, ...), custom_call_target="tpu_custom_call" | custom-call | flops 2147483648 | bytes 6291456 | tf_op jit(solution)/shard_map/forward/pallas_call | solution.py:61
  106.8 10.4 %collective-permute-done.17.refs_1_ = bf16[128,2048]{1,0:T(8,128)(2,1)S(1)} collective-permute-done((bf16[128,2048]{1,0:T(8,128)(2,1)S(1)}, bf16[128,2048]{1,0:T(8,128)(2,1)S(1)}, u32[]{:S(2)}, u32[]{:S(2)}) %collective-permute-start.17) | collective-permute-done | bytes 524320 | tf_op jit(solution)/shard_map/ppermute | solution.py:19
  117.2 10.3 %collective-permute-done.19.refs_3_ = bf16[128,2048]{1,0:T(8,128)(2,1)S(1)} collective-permute-done((bf16[128,2048]{1,0:T(8,128)(2,1)S(1)}, bf16[128,2048]{1,0:T(8,128)(2,1)S(1)}, u32[]{:S(2)}, u32[]{:S(2)}) %collective-permute-start.19) | collective-permute-done | bytes 524320 | tf_op jit(solution)/shard_map/ppermute | solution.py:19
  128.2 1.8 collective-permute-start.26
  130.4 2.0 collective-permute-done.22.refs_1_
  133.2 4.2 %forward.7 = (bf16[256,1024]{1,0:T(8,128)(2,1)S(1)}, bf16[256,1024]{1,0:T(8,128)(2,1)S(1)}) custom-call(s32[2]{0:T(128)S(1)} %get-tuple-element.102.scalars_ref, bf16[1024,1024]{1,0:T(8,128)(2,1)S(1)} %get-tuple-element.62.refs_8_.refs_0_.refs_2_, bf16[1024,1024]{1,0:T(8,128)(2,1)} %collective-permute-done.15.refs_1_.refs_3_, ...), custom_call_target="tpu_custom_call" | custom-call | flops 2147483648 | bytes 6291456 | tf_op jit(solution)/shard_map/forward/pallas_call | solution.py:61
  147.0 4.2 %forward.6 = (bf16[256,1024]{1,0:T(8,128)(2,1)S(1)}, bf16[256,1024]{1,0:T(8,128)(2,1)S(1)}) custom-call(s32[2]{0:T(128)S(1)} %get-tuple-element.103.scalars_ref, bf16[1024,1024]{1,0:T(8,128)(2,1)S(1)} %get-tuple-element.62.refs_8_.refs_0_.refs_2_, bf16[1024,1024]{1,0:T(8,128)(2,1)} %collective-permute-done.15.refs_1_.refs_3_, ...), custom_call_target="tpu_custom_call" | custom-call | flops 2147483648 | bytes 6291456 | tf_op jit(solution)/shard_map/forward/pallas_call | solution.py:61
  151.2 2.5 collective-permute-done.24.refs_3_
  157.6 4.6 %collective-permute-done.32 = bf16[128,640]{1,0:T(8,128)(2,1)S(1)} collective-permute-done((bf16[128,640]{1,0:T(8,128)(2,1)S(1)}, bf16[128,640]{1,0:T(8,128)(2,1)S(1)}, u32[]{:S(2)}, u32[]{:S(2)}) %collective-permute-start.32) | collective-permute-done | bytes 163872 | tf_op jit(solution)/shard_map/ppermute | solution.py:19
  162.4 3.4 %collective-permute-done.28.refs_1_ = bf16[128,1024]{1,0:T(8,128)(2,1)S(1)} collective-permute-done((bf16[128,1024]{1,0:T(8,128)(2,1)S(1)}, bf16[128,1024]{1,0:T(8,128)(2,1)S(1)}, u32[]{:S(2)}, u32[]{:S(2)}) %collective-permute-start.28) | collective-permute-done | bytes 262176 | tf_op jit(solution)/shard_map/ppermute | solution.py:19
  173.3 3.8 %collective-permute-done.43 = bf16[128,640]{1,0:T(8,128)(2,1)S(1)} collective-permute-done((bf16[128,640]{1,0:T(8,128)(2,1)S(1)}, bf16[128,640]{1,0:T(8,128)(2,1)S(1)}, u32[]{:S(2)}, u32[]{:S(2)}) %collective-permute-start.43) | collective-permute-done | bytes 163872 | tf_op jit(solution)/shard_map/ppermute | solution.py:19
  180.8 2.6 collective-permute-start.37
  183.4 1.8 collective-permute-done.46.refs_3_
  185.2 2.5 collective-permute-done.45.refs_2_
  189.2 10.0 %collective-permute-done.38 = bf16[128,640]{1,0:T(8,128)(2,1)S(1)} collective-permute-done((bf16[128,640]{1,0:T(8,128)(2,1)S(1)}, bf16[128,640]{1,0:T(8,128)(2,1)S(1)}, u32[]{:S(2)}, u32[]{:S(2)}) %collective-permute-start.38) | collective-permute-done | bytes 163872 | tf_op jit(solution)/shard_map/ppermute | solution.py:19
  202.8 2.4 out_grad_of.2.refs_4_
  205.1 2.1 collective-permute-done.41.refs_3_
  207.3 2.4 collective-permute-done.40.refs_2_
  211.9 6.8 %collective-permute-done.58 = bf16[128,1024]{1,0:T(8,128)(2,1)S(1)} collective-permute-done((bf16[128,1024]{1,0:T(8,128)(2,1)S(1)}, bf16[128,1024]{1,0:T(8,128)(2,1)S(1)}, u32[]{:S(2)}, u32[]{:S(2)}) %collective-permute-start.58) | collective-permute-done | bytes 262176 | tf_op jit(solution)/shard_map/ppermute | solution.py:19
  221.4 2.4 out_grad_of.3
  226.8 6.4 %collective-permute-done.53 = bf16[128,1024]{1,0:T(8,128)(2,1)S(1)} collective-permute-done((bf16[128,1024]{1,0:T(8,128)(2,1)S(1)}, bf16[128,1024]{1,0:T(8,128)(2,1)S(1)}, u32[]{:S(2)}, u32[]{:S(2)}) %collective-permute-start.53) | collective-permute-done | bytes 262176 | tf_op jit(solution)/shard_map/ppermute | solution.py:19
  234.2 5.1 %collective-permute-done.50 = bf16[128,1024]{1,0:T(8,128)(2,1)S(1)} collective-permute-done((bf16[128,1024]{1,0:T(8,128)(2,1)S(1)}, bf16[128,1024]{1,0:T(8,128)(2,1)S(1)}, u32[]{:S(2)}, u32[]{:S(2)}) %collective-permute-start.50) | collective-permute-done | bytes 262176 | tf_op jit(solution)/shard_map/ppermute | solution.py:19
  241.2 3.2 %collective-permute-done.56 = bf16[256,1024]{1,0:T(8,128)(2,1)S(1)} collective-permute-done((bf16[256,1024]{1,0:T(8,128)(2,1)S(1)}, bf16[256,1024]{1,0:T(8,128)(2,1)S(1)}, u32[]{:S(2)}, u32[]{:S(2)}) %collective-permute-start.56) | collective-permute-done | bytes 524320 | tf_op jit(solution)/shard_map/ppermute | solution.py:19
  245.0 4.3 %collective-permute-done.54 = bf16[256,1024]{1,0:T(8,128)(2,1)S(1)} collective-permute-done((bf16[256,1024]{1,0:T(8,128)(2,1)S(1)}, bf16[256,1024]{1,0:T(8,128)(2,1)S(1)}, u32[]{:S(2)}, u32[]{:S(2)}) %collective-permute-start.54) | collective-permute-done | bytes 524320 | tf_op jit(solution)/shard_map/ppermute | solution.py:19
  250.1 4.0 %collective-permute-done.51 = bf16[256,1024]{1,0:T(8,128)(2,1)S(1)} collective-permute-done((bf16[256,1024]{1,0:T(8,128)(2,1)S(1)}, bf16[256,1024]{1,0:T(8,128)(2,1)S(1)}, u32[]{:S(2)}, u32[]{:S(2)}) %collective-permute-start.51) | collective-permute-done | bytes 524320 | tf_op jit(solution)/shard_map/ppermute | solution.py:19
  254.6 6.4 %weight_grad_of.2.refs_5_ = f32[1024,2048]{1,0:T(8,128)S(1)} custom-call(s32[2]{0:T(128)S(1)} %pad_add_fusion.scalars_ref, bf16[1024,1024]{1,0:T(8,128)(2,1)S(1)} %copy-done.4, bf16[512,1024]{1,0:T(8,128)(2,1)S(1)} %maximum_select_fusion.2.refs_1_, bf16[512,1024]{1,0:T(8,128)(2,1)S(1)} %collective-permute-done.57.refs_2_, ...), custom_call_target="tpu_custom_call" | custom-call | flops 4294967296 | bytes 8388608 | tf_op jit(solution)/shard_map/weight_grad_of/pallas_call | solution.py:61
  263.4 7.0 %weight_grad_of.3 = (f32[1024,2048]{1,0:T(8,128)S(1)}, f32[16,128]{1,0:T(8,128)S(1)}) custom-call(s32[2]{0:T(128)S(1)} %pad_add_fusion.scalars_ref, bf16[1024,1024]{1,0:T(8,128)(2,1)S(1)} %copy-done.2, bf16[512,1024]{1,0:T(8,128)(2,1)S(1)} %maximum_select_fusion.refs_1_, bf16[512,1024]{1,0:T(8,128)(2,1)S(1)} %copy-done.15, ...), custom_call_target="tpu_custom_call" | custom-call | flops 4294967296 | bytes 16777216 | tf_op jit(solution)/shard_map/weight_grad_of/pallas_call | solution.py:61
  270.4 1.9 collective-permute-start.63
  272.3 2.5 collective-permute-start.61
  281.8 2.6 collective-permute-done.67.refs_1_
  284.4 7.6 %update.1 = (f32[1024,2048]{1,0:T(8,128)}, f32[1024,2048]{1,0:T(8,128)}) custom-call(s32[1]{0:T(128)} %constant.21.clone.1.scalars_ref, f32[16,128]{1,0:T(8,128)S(1)} %add_add_fusion.refs_0_, f32[16,128]{1,0:T(8,128)S(1)} %collective-permute-done.67.refs_1_, f32[1024,2048]{1,0:T(8,128)S(1)} %bitcast.9, f32[1024,2048]{1,0:T(8,128)S(1)} %bitcast.11, ...), custom_call_target="tpu_custom_call" | custom-call | flops 8388608 | bytes 41943040 | tf_op jit(solution)/shard_map/update/pallas_call | solution.py:61
  (180 shorter events, 79.9 us)
Async XLA Ops:
  1.9 12.2 %collective-permute-start = (bf16[64,2048]{1,0:T(8,128)(2,1)S(1)}, bf16[64,2048]{1,0:T(8,128)(2,1)S(1)}, u32[]{:S(2)}, u32[]{:S(2)}) collective-permute-start(bf16[64,2048]{1,0:T(8,128)(2,1)S(1)} %get-tuple-element.52.refs_0_), channel_id=1, source_target_pairs={{0,1},{1,2},{2,3},{3,0},{4,5},{5,6},{6,7},{7,4},{8,9},{9,10},{10,1... | collective-permute-start | bytes 786440 | tf_op jit(solution)/shard_map/ppermute | solution.py:152
  5.0 14.8 %collective-permute-start.6 = (bf16[64,2048]{1,0:T(8,128)(2,1)S(1)}, bf16[64,2048]{1,0:T(8,128)(2,1)S(1)}, u32[]{:S(2)}, u32[]{:S(2)}) collective-permute-start(bf16[64,2048]{1,0:T(8,128)(2,1)S(1)} %get-tuple-element.57.refs_0_), channel_id=1, source_target_pairs={{0,1},{1,2},{2,3},{3,0},{4,5},{5,6},{6,7},{7,4},{8,9},{9,10},{10,1... | collective-permute-start | bytes 786440 | tf_op jit(solution)/shard_map/ppermute | solution.py:152
  14.2 11.2 %collective-permute-start.1 = (bf16[64,2048]{1,0:T(8,128)(2,1)S(1)}, bf16[64,2048]{1,0:T(8,128)(2,1)S(1)}, u32[]{:S(2)}, u32[]{:S(2)}) collective-permute-start(bf16[64,2048]{1,0:T(8,128)(2,1)S(1)} %collective-permute-done.refs_1_), channel_id=1, source_target_pairs={{0,1},{1,2},{2,3},{3,0},{4,5},{5,6},{6,7},{7,4},{8,9},{9,10},{10,1... | collective-permute-start | bytes 786440 | tf_op jit(solution)/shard_map/ppermute | solution.py:152
  14.2 39.1 %collective-permute-start.12 = (bf16[128,2048]{1,0:T(8,128)(2,1)S(1)}, bf16[128,2048]{1,0:T(8,128)(2,1)}, u32[]{:S(2)}, u32[]{:S(2)}) collective-permute-start(bf16[128,2048]{1,0:T(8,128)(2,1)S(1)} %get-tuple-element.63.refs_0_), channel_id=1, source_target_pairs={{0,1},{1,2},{2,3},{3,0},{4,5},{5,6},{6,7},{7,4},{8,9},{9,10},{10,1... | collective-permute-start | bytes 1572872 | tf_op jit(solution)/shard_map/ppermute | solution.py:152
  19.8 22.5 %collective-permute-start.7 = (bf16[64,2048]{1,0:T(8,128)(2,1)S(1)}, bf16[64,2048]{1,0:T(8,128)(2,1)S(1)}, u32[]{:S(2)}, u32[]{:S(2)}) collective-permute-start(bf16[64,2048]{1,0:T(8,128)(2,1)S(1)} %collective-permute-done.6.refs_1_), channel_id=1, source_target_pairs={{0,1},{1,2},{2,3},{3,0},{4,5},{5,6},{6,7},{7,4},{8,9},{9,10},{10,1... | collective-permute-start | bytes 786440 | tf_op jit(solution)/shard_map/ppermute | solution.py:152
  25.4 22.5 %collective-permute-start.2 = (bf16[64,2048]{1,0:T(8,128)(2,1)S(1)}, bf16[64,2048]{1,0:T(8,128)(2,1)S(1)}, u32[]{:S(2)}, u32[]{:S(2)}) collective-permute-start(bf16[64,2048]{1,0:T(8,128)(2,1)S(1)} %collective-permute-done.1.refs_2_), channel_id=1, source_target_pairs={{0,1},{1,2},{2,3},{3,0},{4,5},{5,6},{6,7},{7,4},{8,9},{9,10},{10,1... | collective-permute-start | bytes 786440 | tf_op jit(solution)/shard_map/ppermute | solution.py:152
  42.3 11.3 %collective-permute-start.8 = (bf16[64,2048]{1,0:T(8,128)(2,1)S(1)}, bf16[64,2048]{1,0:T(8,128)(2,1)S(1)}, u32[]{:S(2)}, u32[]{:S(2)}) collective-permute-start(bf16[64,2048]{1,0:T(8,128)(2,1)S(1)} %collective-permute-done.7.refs_2_), channel_id=1, source_target_pairs={{0,1},{1,2},{2,3},{3,0},{4,5},{5,6},{6,7},{7,4},{8,9},{9,10},{10,1... | collective-permute-start | bytes 786440 | tf_op jit(solution)/shard_map/ppermute | solution.py:152
  50.0 9.2 %collective-permute-start.3 = (bf16[64,2048]{1,0:T(8,128)(2,1)S(1)}, bf16[64,2048]{1,0:T(8,128)(2,1)S(1)}, u32[]{:S(2)}, u32[]{:S(2)}) collective-permute-start(bf16[64,2048]{1,0:T(8,128)(2,1)S(1)} %get-tuple-element.54), channel_id=1, source_target_pairs={{0,8},{4,12},{8,0},{12,4},{16,24},{20,28},{24,16},{28,20},{1,9},{5... | collective-permute-start | bytes 786440 | tf_op jit(solution)/shard_map/ppermute | solution.py:19
  51.8 11.6 %collective-permute-start.4 = (bf16[64,2048]{1,0:T(8,128)(2,1)S(1)}, bf16[64,2048]{1,0:T(8,128)(2,1)S(1)}, u32[]{:S(2)}, u32[]{:S(2)}) collective-permute-start(bf16[64,2048]{1,0:T(8,128)(2,1)S(1)} %get-tuple-element.55), channel_id=1, source_target_pairs={{0,16},{4,20},{8,24},{12,28},{16,0},{20,4},{24,8},{28,12},{1,17},{... | collective-permute-start | bytes 786440 | tf_op jit(solution)/shard_map/ppermute | solution.py:19
  53.3 21.3 %collective-permute-start.13 = (bf16[128,2048]{1,0:T(8,128)(2,1)}, bf16[128,2048]{1,0:T(8,128)(2,1)S(1)}, u32[]{:S(2)}, u32[]{:S(2)}) collective-permute-start(bf16[128,2048]{1,0:T(8,128)(2,1)} %collective-permute-done.12.refs_1_), channel_id=1, source_target_pairs={{0,1},{1,2},{2,3},{3,0},{4,5},{5,6},{6,7},{7,4},{8,9},{9,10},{10,1... | collective-permute-start | bytes 1572872 | tf_op jit(solution)/shard_map/ppermute | solution.py:152
  53.3 20.3 %collective-permute-start.5 = (bf16[64,2048]{1,0:T(8,128)(2,1)}, bf16[64,2048]{1,0:T(8,128)(2,1)}, u32[]{:S(2)}, u32[]{:S(2)}) collective-permute-start(bf16[64,2048]{1,0:T(8,128)(2,1)} %get-tuple-element.56), channel_id=1, source_target_pairs={{0,24},{4,28},{8,16},{12,20},{16,8},{20,12},{24,0},{28,4},{1,25},{... | collective-permute-start | bytes 786440 | tf_op jit(solution)/shard_map/ppermute | solution.py:19
  55.2 18.4 %collective-permute-start.9 = (bf16[64,2048]{1,0:T(8,128)(2,1)}, bf16[64,2048]{1,0:T(8,128)(2,1)}, u32[]{:S(2)}, u32[]{:S(2)}) collective-permute-start(bf16[64,2048]{1,0:T(8,128)(2,1)} %get-tuple-element.59), channel_id=1, source_target_pairs={{0,8},{4,12},{8,0},{12,4},{16,24},{20,28},{24,16},{28,20},{1,9},{5... | collective-permute-start | bytes 786440 | tf_op jit(solution)/shard_map/ppermute | solution.py:19
  60.0 14.6 %collective-permute-start.10 = (bf16[64,2048]{1,0:T(8,128)(2,1)}, bf16[64,2048]{1,0:T(8,128)(2,1)}, u32[]{:S(2)}, u32[]{:S(2)}) collective-permute-start(bf16[64,2048]{1,0:T(8,128)(2,1)} %get-tuple-element.60), channel_id=1, source_target_pairs={{0,16},{4,20},{8,24},{12,28},{16,0},{20,4},{24,8},{28,12},{1,17},{... | collective-permute-start | bytes 786440 | tf_op jit(solution)/shard_map/ppermute | solution.py:19
  64.0 10.6 %collective-permute-start.11 = (bf16[64,2048]{1,0:T(8,128)(2,1)}, bf16[64,2048]{1,0:T(8,128)(2,1)}, u32[]{:S(2)}, u32[]{:S(2)}) collective-permute-start(bf16[64,2048]{1,0:T(8,128)(2,1)} %get-tuple-element.61), channel_id=1, source_target_pairs={{0,24},{4,28},{8,16},{12,20},{16,8},{20,12},{24,0},{28,4},{1,25},{... | collective-permute-start | bytes 786440 | tf_op jit(solution)/shard_map/ppermute | solution.py:19
  78.3 15.7 %collective-permute-start.16 = (bf16[128,2048]{1,0:T(8,128)(2,1)S(1)}, bf16[128,2048]{1,0:T(8,128)(2,1)}, u32[]{:S(2)}, u32[]{:S(2)}) collective-permute-start(bf16[128,2048]{1,0:T(8,128)(2,1)S(1)} %collective-permute-done.13.refs_9_.refs_2_), channel_id=1, source_target_pairs={{0,1},{1,2},{2,3},{3,0},{4,5},{5,6},{6,7},{7,4},{8,9},{9,10},{10,1... | collective-permute-start | bytes 1572872 | tf_op jit(solution)/shard_map/ppermute | solution.py:152
  89.6 16.0 %collective-permute-start.21 = (bf16[256,1024]{1,0:T(8,128)(2,1)S(1)}, bf16[256,1024]{1,0:T(8,128)(2,1)S(1)}, u32[]{:S(2)}, u32[]{:S(2)}) collective-permute-start(bf16[256,1024]{1,0:T(8,128)(2,1)S(1)} %get-tuple-element.72), channel_id=1, source_target_pairs={{0,16},{4,20},{8,24},{12,28},{16,0},{20,4},{24,8},{28,12},{1,17},{... | collective-permute-start | bytes 1572872 | tf_op jit(solution)/shard_map/ppermute | solution.py:19
  91.2 14.8 %collective-permute-start.20 = (bf16[256,1024]{1,0:T(8,128)(2,1)S(1)}, bf16[256,1024]{1,0:T(8,128)(2,1)S(1)}, u32[]{:S(2)}, u32[]{:S(2)}) collective-permute-start(bf16[256,1024]{1,0:T(8,128)(2,1)S(1)} %get-tuple-element.65.refs_4_.refs_6_), channel_id=1, source_target_pairs={{0,8},{4,12},{8,0},{12,4},{16,24},{20,28},{24,16},{28,20},{1,9},{5... | collective-permute-start | bytes 1572872 | tf_op jit(solution)/shard_map/ppermute | solution.py:19
  96.2 21.0 %collective-permute-start.17 = (bf16[128,2048]{1,0:T(8,128)(2,1)S(1)}, bf16[128,2048]{1,0:T(8,128)(2,1)S(1)}, u32[]{:S(2)}, u32[]{:S(2)}) collective-permute-start(bf16[128,2048]{1,0:T(8,128)(2,1)S(1)} %get-tuple-element.67), channel_id=1, source_target_pairs={{0,8},{4,12},{8,0},{12,4},{16,24},{20,28},{24,16},{28,20},{1,9},{5... | collective-permute-start | bytes 1572872 | tf_op jit(solution)/shard_map/ppermute | solution.py:19
  98.2 19.0 %collective-permute-start.18 = (bf16[128,2048]{1,0:T(8,128)(2,1)S(1)}, bf16[128,2048]{1,0:T(8,128)(2,1)S(1)}, u32[]{:S(2)}, u32[]{:S(2)}) collective-permute-start(bf16[128,2048]{1,0:T(8,128)(2,1)S(1)} %get-tuple-element.68), channel_id=1, source_target_pairs={{0,16},{4,20},{8,24},{12,28},{16,0},{20,4},{24,8},{28,12},{1,17},{... | collective-permute-start | bytes 1572872 | tf_op jit(solution)/shard_map/ppermute | solution.py:19
  98.3 29.1 %collective-permute-start.19 = (bf16[128,2048]{1,0:T(8,128)(2,1)S(1)}, bf16[128,2048]{1,0:T(8,128)(2,1)S(1)}, u32[]{:S(2)}, u32[]{:S(2)}) collective-permute-start(bf16[128,2048]{1,0:T(8,128)(2,1)S(1)} %get-tuple-element.69), channel_id=1, source_target_pairs={{0,24},{4,28},{8,16},{12,20},{16,8},{20,12},{24,0},{28,4},{1,25},{... | collective-permute-start | bytes 1572872 | tf_op jit(solution)/shard_map/ppermute | solution.py:19
  128.2 9.2 %collective-permute-start.26 = (bf16[128,1024]{1,0:T(8,128)(2,1)S(1)}, bf16[128,1024]{1,0:T(8,128)(2,1)S(1)}, u32[]{:S(2)}, u32[]{:S(2)}) collective-permute-start(bf16[128,1024]{1,0:T(8,128)(2,1)S(1)} %get-tuple-element.80), channel_id=1, source_target_pairs={{0,8},{4,12},{8,0},{12,4},{16,24},{20,28},{24,16},{28,20},{1,9},{5... | collective-permute-start | bytes 786440 | tf_op jit(solution)/shard_map/ppermute | solution.py:19
  138.9 14.8 %collective-permute-start.24 = (bf16[256,1024]{1,0:T(8,128)(2,1)S(1)}, bf16[256,1024]{1,0:T(8,128)(2,1)S(1)}, u32[]{:S(2)}, u32[]{:S(2)}) collective-permute-start(bf16[256,1024]{1,0:T(8,128)(2,1)S(1)} %get-tuple-element.77), channel_id=1, source_target_pairs={{0,16},{4,20},{8,24},{12,28},{16,0},{20,4},{24,8},{28,12},{1,17},{... | collective-permute-start | bytes 1572872 | tf_op jit(solution)/shard_map/ppermute | solution.py:19
  139.3 14.8 %collective-permute-start.23 = (bf16[256,1024]{1,0:T(8,128)(2,1)S(1)}, bf16[256,1024]{1,0:T(8,128)(2,1)S(1)}, u32[]{:S(2)}, u32[]{:S(2)}) collective-permute-start(bf16[256,1024]{1,0:T(8,128)(2,1)S(1)} %get-tuple-element.75.refs_4_), channel_id=1, source_target_pairs={{0,8},{4,12},{8,0},{12,4},{16,24},{20,28},{24,16},{28,20},{1,9},{5... | collective-permute-start | bytes 1572872 | tf_op jit(solution)/shard_map/ppermute | solution.py:19
  143.4 14.2 %collective-permute-start.30 = (bf16[128,640]{1,0:T(8,128)(2,1)S(1)}, bf16[128,640]{1,0:T(8,128)(2,1)S(1)}, u32[]{:S(2)}, u32[]{:S(2)}) collective-permute-start(bf16[128,640]{1,0:T(8,128)(2,1)S(1)} %get-tuple-element.87), channel_id=1, source_target_pairs={{0,8},{4,12},{8,0},{12,4},{16,24},{20,28},{24,16},{28,20},{1,9},{5... | collective-permute-start | bytes 491528 | tf_op jit(solution)/shard_map/ppermute | solution.py:19
  144.3 13.3 %collective-permute-start.31 = (bf16[128,640]{1,0:T(8,128)(2,1)S(1)}, bf16[128,640]{1,0:T(8,128)(2,1)S(1)}, u32[]{:S(2)}, u32[]{:S(2)}) collective-permute-start(bf16[128,640]{1,0:T(8,128)(2,1)S(1)} %get-tuple-element.88), channel_id=1, source_target_pairs={{0,16},{4,20},{8,24},{12,28},{16,0},{20,4},{24,8},{28,12},{1,17},{... | collective-permute-start | bytes 491528 | tf_op jit(solution)/shard_map/ppermute | solution.py:19
  145.9 16.3 %collective-permute-start.32 = (bf16[128,640]{1,0:T(8,128)(2,1)S(1)}, bf16[128,640]{1,0:T(8,128)(2,1)S(1)}, u32[]{:S(2)}, u32[]{:S(2)}) collective-permute-start(bf16[128,640]{1,0:T(8,128)(2,1)S(1)} %get-tuple-element.89), channel_id=1, source_target_pairs={{0,24},{4,28},{8,16},{12,20},{16,8},{20,12},{24,0},{28,4},{1,25},{... | collective-permute-start | bytes 491528 | tf_op jit(solution)/shard_map/ppermute | solution.py:19
  154.9 11.0 %collective-permute-start.28 = (bf16[128,1024]{1,0:T(8,128)(2,1)S(1)}, bf16[128,1024]{1,0:T(8,128)(2,1)S(1)}, u32[]{:S(2)}, u32[]{:S(2)}) collective-permute-start(bf16[128,1024]{1,0:T(8,128)(2,1)S(1)} %get-tuple-element.84), channel_id=1, source_target_pairs={{0,16},{4,20},{8,24},{12,28},{16,0},{20,4},{24,8},{28,12},{1,17},{... | collective-permute-start | bytes 786440 | tf_op jit(solution)/shard_map/ppermute | solution.py:19
  156.6 9.4 %collective-permute-start.29 = (bf16[128,1024]{1,0:T(8,128)(2,1)S(1)}, bf16[128,1024]{1,0:T(8,128)(2,1)S(1)}, u32[]{:S(2)}, u32[]{:S(2)}) collective-permute-start(bf16[128,1024]{1,0:T(8,128)(2,1)S(1)} %get-tuple-element.86), channel_id=1, source_target_pairs={{0,8},{4,12},{8,0},{12,4},{16,24},{20,28},{24,16},{28,20},{1,9},{5... | collective-permute-start | bytes 786440 | tf_op jit(solution)/shard_map/ppermute | solution.py:19
  167.8 9.3 %collective-permute-start.43 = (bf16[128,640]{1,0:T(8,128)(2,1)S(1)}, bf16[128,640]{1,0:T(8,128)(2,1)S(1)}, u32[]{:S(2)}, u32[]{:S(2)}) collective-permute-start(bf16[128,640]{1,0:T(8,128)(2,1)S(1)} %add_convert_fusion.1), channel_id=1, source_target_pairs={{0,2},{1,3},{2,0},{3,1},{4,6},{5,7},{6,4},{7,5},{8,10},{9,11},{10,... | collective-permute-start | bytes 491528 | tf_op jit(solution)/shard_map/ppermute | solution.py:19
  169.8 10.2 %collective-permute-start.34 = (bf16[128,640]{1,0:T(8,128)(2,1)S(1)}, bf16[128,640]{1,0:T(8,128)(2,1)S(1)}, u32[]{:S(2)}, u32[]{:S(2)}) collective-permute-start(bf16[128,640]{1,0:T(8,128)(2,1)S(1)} %get-tuple-element.92), channel_id=1, source_target_pairs={{0,8},{4,12},{8,0},{12,4},{16,24},{20,28},{24,16},{28,20},{1,9},{5... | collective-permute-start | bytes 491528 | tf_op jit(solution)/shard_map/ppermute | solution.py:19
  171.0 9.7 %collective-permute-start.35 = (bf16[128,640]{1,0:T(8,128)(2,1)S(1)}, bf16[128,640]{1,0:T(8,128)(2,1)S(1)}, u32[]{:S(2)}, u32[]{:S(2)}) collective-permute-start(bf16[128,640]{1,0:T(8,128)(2,1)S(1)} %get-tuple-element.93), channel_id=1, source_target_pairs={{0,16},{4,20},{8,24},{12,28},{16,0},{20,4},{24,8},{28,12},{1,17},{... | collective-permute-start | bytes 491528 | tf_op jit(solution)/shard_map/ppermute | solution.py:19
  172.2 8.6 %collective-permute-start.36 = (bf16[128,640]{1,0:T(8,128)(2,1)S(1)}, bf16[128,640]{1,0:T(8,128)(2,1)S(1)}, u32[]{:S(2)}, u32[]{:S(2)}) collective-permute-start(bf16[128,640]{1,0:T(8,128)(2,1)S(1)} %get-tuple-element.94), channel_id=1, source_target_pairs={{0,24},{4,28},{8,16},{12,20},{16,8},{20,12},{24,0},{28,4},{1,25},{... | collective-permute-start | bytes 491528 | tf_op jit(solution)/shard_map/ppermute | solution.py:19
  178.9 8.8 %collective-permute-start.45 = (bf16[128,640]{1,0:T(8,128)(2,1)S(1)}, bf16[128,640]{1,0:T(8,128)(2,1)S(1)}, u32[]{:S(2)}, u32[]{:S(2)}) collective-permute-start(bf16[128,640]{1,0:T(8,128)(2,1)S(1)} %add_convert_fusion.refs_0_), channel_id=1, source_target_pairs={{0,16},{4,20},{8,24},{12,28},{16,0},{20,4},{24,8},{28,12},{1,17},{... | collective-permute-start | bytes 491528 | tf_op jit(solution)/shard_map/ppermute | solution.py:19
  188.0 14.8 %collective-permute-start.47 = (bf16[4,128,640]{2,1,0:T(8,128)(2,1)S(1)}, bf16[4,128,640]{2,1,0:T(8,128)(2,1)S(1)}, u32[]{:S(2)}, u32[]{:S(2)}) collective-permute-start(bf16[4,128,640]{2,1,0:T(8,128)(2,1)S(1)} %pile.2.refs_0_), channel_id=1, source_target_pairs={{0,4},{4,0},{8,12},{12,8},{16,20},{20,16},{24,28},{28,24},{1,5},{5... | collective-permute-start | bytes 1966088 | tf_op jit(solution)/shard_map/ppermute | solution.py:19
  188.1 11.1 %collective-permute-start.38 = (bf16[128,640]{1,0:T(8,128)(2,1)S(1)}, bf16[128,640]{1,0:T(8,128)(2,1)S(1)}, u32[]{:S(2)}, u32[]{:S(2)}) collective-permute-start(bf16[128,640]{1,0:T(8,128)(2,1)S(1)} %add_convert_fusion.3), channel_id=1, source_target_pairs={{0,2},{1,3},{2,0},{3,1},{4,6},{5,7},{6,4},{7,5},{8,10},{9,11},{10,... | collective-permute-start | bytes 491528 | tf_op jit(solution)/shard_map/ppermute | solution.py:19
  200.8 8.9 %collective-permute-start.40 = (bf16[128,640]{1,0:T(8,128)(2,1)S(1)}, bf16[128,640]{1,0:T(8,128)(2,1)S(1)}, u32[]{:S(2)}, u32[]{:S(2)}) collective-permute-start(bf16[128,640]{1,0:T(8,128)(2,1)S(1)} %add_convert_fusion.2.refs_0_), channel_id=1, source_target_pairs={{0,16},{4,20},{8,24},{12,28},{16,0},{20,4},{24,8},{28,12},{1,17},{... | collective-permute-start | bytes 491528 | tf_op jit(solution)/shard_map/ppermute | solution.py:19
  209.8 10.4 %collective-permute-start.48 = (bf16[4,128,640]{2,1,0:T(8,128)(2,1)S(1)}, bf16[4,128,640]{2,1,0:T(8,128)(2,1)S(1)}, u32[]{:S(2)}, u32[]{:S(2)}) collective-permute-start(bf16[4,128,640]{2,1,0:T(8,128)(2,1)S(1)} %pile.3.refs_0_), channel_id=1, source_target_pairs={{0,4},{4,0},{8,12},{12,8},{16,20},{20,16},{24,28},{28,24},{1,5},{5... | collective-permute-start | bytes 1966088 | tf_op jit(solution)/shard_map/ppermute | solution.py:19
  209.9 8.8 %collective-permute-start.58 = (bf16[128,1024]{1,0:T(8,128)(2,1)S(1)}, bf16[128,1024]{1,0:T(8,128)(2,1)S(1)}, u32[]{:S(2)}, u32[]{:S(2)}) collective-permute-start(bf16[128,1024]{1,0:T(8,128)(2,1)S(1)} %get-tuple-element.104), channel_id=1, source_target_pairs={{0,8},{4,12},{8,0},{12,4},{16,24},{20,28},{24,16},{28,20},{1,9},{5... | collective-permute-start | bytes 786440 | tf_op jit(solution)/shard_map/ppermute | solution.py:19
  211.1 8.9 %collective-permute-start.49 = (bf16[128,1024]{1,0:T(8,128)(2,1)S(1)}, bf16[128,1024]{1,0:T(8,128)(2,1)S(1)}, u32[]{:S(2)}, u32[]{:S(2)}) collective-permute-start(bf16[128,1024]{1,0:T(8,128)(2,1)S(1)} %get-tuple-element.105), channel_id=1, source_target_pairs={{0,16},{4,20},{8,24},{12,28},{16,0},{20,4},{24,8},{28,12},{1,17},{... | collective-permute-start | bytes 786440 | tf_op jit(solution)/shard_map/ppermute | solution.py:19
  218.8 21.9 %collective-permute-start.59 = (bf16[256,1024]{1,0:T(8,128)(2,1)S(1)}, bf16[256,1024]{1,0:T(8,128)(2,1)S(1)}, u32[]{:S(2)}, u32[]{:S(2)}) collective-permute-start(bf16[256,1024]{1,0:T(8,128)(2,1)S(1)} %maximum_select_fusion.7), channel_id=1, source_target_pairs={{0,16},{4,20},{8,24},{12,28},{16,0},{20,4},{24,8},{28,12},{1,17},{... | collective-permute-start | bytes 1572872 | tf_op jit(solution)/shard_map/ppermute | solution.py:19
  223.8 9.3 %collective-permute-start.53 = (bf16[128,1024]{1,0:T(8,128)(2,1)S(1)}, bf16[128,1024]{1,0:T(8,128)(2,1)S(1)}, u32[]{:S(2)}, u32[]{:S(2)}) collective-permute-start(bf16[128,1024]{1,0:T(8,128)(2,1)S(1)} %get-tuple-element.106), channel_id=1, source_target_pairs={{0,8},{4,12},{8,0},{12,4},{16,24},{20,28},{24,16},{28,20},{1,9},{5... | collective-permute-start | bytes 786440 | tf_op jit(solution)/shard_map/ppermute | solution.py:19
  224.6 14.7 %collective-permute-start.50 = (bf16[128,1024]{1,0:T(8,128)(2,1)S(1)}, bf16[128,1024]{1,0:T(8,128)(2,1)S(1)}, u32[]{:S(2)}, u32[]{:S(2)}) collective-permute-start(bf16[128,1024]{1,0:T(8,128)(2,1)S(1)} %get-tuple-element.107), channel_id=1, source_target_pairs={{0,16},{4,20},{8,24},{12,28},{16,0},{20,4},{24,8},{28,12},{1,17},{... | collective-permute-start | bytes 786440 | tf_op jit(solution)/shard_map/ppermute | solution.py:19
  225.9 18.5 %collective-permute-start.56 = (bf16[256,1024]{1,0:T(8,128)(2,1)S(1)}, bf16[256,1024]{1,0:T(8,128)(2,1)S(1)}, u32[]{:S(2)}, u32[]{:S(2)}) collective-permute-start(bf16[256,1024]{1,0:T(8,128)(2,1)S(1)} %maximum_select_fusion.4.refs_6_), channel_id=1, source_target_pairs={{0,8},{4,12},{8,0},{12,4},{16,24},{20,28},{24,16},{28,20},{1,9},{5... | collective-permute-start | bytes 1572872 | tf_op jit(solution)/shard_map/ppermute | solution.py:19
  233.3 16.0 %collective-permute-start.54 = (bf16[256,1024]{1,0:T(8,128)(2,1)S(1)}, bf16[256,1024]{1,0:T(8,128)(2,1)S(1)}, u32[]{:S(2)}, u32[]{:S(2)}) collective-permute-start(bf16[256,1024]{1,0:T(8,128)(2,1)S(1)} %maximum_select_fusion.6), channel_id=1, source_target_pairs={{0,16},{4,20},{8,24},{12,28},{16,0},{20,4},{24,8},{28,12},{1,17},{... | collective-permute-start | bytes 1572872 | tf_op jit(solution)/shard_map/ppermute | solution.py:19
  239.4 14.6 %collective-permute-start.51 = (bf16[256,1024]{1,0:T(8,128)(2,1)S(1)}, bf16[256,1024]{1,0:T(8,128)(2,1)S(1)}, u32[]{:S(2)}, u32[]{:S(2)}) collective-permute-start(bf16[256,1024]{1,0:T(8,128)(2,1)S(1)} %maximum_select_fusion.5), channel_id=1, source_target_pairs={{0,8},{4,12},{8,0},{12,4},{16,24},{20,28},{24,16},{28,20},{1,9},{5... | collective-permute-start | bytes 1572872 | tf_op jit(solution)/shard_map/ppermute | solution.py:19
  241.1 13.5 %collective-permute-start.60 = (bf16[512,1024]{1,0:T(8,128)(2,1)S(1)}, bf16[512,1024]{1,0:T(8,128)(2,1)S(1)}, u32[]{:S(2)}, u32[]{:S(2)}) collective-permute-start(bf16[512,1024]{1,0:T(8,128)(2,1)S(1)} %maximum_select_fusion.3.refs_3_), channel_id=1, source_target_pairs={{0,4},{4,0},{8,12},{12,8},{16,20},{20,16},{24,28},{28,24},{1,5},{5... | collective-permute-start | bytes 3145736 | tf_op jit(solution)/shard_map/ppermute | solution.py:19
  244.9 9.7 %collective-permute-start.57 = (bf16[512,1024]{1,0:T(8,128)(2,1)S(1)}, bf16[512,1024]{1,0:T(8,128)(2,1)S(1)}, u32[]{:S(2)}, u32[]{:S(2)}) collective-permute-start(bf16[512,1024]{1,0:T(8,128)(2,1)S(1)} %maximum_select_fusion.2.refs_1_), channel_id=1, source_target_pairs={{0,4},{4,0},{8,12},{12,8},{16,20},{20,16},{24,28},{28,24},{1,5},{5... | collective-permute-start | bytes 3145736 | tf_op jit(solution)/shard_map/ppermute | solution.py:19
  250.0 11.0 %collective-permute-start.55 = (bf16[512,1024]{1,0:T(8,128)(2,1)S(1)}, bf16[512,1024]{1,0:T(8,128)(2,1)S(1)}, u32[]{:S(2)}, u32[]{:S(2)}) collective-permute-start(bf16[512,1024]{1,0:T(8,128)(2,1)S(1)} %maximum_select_fusion.1.refs_3_), channel_id=1, source_target_pairs={{0,4},{4,0},{8,12},{12,8},{16,20},{20,16},{24,28},{28,24},{1,5},{5... | collective-permute-start | bytes 3145736 | tf_op jit(solution)/shard_map/ppermute | solution.py:19
  (40 other events, 264.0 us)

commit v6 on v5

--- a/solution.py
+++ b/solution.py
@@ -122,7 +122,7 @@
             pl.BlockSpec((step, depth), lambda k, j, c: (jnp.where(k == 1, j, 0), 0)),
             pl.BlockSpec((8, 128), lambda k, j, c: (0, 0)),
         ],
-        grid=(2, 2 * steps), after=after, flops=2 * depth * width, moved=6 * depth * width, limit=16, name="turn_weight",
+        grid=(2, 2 * steps), after=after, flops=2 * depth * width, moved=6 * depth * width, limit=54, name="turn_weight",
     )
 
 
@@ -170,7 +170,7 @@
     return run(
         body, jnp.stack(back), shares, [whole(share) for share in shares],
         [like(shape, BF16)] * n_chip, [whole(shares[0])] * n_chip,
-        after=after, moved=4 * n_chip * shape[0] * shape[1], limit=16, name="choose",
+        after=after, moved=4 * n_chip * shape[0] * shape[1], limit=10, name="choose",
     )
 
 
@@ -189,7 +189,7 @@
     out = like((len(operands) * count, width), BF16)
     (images,) = run(
         body, place, operands, [whole(piece) for piece in operands], [out], [whole(out)],
-        after=after, moved=4 * len(operands) * count * width, limit=16, name="collect",
+        after=after, moved=4 * len(operands) * count * width, limit=10, name="collect",
     )
     return images
 
@@ -213,7 +213,7 @@
     out = like((2 * n_chip * count, width), BF16)
     (columns,) = run(
         body, place, [own, other], [whole(own), whole(other)], [out], [whole(out)], after=after,
-        moved=8 * n_chip * count * width, limit=24, name="assemble",
+        moved=8 * n_chip * count * width, limit=12, name="assemble",
     )
     return columns
 
@@ -243,14 +243,17 @@
     steps = out_rows // step
 
     def body(bits_ref, own_a, other_a, own_b, other_b, columns_ref, out_a, out_b):
-        for own_ref, other_ref, out_ref in ((own_a, other_a, out_a), (own_b, other_b, out_b)):
-            block = lax.dot_general(
-                own_ref[...], columns_ref[:, :depth], ROWS_BY_ROWS, preferred_element_type=F32
-            )
-            block += lax.dot_general(
-                other_ref[...], columns_ref[:, depth:], ROWS_BY_ROWS, preferred_element_type=F32
-            )
-            out_ref[...] = (block - jnp.mean(block, 1, keepdims=True)).astype(BF16)
+        own = jnp.concatenate([own_a[...], own_b[...]], 0)
+        other = jnp.concatenate([other_a[...], other_b[...]], 0)
+        block = lax.dot_general(
+            own, columns_ref[:, :depth], ROWS_BY_ROWS, preferred_element_type=F32
+        )
+        block += lax.dot_general(
+            other, columns_ref[:, depth:], ROWS_BY_ROWS, preferred_element_type=F32
+        )
+        block = (block - jnp.mean(block, 1, keepdims=True)).astype(BF16)
+        out_a[...] = block[:step]
+        out_b[...] = block[step:]
 
     def of_path(path):
         return pl.BlockSpec((step, depth), lambda i, b: ((2 * path + b[path]) * steps + i, 0))
@@ -332,6 +335,38 @@
         scratch=[pltpu.VMEM((2 * rows, 2 * batch), BF16)], after=after,
         flops=4 * rows * width * batch // 2, moved=8 * rows * batch, limit=24, name="gram_rows",
     )
+
+
+def join_after(mine, other, bit, after):
+    rows, width = mine.shape
+
+    def body(bit_ref, mine_ref, other_ref, out_ref):
+        first = pl.multiple_of(bit_ref[0] * rows, rows)
+        second = pl.multiple_of((1 - bit_ref[0]) * rows, rows)
+        out_ref[pl.ds(first, rows), :] = mine_ref[...]
+        out_ref[pl.ds(second, rows), :] = other_ref[...]
+
+    out = like((2 * rows, width), BF16)
+    (joined,) = run(
+        body, bit.reshape(1), [mine, other], [whole(mine), whole(other)], [out], [whole(out)],
+        after=after, moved=8 * rows * width, limit=8, name="join_after",
+    )
+    return joined
+
+
+def add_up(parts, after=()):
+    def body(_, *refs):
+        total = refs[0][...].astype(F32)
+        for ref in refs[1:-1]:
+            total += ref[...].astype(F32)
+        refs[-1][...] = total.astype(BF16)
+
+    (out,) = run(
+        body, jnp.zeros((1,), jnp.int32), parts, [whole(part) for part in parts],
+        [like(parts[0].shape, BF16)], [whole(parts[0])], after=after,
+        moved=4 * len(parts) * parts[0].size, limit=8, name="add_up",
+    )
+    return out
 
 
 def pile(parts, after=()):
@@ -484,26 +519,31 @@
     def send_on(v, level, send):
         return [swap(send[p], "dp", 1 << orders[p][level]) for p in range(2)]
 
-    def sum_plane(rows):
-        total = rows[0].astype(F32)
-        for mask in range(1, n_chip):
-            total += swap(rows[mask], "dp", 2 * mask).astype(F32)
-        return total.astype(BF16)
-
-    def sum_line(total, bit):
-        return (total.astype(F32) + swap(total, "feat", 1 << bit).astype(F32)).astype(BF16)
+    def sum_plane(rows, after=()):
+        parts = [rows[0]] + [swap(rows[mask], "dp", 2 * mask) for mask in range(1, n_chip)]
+        return add_up(parts, after=after)
+
+    def sum_line(total, bit, after=()):
+        return add_up([total, swap(total, "feat", 1 << bit)], after=after)
 
     def spread_gram(total, after=()):
         parts = [total] + [swap(total, "dp", 2 * mask) for mask in range(1, n_chip)]
         own = pile(parts, after=after)
         return own, swap(own, "dp", 1)
 
-    def gather_step(parts, step):
-        bits_of = [order[len(order) - 1 - step] for order in orders]
-        return [
-            join(part, swap(part, "dp", 1 << bit), bit_value("dp", bit))
-            for part, bit in zip(parts, bits_of)
-        ]
+    def gather_step(parts, step, after=None):
+        out = []
+        for part, order in zip(parts, orders):
+            bit = order[len(order) - 1 - step]
+            other = swap(part, "dp", 1 << bit)
+            if after is None:
+                out.append(join(part, other, bit_value("dp", bit)))
+            else:
+                out.append(join_after(part, other, bit_value("dp", bit), after))
+        return out
+
+    def with_swapped(parts):
+        return [one for own in parts for one in (own, swap(own, "dp", 1))]
 
     columns, turned, send, keep, got, gram, normed, half, inverse, rows = (
         [None] * 2 for _ in range(10)
@@ -529,35 +569,38 @@
     got[0] = send_on(0, 0, send[0])
     normed[1], half[1], inverse[1] = normalise(keep[1], got[1], after=ahead)
     rows[1] = list(gram_rows(place, half[1], swap(half[1], "dp", 1), n_chip))
-    gram[1] = sum_plane(rows[1])
     keep[0] = forward(bits, turned_own, turned_other, columns[0], after=[turned[0], send[1][0]])
     for level in range(1, len(high)):
         send[0], keep[0] = add_halves(bits_at(level), keep[0], got[0], after=[rows[1][0]])
         got[0] = send_on(0, level, send[0])
+    gram[1] = sum_plane(rows[1], after=[send[0][0]])
     normed[0], half[0], inverse[0] = normalise(keep[0], got[0], after=[gram[1]])
     rows[0] = list(gram_rows(place, half[0], swap(half[0], "dp", 1), n_chip))
-    for bit in line_bits:
-        gram[1] = sum_line(gram[1], bit)
-    gram[1] = spread_gram(gram[1])
+    last = line_bits[-1]
+    for bit in line_bits[:-1]:
+        gram[1] = sum_line(gram[1], bit, after=[rows[0][0]])
+    gram[0] = sum_plane(rows[0])
+    gram[1] = sum_line(gram[1], last, after=[gram[0]])
+    for bit in line_bits[:-1]:
+        gram[0] = sum_line(gram[0], bit)
+    gram[1] = spread_gram(gram[1], after=[gram[0]])
+    gram[0] = sum_line(gram[0], last)
     out_grad = [None] * 2
-    out_grad[0] = out_grad_of(place, *gram[1], normed[0], half[0], half[1], inverse[0])
-    gram[0] = sum_plane(rows[0])
-    for bit in line_bits:
-        gram[0] = sum_line(gram[0], bit)
-    gram[0] = spread_gram(gram[0], after=[out_grad[0]])
+    out_grad[0] = out_grad_of(
+        place, *gram[1], normed[0], half[0], half[1], inverse[0], after=[gram[0]]
+    )
+    gram[0] = spread_gram(gram[0])
     share = out_grad[0].shape[0] // 2
-    parts = [None] * 2
-    parts[0] = gather_step([out_grad[0][:share], out_grad[0][share:]], 0)
-    out_grad[1] = out_grad_of(
-        place, *gram[0], normed[1], half[1], half[0], inverse[1], after=[parts[0][0]]
-    )
-    parts[1] = gather_step([out_grad[1][:share], out_grad[1][share:]], 0)
+    parts = gather_step([out_grad[0][:share], out_grad[0][share:]], 0, after=[gram[0][0]])
+    out_grad[1] = out_grad_of(place, *gram[0], normed[1], half[1], half[0], inverse[1])
+    last_parts = gather_step([out_grad[1][:share], out_grad[1][share:]], 0)
     for step in range(1, len(high)):
-        parts = [gather_step(part, step) for part in parts]
-    gathered = [[one for own in part for one in (own, swap(own, "dp", 1))] for part in parts]
-    (base,) = weight_grad_of(place, turned[0], gathered[0])
+        parts = gather_step(parts, step, after=last_parts)
+    (base,) = weight_grad_of(place, turned[0], with_swapped(parts))
+    for step in range(1, len(high)):
+        last_parts = gather_step(last_parts, step, after=[base] if step == len(high) - 1 else None)
     weight_grad, squares = weight_grad_of(
-        place, turned[1], gathered[1], base, weight_squares
+        place, turned[1], with_swapped(last_parts), base, weight_squares
     )
     return update(sum_everywhere(squares), weight, velocity, weight_grad)
 

time: 292 us -> 302 us (1.034)
  waiting for transfers between devices: 146 us -> 166 us
  local copies, waits for them, and re-layouts: 10.4 us -> 7.02 us
    ppermute x52, waiting for transfers between devices: 97.9 us -> 120 us  [swap(): lax.ppermute(value, axis, [(i, i ^ mask) for i in range(lax.axis_size(axi...]
    unnamed x40 -> x30, local copies, waits for them, and re-layouts: 10.3 us -> 6.94 us
    pallas_call x28 -> x40, Pallas kernels: 68.1 us -> 66.5 us  [run(): pl.pallas_call(kernel, grid_spec=pltpu.PrefetchScalarGridSpec(num_scalar_...]
  transfers between devices with their start and end apart: 68 -> 68, of which waited for: 40 -> 45; matrix products, arithmetic and copies ran while one was open for 1% -> 0% of each run, Pallas kernels for 17% -> 16%
where the time goes in v6:
time: 302 us
  waiting for transfers between devices  166 us (55%)
  Pallas kernels  66.5 us (22%)
  starting transfers between devices  60.8 us (20%)
  local copies, waits for them, and re-layouts  7.02 us (2%)
    ppermute x52, waiting for transfers between devices, swap(): lax.ppermute(value, axis, [(i, i ^ mask) for i in range(lax.axis_size(axi...  120 us
    pallas_call x40, Pallas kernels, run(): pl.pallas_call(kernel, grid_spec=pltpu.PrefetchScalarGridSpec(num_scalar_...  66.5 us
    ppermute x52, starting transfers between devices, swap(): lax.ppermute(value, axis, [(i, i ^ mask) for i in range(lax.axis_size(axi...  46.4 us
    ppermute x9, waiting for transfers between devices, go_round(): shares.append(lax.ppermute(shares[-1], 'feat', ring))  40.4 us
    ppermute x7, starting transfers between devices, sum_everywhere(): lax.ppermute(value, axes, [(i, i ^ mask) for i in range(count)])  7.78 us
    unnamed x30, local copies, waits for them, and re-layouts  6.94 us
    ppermute x9, starting transfers between devices, go_round(): shares.append(lax.ppermute(shares[-1], 'feat', ring))  6.63 us
  transfers between devices with their start and end apart: 68, of which 45 were waited for; matrix products, arithmetic and copies ran while one was open for 0% of the time, Pallas kernels for 16%

profile of v6, /device:TPU:0, one launch (start us, length us, event | category | flops | bytes accessed | tf_op | source)
XLA Modules:
  0.0 302.0 jit_solution(5921523904776984052)
XLA Ops:
  1.9 3.1 %collective-permute-start = (bf16[64,2048]{1,0:T(8,128)(2,1)S(1)}, bf16[64,2048]{1,0:T(8,128)(2,1)S(1)}, u32[]{:S(2)}, u32[]{:S(2)}) collective-permute-start(bf16[64,2048]{1,0:T(8,128)(2,1)S(1)} %get-tuple-element.52.refs_0_), channel_id=1, source_target_pairs={{0,1},{1,2},{2,3},{3,0},{4,5},{5,6},{6,7},{7,4},{8,9},{9,10},{10,1... | collective-permute-start | bytes 786440 | tf_op jit(solution)/shard_map/ppermute | solution.py:152
  6.6 7.6 %collective-permute-done.refs_1_ = bf16[64,2048]{1,0:T(8,128)(2,1)S(1)} collective-permute-done((bf16[64,2048]{1,0:T(8,128)(2,1)S(1)}, bf16[64,2048]{1,0:T(8,128)(2,1)S(1)}, u32[]{:S(2)}, u32[]{:S(2)}) %collective-permute-start) | collective-permute-done | bytes 262176 | tf_op jit(solution)/shard_map/ppermute | solution.py:152
  15.8 4.0 %collective-permute-done.6.refs_1_ = bf16[64,2048]{1,0:T(8,128)(2,1)S(1)} collective-permute-done((bf16[64,2048]{1,0:T(8,128)(2,1)S(1)}, bf16[64,2048]{1,0:T(8,128)(2,1)S(1)}, u32[]{:S(2)}, u32[]{:S(2)}) %collective-permute-start.6) | collective-permute-done | bytes 262176 | tf_op jit(solution)/shard_map/ppermute | solution.py:152
  19.8 5.6 %collective-permute-done.1.refs_2_ = bf16[64,2048]{1,0:T(8,128)(2,1)S(1)} collective-permute-done((bf16[64,2048]{1,0:T(8,128)(2,1)S(1)}, bf16[64,2048]{1,0:T(8,128)(2,1)S(1)}, u32[]{:S(2)}, u32[]{:S(2)}) %collective-permute-start.1) | collective-permute-done | bytes 262176 | tf_op jit(solution)/shard_map/ppermute | solution.py:152
  25.5 16.7 %collective-permute-done.7.refs_2_ = bf16[64,2048]{1,0:T(8,128)(2,1)S(1)} collective-permute-done((bf16[64,2048]{1,0:T(8,128)(2,1)S(1)}, bf16[64,2048]{1,0:T(8,128)(2,1)S(1)}, u32[]{:S(2)}, u32[]{:S(2)}) %collective-permute-start.7) | collective-permute-done | bytes 262176 | tf_op jit(solution)/shard_map/ppermute | solution.py:152
  42.3 5.6 %collective-permute-done.2.refs_3_ = bf16[64,2048]{1,0:T(8,128)(2,1)S(1)} collective-permute-done((bf16[64,2048]{1,0:T(8,128)(2,1)S(1)}, bf16[64,2048]{1,0:T(8,128)(2,1)S(1)}, u32[]{:S(2)}, u32[]{:S(2)}) %collective-permute-start.2) | collective-permute-done | bytes 262176 | tf_op jit(solution)/shard_map/ppermute | solution.py:152
  49.3 1.7 collective-permute-start.3
  55.1 1.7 collective-permute-start.9
  58.5 1.8 collective-permute-start.10
  63.4 8.5 %turn_weight.1 = (bf16[1024,1024]{1,0:T(8,128)(2,1)}, bf16[1024,1024]{1,0:T(8,128)(2,1)}, f32[8,128]{1,0:T(8,128)}) custom-call(s32[1]{0:T(128)} %bitcast.1.scalars_ref, f32[1024,2048]{1,0:T(8,128)} %refs_2_.1, bf16[64,2048]{1,0:T(8,128)(2,1)} %copy-done.7), custom_call_target="tpu_custom_call" | custom-call | flops 4194304 | bytes 12582912 | tf_op jit(solution)/shard_map/turn_weight/pallas_call | solution.py:61
  72.0 1.8 collective-permute-done.10.refs_6_
  75.4 2.0 collect.2.refs_0_
  78.2 6.3 %collective-permute-done.14.refs_1_ = bf16[512,2048]{1,0:T(8,128)(2,1)} collective-permute-done((bf16[512,2048]{1,0:T(8,128)(2,1)}, bf16[512,2048]{1,0:T(8,128)(2,1)}, u32[]{:S(2)}, u32[]{:S(2)}) %collective-permute-start.14) | collective-permute-done | bytes 2097184 | tf_op jit(solution)/shard_map/ppermute | solution.py:19
  84.5 3.0 %assemble.2.refs_0_.refs_4_ = bf16[1024,2048]{1,0:T(8,128)(2,1)S(1)} custom-call(s32[2]{0:T(128)S(1)} %pad_add_fusion.scalars_ref, bf16[512,2048]{1,0:T(8,128)(2,1)} %collect.2.refs_0_, bf16[512,2048]{1,0:T(8,128)(2,1)} %collective-permute-done.14.refs_1_), custom_call_target="tpu_custom_call" | custom-call | bytes 8388608 | tf_op jit(solution)/shard_map/assemble/pallas_call | solution.py:61
  87.5 3.0 forward.4
  93.6 2.0 choose.5
  100.5 3.0 forward.5
  103.5 1.9 collective-permute-done.21.refs_3_
  107.7 10.4 %collective-permute-done.17.refs_1_ = bf16[128,2048]{1,0:T(8,128)(2,1)S(1)} collective-permute-done((bf16[128,2048]{1,0:T(8,128)(2,1)S(1)}, bf16[128,2048]{1,0:T(8,128)(2,1)S(1)}, u32[]{:S(2)}, u32[]{:S(2)}) %collective-permute-start.17) | collective-permute-done | bytes 524320 | tf_op jit(solution)/shard_map/ppermute | solution.py:19
  118.2 10.0 %collective-permute-done.19.refs_3_ = bf16[128,2048]{1,0:T(8,128)(2,1)S(1)} collective-permute-done((bf16[128,2048]{1,0:T(8,128)(2,1)S(1)}, bf16[128,2048]{1,0:T(8,128)(2,1)S(1)}, u32[]{:S(2)}, u32[]{:S(2)}) %collective-permute-start.19) | collective-permute-done | bytes 524320 | tf_op jit(solution)/shard_map/ppermute | solution.py:19
  131.1 2.0 collective-permute-done.22.refs_1_
  134.0 3.0 forward.7
  143.0 3.0 forward.6
  147.4 6.1 %collective-permute-done.24.refs_3_ = bf16[256,1024]{1,0:T(8,128)(2,1)S(1)} collective-permute-done((bf16[256,1024]{1,0:T(8,128)(2,1)S(1)}, bf16[256,1024]{1,0:T(8,128)(2,1)S(1)}, u32[]{:S(2)}, u32[]{:S(2)}) %collective-permute-start.24) | collective-permute-done | bytes 524320 | tf_op jit(solution)/shard_map/ppermute | solution.py:19
  160.4 7.3 %collective-permute-done.30.refs_1_ = bf16[128,640]{1,0:T(8,128)(2,1)S(1)} collective-permute-done((bf16[128,640]{1,0:T(8,128)(2,1)S(1)}, bf16[128,640]{1,0:T(8,128)(2,1)S(1)}, u32[]{:S(2)}, u32[]{:S(2)}) %collective-permute-start.30) | collective-permute-done | bytes 163872 | tf_op jit(solution)/shard_map/ppermute | solution.py:19
  167.6 3.0 %collective-permute-done.31.refs_2_ = bf16[128,640]{1,0:T(8,128)(2,1)S(1)} collective-permute-done((bf16[128,640]{1,0:T(8,128)(2,1)S(1)}, bf16[128,640]{1,0:T(8,128)(2,1)S(1)}, u32[]{:S(2)}, u32[]{:S(2)}) %collective-permute-start.31) | collective-permute-done | bytes 163872 | tf_op jit(solution)/shard_map/ppermute | solution.py:19
  171.3 1.8 collective-permute-done.33.refs_1_
  176.3 1.8 collective-permute-start.36
  179.1 2.5 collective-permute-done.34.refs_1_
  181.6 2.9 collective-permute-done.35.refs_2_
  184.9 3.2 %collective-permute-done.46.refs_1_ = bf16[128,640]{1,0:T(8,128)(2,1)S(1)} collective-permute-done((bf16[128,640]{1,0:T(8,128)(2,1)S(1)}, bf16[128,640]{1,0:T(8,128)(2,1)S(1)}, u32[]{:S(2)}, u32[]{:S(2)}) %collective-permute-start.46) | collective-permute-done | bytes 163872 | tf_op jit(solution)/shard_map/ppermute | solution.py:19
  191.8 4.5 %collective-permute-done.49.refs_3_ = bf16[128,640]{1,0:T(8,128)(2,1)S(1)} collective-permute-done((bf16[128,640]{1,0:T(8,128)(2,1)S(1)}, bf16[128,640]{1,0:T(8,128)(2,1)S(1)}, u32[]{:S(2)}, u32[]{:S(2)}) %collective-permute-start.49) | collective-permute-done | bytes 163872 | tf_op jit(solution)/shard_map/ppermute | solution.py:19
  196.3 2.4 collective-permute-done.48.refs_2_
  198.9 10.5 %collective-permute-done.38.refs_1_ = bf16[128,640]{1,0:T(8,128)(2,1)S(1)} collective-permute-done((bf16[128,640]{1,0:T(8,128)(2,1)S(1)}, bf16[128,640]{1,0:T(8,128)(2,1)S(1)}, u32[]{:S(2)}, u32[]{:S(2)}) %collective-permute-start.38) | collective-permute-done | bytes 163872 | tf_op jit(solution)/shard_map/ppermute | solution.py:19
  209.4 1.7 collective-permute-start.41
  213.0 4.5 %collective-permute-done.41.refs_3_ = bf16[128,640]{1,0:T(8,128)(2,1)S(1)} collective-permute-done((bf16[128,640]{1,0:T(8,128)(2,1)S(1)}, bf16[128,640]{1,0:T(8,128)(2,1)S(1)}, u32[]{:S(2)}, u32[]{:S(2)}) %collective-permute-start.41) | collective-permute-done | bytes 163872 | tf_op jit(solution)/shard_map/ppermute | solution.py:19
  217.5 2.6 collective-permute-done.40.refs_2_
  220.2 2.4 out_grad_of.3
  224.9 6.5 %collective-permute-done.51.refs_1_ = bf16[128,1024]{1,0:T(8,128)(2,1)S(1)} collective-permute-done((bf16[128,1024]{1,0:T(8,128)(2,1)S(1)}, bf16[128,1024]{1,0:T(8,128)(2,1)S(1)}, u32[]{:S(2)}, u32[]{:S(2)}) %collective-permute-start.51) | collective-permute-done | bytes 262176 | tf_op jit(solution)/shard_map/ppermute | solution.py:19
  233.8 2.3 out_grad_of.2
  238.1 12.6 %collective-permute-done.53 = bf16[128,1024]{1,0:T(8,128)(2,1)S(1)} collective-permute-done((bf16[128,1024]{1,0:T(8,128)(2,1)S(1)}, bf16[128,1024]{1,0:T(8,128)(2,1)S(1)}, u32[]{:S(2)}, u32[]{:S(2)}) %collective-permute-start.53) | collective-permute-done | bytes 262176 | tf_op jit(solution)/shard_map/ppermute | solution.py:19
  255.8 6.7 %weight_grad_of.2.refs_2_.refs_5_ = f32[1024,2048]{1,0:T(8,128)S(1)} custom-call(s32[2]{0:T(128)S(1)} %pad_add_fusion.scalars_ref, bf16[1024,1024]{1,0:T(8,128)(2,1)S(1)} %copy-done.6, bf16[512,1024]{1,0:T(8,128)(2,1)S(1)} %join_after.7.refs_1_, bf16[512,1024]{1,0:T(8,128)(2,1)S(1)} %collective-permute-done.54.refs_2_, ...), custom_call_target="tpu_custom_call" | custom-call | flops 4294967296 | bytes 8388608 | tf_op jit(solution)/shard_map/weight_grad_of/pallas_call | solution.py:61
  262.4 3.7 %collective-permute-done.44.refs_1_ = bf16[256,1024]{1,0:T(8,128)(2,1)S(1)} collective-permute-done((bf16[256,1024]{1,0:T(8,128)(2,1)S(1)}, bf16[256,1024]{1,0:T(8,128)(2,1)S(1)}, u32[]{:S(2)}, u32[]{:S(2)}) %collective-permute-start.44) | collective-permute-done | bytes 524320 | tf_op jit(solution)/shard_map/ppermute | solution.py:19
  270.5 7.1 %weight_grad_of.3 = (f32[1024,2048]{1,0:T(8,128)S(1)}, f32[16,128]{1,0:T(8,128)S(1)}) custom-call(s32[2]{0:T(128)S(1)} %pad_add_fusion.scalars_ref, bf16[1024,1024]{1,0:T(8,128)(2,1)S(1)} %copy-done.4, bf16[512,1024]{1,0:T(8,128)(2,1)S(1)} %join_after.10.refs_1_, bf16[512,1024]{1,0:T(8,128)(2,1)S(1)} %collective-permute-done.58.refs_2_, ...), custom_call_target="tpu_custom_call" | custom-call | flops 4294967296 | bytes 16777216 | tf_op jit(solution)/shard_map/weight_grad_of/pallas_call | solution.py:61
  279.0 3.0 collective-permute-start.61
  288.9 2.3 collective-permute-done.67.refs_1_
  291.1 3.4 %copy-done.2 = f32[1024,2048]{1,0:T(8,128)S(1)} copy-done((f32[1024,2048]{1,0:T(8,128)S(1)}, f32[1024,2048]{1,0:T(8,128)}, u32[]{:S(2)}) %copy-start.2) | copy-done | bytes 8388632
  294.5 7.4 %update.1 = (f32[1024,2048]{1,0:T(8,128)}, f32[1024,2048]{1,0:T(8,128)}) custom-call(s32[1]{0:T(128)} %constant.21.clone.1.scalars_ref, f32[16,128]{1,0:T(8,128)S(1)} %add_add_fusion.refs_0_, f32[16,128]{1,0:T(8,128)S(1)} %collective-permute-done.67.refs_1_, f32[1024,2048]{1,0:T(8,128)S(1)} %bitcast.9, f32[1024,2048]{1,0:T(8,128)S(1)} %copy-done.2, ...), custom_call_target="tpu_custom_call" | custom-call | flops 8388608 | bytes 41943040 | tf_op jit(solution)/shard_map/update/pallas_call | solution.py:61
  (169 shorter events, 81.0 us)
Async XLA Ops:
  1.9 12.2 %collective-permute-start = (bf16[64,2048]{1,0:T(8,128)(2,1)S(1)}, bf16[64,2048]{1,0:T(8,128)(2,1)S(1)}, u32[]{:S(2)}, u32[]{:S(2)}) collective-permute-start(bf16[64,2048]{1,0:T(8,128)(2,1)S(1)} %get-tuple-element.52.refs_0_), channel_id=1, source_target_pairs={{0,1},{1,2},{2,3},{3,0},{4,5},{5,6},{6,7},{7,4},{8,9},{9,10},{10,1... | collective-permute-start | bytes 786440 | tf_op jit(solution)/shard_map/ppermute | solution.py:152
  5.0 14.8 %collective-permute-start.6 = (bf16[64,2048]{1,0:T(8,128)(2,1)S(1)}, bf16[64,2048]{1,0:T(8,128)(2,1)S(1)}, u32[]{:S(2)}, u32[]{:S(2)}) collective-permute-start(bf16[64,2048]{1,0:T(8,128)(2,1)S(1)} %get-tuple-element.57.refs_0_), channel_id=1, source_target_pairs={{0,1},{1,2},{2,3},{3,0},{4,5},{5,6},{6,7},{7,4},{8,9},{9,10},{10,1... | collective-permute-start | bytes 786440 | tf_op jit(solution)/shard_map/ppermute | solution.py:152
  14.2 11.2 %collective-permute-start.1 = (bf16[64,2048]{1,0:T(8,128)(2,1)S(1)}, bf16[64,2048]{1,0:T(8,128)(2,1)S(1)}, u32[]{:S(2)}, u32[]{:S(2)}) collective-permute-start(bf16[64,2048]{1,0:T(8,128)(2,1)S(1)} %collective-permute-done.refs_1_), channel_id=1, source_target_pairs={{0,1},{1,2},{2,3},{3,0},{4,5},{5,6},{6,7},{7,4},{8,9},{9,10},{10,1... | collective-permute-start | bytes 786440 | tf_op jit(solution)/shard_map/ppermute | solution.py:152
  14.2 38.3 %collective-permute-start.12 = (bf16[128,2048]{1,0:T(8,128)(2,1)S(1)}, bf16[128,2048]{1,0:T(8,128)(2,1)S(1)}, u32[]{:S(2)}, u32[]{:S(2)}) collective-permute-start(bf16[128,2048]{1,0:T(8,128)(2,1)S(1)} %get-tuple-element.63.refs_0_), channel_id=1, source_target_pairs={{0,1},{1,2},{2,3},{3,0},{4,5},{5,6},{6,7},{7,4},{8,9},{9,10},{10,1... | collective-permute-start | bytes 1572872 | tf_op jit(solution)/shard_map/ppermute | solution.py:152
  19.8 22.5 %collective-permute-start.7 = (bf16[64,2048]{1,0:T(8,128)(2,1)S(1)}, bf16[64,2048]{1,0:T(8,128)(2,1)S(1)}, u32[]{:S(2)}, u32[]{:S(2)}) collective-permute-start(bf16[64,2048]{1,0:T(8,128)(2,1)S(1)} %collective-permute-done.6.refs_1_), channel_id=1, source_target_pairs={{0,1},{1,2},{2,3},{3,0},{4,5},{5,6},{6,7},{7,4},{8,9},{9,10},{10,1... | collective-permute-start | bytes 786440 | tf_op jit(solution)/shard_map/ppermute | solution.py:152
  25.4 22.5 %collective-permute-start.2 = (bf16[64,2048]{1,0:T(8,128)(2,1)S(1)}, bf16[64,2048]{1,0:T(8,128)(2,1)S(1)}, u32[]{:S(2)}, u32[]{:S(2)}) collective-permute-start(bf16[64,2048]{1,0:T(8,128)(2,1)S(1)} %collective-permute-done.1.refs_2_), channel_id=1, source_target_pairs={{0,1},{1,2},{2,3},{3,0},{4,5},{5,6},{6,7},{7,4},{8,9},{9,10},{10,1... | collective-permute-start | bytes 786440 | tf_op jit(solution)/shard_map/ppermute | solution.py:152
  42.3 10.6 %collective-permute-start.8 = (bf16[64,2048]{1,0:T(8,128)(2,1)S(1)}, bf16[64,2048]{1,0:T(8,128)(2,1)S(1)}, u32[]{:S(2)}, u32[]{:S(2)}) collective-permute-start(bf16[64,2048]{1,0:T(8,128)(2,1)S(1)} %collective-permute-done.7.refs_2_), channel_id=1, source_target_pairs={{0,1},{1,2},{2,3},{3,0},{4,5},{5,6},{6,7},{7,4},{8,9},{9,10},{10,1... | collective-permute-start | bytes 786440 | tf_op jit(solution)/shard_map/ppermute | solution.py:152
  49.3 9.2 %collective-permute-start.3 = (bf16[64,2048]{1,0:T(8,128)(2,1)S(1)}, bf16[64,2048]{1,0:T(8,128)(2,1)S(1)}, u32[]{:S(2)}, u32[]{:S(2)}) collective-permute-start(bf16[64,2048]{1,0:T(8,128)(2,1)S(1)} %get-tuple-element.54), channel_id=1, source_target_pairs={{0,8},{4,12},{8,0},{12,4},{16,24},{20,28},{24,16},{28,20},{1,9},{5... | collective-permute-start | bytes 786440 | tf_op jit(solution)/shard_map/ppermute | solution.py:19
  51.0 10.8 %collective-permute-start.4 = (bf16[64,2048]{1,0:T(8,128)(2,1)S(1)}, bf16[64,2048]{1,0:T(8,128)(2,1)S(1)}, u32[]{:S(2)}, u32[]{:S(2)}) collective-permute-start(bf16[64,2048]{1,0:T(8,128)(2,1)S(1)} %get-tuple-element.55), channel_id=1, source_target_pairs={{0,16},{4,20},{8,24},{12,28},{16,0},{20,4},{24,8},{28,12},{1,17},{... | collective-permute-start | bytes 786440 | tf_op jit(solution)/shard_map/ppermute | solution.py:19
  52.5 21.2 %collective-permute-start.13 = (bf16[128,2048]{1,0:T(8,128)(2,1)S(1)}, bf16[128,2048]{1,0:T(8,128)(2,1)S(1)}, u32[]{:S(2)}, u32[]{:S(2)}) collective-permute-start(bf16[128,2048]{1,0:T(8,128)(2,1)S(1)} %collective-permute-done.12.refs_1_), channel_id=1, source_target_pairs={{0,1},{1,2},{2,3},{3,0},{4,5},{5,6},{6,7},{7,4},{8,9},{9,10},{10,1... | collective-permute-start | bytes 1572872 | tf_op jit(solution)/shard_map/ppermute | solution.py:152
  52.5 19.4 %collective-permute-start.5 = (bf16[64,2048]{1,0:T(8,128)(2,1)}, bf16[64,2048]{1,0:T(8,128)(2,1)S(1)}, u32[]{:S(2)}, u32[]{:S(2)}) collective-permute-start(bf16[64,2048]{1,0:T(8,128)(2,1)} %get-tuple-element.56), channel_id=1, source_target_pairs={{0,24},{4,28},{8,16},{12,20},{16,8},{20,12},{24,0},{28,4},{1,25},{... | collective-permute-start | bytes 786440 | tf_op jit(solution)/shard_map/ppermute | solution.py:19
  55.1 16.8 %collective-permute-start.9 = (bf16[64,2048]{1,0:T(8,128)(2,1)}, bf16[64,2048]{1,0:T(8,128)(2,1)S(1)}, u32[]{:S(2)}, u32[]{:S(2)}) collective-permute-start(bf16[64,2048]{1,0:T(8,128)(2,1)} %get-tuple-element.59), channel_id=1, source_target_pairs={{0,8},{4,12},{8,0},{12,4},{16,24},{20,28},{24,16},{28,20},{1,9},{5... | collective-permute-start | bytes 786440 | tf_op jit(solution)/shard_map/ppermute | solution.py:19
  58.5 15.2 %collective-permute-start.10 = (bf16[64,2048]{1,0:T(8,128)(2,1)}, bf16[64,2048]{1,0:T(8,128)(2,1)S(1)}, u32[]{:S(2)}, u32[]{:S(2)}) collective-permute-start(bf16[64,2048]{1,0:T(8,128)(2,1)} %get-tuple-element.60), channel_id=1, source_target_pairs={{0,16},{4,20},{8,24},{12,28},{16,0},{20,4},{24,8},{28,12},{1,17},{... | collective-permute-start | bytes 786440 | tf_op jit(solution)/shard_map/ppermute | solution.py:19
  61.9 11.9 %collective-permute-start.11 = (bf16[64,2048]{1,0:T(8,128)(2,1)}, bf16[64,2048]{1,0:T(8,128)(2,1)S(1)}, u32[]{:S(2)}, u32[]{:S(2)}) collective-permute-start(bf16[64,2048]{1,0:T(8,128)(2,1)} %get-tuple-element.61), channel_id=1, source_target_pairs={{0,24},{4,28},{8,16},{12,20},{16,8},{20,12},{24,0},{28,4},{1,25},{... | collective-permute-start | bytes 786440 | tf_op jit(solution)/shard_map/ppermute | solution.py:19
  77.3 10.2 %collective-permute-start.15 = (bf16[1024,1024]{1,0:T(8,128)(2,1)}, bf16[1024,1024]{1,0:T(8,128)(2,1)S(1)}, u32[]{:S(2)}, u32[]{:S(2)}) collective-permute-start(bf16[1024,1024]{1,0:T(8,128)(2,1)} %get-tuple-element.64), channel_id=1, source_target_pairs={{0,4},{4,0},{8,12},{12,8},{16,20},{20,16},{24,28},{28,24},{1,5},{5... | collective-permute-start | bytes 6291464 | tf_op jit(solution)/shard_map/ppermute | solution.py:19
  77.9 15.7 %collective-permute-start.16 = (bf16[128,2048]{1,0:T(8,128)(2,1)S(1)}, bf16[128,2048]{1,0:T(8,128)(2,1)}, u32[]{:S(2)}, u32[]{:S(2)}) collective-permute-start(bf16[128,2048]{1,0:T(8,128)(2,1)S(1)} %collective-permute-done.13.refs_9_.refs_2_), channel_id=1, source_target_pairs={{0,1},{1,2},{2,3},{3,0},{4,5},{5,6},{6,7},{7,4},{8,9},{9,10},{10,1... | collective-permute-start | bytes 1572872 | tf_op jit(solution)/shard_map/ppermute | solution.py:152
  90.5 14.8 %collective-permute-start.21 = (bf16[256,1024]{1,0:T(8,128)(2,1)S(1)}, bf16[256,1024]{1,0:T(8,128)(2,1)S(1)}, u32[]{:S(2)}, u32[]{:S(2)}) collective-permute-start(bf16[256,1024]{1,0:T(8,128)(2,1)S(1)} %get-tuple-element.72), channel_id=1, source_target_pairs={{0,16},{4,20},{8,24},{12,28},{16,0},{20,4},{24,8},{28,12},{1,17},{... | collective-permute-start | bytes 1572872 | tf_op jit(solution)/shard_map/ppermute | solution.py:19
  92.1 14.8 %collective-permute-start.20 = (bf16[256,1024]{1,0:T(8,128)(2,1)S(1)}, bf16[256,1024]{1,0:T(8,128)(2,1)S(1)}, u32[]{:S(2)}, u32[]{:S(2)}) collective-permute-start(bf16[256,1024]{1,0:T(8,128)(2,1)S(1)} %get-tuple-element.65.refs_4_.refs_6_), channel_id=1, source_target_pairs={{0,8},{4,12},{8,0},{12,4},{16,24},{20,28},{24,16},{28,20},{1,9},{5... | collective-permute-start | bytes 1572872 | tf_op jit(solution)/shard_map/ppermute | solution.py:19
  95.6 22.6 %collective-permute-start.17 = (bf16[128,2048]{1,0:T(8,128)(2,1)S(1)}, bf16[128,2048]{1,0:T(8,128)(2,1)S(1)}, u32[]{:S(2)}, u32[]{:S(2)}) collective-permute-start(bf16[128,2048]{1,0:T(8,128)(2,1)S(1)} %get-tuple-element.67), channel_id=1, source_target_pairs={{0,8},{4,12},{8,0},{12,4},{16,24},{20,28},{24,16},{28,20},{1,9},{5... | collective-permute-start | bytes 1572872 | tf_op jit(solution)/shard_map/ppermute | solution.py:19
  96.9 21.3 %collective-permute-start.18 = (bf16[128,2048]{1,0:T(8,128)(2,1)S(1)}, bf16[128,2048]{1,0:T(8,128)(2,1)S(1)}, u32[]{:S(2)}, u32[]{:S(2)}) collective-permute-start(bf16[128,2048]{1,0:T(8,128)(2,1)S(1)} %get-tuple-element.68), channel_id=1, source_target_pairs={{0,16},{4,20},{8,24},{12,28},{16,0},{20,4},{24,8},{28,12},{1,17},{... | collective-permute-start | bytes 1572872 | tf_op jit(solution)/shard_map/ppermute | solution.py:19
  97.7 30.5 %collective-permute-start.19 = (bf16[128,2048]{1,0:T(8,128)(2,1)S(1)}, bf16[128,2048]{1,0:T(8,128)(2,1)S(1)}, u32[]{:S(2)}, u32[]{:S(2)}) collective-permute-start(bf16[128,2048]{1,0:T(8,128)(2,1)S(1)} %get-tuple-element.69), channel_id=1, source_target_pairs={{0,24},{4,28},{8,16},{12,20},{16,8},{20,12},{24,0},{28,4},{1,25},{... | collective-permute-start | bytes 1572872 | tf_op jit(solution)/shard_map/ppermute | solution.py:19
  129.0 8.7 %collective-permute-start.26 = (bf16[128,1024]{1,0:T(8,128)(2,1)S(1)}, bf16[128,1024]{1,0:T(8,128)(2,1)S(1)}, u32[]{:S(2)}, u32[]{:S(2)}) collective-permute-start(bf16[128,1024]{1,0:T(8,128)(2,1)S(1)} %get-tuple-element.80), channel_id=1, source_target_pairs={{0,8},{4,12},{8,0},{12,4},{16,24},{20,28},{24,16},{28,20},{1,9},{5... | collective-permute-start | bytes 786440 | tf_op jit(solution)/shard_map/ppermute | solution.py:19
  130.3 8.4 %collective-permute-start.25 = (bf16[128,1024]{1,0:T(8,128)(2,1)S(1)}, bf16[128,1024]{1,0:T(8,128)(2,1)S(1)}, u32[]{:S(2)}, u32[]{:S(2)}) collective-permute-start(bf16[128,1024]{1,0:T(8,128)(2,1)S(1)} %get-tuple-element.73.refs_4_.refs_6_), channel_id=1, source_target_pairs={{0,16},{4,20},{8,24},{12,28},{16,0},{20,4},{24,8},{28,12},{1,17},{... | collective-permute-start | bytes 786440 | tf_op jit(solution)/shard_map/ppermute | solution.py:19
  139.1 14.3 %collective-permute-start.24 = (bf16[256,1024]{1,0:T(8,128)(2,1)S(1)}, bf16[256,1024]{1,0:T(8,128)(2,1)S(1)}, u32[]{:S(2)}, u32[]{:S(2)}) collective-permute-start(bf16[256,1024]{1,0:T(8,128)(2,1)S(1)} %get-tuple-element.77), channel_id=1, source_target_pairs={{0,16},{4,20},{8,24},{12,28},{16,0},{20,4},{24,8},{28,12},{1,17},{... | collective-permute-start | bytes 1572872 | tf_op jit(solution)/shard_map/ppermute | solution.py:19
  140.0 14.0 %collective-permute-start.23 = (bf16[256,1024]{1,0:T(8,128)(2,1)S(1)}, bf16[256,1024]{1,0:T(8,128)(2,1)S(1)}, u32[]{:S(2)}, u32[]{:S(2)}) collective-permute-start(bf16[256,1024]{1,0:T(8,128)(2,1)S(1)} %get-tuple-element.75.refs_4_), channel_id=1, source_target_pairs={{0,8},{4,12},{8,0},{12,4},{16,24},{20,28},{24,16},{28,20},{1,9},{5... | collective-permute-start | bytes 1572872 | tf_op jit(solution)/shard_map/ppermute | solution.py:19
  154.8 15.9 %collective-permute-start.29 = (bf16[128,1024]{1,0:T(8,128)(2,1)S(1)}, bf16[128,1024]{1,0:T(8,128)(2,1)S(1)}, u32[]{:S(2)}, u32[]{:S(2)}) collective-permute-start(bf16[128,1024]{1,0:T(8,128)(2,1)S(1)} %get-tuple-element.86), channel_id=1, source_target_pairs={{0,8},{4,12},{8,0},{12,4},{16,24},{20,28},{24,16},{28,20},{1,9},{5... | collective-permute-start | bytes 786440 | tf_op jit(solution)/shard_map/ppermute | solution.py:19
  156.4 14.4 %collective-permute-start.28 = (bf16[128,1024]{1,0:T(8,128)(2,1)S(1)}, bf16[128,1024]{1,0:T(8,128)(2,1)S(1)}, u32[]{:S(2)}, u32[]{:S(2)}) collective-permute-start(bf16[128,1024]{1,0:T(8,128)(2,1)S(1)} %get-tuple-element.84.refs_4_), channel_id=1, source_target_pairs={{0,16},{4,20},{8,24},{12,28},{16,0},{20,4},{24,8},{28,12},{1,17},{... | collective-permute-start | bytes 786440 | tf_op jit(solution)/shard_map/ppermute | solution.py:19
  156.9 10.8 %collective-permute-start.30 = (bf16[128,640]{1,0:T(8,128)(2,1)S(1)}, bf16[128,640]{1,0:T(8,128)(2,1)S(1)}, u32[]{:S(2)}, u32[]{:S(2)}) collective-permute-start(bf16[128,640]{1,0:T(8,128)(2,1)S(1)} %get-tuple-element.87), channel_id=1, source_target_pairs={{0,8},{4,12},{8,0},{12,4},{16,24},{20,28},{24,16},{28,20},{1,9},{5... | collective-permute-start | bytes 491528 | tf_op jit(solution)/shard_map/ppermute | solution.py:19
  158.1 12.6 %collective-permute-start.31 = (bf16[128,640]{1,0:T(8,128)(2,1)S(1)}, bf16[128,640]{1,0:T(8,128)(2,1)S(1)}, u32[]{:S(2)}, u32[]{:S(2)}) collective-permute-start(bf16[128,640]{1,0:T(8,128)(2,1)S(1)} %get-tuple-element.88), channel_id=1, source_target_pairs={{0,16},{4,20},{8,24},{12,28},{16,0},{20,4},{24,8},{28,12},{1,17},{... | collective-permute-start | bytes 491528 | tf_op jit(solution)/shard_map/ppermute | solution.py:19
  158.9 11.7 %collective-permute-start.32 = (bf16[128,640]{1,0:T(8,128)(2,1)S(1)}, bf16[128,640]{1,0:T(8,128)(2,1)S(1)}, u32[]{:S(2)}, u32[]{:S(2)}) collective-permute-start(bf16[128,640]{1,0:T(8,128)(2,1)S(1)} %get-tuple-element.89), channel_id=1, source_target_pairs={{0,24},{4,28},{8,16},{12,20},{16,8},{20,12},{24,0},{28,4},{1,25},{... | collective-permute-start | bytes 491528 | tf_op jit(solution)/shard_map/ppermute | solution.py:19
  175.1 9.5 %collective-permute-start.35 = (bf16[128,640]{1,0:T(8,128)(2,1)S(1)}, bf16[128,640]{1,0:T(8,128)(2,1)S(1)}, u32[]{:S(2)}, u32[]{:S(2)}) collective-permute-start(bf16[128,640]{1,0:T(8,128)(2,1)S(1)} %get-tuple-element.93), channel_id=1, source_target_pairs={{0,16},{4,20},{8,24},{12,28},{16,0},{20,4},{24,8},{28,12},{1,17},{... | collective-permute-start | bytes 491528 | tf_op jit(solution)/shard_map/ppermute | solution.py:19
  176.3 8.3 %collective-permute-start.36 = (bf16[128,640]{1,0:T(8,128)(2,1)S(1)}, bf16[128,640]{1,0:T(8,128)(2,1)S(1)}, u32[]{:S(2)}, u32[]{:S(2)}) collective-permute-start(bf16[128,640]{1,0:T(8,128)(2,1)S(1)} %get-tuple-element.94), channel_id=1, source_target_pairs={{0,24},{4,28},{8,16},{12,20},{16,8},{20,12},{24,0},{28,4},{1,25},{... | collective-permute-start | bytes 491528 | tf_op jit(solution)/shard_map/ppermute | solution.py:19
  178.1 10.1 %collective-permute-start.46 = (bf16[128,640]{1,0:T(8,128)(2,1)S(1)}, bf16[128,640]{1,0:T(8,128)(2,1)S(1)}, u32[]{:S(2)}, u32[]{:S(2)}) collective-permute-start(bf16[128,640]{1,0:T(8,128)(2,1)S(1)} %add_up.10.refs_0_), channel_id=1, source_target_pairs={{0,2},{1,3},{2,0},{3,1},{4,6},{5,7},{6,4},{7,5},{8,10},{9,11},{10,... | collective-permute-start | bytes 491528 | tf_op jit(solution)/shard_map/ppermute | solution.py:19
  189.5 9.1 %collective-permute-start.48 = (bf16[128,640]{1,0:T(8,128)(2,1)S(1)}, bf16[128,640]{1,0:T(8,128)(2,1)S(1)}, u32[]{:S(2)}, u32[]{:S(2)}) collective-permute-start(bf16[128,640]{1,0:T(8,128)(2,1)S(1)} %add_up.11.refs_0_), channel_id=1, source_target_pairs={{0,16},{4,20},{8,24},{12,28},{16,0},{20,4},{24,8},{28,12},{1,17},{... | collective-permute-start | bytes 491528 | tf_op jit(solution)/shard_map/ppermute | solution.py:19
  190.3 8.4 %collective-permute-start.47 = (bf16[128,640]{1,0:T(8,128)(2,1)S(1)}, bf16[128,640]{1,0:T(8,128)(2,1)S(1)}, u32[]{:S(2)}, u32[]{:S(2)}) collective-permute-start(bf16[128,640]{1,0:T(8,128)(2,1)S(1)} %add_up.11.refs_0_), channel_id=1, source_target_pairs={{0,8},{4,12},{8,0},{12,4},{16,24},{20,28},{24,16},{28,20},{1,9},{5... | collective-permute-start | bytes 491528 | tf_op jit(solution)/shard_map/ppermute | solution.py:19
  198.7 21.5 %collective-permute-start.50 = (bf16[4,128,640]{2,1,0:T(8,128)(2,1)S(1)}, bf16[4,128,640]{2,1,0:T(8,128)(2,1)S(1)}, u32[]{:S(2)}, u32[]{:S(2)}) collective-permute-start(bf16[4,128,640]{2,1,0:T(8,128)(2,1)S(1)} %pile.3.refs_0_), channel_id=1, source_target_pairs={{0,4},{4,0},{8,12},{12,8},{16,20},{20,16},{24,28},{28,24},{1,5},{5... | collective-permute-start | bytes 1966088 | tf_op jit(solution)/shard_map/ppermute | solution.py:19
  198.8 10.5 %collective-permute-start.38 = (bf16[128,640]{1,0:T(8,128)(2,1)S(1)}, bf16[128,640]{1,0:T(8,128)(2,1)S(1)}, u32[]{:S(2)}, u32[]{:S(2)}) collective-permute-start(bf16[128,640]{1,0:T(8,128)(2,1)S(1)} %add_up.8.refs_0_.refs_4_), channel_id=1, source_target_pairs={{0,2},{1,3},{2,0},{3,1},{4,6},{5,7},{6,4},{7,5},{8,10},{9,11},{10,... | collective-permute-start | bytes 491528 | tf_op jit(solution)/shard_map/ppermute | solution.py:19
  211.2 8.9 %collective-permute-start.40 = (bf16[128,640]{1,0:T(8,128)(2,1)S(1)}, bf16[128,640]{1,0:T(8,128)(2,1)S(1)}, u32[]{:S(2)}, u32[]{:S(2)}) collective-permute-start(bf16[128,640]{1,0:T(8,128)(2,1)S(1)} %add_up.9.refs_0_.refs_6_), channel_id=1, source_target_pairs={{0,16},{4,20},{8,24},{12,28},{16,0},{20,4},{24,8},{28,12},{1,17},{... | collective-permute-start | bytes 491528 | tf_op jit(solution)/shard_map/ppermute | solution.py:19
  211.8 8.3 %collective-permute-start.39 = (bf16[128,640]{1,0:T(8,128)(2,1)S(1)}, bf16[128,640]{1,0:T(8,128)(2,1)S(1)}, u32[]{:S(2)}, u32[]{:S(2)}) collective-permute-start(bf16[128,640]{1,0:T(8,128)(2,1)S(1)} %add_up.9.refs_0_.refs_6_), channel_id=1, source_target_pairs={{0,8},{4,12},{8,0},{12,4},{16,24},{20,28},{24,16},{28,20},{1,9},{5... | collective-permute-start | bytes 491528 | tf_op jit(solution)/shard_map/ppermute | solution.py:19
  220.1 13.7 %collective-permute-start.42 = (bf16[4,128,640]{2,1,0:T(8,128)(2,1)S(1)}, bf16[4,128,640]{2,1,0:T(8,128)(2,1)S(1)}, u32[]{:S(2)}, u32[]{:S(2)}) collective-permute-start(bf16[4,128,640]{2,1,0:T(8,128)(2,1)S(1)} %pile.2.refs_0_.refs_2_), channel_id=1, source_target_pairs={{0,4},{4,0},{8,12},{12,8},{16,20},{20,16},{24,28},{28,24},{1,5},{5... | collective-permute-start | bytes 1966088 | tf_op jit(solution)/shard_map/ppermute | solution.py:19
  222.6 8.8 %collective-permute-start.51 = (bf16[128,1024]{1,0:T(8,128)(2,1)S(1)}, bf16[128,1024]{1,0:T(8,128)(2,1)S(1)}, u32[]{:S(2)}, u32[]{:S(2)}) collective-permute-start(bf16[128,1024]{1,0:T(8,128)(2,1)S(1)} %get-tuple-element.105.refs_0_), channel_id=1, source_target_pairs={{0,16},{4,20},{8,24},{12,28},{16,0},{20,4},{24,8},{28,12},{1,17},{... | collective-permute-start | bytes 786440 | tf_op jit(solution)/shard_map/ppermute | solution.py:19
  223.3 9.0 %collective-permute-start.55 = (bf16[128,1024]{1,0:T(8,128)(2,1)S(1)}, bf16[128,1024]{1,0:T(8,128)(2,1)S(1)}, u32[]{:S(2)}, u32[]{:S(2)}) collective-permute-start(bf16[128,1024]{1,0:T(8,128)(2,1)S(1)} %get-tuple-element.104.refs_0_), channel_id=1, source_target_pairs={{0,8},{4,12},{8,0},{12,4},{16,24},{20,28},{24,16},{28,20},{1,9},{5... | collective-permute-start | bytes 786440 | tf_op jit(solution)/shard_map/ppermute | solution.py:19
  231.4 20.0 %collective-permute-start.52 = (bf16[256,1024]{1,0:T(8,128)(2,1)S(1)}, bf16[256,1024]{1,0:T(8,128)(2,1)S(1)}, u32[]{:S(2)}, u32[]{:S(2)}) collective-permute-start(bf16[256,1024]{1,0:T(8,128)(2,1)S(1)} %join_after.6.refs_0_), channel_id=1, source_target_pairs={{0,8},{4,12},{8,0},{12,4},{16,24},{20,28},{24,16},{28,20},{1,9},{5... | collective-permute-start | bytes 1572872 | tf_op jit(solution)/shard_map/ppermute | solution.py:19
  232.4 19.3 %collective-permute-start.56 = (bf16[256,1024]{1,0:T(8,128)(2,1)S(1)}, bf16[256,1024]{1,0:T(8,128)(2,1)S(1)}, u32[]{:S(2)}, u32[]{:S(2)}) collective-permute-start(bf16[256,1024]{1,0:T(8,128)(2,1)S(1)} %join_after.8.refs_0_), channel_id=1, source_target_pairs={{0,16},{4,20},{8,24},{12,28},{16,0},{20,4},{24,8},{28,12},{1,17},{... | collective-permute-start | bytes 1572872 | tf_op jit(solution)/shard_map/ppermute | solution.py:19
  236.2 14.4 %collective-permute-start.53 = (bf16[128,1024]{1,0:T(8,128)(2,1)S(1)}, bf16[128,1024]{1,0:T(8,128)(2,1)S(1)}, u32[]{:S(2)}, u32[]{:S(2)}) collective-permute-start(bf16[128,1024]{1,0:T(8,128)(2,1)S(1)} %get-tuple-element.106), channel_id=1, source_target_pairs={{0,8},{4,12},{8,0},{12,4},{16,24},{20,28},{24,16},{28,20},{1,9},{5... | collective-permute-start | bytes 786440 | tf_op jit(solution)/shard_map/ppermute | solution.py:19
  236.7 14.6 %collective-permute-start.43 = (bf16[128,1024]{1,0:T(8,128)(2,1)S(1)}, bf16[128,1024]{1,0:T(8,128)(2,1)S(1)}, u32[]{:S(2)}, u32[]{:S(2)}) collective-permute-start(bf16[128,1024]{1,0:T(8,128)(2,1)S(1)} %get-tuple-element.107), channel_id=1, source_target_pairs={{0,16},{4,20},{8,24},{12,28},{16,0},{20,4},{24,8},{28,12},{1,17},{... | collective-permute-start | bytes 786440 | tf_op jit(solution)/shard_map/ppermute | solution.py:19
  252.3 13.9 %collective-permute-start.44 = (bf16[256,1024]{1,0:T(8,128)(2,1)S(1)}, bf16[256,1024]{1,0:T(8,128)(2,1)S(1)}, u32[]{:S(2)}, u32[]{:S(2)}) collective-permute-start(bf16[256,1024]{1,0:T(8,128)(2,1)S(1)} %maximum_select_fusion.refs_2_.refs_0_), channel_id=1, source_target_pairs={{0,8},{4,12},{8,0},{12,4},{16,24},{20,28},{24,16},{28,20},{1,9},{5... | collective-permute-start | bytes 1572872 | tf_op jit(solution)/shard_map/ppermute | solution.py:19
  253.5 13.6 %collective-permute-start.59 = (bf16[256,1024]{1,0:T(8,128)(2,1)S(1)}, bf16[256,1024]{1,0:T(8,128)(2,1)S(1)}, u32[]{:S(2)}, u32[]{:S(2)}) collective-permute-start(bf16[256,1024]{1,0:T(8,128)(2,1)S(1)} %maximum_select_fusion.1.refs_3_.refs_0_), channel_id=1, source_target_pairs={{0,16},{4,20},{8,24},{12,28},{16,0},{20,4},{24,8},{28,12},{1,17},{... | collective-permute-start | bytes 1572872 | tf_op jit(solution)/shard_map/ppermute | solution.py:19
  (35 other events, 209.8 us)

commit v7 on v6

--- a/solution.py
+++ b/solution.py
@@ -52,7 +52,7 @@
 
 
 def run(body, scalars, operands, in_specs, outs, out_specs, grid=(1,), scratch=(), after=(),
-        flops=0, moved=0, limit=32, name=None):
+        flops=0, moved=0, limit=32, name=None, aliases=None):
     n_in, n_after = len(operands), len(after)
 
     def kernel(scalars_ref, *refs):
@@ -71,6 +71,7 @@
         compiler_params=pltpu.CompilerParams(vmem_limit_bytes=limit * MIB),
         cost_estimate=pl.CostEstimate(flops=flops, bytes_accessed=moved, transcendentals=0),
         name=name,
+        input_output_aliases=aliases or {},
     )(scalars, *operands, *after)
 
 
@@ -101,11 +102,12 @@
 
         @pl.when(first)
         def _():
-            square_ref[...] = square
+            square_ref[:8, :] = jnp.zeros_like(square)
+            square_ref[8:, :] = square
 
         @pl.when(jnp.logical_not(first))
         def _():
-            square_ref[...] += square
+            square_ref[8:, :] += square
 
     out = like((2 * quarter, depth), BF16)
     return run(
@@ -116,13 +118,13 @@
                 lambda k, j, c: (0, (2 * (j // steps) + (c[0] ^ (1 - k))) * steps + j % steps),
             )
         ],
-        [out, out, like((8, 128), F32)],
+        [out, out, like((16, 128), F32)],
         [
             pl.BlockSpec((step, depth), lambda k, j, c: (jnp.where(k == 0, j, 2 * steps - 1), 0)),
             pl.BlockSpec((step, depth), lambda k, j, c: (jnp.where(k == 1, j, 0), 0)),
-            pl.BlockSpec((8, 128), lambda k, j, c: (0, 0)),
+            pl.BlockSpec((16, 128), lambda k, j, c: (0, 0)),
         ],
-        grid=(2, 2 * steps), after=after, flops=2 * depth * width, moved=6 * depth * width, limit=54, name="turn_weight",
+        grid=(2, 2 * steps), after=after, flops=2 * depth * width, moved=6 * depth * width, limit=16, name="turn_weight",
     )
 
 
@@ -427,42 +429,53 @@
     return out_grad
 
 
-def weight_grad_of(place, turned, pieces, base=None, weight_squares=None, after=()):
+def weight_grad_of(place, turned, pieces, flips, base=None, done=None, weight_squares=None):
     depth, batch = turned.shape
-    cols = pieces[0].shape[0]
-    last = base is not None
+    cols, n_piece = pieces[0].shape[0], len(pieces)
+    n_path = 2
+    squares = weight_squares is not None
+    rest = [one for one in (base, done, weight_squares) if one is not None]
 
     def body(place_ref, turned_ref, *refs):
-        if last:
-            base_ref, weight_squares_ref, out_ref, square_ref = refs[4:]
-        else:
-            (out_ref,) = refs[4:]
-        for index in range(4):
+        base_ref = refs[n_piece] if base is not None else None
+        squares_in_ref = refs[n_piece + len(rest) - 1] if squares else None
+        out_ref = refs[n_piece + len(rest)]
+        for index in range(n_piece):
 
             @pl.when(pl.program_id(0) == index)
             def _():
                 total = lax.dot_general(
                     turned_ref[...], refs[index][...], ROWS_BY_ROWS, preferred_element_type=F32
                 )
-                if last:
+                if base is not None:
                     total += base_ref[...]
-                    square = fold(total * total)
+                if squares:
+                    square_ref = refs[-1]
                     if index == 0:
-                        square_ref[:8, :] = square
-                        square_ref[8:, :] = weight_squares_ref[...]
-                    else:
-                        square_ref[:8, :] += square
+                        square_ref[...] = squares_in_ref[...]
+                    square_ref[:8, :] += fold(total * total)
                 out_ref[...] = total
 
-    tile = pl.BlockSpec((depth, cols), lambda j, s: (0, (j >> 1) * 2 + ((j & 1) ^ s[1])))
+    def column(j, s):
+        if len(flips) == 1:
+            return j * n_path + (s[1] ^ flips[0])
+        return (j >> 1) * n_path + ((j & 1) ^ s[1])
+
+    tile = pl.BlockSpec((depth, cols), lambda j, s: (0, column(j, s)))
     square = pl.BlockSpec((16, 128), lambda j, s: (0, 0))
     operands = [turned, *pieces]
+    rest_specs = [tile] if base is not None else []
+    if done is not None:
+        rest_specs.append(pl.BlockSpec(memory_space=pl.ANY))
+    if squares:
+        rest_specs.append(whole(weight_squares))
     return run(
-        body, place, operands + ([base, weight_squares] if last else []),
-        [whole(one) for one in operands] + ([tile, whole(weight_squares)] if last else []),
-        [like((depth, 4 * cols), F32)] + ([like((16, 128), F32)] if last else []),
-        [tile] + ([square] if last else []), grid=(4,), after=after,
-        flops=8 * cols * batch * depth, moved=16 * depth * cols * (2 if last else 1), limit=20, name="weight_grad_of",
+        body, place, operands + rest, [whole(one) for one in operands] + rest_specs,
+        [like((depth, 4 * cols), F32)] + ([like((16, 128), F32)] if squares else []),
+        [tile] + ([square] if squares else []), grid=(n_piece,),
+        flops=2 * n_piece * cols * batch * depth, moved=4 * n_piece * depth * cols, limit=20,
+        aliases={1 + len(operands) + len(rest_specs) - 1 - squares: 0} if done is not None else {},
+        name="weight_grad_of",
     )
 
 
@@ -519,12 +532,14 @@
     def send_on(v, level, send):
         return [swap(send[p], "dp", 1 << orders[p][level]) for p in range(2)]
 
-    def sum_plane(rows, after=()):
-        parts = [rows[0]] + [swap(rows[mask], "dp", 2 * mask) for mask in range(1, n_chip)]
-        return add_up(parts, after=after)
-
-    def sum_line(total, bit, after=()):
-        return add_up([total, swap(total, "feat", 1 << bit)], after=after)
+    def sum_plane(rows):
+        total = rows[0].astype(F32)
+        for mask in range(1, n_chip):
+            total += swap(rows[mask], "dp", 2 * mask).astype(F32)
+        return total.astype(BF16)
+
+    def sum_line(total, bit):
+        return (total.astype(F32) + swap(total, "feat", 1 << bit).astype(F32)).astype(BF16)
 
     def spread_gram(total, after=()):
         parts = [total] + [swap(total, "dp", 2 * mask) for mask in range(1, n_chip)]
@@ -573,34 +588,35 @@
     for level in range(1, len(high)):
         send[0], keep[0] = add_halves(bits_at(level), keep[0], got[0], after=[rows[1][0]])
         got[0] = send_on(0, level, send[0])
-    gram[1] = sum_plane(rows[1], after=[send[0][0]])
+    gram[1] = sum_plane(rows[1])
     normed[0], half[0], inverse[0] = normalise(keep[0], got[0], after=[gram[1]])
     rows[0] = list(gram_rows(place, half[0], swap(half[0], "dp", 1), n_chip))
-    last = line_bits[-1]
-    for bit in line_bits[:-1]:
-        gram[1] = sum_line(gram[1], bit, after=[rows[0][0]])
+    for bit in line_bits:
+        gram[1] = sum_line(gram[1], bit)
+    gram[1] = spread_gram(gram[1])
     gram[0] = sum_plane(rows[0])
-    gram[1] = sum_line(gram[1], last, after=[gram[0]])
-    for bit in line_bits[:-1]:
+    for bit in line_bits:
         gram[0] = sum_line(gram[0], bit)
-    gram[1] = spread_gram(gram[1], after=[gram[0]])
-    gram[0] = sum_line(gram[0], last)
     out_grad = [None] * 2
     out_grad[0] = out_grad_of(
         place, *gram[1], normed[0], half[0], half[1], inverse[0], after=[gram[0]]
     )
-    gram[0] = spread_gram(gram[0])
+    gram[0] = spread_gram(gram[0], after=[out_grad[0]])
     share = out_grad[0].shape[0] // 2
-    parts = gather_step([out_grad[0][:share], out_grad[0][share:]], 0, after=[gram[0][0]])
     out_grad[1] = out_grad_of(place, *gram[0], normed[1], half[1], half[0], inverse[1])
+    parts = gather_step([out_grad[0][:share], out_grad[0][share:]], 0, after=[out_grad[1]])
     last_parts = gather_step([out_grad[1][:share], out_grad[1][share:]], 0)
     for step in range(1, len(high)):
         parts = gather_step(parts, step, after=last_parts)
-    (base,) = weight_grad_of(place, turned[0], with_swapped(parts))
+    (base,) = weight_grad_of(place, turned[0], with_swapped(parts), (0, 1))
     for step in range(1, len(high)):
         last_parts = gather_step(last_parts, step, after=[base] if step == len(high) - 1 else None)
+    swapped = [swap(part, "dp", 1) for part in last_parts]
     weight_grad, squares = weight_grad_of(
-        place, turned[1], with_swapped(last_parts), base, weight_squares
+        place, turned[1], last_parts, (0,), base, None, weight_squares
+    )
+    weight_grad, squares = weight_grad_of(
+        place, turned[1], swapped, (1,), base, weight_grad, squares
     )
     return update(sum_everywhere(squares), weight, velocity, weight_grad)
 

time: 302 us -> 288 us (0.954)
  waiting for transfers between devices: 166 us -> 142 us
  local copies, waits for them, and re-layouts: 7.02 us -> 11.1 us
    ppermute x52, waiting for transfers between devices: 120 us -> 94 us  [swap(): lax.ppermute(value, axis, [(i, i ^ mask) for i in range(lax.axis_size(axi...]
    unnamed x30, local copies, waits for them, and re-layouts: 6.94 us -> 11 us
    pallas_call x40 -> x35, Pallas kernels: 66.5 us -> 69.2 us  [run(): pl.pallas_call(kernel, grid_spec=pltpu.PrefetchScalarGridSpec(num_scalar_...]
  transfers between devices with their start and end apart: 68 -> 68, of which waited for: 45 -> 41; matrix products, arithmetic and copies ran while one was open for 0% -> 0% of each run, Pallas kernels for 16% -> 19%
where the time goes in v7:
time: 288 us
  waiting for transfers between devices  142 us (49%)
  Pallas kernels  69.2 us (24%)
  starting transfers between devices  63.3 us (22%)
  local copies, waits for them, and re-layouts  11.1 us (4%)
    ppermute x52, waiting for transfers between devices, swap(): lax.ppermute(value, axis, [(i, i ^ mask) for i in range(lax.axis_size(axi...  94 us
    pallas_call x35, Pallas kernels, run(): pl.pallas_call(kernel, grid_spec=pltpu.PrefetchScalarGridSpec(num_scalar_...  69.2 us
    ppermute x52, starting transfers between devices, swap(): lax.ppermute(value, axis, [(i, i ^ mask) for i in range(lax.axis_size(axi...  49.2 us
    ppermute x9, waiting for transfers between devices, go_round(): shares.append(lax.ppermute(shares[-1], 'feat', ring))  41.9 us
    unnamed x30, local copies, waits for them, and re-layouts  11 us
    ppermute x7, starting transfers between devices, sum_everywhere(): lax.ppermute(value, axes, [(i, i ^ mask) for i in range(count)])  7.46 us
    ppermute x9, starting transfers between devices, go_round(): shares.append(lax.ppermute(shares[-1], 'feat', ring))  6.63 us
    ppermute x7, waiting for transfers between devices, sum_everywhere(): lax.ppermute(value, axes, [(i, i ^ mask) for i in range(count)])  6.51 us
  transfers between devices with their start and end apart: 68, of which 41 were waited for; matrix products, arithmetic and copies ran while one was open for 0% of the time, Pallas kernels for 19%

profile of v7, /device:TPU:0, one launch (start us, length us, event | category | flops | bytes accessed | tf_op | source)
XLA Modules:
  0.0 288.0 jit_solution(1455662417425753472)
XLA Ops:
  1.9 3.1 %collective-permute-start = (bf16[64,2048]{1,0:T(8,128)(2,1)S(1)}, bf16[64,2048]{1,0:T(8,128)(2,1)S(1)}, u32[]{:S(2)}, u32[]{:S(2)}) collective-permute-start(bf16[64,2048]{1,0:T(8,128)(2,1)S(1)} %get-tuple-element.54.refs_0_), channel_id=1, source_target_pairs={{0,1},{1,2},{2,3},{3,0},{4,5},{5,6},{6,7},{7,4},{8,9},{9,10},{10,1... | collective-permute-start | bytes 786440 | tf_op jit(solution)/shard_map/ppermute | solution.py:154
  6.6 7.6 %collective-permute-done.refs_1_ = bf16[64,2048]{1,0:T(8,128)(2,1)S(1)} collective-permute-done((bf16[64,2048]{1,0:T(8,128)(2,1)S(1)}, bf16[64,2048]{1,0:T(8,128)(2,1)S(1)}, u32[]{:S(2)}, u32[]{:S(2)}) %collective-permute-start) | collective-permute-done | bytes 262176 | tf_op jit(solution)/shard_map/ppermute | solution.py:154
  15.8 4.0 %collective-permute-done.6.refs_1_ = bf16[64,2048]{1,0:T(8,128)(2,1)S(1)} collective-permute-done((bf16[64,2048]{1,0:T(8,128)(2,1)S(1)}, bf16[64,2048]{1,0:T(8,128)(2,1)S(1)}, u32[]{:S(2)}, u32[]{:S(2)}) %collective-permute-start.6) | collective-permute-done | bytes 262176 | tf_op jit(solution)/shard_map/ppermute | solution.py:154
  19.8 5.6 %collective-permute-done.1.refs_2_ = bf16[64,2048]{1,0:T(8,128)(2,1)S(1)} collective-permute-done((bf16[64,2048]{1,0:T(8,128)(2,1)S(1)}, bf16[64,2048]{1,0:T(8,128)(2,1)S(1)}, u32[]{:S(2)}, u32[]{:S(2)}) %collective-permute-start.1) | collective-permute-done | bytes 262176 | tf_op jit(solution)/shard_map/ppermute | solution.py:154
  25.5 16.7 %collective-permute-done.7.refs_2_ = bf16[64,2048]{1,0:T(8,128)(2,1)S(1)} collective-permute-done((bf16[64,2048]{1,0:T(8,128)(2,1)S(1)}, bf16[64,2048]{1,0:T(8,128)(2,1)S(1)}, u32[]{:S(2)}, u32[]{:S(2)}) %collective-permute-start.7) | collective-permute-done | bytes 262176 | tf_op jit(solution)/shard_map/ppermute | solution.py:154
  42.3 5.6 %collective-permute-done.2.refs_3_ = bf16[64,2048]{1,0:T(8,128)(2,1)S(1)} collective-permute-done((bf16[64,2048]{1,0:T(8,128)(2,1)S(1)}, bf16[64,2048]{1,0:T(8,128)(2,1)S(1)}, u32[]{:S(2)}, u32[]{:S(2)}) %collective-permute-start.2) | collective-permute-done | bytes 262176 | tf_op jit(solution)/shard_map/ppermute | solution.py:154
  56.8 2.4 collective-permute-done.3.refs_1_
  60.0 1.8 collective-permute-start.10
  65.6 3.4 %copy-done = f32[1024,2048]{1,0:T(8,128)S(1)} copy-done((f32[1024,2048]{1,0:T(8,128)S(1)}, f32[1024,2048]{1,0:T(8,128)}, u32[]{:S(2)}) %copy-start) | copy-done | bytes 8388632
  69.0 4.6 %turn_weight.1 = (bf16[1024,1024]{1,0:T(8,128)(2,1)}, bf16[1024,1024]{1,0:T(8,128)(2,1)S(1)}, f32[16,128]{1,0:T(8,128)S(1)}) custom-call(s32[1]{0:T(128)} %bitcast.1.scalars_ref, f32[1024,2048]{1,0:T(8,128)S(1)} %copy-done, bf16[64,2048]{1,0:T(8,128)(2,1)S(1)} %get-tuple-element.60.refs_1_.refs_4_), custom_call_target="tpu_custom_call" | custom-call | flops 4194304 | bytes 12582912 | tf_op jit(solution)/shard_map/turn_weight/pallas_call | solution.py:61
  74.6 3.2 %collect.2.refs_0_ = bf16[512,2048]{1,0:T(8,128)(2,1)} custom-call(s32[2]{0:T(128)S(1)} %pad_add_fusion.scalars_ref, bf16[64,2048]{1,0:T(8,128)(2,1)S(1)} %copy-done.8, bf16[64,2048]{1,0:T(8,128)(2,1)S(1)} %copy-done.10, bf16[64,2048]{1,0:T(8,128)(2,1)S(1)} %copy-done.12, bf16[64,2048]{1,0:T(8,128)(2,1)} %collective-permute-done.5.refs_3_, ...), custom_call_target="tpu_custom_call" | custom-call | bytes 4194304 | tf_op jit(solution)/shard_map/collect/pallas_call | solution.py:61
  78.7 3.6 %collective-permute-done.14.refs_1_ = bf16[512,2048]{1,0:T(8,128)(2,1)} collective-permute-done((bf16[512,2048]{1,0:T(8,128)(2,1)}, bf16[512,2048]{1,0:T(8,128)(2,1)}, u32[]{:S(2)}, u32[]{:S(2)}) %collective-permute-start.14) | collective-permute-done | bytes 2097184 | tf_op jit(solution)/shard_map/ppermute | solution.py:19
  82.3 3.0 %assemble.2.refs_0_.refs_4_ = bf16[1024,2048]{1,0:T(8,128)(2,1)S(1)} custom-call(s32[2]{0:T(128)S(1)} %pad_add_fusion.scalars_ref, bf16[512,2048]{1,0:T(8,128)(2,1)} %collect.2.refs_0_, bf16[512,2048]{1,0:T(8,128)(2,1)} %collective-permute-done.14.refs_1_), custom_call_target="tpu_custom_call" | custom-call | bytes 8388608 | tf_op jit(solution)/shard_map/assemble/pallas_call | solution.py:61
  85.4 4.2 %forward.4 = (bf16[256,1024]{1,0:T(8,128)(2,1)S(1)}, bf16[256,1024]{1,0:T(8,128)(2,1)S(1)}) custom-call(s32[2]{0:T(128)S(1)} %get-tuple-element.106.scalars_ref, bf16[1024,1024]{1,0:T(8,128)(2,1)S(1)} %get-tuple-element.64.refs_8_.refs_0_.refs_2_, bf16[1024,1024]{1,0:T(8,128)(2,1)} %collective-permute-done.15.refs_1_.refs_3_, ...), custom_call_target="tpu_custom_call" | custom-call | flops 2147483648 | bytes 6291456 | tf_op jit(solution)/shard_map/forward/pallas_call | solution.py:61
  91.7 2.4 collective-permute-done.16.refs_3_
  94.1 2.2 choose.5
  96.2 2.0 collective-permute-start.17
  101.1 4.4 %forward.5 = (bf16[256,1024]{1,0:T(8,128)(2,1)S(1)}, bf16[256,1024]{1,0:T(8,128)(2,1)S(1)}) custom-call(s32[2]{0:T(128)S(1)} %get-tuple-element.107.scalars_ref, bf16[1024,1024]{1,0:T(8,128)(2,1)S(1)} %get-tuple-element.64.refs_8_.refs_0_.refs_2_, bf16[1024,1024]{1,0:T(8,128)(2,1)} %collective-permute-done.15.refs_1_.refs_3_, ...), custom_call_target="tpu_custom_call" | custom-call | flops 2147483648 | bytes 6291456 | tf_op jit(solution)/shard_map/forward/pallas_call | solution.py:61
  106.7 10.4 %collective-permute-done.17.refs_1_ = bf16[128,2048]{1,0:T(8,128)(2,1)S(1)} collective-permute-done((bf16[128,2048]{1,0:T(8,128)(2,1)S(1)}, bf16[128,2048]{1,0:T(8,128)(2,1)S(1)}, u32[]{:S(2)}, u32[]{:S(2)}) %collective-permute-start.17) | collective-permute-done | bytes 524320 | tf_op jit(solution)/shard_map/ppermute | solution.py:19
  117.2 10.3 %collective-permute-done.19.refs_3_ = bf16[128,2048]{1,0:T(8,128)(2,1)S(1)} collective-permute-done((bf16[128,2048]{1,0:T(8,128)(2,1)S(1)}, bf16[128,2048]{1,0:T(8,128)(2,1)S(1)}, u32[]{:S(2)}, u32[]{:S(2)}) %collective-permute-start.19) | collective-permute-done | bytes 524320 | tf_op jit(solution)/shard_map/ppermute | solution.py:19
  128.2 1.8 collective-permute-start.26
  130.4 2.0 collective-permute-done.22.refs_1_
  133.2 4.2 %forward.7 = (bf16[256,1024]{1,0:T(8,128)(2,1)S(1)}, bf16[256,1024]{1,0:T(8,128)(2,1)S(1)}) custom-call(s32[2]{0:T(128)S(1)} %get-tuple-element.106.scalars_ref, bf16[1024,1024]{1,0:T(8,128)(2,1)S(1)} %get-tuple-element.64.refs_8_.refs_0_.refs_2_, bf16[1024,1024]{1,0:T(8,128)(2,1)} %collective-permute-done.15.refs_1_.refs_3_, ...), custom_call_target="tpu_custom_call" | custom-call | flops 2147483648 | bytes 6291456 | tf_op jit(solution)/shard_map/forward/pallas_call | solution.py:61
  147.0 4.2 %forward.6 = (bf16[256,1024]{1,0:T(8,128)(2,1)S(1)}, bf16[256,1024]{1,0:T(8,128)(2,1)S(1)}) custom-call(s32[2]{0:T(128)S(1)} %get-tuple-element.107.scalars_ref, bf16[1024,1024]{1,0:T(8,128)(2,1)S(1)} %get-tuple-element.64.refs_8_.refs_0_.refs_2_, bf16[1024,1024]{1,0:T(8,128)(2,1)} %collective-permute-done.15.refs_1_.refs_3_, ...), custom_call_target="tpu_custom_call" | custom-call | flops 2147483648 | bytes 6291456 | tf_op jit(solution)/shard_map/forward/pallas_call | solution.py:61
  151.2 2.5 collective-permute-done.24.refs_3_
  157.6 4.6 %collective-permute-done.32 = bf16[128,640]{1,0:T(8,128)(2,1)S(1)} collective-permute-done((bf16[128,640]{1,0:T(8,128)(2,1)S(1)}, bf16[128,640]{1,0:T(8,128)(2,1)S(1)}, u32[]{:S(2)}, u32[]{:S(2)}) %collective-permute-start.32) | collective-permute-done | bytes 163872 | tf_op jit(solution)/shard_map/ppermute | solution.py:19
  162.4 3.4 %collective-permute-done.28.refs_1_ = bf16[128,1024]{1,0:T(8,128)(2,1)S(1)} collective-permute-done((bf16[128,1024]{1,0:T(8,128)(2,1)S(1)}, bf16[128,1024]{1,0:T(8,128)(2,1)S(1)}, u32[]{:S(2)}, u32[]{:S(2)}) %collective-permute-start.28) | collective-permute-done | bytes 262176 | tf_op jit(solution)/shard_map/ppermute | solution.py:19
  173.3 3.8 %collective-permute-done.43 = bf16[128,640]{1,0:T(8,128)(2,1)S(1)} collective-permute-done((bf16[128,640]{1,0:T(8,128)(2,1)S(1)}, bf16[128,640]{1,0:T(8,128)(2,1)S(1)}, u32[]{:S(2)}, u32[]{:S(2)}) %collective-permute-start.43) | collective-permute-done | bytes 163872 | tf_op jit(solution)/shard_map/ppermute | solution.py:19
  177.1 1.8 collective-permute-start.46
  180.8 2.6 collective-permute-start.37
  183.4 1.8 collective-permute-done.46.refs_3_
  185.2 2.5 collective-permute-done.45.refs_2_
  189.1 10.0 %collective-permute-done.38 = bf16[128,640]{1,0:T(8,128)(2,1)S(1)} collective-permute-done((bf16[128,640]{1,0:T(8,128)(2,1)S(1)}, bf16[128,640]{1,0:T(8,128)(2,1)S(1)}, u32[]{:S(2)}, u32[]{:S(2)}) %collective-permute-start.38) | collective-permute-done | bytes 163872 | tf_op jit(solution)/shard_map/ppermute | solution.py:19
  202.8 2.4 out_grad_of.2.refs_4_
  205.1 2.1 collective-permute-done.41.refs_3_
  207.3 2.4 collective-permute-done.40.refs_2_
  211.9 2.4 out_grad_of.3.refs_2_
  214.3 4.3 %collective-permute-done.55.refs_1_ = bf16[128,1024]{1,0:T(8,128)(2,1)S(1)} collective-permute-done((bf16[128,1024]{1,0:T(8,128)(2,1)S(1)}, bf16[128,1024]{1,0:T(8,128)(2,1)S(1)}, u32[]{:S(2)}, u32[]{:S(2)}) %collective-permute-start.55) | collective-permute-done | bytes 262176 | tf_op jit(solution)/shard_map/ppermute | solution.py:19
  223.0 15.9 %collective-permute-done.53 = bf16[128,1024]{1,0:T(8,128)(2,1)S(1)} collective-permute-done((bf16[128,1024]{1,0:T(8,128)(2,1)S(1)}, bf16[128,1024]{1,0:T(8,128)(2,1)S(1)}, u32[]{:S(2)}, u32[]{:S(2)}) %collective-permute-start.53) | collective-permute-done | bytes 262176 | tf_op jit(solution)/shard_map/ppermute | solution.py:19
  243.5 6.6 %weight_grad_of.3.refs_2_.refs_3_ = f32[1024,2048]{1,0:T(8,128)S(1)} custom-call(s32[2]{0:T(128)S(1)} %pad_add_fusion.scalars_ref, bf16[1024,1024]{1,0:T(8,128)(2,1)S(1)} %copy-done.5, bf16[512,1024]{1,0:T(8,128)(2,1)S(1)} %join_after.7.refs_1_, bf16[512,1024]{1,0:T(8,128)(2,1)S(1)} %collective-permute-done.54.refs_2_, ...), custom_call_target="tpu_custom_call" | custom-call | flops 4294967296 | bytes 8388608 | tf_op jit(solution)/shard_map/weight_grad_of/pallas_call | solution.py:61
  250.2 3.8 %collective-permute-done.50.refs_1_ = bf16[256,1024]{1,0:T(8,128)(2,1)S(1)} collective-permute-done((bf16[256,1024]{1,0:T(8,128)(2,1)S(1)}, bf16[256,1024]{1,0:T(8,128)(2,1)S(1)}, u32[]{:S(2)}, u32[]{:S(2)}) %collective-permute-start.50) | collective-permute-done | bytes 524320 | tf_op jit(solution)/shard_map/ppermute | solution.py:19
  255.6 3.8 %weight_grad_of.4 = (f32[1024,2048]{1,0:T(8,128)S(1)}, f32[16,128]{1,0:T(8,128)S(1)}) custom-call(s32[2]{0:T(128)S(1)} %pad_add_fusion.scalars_ref, bf16[1024,1024]{1,0:T(8,128)(2,1)S(1)} %copy-done.2, bf16[512,1024]{1,0:T(8,128)(2,1)S(1)} %join_after.10.refs_1_, bf16[512,1024]{1,0:T(8,128)(2,1)S(1)} %join_after.11.refs_2_, ...), custom_call_target="tpu_custom_call" | custom-call | flops 2147483648 | bytes 4194304 | tf_op jit(solution)/shard_map/weight_grad_of/pallas_call | solution.py:61
  259.4 3.8 %weight_grad_of.5 = (f32[1024,2048]{1,0:T(8,128)S(1)}, f32[16,128]{1,0:T(8,128)S(1)}) custom-call(s32[2]{0:T(128)S(1)} %pad_add_fusion.scalars_ref, bf16[1024,1024]{1,0:T(8,128)(2,1)S(1)} %copy-done.2, bf16[512,1024]{1,0:T(8,128)(2,1)S(1)} %collective-permute-done.58.refs_1_, ...), custom_call_target="tpu_custom_call", output_to_operand_aliasing={{0}: (5, {})} | custom-call | flops 2147483648 | bytes 4194304 | tf_op jit(solution)/shard_map/weight_grad_of/pallas_call | solution.py:61
  263.2 1.9 collective-permute-start.63
  265.1 2.5 collective-permute-start.61
  274.6 2.6 collective-permute-done.67.refs_1_
  277.2 3.4 %copy-done.3 = f32[1024,2048]{1,0:T(8,128)S(1)} copy-done((f32[1024,2048]{1,0:T(8,128)S(1)}, f32[1024,2048]{1,0:T(8,128)}, u32[]{:S(2)}) %copy-start.3) | copy-done | bytes 8388632
  280.6 7.5 %update.1 = (f32[1024,2048]{1,0:T(8,128)}, f32[1024,2048]{1,0:T(8,128)}) custom-call(s32[1]{0:T(128)} %constant.21.clone.1.scalars_ref, f32[16,128]{1,0:T(8,128)S(1)} %add_add_fusion.refs_0_, f32[16,128]{1,0:T(8,128)S(1)} %collective-permute-done.67.refs_1_, f32[1024,2048]{1,0:T(8,128)S(1)} %bitcast.9, f32[1024,2048]{1,0:T(8,128)S(1)} %copy-done.3, ...), custom_call_target="tpu_custom_call" | custom-call | flops 8388608 | bytes 41943040 | tf_op jit(solution)/shard_map/update/pallas_call | solution.py:61
  (170 shorter events, 75.8 us)
Async XLA Ops:
  1.9 12.2 %collective-permute-start = (bf16[64,2048]{1,0:T(8,128)(2,1)S(1)}, bf16[64,2048]{1,0:T(8,128)(2,1)S(1)}, u32[]{:S(2)}, u32[]{:S(2)}) collective-permute-start(bf16[64,2048]{1,0:T(8,128)(2,1)S(1)} %get-tuple-element.54.refs_0_), channel_id=1, source_target_pairs={{0,1},{1,2},{2,3},{3,0},{4,5},{5,6},{6,7},{7,4},{8,9},{9,10},{10,1... | collective-permute-start | bytes 786440 | tf_op jit(solution)/shard_map/ppermute | solution.py:154
  5.0 14.8 %collective-permute-start.6 = (bf16[64,2048]{1,0:T(8,128)(2,1)S(1)}, bf16[64,2048]{1,0:T(8,128)(2,1)S(1)}, u32[]{:S(2)}, u32[]{:S(2)}) collective-permute-start(bf16[64,2048]{1,0:T(8,128)(2,1)S(1)} %get-tuple-element.59.refs_0_), channel_id=1, source_target_pairs={{0,1},{1,2},{2,3},{3,0},{4,5},{5,6},{6,7},{7,4},{8,9},{9,10},{10,1... | collective-permute-start | bytes 786440 | tf_op jit(solution)/shard_map/ppermute | solution.py:154
  14.2 11.2 %collective-permute-start.1 = (bf16[64,2048]{1,0:T(8,128)(2,1)S(1)}, bf16[64,2048]{1,0:T(8,128)(2,1)S(1)}, u32[]{:S(2)}, u32[]{:S(2)}) collective-permute-start(bf16[64,2048]{1,0:T(8,128)(2,1)S(1)} %collective-permute-done.refs_1_), channel_id=1, source_target_pairs={{0,1},{1,2},{2,3},{3,0},{4,5},{5,6},{6,7},{7,4},{8,9},{9,10},{10,1... | collective-permute-start | bytes 786440 | tf_op jit(solution)/shard_map/ppermute | solution.py:154
  14.2 39.1 %collective-permute-start.12 = (bf16[128,2048]{1,0:T(8,128)(2,1)S(1)}, bf16[128,2048]{1,0:T(8,128)(2,1)}, u32[]{:S(2)}, u32[]{:S(2)}) collective-permute-start(bf16[128,2048]{1,0:T(8,128)(2,1)S(1)} %get-tuple-element.65.refs_0_), channel_id=1, source_target_pairs={{0,1},{1,2},{2,3},{3,0},{4,5},{5,6},{6,7},{7,4},{8,9},{9,10},{10,1... | collective-permute-start | bytes 1572872 | tf_op jit(solution)/shard_map/ppermute | solution.py:154
  19.8 22.5 %collective-permute-start.7 = (bf16[64,2048]{1,0:T(8,128)(2,1)S(1)}, bf16[64,2048]{1,0:T(8,128)(2,1)S(1)}, u32[]{:S(2)}, u32[]{:S(2)}) collective-permute-start(bf16[64,2048]{1,0:T(8,128)(2,1)S(1)} %collective-permute-done.6.refs_1_), channel_id=1, source_target_pairs={{0,1},{1,2},{2,3},{3,0},{4,5},{5,6},{6,7},{7,4},{8,9},{9,10},{10,1... | collective-permute-start | bytes 786440 | tf_op jit(solution)/shard_map/ppermute | solution.py:154
  25.4 22.5 %collective-permute-start.2 = (bf16[64,2048]{1,0:T(8,128)(2,1)S(1)}, bf16[64,2048]{1,0:T(8,128)(2,1)S(1)}, u32[]{:S(2)}, u32[]{:S(2)}) collective-permute-start(bf16[64,2048]{1,0:T(8,128)(2,1)S(1)} %collective-permute-done.1.refs_2_), channel_id=1, source_target_pairs={{0,1},{1,2},{2,3},{3,0},{4,5},{5,6},{6,7},{7,4},{8,9},{9,10},{10,1... | collective-permute-start | bytes 786440 | tf_op jit(solution)/shard_map/ppermute | solution.py:154
  42.3 11.3 %collective-permute-start.8 = (bf16[64,2048]{1,0:T(8,128)(2,1)S(1)}, bf16[64,2048]{1,0:T(8,128)(2,1)S(1)}, u32[]{:S(2)}, u32[]{:S(2)}) collective-permute-start(bf16[64,2048]{1,0:T(8,128)(2,1)S(1)} %collective-permute-done.7.refs_2_), channel_id=1, source_target_pairs={{0,1},{1,2},{2,3},{3,0},{4,5},{5,6},{6,7},{7,4},{8,9},{9,10},{10,1... | collective-permute-start | bytes 786440 | tf_op jit(solution)/shard_map/ppermute | solution.py:154
  50.0 9.2 %collective-permute-start.3 = (bf16[64,2048]{1,0:T(8,128)(2,1)S(1)}, bf16[64,2048]{1,0:T(8,128)(2,1)S(1)}, u32[]{:S(2)}, u32[]{:S(2)}) collective-permute-start(bf16[64,2048]{1,0:T(8,128)(2,1)S(1)} %get-tuple-element.56), channel_id=1, source_target_pairs={{0,8},{4,12},{8,0},{12,4},{16,24},{20,28},{24,16},{28,20},{1,9},{5... | collective-permute-start | bytes 786440 | tf_op jit(solution)/shard_map/ppermute | solution.py:19
  51.7 11.6 %collective-permute-start.4 = (bf16[64,2048]{1,0:T(8,128)(2,1)S(1)}, bf16[64,2048]{1,0:T(8,128)(2,1)S(1)}, u32[]{:S(2)}, u32[]{:S(2)}) collective-permute-start(bf16[64,2048]{1,0:T(8,128)(2,1)S(1)} %get-tuple-element.57), channel_id=1, source_target_pairs={{0,16},{4,20},{8,24},{12,28},{16,0},{20,4},{24,8},{28,12},{1,17},{... | collective-permute-start | bytes 786440 | tf_op jit(solution)/shard_map/ppermute | solution.py:19
  53.3 21.3 %collective-permute-start.13 = (bf16[128,2048]{1,0:T(8,128)(2,1)}, bf16[128,2048]{1,0:T(8,128)(2,1)S(1)}, u32[]{:S(2)}, u32[]{:S(2)}) collective-permute-start(bf16[128,2048]{1,0:T(8,128)(2,1)} %collective-permute-done.12.refs_1_), channel_id=1, source_target_pairs={{0,1},{1,2},{2,3},{3,0},{4,5},{5,6},{6,7},{7,4},{8,9},{9,10},{10,1... | collective-permute-start | bytes 1572872 | tf_op jit(solution)/shard_map/ppermute | solution.py:154
  53.3 20.3 %collective-permute-start.5 = (bf16[64,2048]{1,0:T(8,128)(2,1)}, bf16[64,2048]{1,0:T(8,128)(2,1)}, u32[]{:S(2)}, u32[]{:S(2)}) collective-permute-start(bf16[64,2048]{1,0:T(8,128)(2,1)} %get-tuple-element.58), channel_id=1, source_target_pairs={{0,24},{4,28},{8,16},{12,20},{16,8},{20,12},{24,0},{28,4},{1,25},{... | collective-permute-start | bytes 786440 | tf_op jit(solution)/shard_map/ppermute | solution.py:19
  55.1 18.5 %collective-permute-start.9 = (bf16[64,2048]{1,0:T(8,128)(2,1)}, bf16[64,2048]{1,0:T(8,128)(2,1)}, u32[]{:S(2)}, u32[]{:S(2)}) collective-permute-start(bf16[64,2048]{1,0:T(8,128)(2,1)} %get-tuple-element.61), channel_id=1, source_target_pairs={{0,8},{4,12},{8,0},{12,4},{16,24},{20,28},{24,16},{28,20},{1,9},{5... | collective-permute-start | bytes 786440 | tf_op jit(solution)/shard_map/ppermute | solution.py:19
  60.0 14.6 %collective-permute-start.10 = (bf16[64,2048]{1,0:T(8,128)(2,1)}, bf16[64,2048]{1,0:T(8,128)(2,1)}, u32[]{:S(2)}, u32[]{:S(2)}) collective-permute-start(bf16[64,2048]{1,0:T(8,128)(2,1)} %get-tuple-element.62), channel_id=1, source_target_pairs={{0,16},{4,20},{8,24},{12,28},{16,0},{20,4},{24,8},{28,12},{1,17},{... | collective-permute-start | bytes 786440 | tf_op jit(solution)/shard_map/ppermute | solution.py:19
  64.0 10.6 %collective-permute-start.11 = (bf16[64,2048]{1,0:T(8,128)(2,1)}, bf16[64,2048]{1,0:T(8,128)(2,1)}, u32[]{:S(2)}, u32[]{:S(2)}) collective-permute-start(bf16[64,2048]{1,0:T(8,128)(2,1)} %get-tuple-element.63), channel_id=1, source_target_pairs={{0,24},{4,28},{8,16},{12,20},{16,8},{20,12},{24,0},{28,4},{1,25},{... | collective-permute-start | bytes 786440 | tf_op jit(solution)/shard_map/ppermute | solution.py:19
  78.3 15.7 %collective-permute-start.16 = (bf16[128,2048]{1,0:T(8,128)(2,1)S(1)}, bf16[128,2048]{1,0:T(8,128)(2,1)}, u32[]{:S(2)}, u32[]{:S(2)}) collective-permute-start(bf16[128,2048]{1,0:T(8,128)(2,1)S(1)} %collective-permute-done.13.refs_9_.refs_2_), channel_id=1, source_target_pairs={{0,1},{1,2},{2,3},{3,0},{4,5},{5,6},{6,7},{7,4},{8,9},{9,10},{10,1... | collective-permute-start | bytes 1572872 | tf_op jit(solution)/shard_map/ppermute | solution.py:154
  89.6 16.0 %collective-permute-start.21 = (bf16[256,1024]{1,0:T(8,128)(2,1)S(1)}, bf16[256,1024]{1,0:T(8,128)(2,1)S(1)}, u32[]{:S(2)}, u32[]{:S(2)}) collective-permute-start(bf16[256,1024]{1,0:T(8,128)(2,1)S(1)} %get-tuple-element.74), channel_id=1, source_target_pairs={{0,16},{4,20},{8,24},{12,28},{16,0},{20,4},{24,8},{28,12},{1,17},{... | collective-permute-start | bytes 1572872 | tf_op jit(solution)/shard_map/ppermute | solution.py:19
  91.2 14.8 %collective-permute-start.20 = (bf16[256,1024]{1,0:T(8,128)(2,1)S(1)}, bf16[256,1024]{1,0:T(8,128)(2,1)S(1)}, u32[]{:S(2)}, u32[]{:S(2)}) collective-permute-start(bf16[256,1024]{1,0:T(8,128)(2,1)S(1)} %get-tuple-element.67.refs_4_.refs_6_), channel_id=1, source_target_pairs={{0,8},{4,12},{8,0},{12,4},{16,24},{20,28},{24,16},{28,20},{1,9},{5... | collective-permute-start | bytes 1572872 | tf_op jit(solution)/shard_map/ppermute | solution.py:19
  96.2 21.0 %collective-permute-start.17 = (bf16[128,2048]{1,0:T(8,128)(2,1)S(1)}, bf16[128,2048]{1,0:T(8,128)(2,1)S(1)}, u32[]{:S(2)}, u32[]{:S(2)}) collective-permute-start(bf16[128,2048]{1,0:T(8,128)(2,1)S(1)} %get-tuple-element.69), channel_id=1, source_target_pairs={{0,8},{4,12},{8,0},{12,4},{16,24},{20,28},{24,16},{28,20},{1,9},{5... | collective-permute-start | bytes 1572872 | tf_op jit(solution)/shard_map/ppermute | solution.py:19
  98.2 19.0 %collective-permute-start.18 = (bf16[128,2048]{1,0:T(8,128)(2,1)S(1)}, bf16[128,2048]{1,0:T(8,128)(2,1)S(1)}, u32[]{:S(2)}, u32[]{:S(2)}) collective-permute-start(bf16[128,2048]{1,0:T(8,128)(2,1)S(1)} %get-tuple-element.70), channel_id=1, source_target_pairs={{0,16},{4,20},{8,24},{12,28},{16,0},{20,4},{24,8},{28,12},{1,17},{... | collective-permute-start | bytes 1572872 | tf_op jit(solution)/shard_map/ppermute | solution.py:19
  98.3 29.1 %collective-permute-start.19 = (bf16[128,2048]{1,0:T(8,128)(2,1)S(1)}, bf16[128,2048]{1,0:T(8,128)(2,1)S(1)}, u32[]{:S(2)}, u32[]{:S(2)}) collective-permute-start(bf16[128,2048]{1,0:T(8,128)(2,1)S(1)} %get-tuple-element.71), channel_id=1, source_target_pairs={{0,24},{4,28},{8,16},{12,20},{16,8},{20,12},{24,0},{28,4},{1,25},{... | collective-permute-start | bytes 1572872 | tf_op jit(solution)/shard_map/ppermute | solution.py:19
  128.2 9.2 %collective-permute-start.26 = (bf16[128,1024]{1,0:T(8,128)(2,1)S(1)}, bf16[128,1024]{1,0:T(8,128)(2,1)S(1)}, u32[]{:S(2)}, u32[]{:S(2)}) collective-permute-start(bf16[128,1024]{1,0:T(8,128)(2,1)S(1)} %get-tuple-element.82), channel_id=1, source_target_pairs={{0,8},{4,12},{8,0},{12,4},{16,24},{20,28},{24,16},{28,20},{1,9},{5... | collective-permute-start | bytes 786440 | tf_op jit(solution)/shard_map/ppermute | solution.py:19
  130.0 8.4 %collective-permute-start.25 = (bf16[128,1024]{1,0:T(8,128)(2,1)S(1)}, bf16[128,1024]{1,0:T(8,128)(2,1)S(1)}, u32[]{:S(2)}, u32[]{:S(2)}) collective-permute-start(bf16[128,1024]{1,0:T(8,128)(2,1)S(1)} %get-tuple-element.75.refs_4_.refs_6_), channel_id=1, source_target_pairs={{0,16},{4,20},{8,24},{12,28},{16,0},{20,4},{24,8},{28,12},{1,17},{... | collective-permute-start | bytes 786440 | tf_op jit(solution)/shard_map/ppermute | solution.py:19
  138.9 14.8 %collective-permute-start.24 = (bf16[256,1024]{1,0:T(8,128)(2,1)S(1)}, bf16[256,1024]{1,0:T(8,128)(2,1)S(1)}, u32[]{:S(2)}, u32[]{:S(2)}) collective-permute-start(bf16[256,1024]{1,0:T(8,128)(2,1)S(1)} %get-tuple-element.79), channel_id=1, source_target_pairs={{0,16},{4,20},{8,24},{12,28},{16,0},{20,4},{24,8},{28,12},{1,17},{... | collective-permute-start | bytes 1572872 | tf_op jit(solution)/shard_map/ppermute | solution.py:19
  139.3 14.8 %collective-permute-start.23 = (bf16[256,1024]{1,0:T(8,128)(2,1)S(1)}, bf16[256,1024]{1,0:T(8,128)(2,1)S(1)}, u32[]{:S(2)}, u32[]{:S(2)}) collective-permute-start(bf16[256,1024]{1,0:T(8,128)(2,1)S(1)} %get-tuple-element.77.refs_4_), channel_id=1, source_target_pairs={{0,8},{4,12},{8,0},{12,4},{16,24},{20,28},{24,16},{28,20},{1,9},{5... | collective-permute-start | bytes 1572872 | tf_op jit(solution)/shard_map/ppermute | solution.py:19
  143.4 14.2 %collective-permute-start.30 = (bf16[128,640]{1,0:T(8,128)(2,1)S(1)}, bf16[128,640]{1,0:T(8,128)(2,1)S(1)}, u32[]{:S(2)}, u32[]{:S(2)}) collective-permute-start(bf16[128,640]{1,0:T(8,128)(2,1)S(1)} %get-tuple-element.89), channel_id=1, source_target_pairs={{0,8},{4,12},{8,0},{12,4},{16,24},{20,28},{24,16},{28,20},{1,9},{5... | collective-permute-start | bytes 491528 | tf_op jit(solution)/shard_map/ppermute | solution.py:19
  144.3 13.3 %collective-permute-start.31 = (bf16[128,640]{1,0:T(8,128)(2,1)S(1)}, bf16[128,640]{1,0:T(8,128)(2,1)S(1)}, u32[]{:S(2)}, u32[]{:S(2)}) collective-permute-start(bf16[128,640]{1,0:T(8,128)(2,1)S(1)} %get-tuple-element.90), channel_id=1, source_target_pairs={{0,16},{4,20},{8,24},{12,28},{16,0},{20,4},{24,8},{28,12},{1,17},{... | collective-permute-start | bytes 491528 | tf_op jit(solution)/shard_map/ppermute | solution.py:19
  145.9 16.3 %collective-permute-start.32 = (bf16[128,640]{1,0:T(8,128)(2,1)S(1)}, bf16[128,640]{1,0:T(8,128)(2,1)S(1)}, u32[]{:S(2)}, u32[]{:S(2)}) collective-permute-start(bf16[128,640]{1,0:T(8,128)(2,1)S(1)} %get-tuple-element.91), channel_id=1, source_target_pairs={{0,24},{4,28},{8,16},{12,20},{16,8},{20,12},{24,0},{28,4},{1,25},{... | collective-permute-start | bytes 491528 | tf_op jit(solution)/shard_map/ppermute | solution.py:19
  154.9 11.0 %collective-permute-start.28 = (bf16[128,1024]{1,0:T(8,128)(2,1)S(1)}, bf16[128,1024]{1,0:T(8,128)(2,1)S(1)}, u32[]{:S(2)}, u32[]{:S(2)}) collective-permute-start(bf16[128,1024]{1,0:T(8,128)(2,1)S(1)} %get-tuple-element.86), channel_id=1, source_target_pairs={{0,16},{4,20},{8,24},{12,28},{16,0},{20,4},{24,8},{28,12},{1,17},{... | collective-permute-start | bytes 786440 | tf_op jit(solution)/shard_map/ppermute | solution.py:19
  156.6 9.4 %collective-permute-start.29 = (bf16[128,1024]{1,0:T(8,128)(2,1)S(1)}, bf16[128,1024]{1,0:T(8,128)(2,1)S(1)}, u32[]{:S(2)}, u32[]{:S(2)}) collective-permute-start(bf16[128,1024]{1,0:T(8,128)(2,1)S(1)} %get-tuple-element.88), channel_id=1, source_target_pairs={{0,8},{4,12},{8,0},{12,4},{16,24},{20,28},{24,16},{28,20},{1,9},{5... | collective-permute-start | bytes 786440 | tf_op jit(solution)/shard_map/ppermute | solution.py:19
  167.8 9.3 %collective-permute-start.43 = (bf16[128,640]{1,0:T(8,128)(2,1)S(1)}, bf16[128,640]{1,0:T(8,128)(2,1)S(1)}, u32[]{:S(2)}, u32[]{:S(2)}) collective-permute-start(bf16[128,640]{1,0:T(8,128)(2,1)S(1)} %add_convert_fusion.1), channel_id=1, source_target_pairs={{0,2},{1,3},{2,0},{3,1},{4,6},{5,7},{6,4},{7,5},{8,10},{9,11},{10,... | collective-permute-start | bytes 491528 | tf_op jit(solution)/shard_map/ppermute | solution.py:19
  169.8 10.2 %collective-permute-start.34 = (bf16[128,640]{1,0:T(8,128)(2,1)S(1)}, bf16[128,640]{1,0:T(8,128)(2,1)S(1)}, u32[]{:S(2)}, u32[]{:S(2)}) collective-permute-start(bf16[128,640]{1,0:T(8,128)(2,1)S(1)} %get-tuple-element.94), channel_id=1, source_target_pairs={{0,8},{4,12},{8,0},{12,4},{16,24},{20,28},{24,16},{28,20},{1,9},{5... | collective-permute-start | bytes 491528 | tf_op jit(solution)/shard_map/ppermute | solution.py:19
  171.0 9.7 %collective-permute-start.35 = (bf16[128,640]{1,0:T(8,128)(2,1)S(1)}, bf16[128,640]{1,0:T(8,128)(2,1)S(1)}, u32[]{:S(2)}, u32[]{:S(2)}) collective-permute-start(bf16[128,640]{1,0:T(8,128)(2,1)S(1)} %get-tuple-element.95), channel_id=1, source_target_pairs={{0,16},{4,20},{8,24},{12,28},{16,0},{20,4},{24,8},{28,12},{1,17},{... | collective-permute-start | bytes 491528 | tf_op jit(solution)/shard_map/ppermute | solution.py:19
  172.2 8.5 %collective-permute-start.36 = (bf16[128,640]{1,0:T(8,128)(2,1)S(1)}, bf16[128,640]{1,0:T(8,128)(2,1)S(1)}, u32[]{:S(2)}, u32[]{:S(2)}) collective-permute-start(bf16[128,640]{1,0:T(8,128)(2,1)S(1)} %get-tuple-element.96), channel_id=1, source_target_pairs={{0,24},{4,28},{8,16},{12,20},{16,8},{20,12},{24,0},{28,4},{1,25},{... | collective-permute-start | bytes 491528 | tf_op jit(solution)/shard_map/ppermute | solution.py:19
  177.1 8.1 %collective-permute-start.46 = (bf16[128,640]{1,0:T(8,128)(2,1)S(1)}, bf16[128,640]{1,0:T(8,128)(2,1)S(1)}, u32[]{:S(2)}, u32[]{:S(2)}) collective-permute-start(bf16[128,640]{1,0:T(8,128)(2,1)S(1)} %add_convert_fusion.refs_0_), channel_id=1, source_target_pairs={{0,24},{4,28},{8,16},{12,20},{16,8},{20,12},{24,0},{28,4},{1,25},{... | collective-permute-start | bytes 491528 | tf_op jit(solution)/shard_map/ppermute | solution.py:19
  178.9 8.8 %collective-permute-start.45 = (bf16[128,640]{1,0:T(8,128)(2,1)S(1)}, bf16[128,640]{1,0:T(8,128)(2,1)S(1)}, u32[]{:S(2)}, u32[]{:S(2)}) collective-permute-start(bf16[128,640]{1,0:T(8,128)(2,1)S(1)} %add_convert_fusion.refs_0_), channel_id=1, source_target_pairs={{0,16},{4,20},{8,24},{12,28},{16,0},{20,4},{24,8},{28,12},{1,17},{... | collective-permute-start | bytes 491528 | tf_op jit(solution)/shard_map/ppermute | solution.py:19
  180.0 7.9 %collective-permute-start.44 = (bf16[128,640]{1,0:T(8,128)(2,1)S(1)}, bf16[128,640]{1,0:T(8,128)(2,1)S(1)}, u32[]{:S(2)}, u32[]{:S(2)}) collective-permute-start(bf16[128,640]{1,0:T(8,128)(2,1)S(1)} %add_convert_fusion.refs_0_), channel_id=1, source_target_pairs={{0,8},{4,12},{8,0},{12,4},{16,24},{20,28},{24,16},{28,20},{1,9},{5... | collective-permute-start | bytes 491528 | tf_op jit(solution)/shard_map/ppermute | solution.py:19
  187.9 14.8 %collective-permute-start.47 = (bf16[4,128,640]{2,1,0:T(8,128)(2,1)S(1)}, bf16[4,128,640]{2,1,0:T(8,128)(2,1)S(1)}, u32[]{:S(2)}, u32[]{:S(2)}) collective-permute-start(bf16[4,128,640]{2,1,0:T(8,128)(2,1)S(1)} %pile.2.refs_0_), channel_id=1, source_target_pairs={{0,4},{4,0},{8,12},{12,8},{16,20},{20,16},{24,28},{28,24},{1,5},{5... | collective-permute-start | bytes 1966088 | tf_op jit(solution)/shard_map/ppermute | solution.py:19
  188.1 11.1 %collective-permute-start.38 = (bf16[128,640]{1,0:T(8,128)(2,1)S(1)}, bf16[128,640]{1,0:T(8,128)(2,1)S(1)}, u32[]{:S(2)}, u32[]{:S(2)}) collective-permute-start(bf16[128,640]{1,0:T(8,128)(2,1)S(1)} %add_convert_fusion.3), channel_id=1, source_target_pairs={{0,2},{1,3},{2,0},{3,1},{4,6},{5,7},{6,4},{7,5},{8,10},{9,11},{10,... | collective-permute-start | bytes 491528 | tf_op jit(solution)/shard_map/ppermute | solution.py:19
  199.2 8.1 %collective-permute-start.41 = (bf16[128,640]{1,0:T(8,128)(2,1)S(1)}, bf16[128,640]{1,0:T(8,128)(2,1)S(1)}, u32[]{:S(2)}, u32[]{:S(2)}) collective-permute-start(bf16[128,640]{1,0:T(8,128)(2,1)S(1)} %add_convert_fusion.2.refs_6_.refs_0_), channel_id=1, source_target_pairs={{0,24},{4,28},{8,16},{12,20},{16,8},{20,12},{24,0},{28,4},{1,25},{... | collective-permute-start | bytes 491528 | tf_op jit(solution)/shard_map/ppermute | solution.py:19
  200.8 8.9 %collective-permute-start.40 = (bf16[128,640]{1,0:T(8,128)(2,1)S(1)}, bf16[128,640]{1,0:T(8,128)(2,1)S(1)}, u32[]{:S(2)}, u32[]{:S(2)}) collective-permute-start(bf16[128,640]{1,0:T(8,128)(2,1)S(1)} %add_convert_fusion.2.refs_6_.refs_0_), channel_id=1, source_target_pairs={{0,16},{4,20},{8,24},{12,28},{16,0},{20,4},{24,8},{28,12},{1,17},{... | collective-permute-start | bytes 491528 | tf_op jit(solution)/shard_map/ppermute | solution.py:19
  209.9 8.8 %collective-permute-start.55 = (bf16[128,1024]{1,0:T(8,128)(2,1)S(1)}, bf16[128,1024]{1,0:T(8,128)(2,1)S(1)}, u32[]{:S(2)}, u32[]{:S(2)}) collective-permute-start(bf16[128,1024]{1,0:T(8,128)(2,1)S(1)} %get-tuple-element.108.refs_0_), channel_id=1, source_target_pairs={{0,8},{4,12},{8,0},{12,4},{16,24},{20,28},{24,16},{28,20},{1,9},{5... | collective-permute-start | bytes 786440 | tf_op jit(solution)/shard_map/ppermute | solution.py:19
  211.1 8.9 %collective-permute-start.51 = (bf16[128,1024]{1,0:T(8,128)(2,1)S(1)}, bf16[128,1024]{1,0:T(8,128)(2,1)S(1)}, u32[]{:S(2)}, u32[]{:S(2)}) collective-permute-start(bf16[128,1024]{1,0:T(8,128)(2,1)S(1)} %get-tuple-element.109.refs_0_), channel_id=1, source_target_pairs={{0,16},{4,20},{8,24},{12,28},{16,0},{20,4},{24,8},{28,12},{1,17},{... | collective-permute-start | bytes 786440 | tf_op jit(solution)/shard_map/ppermute | solution.py:19
  218.7 20.7 %collective-permute-start.56 = (bf16[256,1024]{1,0:T(8,128)(2,1)S(1)}, bf16[256,1024]{1,0:T(8,128)(2,1)S(1)}, u32[]{:S(2)}, u32[]{:S(2)}) collective-permute-start(bf16[256,1024]{1,0:T(8,128)(2,1)S(1)} %join_after.8.refs_0_), channel_id=1, source_target_pairs={{0,16},{4,20},{8,24},{12,28},{16,0},{20,4},{24,8},{28,12},{1,17},{... | collective-permute-start | bytes 1572872 | tf_op jit(solution)/shard_map/ppermute | solution.py:19
  220.0 19.2 %collective-permute-start.52 = (bf16[256,1024]{1,0:T(8,128)(2,1)S(1)}, bf16[256,1024]{1,0:T(8,128)(2,1)S(1)}, u32[]{:S(2)}, u32[]{:S(2)}) collective-permute-start(bf16[256,1024]{1,0:T(8,128)(2,1)S(1)} %join_after.6.refs_0_), channel_id=1, source_target_pairs={{0,8},{4,12},{8,0},{12,4},{16,24},{20,28},{24,16},{28,20},{1,9},{5... | collective-permute-start | bytes 1572872 | tf_op jit(solution)/shard_map/ppermute | solution.py:19
  220.8 18.1 %collective-permute-start.53 = (bf16[128,1024]{1,0:T(8,128)(2,1)S(1)}, bf16[128,1024]{1,0:T(8,128)(2,1)S(1)}, u32[]{:S(2)}, u32[]{:S(2)}) collective-permute-start(bf16[128,1024]{1,0:T(8,128)(2,1)S(1)} %get-tuple-element.110), channel_id=1, source_target_pairs={{0,8},{4,12},{8,0},{12,4},{16,24},{20,28},{24,16},{28,20},{1,9},{5... | collective-permute-start | bytes 786440 | tf_op jit(solution)/shard_map/ppermute | solution.py:19
  222.2 16.9 %collective-permute-start.49 = (bf16[128,1024]{1,0:T(8,128)(2,1)S(1)}, bf16[128,1024]{1,0:T(8,128)(2,1)S(1)}, u32[]{:S(2)}, u32[]{:S(2)}) collective-permute-start(bf16[128,1024]{1,0:T(8,128)(2,1)S(1)} %get-tuple-element.111), channel_id=1, source_target_pairs={{0,16},{4,20},{8,24},{12,28},{16,0},{20,4},{24,8},{28,12},{1,17},{... | collective-permute-start | bytes 786440 | tf_op jit(solution)/shard_map/ppermute | solution.py:19
  240.0 13.9 %collective-permute-start.50 = (bf16[256,1024]{1,0:T(8,128)(2,1)S(1)}, bf16[256,1024]{1,0:T(8,128)(2,1)S(1)}, u32[]{:S(2)}, u32[]{:S(2)}) collective-permute-start(bf16[256,1024]{1,0:T(8,128)(2,1)S(1)} %maximum_select_fusion.refs_2_.refs_0_), channel_id=1, source_target_pairs={{0,8},{4,12},{8,0},{12,4},{16,24},{20,28},{24,16},{28,20},{1,9},{5... | collective-permute-start | bytes 1572872 | tf_op jit(solution)/shard_map/ppermute | solution.py:19
  240.7 13.6 %collective-permute-start.59 = (bf16[256,1024]{1,0:T(8,128)(2,1)S(1)}, bf16[256,1024]{1,0:T(8,128)(2,1)S(1)}, u32[]{:S(2)}, u32[]{:S(2)}) collective-permute-start(bf16[256,1024]{1,0:T(8,128)(2,1)S(1)} %maximum_select_fusion.1.refs_3_.refs_0_), channel_id=1, source_target_pairs={{0,16},{4,20},{8,24},{12,28},{16,0},{20,4},{24,8},{28,12},{1,17},{... | collective-permute-start | bytes 1572872 | tf_op jit(solution)/shard_map/ppermute | solution.py:19
  (35 other events, 187.0 us)

commit v8 on v6

--- a/solution.py
+++ b/solution.py
@@ -52,7 +52,7 @@
 
 
 def run(body, scalars, operands, in_specs, outs, out_specs, grid=(1,), scratch=(), after=(),
-        flops=0, moved=0, limit=32, name=None):
+        flops=0, moved=0, limit=32, name=None, aliases=None):
     n_in, n_after = len(operands), len(after)
 
     def kernel(scalars_ref, *refs):
@@ -71,6 +71,7 @@
         compiler_params=pltpu.CompilerParams(vmem_limit_bytes=limit * MIB),
         cost_estimate=pl.CostEstimate(flops=flops, bytes_accessed=moved, transcendentals=0),
         name=name,
+        input_output_aliases=aliases or {},
     )(scalars, *operands, *after)
 
 
@@ -101,11 +102,12 @@
 
         @pl.when(first)
         def _():
-            square_ref[...] = square
+            square_ref[:8, :] = jnp.zeros_like(square)
+            square_ref[8:, :] = square
 
         @pl.when(jnp.logical_not(first))
         def _():
-            square_ref[...] += square
+            square_ref[8:, :] += square
 
     out = like((2 * quarter, depth), BF16)
     return run(
@@ -116,13 +118,13 @@
                 lambda k, j, c: (0, (2 * (j // steps) + (c[0] ^ (1 - k))) * steps + j % steps),
             )
         ],
-        [out, out, like((8, 128), F32)],
+        [out, out, like((16, 128), F32)],
         [
             pl.BlockSpec((step, depth), lambda k, j, c: (jnp.where(k == 0, j, 2 * steps - 1), 0)),
             pl.BlockSpec((step, depth), lambda k, j, c: (jnp.where(k == 1, j, 0), 0)),
-            pl.BlockSpec((8, 128), lambda k, j, c: (0, 0)),
+            pl.BlockSpec((16, 128), lambda k, j, c: (0, 0)),
         ],
-        grid=(2, 2 * steps), after=after, flops=2 * depth * width, moved=6 * depth * width, limit=54, name="turn_weight",
+        grid=(2, 2 * steps), after=after, flops=2 * depth * width, moved=6 * depth * width, limit=16, name="turn_weight",
     )
 
 
@@ -263,7 +265,7 @@
         body, bits, [turned_own, turned_other, turned_own, turned_other, columns],
         [of_path(0), of_path(0), of_path(1), of_path(1), whole(columns)],
         [like((out_rows, batch), BF16)] * 2, [out_spec] * 2, grid=(steps,), after=after,
-        flops=8 * out_rows * depth * batch, moved=8 * out_rows * depth + 4 * batch * depth, name="forward",
+        flops=8 * out_rows * depth * batch, moved=8 * out_rows * depth + 4 * batch * depth, limit=22, name="forward",
     )
 
 
@@ -337,21 +339,25 @@
     )
 
 
-def join_after(mine, other, bit, after):
-    rows, width = mine.shape
-
-    def body(bit_ref, mine_ref, other_ref, out_ref):
-        first = pl.multiple_of(bit_ref[0] * rows, rows)
-        second = pl.multiple_of((1 - bit_ref[0]) * rows, rows)
-        out_ref[pl.ds(first, rows), :] = mine_ref[...]
-        out_ref[pl.ds(second, rows), :] = other_ref[...]
-
-    out = like((2 * rows, width), BF16)
-    (joined,) = run(
-        body, bit.reshape(1), [mine, other], [whole(mine), whole(other)], [out], [whole(out)],
-        after=after, moved=8 * rows * width, limit=8, name="join_after",
-    )
-    return joined
+def join_all(mine, other, bits, after=()):
+    count = len(mine)
+
+    def body(bits_ref, *refs):
+        for index in range(count):
+            rows = mine[index].shape[0]
+            bit = bits_ref[index]
+            first = pl.multiple_of(bit * rows, rows)
+            second = pl.multiple_of((1 - bit) * rows, rows)
+            out_ref = refs[2 * count + index]
+            out_ref[pl.ds(first, rows), :] = refs[index][...]
+            out_ref[pl.ds(second, rows), :] = refs[count + index][...]
+
+    outs = [like((2 * one.shape[0], one.shape[1]), BF16) for one in mine]
+    return run(
+        body, jnp.stack(bits), [*mine, *other], [whole(one) for one in [*mine, *other]],
+        outs, [whole(out) for out in outs], after=after,
+        moved=8 * sum(one.size for one in mine), limit=12, name="join_all",
+    )
 
 
 def add_up(parts, after=()):
@@ -427,42 +433,43 @@
     return out_grad
 
 
-def weight_grad_of(place, turned, pieces, base=None, weight_squares=None, after=()):
-    depth, batch = turned.shape
+def weight_grad_of(place, turned, pieces, flip, squares, done=None):
+    depth, batch = turned[0].shape
     cols = pieces[0].shape[0]
-    last = base is not None
-
-    def body(place_ref, turned_ref, *refs):
-        if last:
-            base_ref, weight_squares_ref, out_ref, square_ref = refs[4:]
-        else:
-            (out_ref,) = refs[4:]
-        for index in range(4):
-
-            @pl.when(pl.program_id(0) == index)
+    n_path = len(pieces) // 2
+
+    def body(place_ref, first_ref, second_ref, *refs):
+        square_in_ref = refs[len(pieces)]
+        out_ref, square_ref = refs[-2:]
+        for path in range(n_path):
+
+            @pl.when(pl.program_id(0) == path)
             def _():
                 total = lax.dot_general(
-                    turned_ref[...], refs[index][...], ROWS_BY_ROWS, preferred_element_type=F32
+                    first_ref[...], refs[path][...], ROWS_BY_ROWS, preferred_element_type=F32
                 )
-                if last:
-                    total += base_ref[...]
-                    square = fold(total * total)
-                    if index == 0:
-                        square_ref[:8, :] = square
-                        square_ref[8:, :] = weight_squares_ref[...]
-                    else:
-                        square_ref[:8, :] += square
+                total += lax.dot_general(
+                    second_ref[...], refs[n_path + path][...], ROWS_BY_ROWS,
+                    preferred_element_type=F32,
+                )
+                if path == 0:
+                    square_ref[...] = square_in_ref[...]
+                square_ref[:8, :] += fold(total * total)
                 out_ref[...] = total
 
-    tile = pl.BlockSpec((depth, cols), lambda j, s: (0, (j >> 1) * 2 + ((j & 1) ^ s[1])))
-    square = pl.BlockSpec((16, 128), lambda j, s: (0, 0))
-    operands = [turned, *pieces]
-    return run(
-        body, place, operands + ([base, weight_squares] if last else []),
-        [whole(one) for one in operands] + ([tile, whole(weight_squares)] if last else []),
-        [like((depth, 4 * cols), F32)] + ([like((16, 128), F32)] if last else []),
-        [tile] + ([square] if last else []), grid=(4,), after=after,
-        flops=8 * cols * batch * depth, moved=16 * depth * cols * (2 if last else 1), limit=20, name="weight_grad_of",
+    operands = [*turned, *pieces, squares] + ([] if done is None else [done])
+    specs = [whole(one) for one in [*turned, *pieces, squares]]
+    if done is not None:
+        specs.append(pl.BlockSpec(memory_space=pl.ANY))
+    return run(
+        body, place, operands, specs,
+        [like((depth, 2 * n_path * cols), F32), like(squares.shape, F32)],
+        [
+            pl.BlockSpec((depth, cols), lambda j, s: (0, 2 * j + (s[1] ^ flip))),
+            pl.BlockSpec(squares.shape, lambda j, s: (0, 0)),
+        ],
+        grid=(n_path,), flops=4 * n_path * cols * batch * depth, moved=4 * n_path * depth * cols,
+        limit=22, aliases={len(operands): 0} if done is not None else {}, name="weight_grad_of",
     )
 
 
@@ -511,17 +518,15 @@
             own[mask] = swap(own[mask], "dp", 2 * mask)
         return own
 
-    def both_cores(own, collect_after=(), after=()):
-        images = collect(place, own, after=collect_after)
-        other = swap(images, "dp", 1)
-        return assemble(place, images, other, view_features.shape[1], after=after)
+    def both_cores(images):
+        return assemble(place, images, swap(images, "dp", 1), view_features.shape[1])
 
     def send_on(v, level, send):
         return [swap(send[p], "dp", 1 << orders[p][level]) for p in range(2)]
 
     def sum_plane(rows, after=()):
-        parts = [rows[0]] + [swap(rows[mask], "dp", 2 * mask) for mask in range(1, n_chip)]
-        return add_up(parts, after=after)
+        others = [swap(rows[mask], "dp", 2 * mask) for mask in range(1, n_chip)]
+        return add_up([rows[0], *others], after=after)
 
     def sum_line(total, bit, after=()):
         return add_up([total, swap(total, "feat", 1 << bit)], after=after)
@@ -531,16 +536,10 @@
         own = pile(parts, after=after)
         return own, swap(own, "dp", 1)
 
-    def gather_step(parts, step, after=None):
-        out = []
-        for part, order in zip(parts, orders):
-            bit = order[len(order) - 1 - step]
-            other = swap(part, "dp", 1 << bit)
-            if after is None:
-                out.append(join(part, other, bit_value("dp", bit)))
-            else:
-                out.append(join_after(part, other, bit_value("dp", bit), after))
-        return out
+    def gather_step(parts, step, after=()):
+        bits = [order[len(order) - 1 - step] for order in orders] * (len(parts) // 2)
+        other = [swap(part, "dp", 1 << bit) for part, bit in zip(parts, bits)]
+        return join_all(parts, other, [bit_value("dp", bit) for bit in bits], after=after)
 
     def with_swapped(parts):
         return [one for own in parts for one in (own, swap(own, "dp", 1))]
@@ -553,55 +552,45 @@
     pieces = [cross_plane(part) for part in shares[1]]
     sent, turned_own, weight_squares = turn_weight(weight, core, after=[pieces[1][0]])
     turned_other = swap(sent, "dp", 1)
-    columns[1] = both_cores(pieces, collect_after=[turned_own, shares[0][0][-2]])
+    images = collect(place, pieces, after=[turned_own, shares[0][0][-2]])
+    columns[1] = both_cores(images)
     turned[1] = turn_columns(columns[1])
-    send[1] = forward(1 - bits, turned_own, turned_other, columns[1])
+    images = collect(place, [cross_plane(part, [images]) for part in shares[0]])
+    send[1] = forward(1 - bits, turned_own, turned_other, columns[1], after=[images])
     got[1] = send_on(1, 0, send[1])
-    pieces = [cross_plane(part, [send[1][0]]) for part in shares[0]]
     keep[1] = forward(bits, turned_own, turned_other, columns[1], after=[turned[1], send[1][0]])
+    columns[0] = both_cores(images)
+    turned[0] = turn_columns(columns[0])
+    send[0] = forward(1 - bits, turned_own, turned_other, columns[0], after=[keep[1][0]])
+    got[0] = send_on(0, 0, send[0])
+    keep[0] = forward(bits, turned_own, turned_other, columns[0], after=[turned[0], send[0][0]])
+    ahead = [keep[0][0]]
     for level in range(1, len(high)):
-        send[1], keep[1] = add_halves(bits_at(level), keep[1], got[1])
-        got[1] = send_on(1, level, send[1])
-    columns[0] = both_cores(pieces, [send[1][0]])
-    turned[0] = turn_columns(columns[0])
-    send[0] = forward(1 - bits, turned_own, turned_other, columns[0])
-    ahead = [send[0][0]]
-    got[0] = send_on(0, 0, send[0])
+        for v in (1, 0):
+            send[v], keep[v] = add_halves(bits_at(level), keep[v], got[v], after=ahead)
+            got[v] = send_on(v, level, send[v])
+            ahead = [send[v][0]]
     normed[1], half[1], inverse[1] = normalise(keep[1], got[1], after=ahead)
     rows[1] = list(gram_rows(place, half[1], swap(half[1], "dp", 1), n_chip))
-    keep[0] = forward(bits, turned_own, turned_other, columns[0], after=[turned[0], send[1][0]])
-    for level in range(1, len(high)):
-        send[0], keep[0] = add_halves(bits_at(level), keep[0], got[0], after=[rows[1][0]])
-        got[0] = send_on(0, level, send[0])
-    gram[1] = sum_plane(rows[1], after=[send[0][0]])
-    normed[0], half[0], inverse[0] = normalise(keep[0], got[0], after=[gram[1]])
+    normed[0], half[0], inverse[0] = normalise(keep[0], got[0], after=[rows[1][0]])
     rows[0] = list(gram_rows(place, half[0], swap(half[0], "dp", 1), n_chip))
-    last = line_bits[-1]
-    for bit in line_bits[:-1]:
-        gram[1] = sum_line(gram[1], bit, after=[rows[0][0]])
-    gram[0] = sum_plane(rows[0])
-    gram[1] = sum_line(gram[1], last, after=[gram[0]])
-    for bit in line_bits[:-1]:
-        gram[0] = sum_line(gram[0], bit)
-    gram[1] = spread_gram(gram[1], after=[gram[0]])
-    gram[0] = sum_line(gram[0], last)
+    gram[1] = sum_plane(rows[1], after=[rows[0][0]])
+    gram[0] = sum_plane(rows[0], after=[gram[1]])
+    for bit in line_bits:
+        gram[1] = sum_line(gram[1], bit, after=[gram[0]])
+        gram[0] = sum_line(gram[0], bit, after=[gram[1]])
+    gram[0] = spread_gram(gram[0])
+    gram[1] = spread_gram(gram[1], after=[gram[0][0]])
     out_grad = [None] * 2
-    out_grad[0] = out_grad_of(
-        place, *gram[1], normed[0], half[0], half[1], inverse[0], after=[gram[0]]
-    )
-    gram[0] = spread_gram(gram[0])
+    out_grad[0] = out_grad_of(place, *gram[1], normed[0], half[0], half[1], inverse[0])
     share = out_grad[0].shape[0] // 2
-    parts = gather_step([out_grad[0][:share], out_grad[0][share:]], 0, after=[gram[0][0]])
     out_grad[1] = out_grad_of(place, *gram[0], normed[1], half[1], half[0], inverse[1])
-    last_parts = gather_step([out_grad[1][:share], out_grad[1][share:]], 0)
-    for step in range(1, len(high)):
-        parts = gather_step(parts, step, after=last_parts)
-    (base,) = weight_grad_of(place, turned[0], with_swapped(parts))
-    for step in range(1, len(high)):
-        last_parts = gather_step(last_parts, step, after=[base] if step == len(high) - 1 else None)
-    weight_grad, squares = weight_grad_of(
-        place, turned[1], with_swapped(last_parts), base, weight_squares
-    )
+    parts = [one for grad in out_grad for one in (grad[:share], grad[share:])]
+    for step in range(len(high)):
+        parts = gather_step(parts, step)
+    swapped = [swap(part, "dp", 1) for part in parts]
+    weight_grad, squares = weight_grad_of(place, turned, parts, 0, weight_squares)
+    weight_grad, squares = weight_grad_of(place, turned, swapped, 1, squares, weight_grad)
     return update(sum_everywhere(squares), weight, velocity, weight_grad)
 
 

time: 302 us -> 304 us (level)
  waiting for transfers between devices: 166 us -> 155 us
  starting transfers between devices: 60.8 us -> 68.8 us
  Pallas kernels: 66.5 us -> 70.9 us
    ppermute x52, waiting for transfers between devices: 120 us -> 99.8 us  [swap(): lax.ppermute(value, axis, [(i, i ^ mask) for i in range(lax.axis_size(axi...]
    ppermute x9, waiting for transfers between devices: 40.4 us -> 49.2 us  [go_round(): shares.append(lax.ppermute(shares[-1], 'feat', ring))]
    ppermute x52, starting transfers between devices: 46.4 us -> 53.3 us  [swap(): lax.ppermute(value, axis, [(i, i ^ mask) for i in range(lax.axis_size(axi...]
    pallas_call x40 -> x36, Pallas kernels: 66.5 us -> 70.9 us  [run(): pl.pallas_call(kernel, grid_spec=pltpu.PrefetchScalarGridSpec(num_scalar_...]
    unnamed x30 -> x28, local copies, waits for them, and re-layouts: 6.94 us -> 6.74 us
  transfers between devices with their start and end apart: 68 -> 68, of which waited for: 45 -> 40; matrix products, arithmetic and copies ran while one was open for 0% -> 0% of each run, Pallas kernels for 16% -> 18%
where the time goes in v8:
time: 304 us; the launch traced here: 303 us
  waiting for transfers between devices  155 us (51%)
  Pallas kernels  70.9 us (23%)
  starting transfers between devices  68.8 us (23%)
  local copies, waits for them, and re-layouts  6.81 us (2%)
    ppermute x52, waiting for transfers between devices, swap(): lax.ppermute(value, axis, [(i, i ^ mask) for i in range(lax.axis_size(axi...  99.8 us
    pallas_call x36, Pallas kernels, run(): pl.pallas_call(kernel, grid_spec=pltpu.PrefetchScalarGridSpec(num_scalar_...  70.9 us
    ppermute x52, starting transfers between devices, swap(): lax.ppermute(value, axis, [(i, i ^ mask) for i in range(lax.axis_size(axi...  53.3 us
    ppermute x9, waiting for transfers between devices, go_round(): shares.append(lax.ppermute(shares[-1], 'feat', ring))  49.2 us
    ppermute x9, starting transfers between devices, go_round(): shares.append(lax.ppermute(shares[-1], 'feat', ring))  7.94 us
    ppermute x7, starting transfers between devices, sum_everywhere(): lax.ppermute(value, axes, [(i, i ^ mask) for i in range(count)])  7.59 us
    unnamed x28, local copies, waits for them, and re-layouts  6.74 us
    ppermute x7, waiting for transfers between devices, sum_everywhere(): lax.ppermute(value, axes, [(i, i ^ mask) for i in range(count)])  6.23 us
  transfers between devices with their start and end apart: 68, of which 40 were waited for; matrix products, arithmetic and copies ran while one was open for 0% of the time, Pallas kernels for 18%

profile of v8, /device:TPU:0, one launch (start us, length us, event | category | flops | bytes accessed | tf_op | source)
XLA Modules:
  0.0 303.2 jit_solution(8381885781479646542)
XLA Ops:
  1.9 3.1 %collective-permute-start = (bf16[128,2048]{1,0:T(8,128)(2,1)S(1)}, bf16[128,2048]{1,0:T(8,128)(2,1)S(1)}, u32[]{:S(2)}, u32[]{:S(2)}) collective-permute-start(bf16[128,2048]{1,0:T(8,128)(2,1)S(1)} %get-tuple-element.62.refs_0_), channel_id=1, source_target_pairs={{0,1},{1,2},{2,3},{3,0},{4,5},{5,6},{6,7},{7,4},{8,9},{9,10},{10,1... | collective-permute-start | bytes 1572872 | tf_op jit(solution)/shard_map/ppermute | solution.py:154
  8.2 17.2 %collective-permute-done.3.refs_1_ = bf16[64,2048]{1,0:T(8,128)(2,1)S(1)} collective-permute-done((bf16[64,2048]{1,0:T(8,128)(2,1)S(1)}, bf16[64,2048]{1,0:T(8,128)(2,1)S(1)}, u32[]{:S(2)}, u32[]{:S(2)}) %collective-permute-start.3) | collective-permute-done | bytes 262176 | tf_op jit(solution)/shard_map/ppermute | solution.py:154
  27.0 4.0 %collective-permute-done.9.refs_1_ = bf16[64,2048]{1,0:T(8,128)(2,1)S(1)} collective-permute-done((bf16[64,2048]{1,0:T(8,128)(2,1)S(1)}, bf16[64,2048]{1,0:T(8,128)(2,1)S(1)}, u32[]{:S(2)}, u32[]{:S(2)}) %collective-permute-start.9) | collective-permute-done | bytes 262176 | tf_op jit(solution)/shard_map/ppermute | solution.py:154
  31.0 5.6 %collective-permute-done.4.refs_2_ = bf16[64,2048]{1,0:T(8,128)(2,1)S(1)} collective-permute-done((bf16[64,2048]{1,0:T(8,128)(2,1)S(1)}, bf16[64,2048]{1,0:T(8,128)(2,1)S(1)}, u32[]{:S(2)}, u32[]{:S(2)}) %collective-permute-start.4) | collective-permute-done | bytes 262176 | tf_op jit(solution)/shard_map/ppermute | solution.py:154
  36.7 16.7 %collective-permute-done.10.refs_2_ = bf16[64,2048]{1,0:T(8,128)(2,1)S(1)} collective-permute-done((bf16[64,2048]{1,0:T(8,128)(2,1)S(1)}, bf16[64,2048]{1,0:T(8,128)(2,1)S(1)}, u32[]{:S(2)}, u32[]{:S(2)}) %collective-permute-start.10) | collective-permute-done | bytes 262176 | tf_op jit(solution)/shard_map/ppermute | solution.py:154
  53.5 5.6 %collective-permute-done.5.refs_3_ = bf16[64,2048]{1,0:T(8,128)(2,1)S(1)} collective-permute-done((bf16[64,2048]{1,0:T(8,128)(2,1)S(1)}, bf16[64,2048]{1,0:T(8,128)(2,1)S(1)}, u32[]{:S(2)}, u32[]{:S(2)}) %collective-permute-start.5) | collective-permute-done | bytes 262176 | tf_op jit(solution)/shard_map/ppermute | solution.py:154
  68.1 2.4 collective-permute-done.6.refs_1_
  71.2 1.8 collective-permute-start.13
  76.9 3.4 %copy-done = f32[1024,2048]{1,0:T(8,128)S(1)} copy-done((f32[1024,2048]{1,0:T(8,128)S(1)}, f32[1024,2048]{1,0:T(8,128)}, u32[]{:S(2)}) %copy-start) | copy-done | bytes 8388632
  80.3 4.6 %turn_weight.1 = (bf16[1024,1024]{1,0:T(8,128)(2,1)}, bf16[1024,1024]{1,0:T(8,128)(2,1)S(1)}, f32[16,128]{1,0:T(8,128)S(1)}) custom-call(s32[1]{0:T(128)} %bitcast.1.scalars_ref, f32[1024,2048]{1,0:T(8,128)S(1)} %copy-done, bf16[64,2048]{1,0:T(8,128)(2,1)S(1)} %get-tuple-element.69.refs_1_.refs_4_), custom_call_target="tpu_custom_call" | custom-call | flops 4194304 | bytes 12582912 | tf_op jit(solution)/shard_map/turn_weight/pallas_call | solution.py:61
  85.9 3.2 %collect.2.refs_4_.refs_0_ = bf16[512,2048]{1,0:T(8,128)(2,1)} custom-call(s32[2]{0:T(128)S(1)} %pad_add_fusion.scalars_ref, bf16[64,2048]{1,0:T(8,128)(2,1)S(1)} %copy-done.5, bf16[64,2048]{1,0:T(8,128)(2,1)S(1)} %copy-done.7, bf16[64,2048]{1,0:T(8,128)(2,1)S(1)} %copy-done.9, bf16[64,2048]{1,0:T(8,128)(2,1)} %collective-permute-done.8.refs_3_, ...), custom_call_target="tpu_custom_call" | custom-call | bytes 4194304 | tf_op jit(solution)/shard_map/collect/pallas_call | solution.py:61
  89.1 1.8 choose.5
  90.9 2.0 collective-permute-start.15
  95.0 10.8 %collective-permute-done.15.refs_1_ = bf16[128,2048]{1,0:T(8,128)(2,1)S(1)} collective-permute-done((bf16[128,2048]{1,0:T(8,128)(2,1)S(1)}, bf16[128,2048]{1,0:T(8,128)(2,1)S(1)}, u32[]{:S(2)}, u32[]{:S(2)}) %collective-permute-start.15) | collective-permute-done | bytes 524320 | tf_op jit(solution)/shard_map/ppermute | solution.py:19
  105.8 7.9 %collective-permute-done.16.refs_2_ = bf16[128,2048]{1,0:T(8,128)(2,1)S(1)} collective-permute-done((bf16[128,2048]{1,0:T(8,128)(2,1)S(1)}, bf16[128,2048]{1,0:T(8,128)(2,1)S(1)}, u32[]{:S(2)}, u32[]{:S(2)}) %collective-permute-start.16) | collective-permute-done | bytes 524320 | tf_op jit(solution)/shard_map/ppermute | solution.py:19
  113.7 2.0 collect.3.refs_0_.refs_5_
  115.8 3.0 %assemble.3.refs_0_.refs_4_ = bf16[1024,2048]{1,0:T(8,128)(2,1)S(1)} custom-call(s32[2]{0:T(128)S(1)} %pad_add_fusion.scalars_ref, bf16[512,2048]{1,0:T(8,128)(2,1)} %collect.2.refs_4_.refs_0_, bf16[512,2048]{1,0:T(8,128)(2,1)} %collective-permute-done.19.refs_1_), custom_call_target="tpu_custom_call" | custom-call | bytes 8388608 | tf_op jit(solution)/shard_map/assemble/pallas_call | solution.py:61
  120.1 4.2 %forward.4 = (bf16[256,1024]{1,0:T(8,128)(2,1)S(1)}, bf16[256,1024]{1,0:T(8,128)(2,1)S(1)}) custom-call(s32[2]{0:T(128)S(1)} %get-tuple-element.122.scalars_ref, bf16[1024,1024]{1,0:T(8,128)(2,1)S(1)} %get-tuple-element.73.refs_8_.refs_0_.refs_2_, bf16[1024,1024]{1,0:T(8,128)(2,1)} %collective-permute-done.20.refs_1_.refs_3_, ...), custom_call_target="tpu_custom_call" | custom-call | flops 2147483648 | bytes 6291456 | tf_op jit(solution)/shard_map/forward/pallas_call | solution.py:61
  126.5 4.2 %forward.5 = (bf16[256,1024]{1,0:T(8,128)(2,1)S(1)}, bf16[256,1024]{1,0:T(8,128)(2,1)S(1)}) custom-call(s32[2]{0:T(128)S(1)} %get-tuple-element.123.scalars_ref, bf16[1024,1024]{1,0:T(8,128)(2,1)S(1)} %get-tuple-element.73.refs_8_.refs_0_.refs_2_, bf16[1024,1024]{1,0:T(8,128)(2,1)} %collective-permute-done.20.refs_1_.refs_3_, ...), custom_call_target="tpu_custom_call" | custom-call | flops 2147483648 | bytes 6291456 | tf_op jit(solution)/shard_map/forward/pallas_call | solution.py:61
  130.7 3.0 %assemble.2.refs_0_.refs_4_ = bf16[1024,2048]{1,0:T(8,128)(2,1)S(1)} custom-call(s32[2]{0:T(128)S(1)} %pad_add_fusion.scalars_ref, bf16[512,2048]{1,0:T(8,128)(2,1)} %collect.3.refs_0_.refs_5_, bf16[512,2048]{1,0:T(8,128)(2,1)} %collective-permute-done.18.refs_1_), custom_call_target="tpu_custom_call" | custom-call | bytes 8388608 | tf_op jit(solution)/shard_map/assemble/pallas_call | solution.py:61
  133.7 4.2 %forward.6 = (bf16[256,1024]{1,0:T(8,128)(2,1)S(1)}, bf16[256,1024]{1,0:T(8,128)(2,1)S(1)}) custom-call(s32[2]{0:T(128)S(1)} %get-tuple-element.122.scalars_ref, bf16[1024,1024]{1,0:T(8,128)(2,1)S(1)} %get-tuple-element.73.refs_8_.refs_0_.refs_2_, bf16[1024,1024]{1,0:T(8,128)(2,1)} %collective-permute-done.20.refs_1_.refs_3_, ...), custom_call_target="tpu_custom_call" | custom-call | flops 2147483648 | bytes 6291456 | tf_op jit(solution)/shard_map/forward/pallas_call | solution.py:61
  141.5 4.2 %forward.7 = (bf16[256,1024]{1,0:T(8,128)(2,1)S(1)}, bf16[256,1024]{1,0:T(8,128)(2,1)S(1)}) custom-call(s32[2]{0:T(128)S(1)} %get-tuple-element.123.scalars_ref, bf16[1024,1024]{1,0:T(8,128)(2,1)S(1)} %get-tuple-element.73.refs_8_.refs_0_.refs_2_, bf16[1024,1024]{1,0:T(8,128)(2,1)} %collective-permute-done.20.refs_1_.refs_3_, ...), custom_call_target="tpu_custom_call" | custom-call | flops 2147483648 | bytes 6291456 | tf_op jit(solution)/shard_map/forward/pallas_call | solution.py:61
  148.7 4.1 %collective-permute-done.26.refs_3_ = bf16[256,1024]{1,0:T(8,128)(2,1)S(1)} collective-permute-done((bf16[256,1024]{1,0:T(8,128)(2,1)S(1)}, bf16[256,1024]{1,0:T(8,128)(2,1)S(1)}, u32[]{:S(2)}, u32[]{:S(2)}) %collective-permute-start.26) | collective-permute-done | bytes 524320 | tf_op jit(solution)/shard_map/ppermute | solution.py:19
  154.1 3.5 %collective-permute-done.24.refs_3_ = bf16[128,1024]{1,0:T(8,128)(2,1)S(1)} collective-permute-done((bf16[128,1024]{1,0:T(8,128)(2,1)S(1)}, bf16[128,1024]{1,0:T(8,128)(2,1)S(1)}, u32[]{:S(2)}, u32[]{:S(2)}) %collective-permute-start.24) | collective-permute-done | bytes 262176 | tf_op jit(solution)/shard_map/ppermute | solution.py:19
  161.5 5.3 %collective-permute-done.32.refs_3_ = bf16[128,1024]{1,0:T(8,128)(2,1)S(1)} collective-permute-done((bf16[128,1024]{1,0:T(8,128)(2,1)S(1)}, bf16[128,1024]{1,0:T(8,128)(2,1)S(1)}, u32[]{:S(2)}, u32[]{:S(2)}) %collective-permute-start.32) | collective-permute-done | bytes 262176 | tf_op jit(solution)/shard_map/ppermute | solution.py:19
  177.0 1.9 collective-permute-done.29.refs_2_
  180.7 1.9 collective-permute-done.35.refs_1_
  182.6 3.3 %collective-permute-done.36.refs_2_ = bf16[128,640]{1,0:T(8,128)(2,1)S(1)} collective-permute-done((bf16[128,640]{1,0:T(8,128)(2,1)S(1)}, bf16[128,640]{1,0:T(8,128)(2,1)S(1)}, u32[]{:S(2)}, u32[]{:S(2)}) %collective-permute-start.36) | collective-permute-done | bytes 163872 | tf_op jit(solution)/shard_map/ppermute | solution.py:19
  187.4 3.7 %collective-permute-start.38 = (bf16[128,640]{1,0:T(8,128)(2,1)S(1)}, bf16[128,640]{1,0:T(8,128)(2,1)S(1)}, u32[]{:S(2)}, u32[]{:S(2)}) collective-permute-start(bf16[128,640]{1,0:T(8,128)(2,1)S(1)} %add_up.8.refs_2_.refs_0_), channel_id=1, source_target_pairs={{0,2},{1,3},{2,0},{3,1},{4,6},{5,7},{6,4},{7,5},{8,10},{9,11},{10,... | collective-permute-start | bytes 491528 | tf_op jit(solution)/shard_map/ppermute | solution.py:19
  191.1 3.8 %collective-permute-done.39.refs_1_ = bf16[128,640]{1,0:T(8,128)(2,1)S(1)} collective-permute-done((bf16[128,640]{1,0:T(8,128)(2,1)S(1)}, bf16[128,640]{1,0:T(8,128)(2,1)S(1)}, u32[]{:S(2)}, u32[]{:S(2)}) %collective-permute-start.39) | collective-permute-done | bytes 163872 | tf_op jit(solution)/shard_map/ppermute | solution.py:19
  196.1 6.4 %collective-permute-done.38.refs_1_ = bf16[128,640]{1,0:T(8,128)(2,1)S(1)} collective-permute-done((bf16[128,640]{1,0:T(8,128)(2,1)S(1)}, bf16[128,640]{1,0:T(8,128)(2,1)S(1)}, u32[]{:S(2)}, u32[]{:S(2)}) %collective-permute-start.38) | collective-permute-done | bytes 163872 | tf_op jit(solution)/shard_map/ppermute | solution.py:19
  202.6 3.2 %collective-permute-done.43.refs_1_ = bf16[128,640]{1,0:T(8,128)(2,1)S(1)} collective-permute-done((bf16[128,640]{1,0:T(8,128)(2,1)S(1)}, bf16[128,640]{1,0:T(8,128)(2,1)S(1)}, u32[]{:S(2)}, u32[]{:S(2)}) %collective-permute-start.43) | collective-permute-done | bytes 163872 | tf_op jit(solution)/shard_map/ppermute | solution.py:19
  211.9 2.0 collective-permute-done.46.refs_3_
  215.0 2.5 collective-permute-done.45.refs_2_
  217.5 3.4 %collective-permute-done.42.refs_3_ = bf16[128,640]{1,0:T(8,128)(2,1)S(1)} collective-permute-done((bf16[128,640]{1,0:T(8,128)(2,1)S(1)}, bf16[128,640]{1,0:T(8,128)(2,1)S(1)}, u32[]{:S(2)}, u32[]{:S(2)}) %collective-permute-start.42) | collective-permute-done | bytes 163872 | tf_op jit(solution)/shard_map/ppermute | solution.py:19
  221.0 2.3 collective-permute-done.41.refs_2_
  225.5 2.4 out_grad_of.2
  230.0 2.4 out_grad_of.3
  234.6 2.5 collective-permute-done.50.refs_5_
  238.1 3.8 %collective-permute-done.52.refs_7_ = bf16[128,1024]{1,0:T(8,128)(2,1)S(1)} collective-permute-done((bf16[128,1024]{1,0:T(8,128)(2,1)S(1)}, bf16[128,1024]{1,0:T(8,128)(2,1)S(1)}, u32[]{:S(2)}, u32[]{:S(2)}) %collective-permute-start.52) | collective-permute-done | bytes 262176 | tf_op jit(solution)/shard_map/ppermute | solution.py:19
  247.5 10.7 %collective-permute-done.53.refs_4_ = bf16[256,1024]{1,0:T(8,128)(2,1)S(1)} collective-permute-done((bf16[256,1024]{1,0:T(8,128)(2,1)S(1)}, bf16[256,1024]{1,0:T(8,128)(2,1)S(1)}, u32[]{:S(2)}, u32[]{:S(2)}) %collective-permute-start.53) | collective-permute-done | bytes 524320 | tf_op jit(solution)/shard_map/ppermute | solution.py:19
  259.3 8.1 %collective-permute-done.55.refs_6_ = bf16[256,1024]{1,0:T(8,128)(2,1)S(1)} collective-permute-done((bf16[256,1024]{1,0:T(8,128)(2,1)S(1)}, bf16[256,1024]{1,0:T(8,128)(2,1)S(1)}, u32[]{:S(2)}, u32[]{:S(2)}) %collective-permute-start.55) | collective-permute-done | bytes 524320 | tf_op jit(solution)/shard_map/ppermute | solution.py:19
  270.1 5.8 %weight_grad_of.2 = (f32[1024,2048]{1,0:T(8,128)S(1)}, f32[16,128]{1,0:T(8,128)S(1)}) custom-call(s32[2]{0:T(128)S(1)} %pad_add_fusion.scalars_ref, bf16[1024,1024]{1,0:T(8,128)(2,1)S(1)} %turn_columns.2.refs_5_.refs_0_, bf16[1024,1024]{1,0:T(8,128)(2,1)S(1)} %turn_columns.3.refs_5_.refs_1_, bf16[512,1024]{1,0:T(8,128)(2,1)S(1)} %get-tuple-element.113.refs_2_, ...), custom_call_target="tpu_custom_call" | custom-call | flops 4294967296 | bytes 4194304 | tf_op jit(solution)/shard_map/weight_grad_of/pallas_call | solution.py:61
  276.2 5.6 %weight_grad_of.3 = (f32[1024,2048]{1,0:T(8,128)S(1)}, f32[16,128]{1,0:T(8,128)S(1)}) custom-call(s32[2]{0:T(128)S(1)} %pad_add_fusion.scalars_ref, bf16[1024,1024]{1,0:T(8,128)(2,1)S(1)} %turn_columns.2.refs_5_.refs_0_, bf16[1024,1024]{1,0:T(8,128)(2,1)S(1)} %turn_columns.3.refs_5_.refs_1_, ...), custom_call_target="tpu_custom_call", output_to_operand_aliasing={{0}: (8, {})} | custom-call | flops 4294967296 | bytes 4194304 | tf_op jit(solution)/shard_map/weight_grad_of/pallas_call | solution.py:61
  281.9 1.8 collective-permute-start.63
  283.6 2.7 collective-permute-start.61
  293.2 2.5 collective-permute-done.67.refs_1_
  295.8 7.5 %update.1 = (f32[1024,2048]{1,0:T(8,128)}, f32[1024,2048]{1,0:T(8,128)}) custom-call(s32[1]{0:T(128)} %constant.21.clone.1.scalars_ref, f32[16,128]{1,0:T(8,128)S(1)} %add_add_fusion.refs_0_, f32[16,128]{1,0:T(8,128)S(1)} %collective-permute-done.67.refs_1_, f32[1024,2048]{1,0:T(8,128)S(1)} %bitcast.9, f32[1024,2048]{1,0:T(8,128)S(1)} %bitcast.11, ...), custom_call_target="tpu_custom_call" | custom-call | flops 8388608 | bytes 41943040 | tf_op jit(solution)/shard_map/update/pallas_call | solution.py:61
  (164 shorter events, 84.0 us)
Async XLA Ops:
  1.9 23.5 %collective-permute-start = (bf16[128,2048]{1,0:T(8,128)(2,1)S(1)}, bf16[128,2048]{1,0:T(8,128)(2,1)S(1)}, u32[]{:S(2)}, u32[]{:S(2)}) collective-permute-start(bf16[128,2048]{1,0:T(8,128)(2,1)S(1)} %get-tuple-element.62.refs_0_), channel_id=1, source_target_pairs={{0,1},{1,2},{2,3},{3,0},{4,5},{5,6},{6,7},{7,4},{8,9},{9,10},{10,1... | collective-permute-start | bytes 1572872 | tf_op jit(solution)/shard_map/ppermute | solution.py:154
  5.0 20.4 %collective-permute-start.3 = (bf16[64,2048]{1,0:T(8,128)(2,1)S(1)}, bf16[64,2048]{1,0:T(8,128)(2,1)S(1)}, u32[]{:S(2)}, u32[]{:S(2)}) collective-permute-start(bf16[64,2048]{1,0:T(8,128)(2,1)S(1)} %get-tuple-element.63.refs_0_), channel_id=1, source_target_pairs={{0,1},{1,2},{2,3},{3,0},{4,5},{5,6},{6,7},{7,4},{8,9},{9,10},{10,1... | collective-permute-start | bytes 786440 | tf_op jit(solution)/shard_map/ppermute | solution.py:154
  6.6 24.4 %collective-permute-start.9 = (bf16[64,2048]{1,0:T(8,128)(2,1)S(1)}, bf16[64,2048]{1,0:T(8,128)(2,1)S(1)}, u32[]{:S(2)}, u32[]{:S(2)}) collective-permute-start(bf16[64,2048]{1,0:T(8,128)(2,1)S(1)} %get-tuple-element.68.refs_0_), channel_id=1, source_target_pairs={{0,1},{1,2},{2,3},{3,0},{4,5},{5,6},{6,7},{7,4},{8,9},{9,10},{10,1... | collective-permute-start | bytes 786440 | tf_op jit(solution)/shard_map/ppermute | solution.py:154
  25.4 11.2 %collective-permute-start.4 = (bf16[64,2048]{1,0:T(8,128)(2,1)S(1)}, bf16[64,2048]{1,0:T(8,128)(2,1)S(1)}, u32[]{:S(2)}, u32[]{:S(2)}) collective-permute-start(bf16[64,2048]{1,0:T(8,128)(2,1)S(1)} %collective-permute-done.3.refs_1_), channel_id=1, source_target_pairs={{0,1},{1,2},{2,3},{3,0},{4,5},{5,6},{6,7},{7,4},{8,9},{9,10},{10,1... | collective-permute-start | bytes 786440 | tf_op jit(solution)/shard_map/ppermute | solution.py:154
  25.4 39.1 %collective-permute-start.1 = (bf16[128,2048]{1,0:T(8,128)(2,1)S(1)}, bf16[128,2048]{1,0:T(8,128)(2,1)S(1)}, u32[]{:S(2)}, u32[]{:S(2)}) collective-permute-start(bf16[128,2048]{1,0:T(8,128)(2,1)S(1)} %collective-permute-done.refs_1_), channel_id=1, source_target_pairs={{0,1},{1,2},{2,3},{3,0},{4,5},{5,6},{6,7},{7,4},{8,9},{9,10},{10,1... | collective-permute-start | bytes 1572872 | tf_op jit(solution)/shard_map/ppermute | solution.py:154
  31.0 22.5 %collective-permute-start.10 = (bf16[64,2048]{1,0:T(8,128)(2,1)S(1)}, bf16[64,2048]{1,0:T(8,128)(2,1)S(1)}, u32[]{:S(2)}, u32[]{:S(2)}) collective-permute-start(bf16[64,2048]{1,0:T(8,128)(2,1)S(1)} %collective-permute-done.9.refs_1_), channel_id=1, source_target_pairs={{0,1},{1,2},{2,3},{3,0},{4,5},{5,6},{6,7},{7,4},{8,9},{9,10},{10,1... | collective-permute-start | bytes 786440 | tf_op jit(solution)/shard_map/ppermute | solution.py:154
  36.6 22.5 %collective-permute-start.5 = (bf16[64,2048]{1,0:T(8,128)(2,1)S(1)}, bf16[64,2048]{1,0:T(8,128)(2,1)S(1)}, u32[]{:S(2)}, u32[]{:S(2)}) collective-permute-start(bf16[64,2048]{1,0:T(8,128)(2,1)S(1)} %collective-permute-done.4.refs_2_), channel_id=1, source_target_pairs={{0,1},{1,2},{2,3},{3,0},{4,5},{5,6},{6,7},{7,4},{8,9},{9,10},{10,1... | collective-permute-start | bytes 786440 | tf_op jit(solution)/shard_map/ppermute | solution.py:154
  53.5 11.3 %collective-permute-start.11 = (bf16[64,2048]{1,0:T(8,128)(2,1)S(1)}, bf16[64,2048]{1,0:T(8,128)(2,1)S(1)}, u32[]{:S(2)}, u32[]{:S(2)}) collective-permute-start(bf16[64,2048]{1,0:T(8,128)(2,1)S(1)} %collective-permute-done.10.refs_2_), channel_id=1, source_target_pairs={{0,1},{1,2},{2,3},{3,0},{4,5},{5,6},{6,7},{7,4},{8,9},{9,10},{10,1... | collective-permute-start | bytes 786440 | tf_op jit(solution)/shard_map/ppermute | solution.py:154
  61.2 9.2 %collective-permute-start.6 = (bf16[64,2048]{1,0:T(8,128)(2,1)S(1)}, bf16[64,2048]{1,0:T(8,128)(2,1)S(1)}, u32[]{:S(2)}, u32[]{:S(2)}) collective-permute-start(bf16[64,2048]{1,0:T(8,128)(2,1)S(1)} %get-tuple-element.65), channel_id=1, source_target_pairs={{0,8},{4,12},{8,0},{12,4},{16,24},{20,28},{24,16},{28,20},{1,9},{5... | collective-permute-start | bytes 786440 | tf_op jit(solution)/shard_map/ppermute | solution.py:19
  63.0 11.6 %collective-permute-start.7 = (bf16[64,2048]{1,0:T(8,128)(2,1)S(1)}, bf16[64,2048]{1,0:T(8,128)(2,1)S(1)}, u32[]{:S(2)}, u32[]{:S(2)}) collective-permute-start(bf16[64,2048]{1,0:T(8,128)(2,1)S(1)} %get-tuple-element.66), channel_id=1, source_target_pairs={{0,16},{4,20},{8,24},{12,28},{16,0},{20,4},{24,8},{28,12},{1,17},{... | collective-permute-start | bytes 786440 | tf_op jit(solution)/shard_map/ppermute | solution.py:19
  64.5 24.6 %collective-permute-start.2 = (bf16[128,2048]{1,0:T(8,128)(2,1)S(1)}, bf16[128,2048]{1,0:T(8,128)(2,1)}, u32[]{:S(2)}, u32[]{:S(2)}) collective-permute-start(bf16[128,2048]{1,0:T(8,128)(2,1)S(1)} %collective-permute-done.1.refs_9_.refs_2_), channel_id=1, source_target_pairs={{0,1},{1,2},{2,3},{3,0},{4,5},{5,6},{6,7},{7,4},{8,9},{9,10},{10,1... | collective-permute-start | bytes 1572872 | tf_op jit(solution)/shard_map/ppermute | solution.py:154
  64.5 20.4 %collective-permute-start.8 = (bf16[64,2048]{1,0:T(8,128)(2,1)}, bf16[64,2048]{1,0:T(8,128)(2,1)}, u32[]{:S(2)}, u32[]{:S(2)}) collective-permute-start(bf16[64,2048]{1,0:T(8,128)(2,1)} %get-tuple-element.67), channel_id=1, source_target_pairs={{0,24},{4,28},{8,16},{12,20},{16,8},{20,12},{24,0},{28,4},{1,25},{... | collective-permute-start | bytes 786440 | tf_op jit(solution)/shard_map/ppermute | solution.py:19
  66.4 18.5 %collective-permute-start.12 = (bf16[64,2048]{1,0:T(8,128)(2,1)}, bf16[64,2048]{1,0:T(8,128)(2,1)}, u32[]{:S(2)}, u32[]{:S(2)}) collective-permute-start(bf16[64,2048]{1,0:T(8,128)(2,1)} %get-tuple-element.70), channel_id=1, source_target_pairs={{0,8},{4,12},{8,0},{12,4},{16,24},{20,28},{24,16},{28,20},{1,9},{5... | collective-permute-start | bytes 786440 | tf_op jit(solution)/shard_map/ppermute | solution.py:19
  71.2 14.7 %collective-permute-start.13 = (bf16[64,2048]{1,0:T(8,128)(2,1)}, bf16[64,2048]{1,0:T(8,128)(2,1)}, u32[]{:S(2)}, u32[]{:S(2)}) collective-permute-start(bf16[64,2048]{1,0:T(8,128)(2,1)} %get-tuple-element.71), channel_id=1, source_target_pairs={{0,16},{4,20},{8,24},{12,28},{16,0},{20,4},{24,8},{28,12},{1,17},{... | collective-permute-start | bytes 786440 | tf_op jit(solution)/shard_map/ppermute | solution.py:19
  75.3 10.6 %collective-permute-start.14 = (bf16[64,2048]{1,0:T(8,128)(2,1)}, bf16[64,2048]{1,0:T(8,128)(2,1)}, u32[]{:S(2)}, u32[]{:S(2)}) collective-permute-start(bf16[64,2048]{1,0:T(8,128)(2,1)} %get-tuple-element.72), channel_id=1, source_target_pairs={{0,24},{4,28},{8,16},{12,20},{16,8},{20,12},{24,0},{28,4},{1,25},{... | collective-permute-start | bytes 786440 | tf_op jit(solution)/shard_map/ppermute | solution.py:19
  90.9 14.9 %collective-permute-start.15 = (bf16[128,2048]{1,0:T(8,128)(2,1)S(1)}, bf16[128,2048]{1,0:T(8,128)(2,1)S(1)}, u32[]{:S(2)}, u32[]{:S(2)}) collective-permute-start(bf16[128,2048]{1,0:T(8,128)(2,1)S(1)} %get-tuple-element.75), channel_id=1, source_target_pairs={{0,8},{4,12},{8,0},{12,4},{16,24},{20,28},{24,16},{28,20},{1,9},{5... | collective-permute-start | bytes 1572872 | tf_op jit(solution)/shard_map/ppermute | solution.py:19
  92.9 20.7 %collective-permute-start.16 = (bf16[128,2048]{1,0:T(8,128)(2,1)S(1)}, bf16[128,2048]{1,0:T(8,128)(2,1)S(1)}, u32[]{:S(2)}, u32[]{:S(2)}) collective-permute-start(bf16[128,2048]{1,0:T(8,128)(2,1)S(1)} %get-tuple-element.76), channel_id=1, source_target_pairs={{0,16},{4,20},{8,24},{12,28},{16,0},{20,4},{24,8},{28,12},{1,17},{... | collective-permute-start | bytes 1572872 | tf_op jit(solution)/shard_map/ppermute | solution.py:19
  93.0 20.7 %collective-permute-start.17 = (bf16[128,2048]{1,0:T(8,128)(2,1)S(1)}, bf16[128,2048]{1,0:T(8,128)(2,1)S(1)}, u32[]{:S(2)}, u32[]{:S(2)}) collective-permute-start(bf16[128,2048]{1,0:T(8,128)(2,1)S(1)} %get-tuple-element.77), channel_id=1, source_target_pairs={{0,24},{4,28},{8,16},{12,20},{16,8},{20,12},{24,0},{28,4},{1,25},{... | collective-permute-start | bytes 1572872 | tf_op jit(solution)/shard_map/ppermute | solution.py:19
  94.5 21.3 %collective-permute-start.19 = (bf16[512,2048]{1,0:T(8,128)(2,1)}, bf16[512,2048]{1,0:T(8,128)(2,1)}, u32[]{:S(2)}, u32[]{:S(2)}) collective-permute-start(bf16[512,2048]{1,0:T(8,128)(2,1)} %collect.2.refs_4_.refs_0_), channel_id=1, source_target_pairs={{0,4},{4,0},{8,12},{12,8},{16,20},{20,16},{24,28},{28,24},{1,5},{5... | collective-permute-start | bytes 6291464 | tf_op jit(solution)/shard_map/ppermute | solution.py:19
  94.5 25.6 %collective-permute-start.20 = (bf16[1024,1024]{1,0:T(8,128)(2,1)}, bf16[1024,1024]{1,0:T(8,128)(2,1)}, u32[]{:S(2)}, u32[]{:S(2)}) collective-permute-start(bf16[1024,1024]{1,0:T(8,128)(2,1)} %get-tuple-element.78), channel_id=1, source_target_pairs={{0,4},{4,0},{8,12},{12,8},{16,20},{20,16},{24,28},{28,24},{1,5},{5... | collective-permute-start | bytes 6291464 | tf_op jit(solution)/shard_map/ppermute | solution.py:19
  115.7 15.0 %collective-permute-start.18 = (bf16[512,2048]{1,0:T(8,128)(2,1)}, bf16[512,2048]{1,0:T(8,128)(2,1)}, u32[]{:S(2)}, u32[]{:S(2)}) collective-permute-start(bf16[512,2048]{1,0:T(8,128)(2,1)} %collect.3.refs_0_.refs_5_), channel_id=1, source_target_pairs={{0,4},{4,0},{8,12},{12,8},{16,20},{20,16},{24,28},{28,24},{1,5},{5... | collective-permute-start | bytes 6291464 | tf_op jit(solution)/shard_map/ppermute | solution.py:19
  124.3 21.4 %collective-permute-start.22 = (bf16[256,1024]{1,0:T(8,128)(2,1)S(1)}, bf16[256,1024]{1,0:T(8,128)(2,1)S(1)}, u32[]{:S(2)}, u32[]{:S(2)}) collective-permute-start(bf16[256,1024]{1,0:T(8,128)(2,1)S(1)} %get-tuple-element.82), channel_id=1, source_target_pairs={{0,16},{4,20},{8,24},{12,28},{16,0},{20,4},{24,8},{28,12},{1,17},{... | collective-permute-start | bytes 1572872 | tf_op jit(solution)/shard_map/ppermute | solution.py:19
  124.9 20.8 %collective-permute-start.21 = (bf16[256,1024]{1,0:T(8,128)(2,1)S(1)}, bf16[256,1024]{1,0:T(8,128)(2,1)S(1)}, u32[]{:S(2)}, u32[]{:S(2)}) collective-permute-start(bf16[256,1024]{1,0:T(8,128)(2,1)S(1)} %get-tuple-element.79.refs_6_), channel_id=1, source_target_pairs={{0,8},{4,12},{8,0},{12,4},{16,24},{20,28},{24,16},{28,20},{1,9},{5... | collective-permute-start | bytes 1572872 | tf_op jit(solution)/shard_map/ppermute | solution.py:19
  137.9 14.9 %collective-permute-start.26 = (bf16[256,1024]{1,0:T(8,128)(2,1)S(1)}, bf16[256,1024]{1,0:T(8,128)(2,1)S(1)}, u32[]{:S(2)}, u32[]{:S(2)}) collective-permute-start(bf16[256,1024]{1,0:T(8,128)(2,1)S(1)} %get-tuple-element.90), channel_id=1, source_target_pairs={{0,16},{4,20},{8,24},{12,28},{16,0},{20,4},{24,8},{28,12},{1,17},{... | collective-permute-start | bytes 1572872 | tf_op jit(solution)/shard_map/ppermute | solution.py:19
  138.5 14.8 %collective-permute-start.25 = (bf16[256,1024]{1,0:T(8,128)(2,1)S(1)}, bf16[256,1024]{1,0:T(8,128)(2,1)S(1)}, u32[]{:S(2)}, u32[]{:S(2)}) collective-permute-start(bf16[256,1024]{1,0:T(8,128)(2,1)S(1)} %get-tuple-element.83.refs_6_), channel_id=1, source_target_pairs={{0,8},{4,12},{8,0},{12,4},{16,24},{20,28},{24,16},{28,20},{1,9},{5... | collective-permute-start | bytes 1572872 | tf_op jit(solution)/shard_map/ppermute | solution.py:19
  146.5 11.1 %collective-permute-start.24 = (bf16[128,1024]{1,0:T(8,128)(2,1)S(1)}, bf16[128,1024]{1,0:T(8,128)(2,1)S(1)}, u32[]{:S(2)}, u32[]{:S(2)}) collective-permute-start(bf16[128,1024]{1,0:T(8,128)(2,1)S(1)} %get-tuple-element.88), channel_id=1, source_target_pairs={{0,8},{4,12},{8,0},{12,4},{16,24},{20,28},{24,16},{28,20},{1,9},{5... | collective-permute-start | bytes 786440 | tf_op jit(solution)/shard_map/ppermute | solution.py:19
  147.1 10.5 %collective-permute-start.23 = (bf16[128,1024]{1,0:T(8,128)(2,1)S(1)}, bf16[128,1024]{1,0:T(8,128)(2,1)S(1)}, u32[]{:S(2)}, u32[]{:S(2)}) collective-permute-start(bf16[128,1024]{1,0:T(8,128)(2,1)S(1)} %get-tuple-element.86.refs_4_), channel_id=1, source_target_pairs={{0,16},{4,20},{8,24},{12,28},{16,0},{20,4},{24,8},{28,12},{1,17},{... | collective-permute-start | bytes 786440 | tf_op jit(solution)/shard_map/ppermute | solution.py:19
  158.1 8.7 %collective-permute-start.32 = (bf16[128,1024]{1,0:T(8,128)(2,1)S(1)}, bf16[128,1024]{1,0:T(8,128)(2,1)S(1)}, u32[]{:S(2)}, u32[]{:S(2)}) collective-permute-start(bf16[128,1024]{1,0:T(8,128)(2,1)S(1)} %get-tuple-element.99), channel_id=1, source_target_pairs={{0,8},{4,12},{8,0},{12,4},{16,24},{20,28},{24,16},{28,20},{1,9},{5... | collective-permute-start | bytes 786440 | tf_op jit(solution)/shard_map/ppermute | solution.py:19
  169.1 9.9 %collective-permute-start.29 = (bf16[128,640]{1,0:T(8,128)(2,1)S(1)}, bf16[128,640]{1,0:T(8,128)(2,1)S(1)}, u32[]{:S(2)}, u32[]{:S(2)}) collective-permute-start(bf16[128,640]{1,0:T(8,128)(2,1)S(1)} %get-tuple-element.95), channel_id=1, source_target_pairs={{0,16},{4,20},{8,24},{12,28},{16,0},{20,4},{24,8},{28,12},{1,17},{... | collective-permute-start | bytes 491528 | tf_op jit(solution)/shard_map/ppermute | solution.py:19
  173.4 9.2 %collective-permute-start.35 = (bf16[128,640]{1,0:T(8,128)(2,1)S(1)}, bf16[128,640]{1,0:T(8,128)(2,1)S(1)}, u32[]{:S(2)}, u32[]{:S(2)}) collective-permute-start(bf16[128,640]{1,0:T(8,128)(2,1)S(1)} %get-tuple-element.102), channel_id=1, source_target_pairs={{0,8},{4,12},{8,0},{12,4},{16,24},{20,28},{24,16},{28,20},{1,9},{5... | collective-permute-start | bytes 491528 | tf_op jit(solution)/shard_map/ppermute | solution.py:19
  174.0 11.9 %collective-permute-start.36 = (bf16[128,640]{1,0:T(8,128)(2,1)S(1)}, bf16[128,640]{1,0:T(8,128)(2,1)S(1)}, u32[]{:S(2)}, u32[]{:S(2)}) collective-permute-start(bf16[128,640]{1,0:T(8,128)(2,1)S(1)} %get-tuple-element.103), channel_id=1, source_target_pairs={{0,16},{4,20},{8,24},{12,28},{16,0},{20,4},{24,8},{28,12},{1,17},{... | collective-permute-start | bytes 491528 | tf_op jit(solution)/shard_map/ppermute | solution.py:19
  175.5 10.4 %collective-permute-start.37 = (bf16[128,640]{1,0:T(8,128)(2,1)S(1)}, bf16[128,640]{1,0:T(8,128)(2,1)S(1)}, u32[]{:S(2)}, u32[]{:S(2)}) collective-permute-start(bf16[128,640]{1,0:T(8,128)(2,1)S(1)} %get-tuple-element.104), channel_id=1, source_target_pairs={{0,24},{4,28},{8,16},{12,20},{16,8},{20,12},{24,0},{28,4},{1,25},{... | collective-permute-start | bytes 491528 | tf_op jit(solution)/shard_map/ppermute | solution.py:19
  186.0 8.9 %collective-permute-start.39 = (bf16[128,640]{1,0:T(8,128)(2,1)S(1)}, bf16[128,640]{1,0:T(8,128)(2,1)S(1)}, u32[]{:S(2)}, u32[]{:S(2)}) collective-permute-start(bf16[128,640]{1,0:T(8,128)(2,1)S(1)} %add_up.7.refs_2_.refs_0_), channel_id=1, source_target_pairs={{0,1},{1,0},{2,3},{3,2},{4,5},{5,4},{6,7},{7,6},{8,9},{9,8},{10,11... | collective-permute-start | bytes 491528 | tf_op jit(solution)/shard_map/ppermute | solution.py:19
  187.4 15.1 %collective-permute-start.38 = (bf16[128,640]{1,0:T(8,128)(2,1)S(1)}, bf16[128,640]{1,0:T(8,128)(2,1)S(1)}, u32[]{:S(2)}, u32[]{:S(2)}) collective-permute-start(bf16[128,640]{1,0:T(8,128)(2,1)S(1)} %add_up.8.refs_2_.refs_0_), channel_id=1, source_target_pairs={{0,2},{1,3},{2,0},{3,1},{4,6},{5,7},{6,4},{7,5},{8,10},{9,11},{10,... | collective-permute-start | bytes 491528 | tf_op jit(solution)/shard_map/ppermute | solution.py:19
  194.9 10.8 %collective-permute-start.43 = (bf16[128,640]{1,0:T(8,128)(2,1)S(1)}, bf16[128,640]{1,0:T(8,128)(2,1)S(1)}, u32[]{:S(2)}, u32[]{:S(2)}) collective-permute-start(bf16[128,640]{1,0:T(8,128)(2,1)S(1)} %add_up.9.refs_2_.refs_0_), channel_id=1, source_target_pairs={{0,2},{1,3},{2,0},{3,1},{4,6},{5,7},{6,4},{7,5},{8,10},{9,11},{10,... | collective-permute-start | bytes 491528 | tf_op jit(solution)/shard_map/ppermute | solution.py:19
  207.3 10.1 %collective-permute-start.45 = (bf16[128,640]{1,0:T(8,128)(2,1)S(1)}, bf16[128,640]{1,0:T(8,128)(2,1)S(1)}, u32[]{:S(2)}, u32[]{:S(2)}) collective-permute-start(bf16[128,640]{1,0:T(8,128)(2,1)S(1)} %add_up.11.refs_0_), channel_id=1, source_target_pairs={{0,16},{4,20},{8,24},{12,28},{16,0},{20,4},{24,8},{28,12},{1,17},{... | collective-permute-start | bytes 491528 | tf_op jit(solution)/shard_map/ppermute | solution.py:19
  208.4 9.0 %collective-permute-start.44 = (bf16[128,640]{1,0:T(8,128)(2,1)S(1)}, bf16[128,640]{1,0:T(8,128)(2,1)S(1)}, u32[]{:S(2)}, u32[]{:S(2)}) collective-permute-start(bf16[128,640]{1,0:T(8,128)(2,1)S(1)} %add_up.11.refs_0_), channel_id=1, source_target_pairs={{0,8},{4,12},{8,0},{12,4},{16,24},{20,28},{24,16},{28,20},{1,9},{5... | collective-permute-start | bytes 491528 | tf_op jit(solution)/shard_map/ppermute | solution.py:19
  209.4 11.6 %collective-permute-start.42 = (bf16[128,640]{1,0:T(8,128)(2,1)S(1)}, bf16[128,640]{1,0:T(8,128)(2,1)S(1)}, u32[]{:S(2)}, u32[]{:S(2)}) collective-permute-start(bf16[128,640]{1,0:T(8,128)(2,1)S(1)} %add_up.10.refs_2_.refs_0_), channel_id=1, source_target_pairs={{0,24},{4,28},{8,16},{12,20},{16,8},{20,12},{24,0},{28,4},{1,25},{... | collective-permute-start | bytes 491528 | tf_op jit(solution)/shard_map/ppermute | solution.py:19
  210.8 12.4 %collective-permute-start.41 = (bf16[128,640]{1,0:T(8,128)(2,1)S(1)}, bf16[128,640]{1,0:T(8,128)(2,1)S(1)}, u32[]{:S(2)}, u32[]{:S(2)}) collective-permute-start(bf16[128,640]{1,0:T(8,128)(2,1)S(1)} %add_up.10.refs_2_.refs_0_), channel_id=1, source_target_pairs={{0,16},{4,20},{8,24},{12,28},{16,0},{20,4},{24,8},{28,12},{1,17},{... | collective-permute-start | bytes 491528 | tf_op jit(solution)/shard_map/ppermute | solution.py:19
  213.9 9.3 %collective-permute-start.40 = (bf16[128,640]{1,0:T(8,128)(2,1)S(1)}, bf16[128,640]{1,0:T(8,128)(2,1)S(1)}, u32[]{:S(2)}, u32[]{:S(2)}) collective-permute-start(bf16[128,640]{1,0:T(8,128)(2,1)S(1)} %add_up.10.refs_2_.refs_0_), channel_id=1, source_target_pairs={{0,8},{4,12},{8,0},{12,4},{16,24},{20,28},{24,16},{28,20},{1,9},{5... | collective-permute-start | bytes 491528 | tf_op jit(solution)/shard_map/ppermute | solution.py:19
  227.9 9.2 %collective-permute-start.50 = (bf16[128,1024]{1,0:T(8,128)(2,1)S(1)}, bf16[128,1024]{1,0:T(8,128)(2,1)S(1)}, u32[]{:S(2)}, u32[]{:S(2)}) collective-permute-start(bf16[128,1024]{1,0:T(8,128)(2,1)S(1)} %get-tuple-element.126.refs_1_), channel_id=1, source_target_pairs={{0,8},{4,12},{8,0},{12,4},{16,24},{20,28},{24,16},{28,20},{1,9},{5... | collective-permute-start | bytes 786440 | tf_op jit(solution)/shard_map/ppermute | solution.py:19
  228.9 9.2 %collective-permute-start.49 = (bf16[128,1024]{1,0:T(8,128)(2,1)S(1)}, bf16[128,1024]{1,0:T(8,128)(2,1)S(1)}, u32[]{:S(2)}, u32[]{:S(2)}) collective-permute-start(bf16[128,1024]{1,0:T(8,128)(2,1)S(1)} %get-tuple-element.127.refs_0_), channel_id=1, source_target_pairs={{0,16},{4,20},{8,24},{12,28},{16,0},{20,4},{24,8},{28,12},{1,17},{... | collective-permute-start | bytes 786440 | tf_op jit(solution)/shard_map/ppermute | solution.py:19
  232.4 9.5 %collective-permute-start.52 = (bf16[128,1024]{1,0:T(8,128)(2,1)S(1)}, bf16[128,1024]{1,0:T(8,128)(2,1)S(1)}, u32[]{:S(2)}, u32[]{:S(2)}) collective-permute-start(bf16[128,1024]{1,0:T(8,128)(2,1)S(1)} %get-tuple-element.124.refs_3_), channel_id=1, source_target_pairs={{0,8},{4,12},{8,0},{12,4},{16,24},{20,28},{24,16},{28,20},{1,9},{5... | collective-permute-start | bytes 786440 | tf_op jit(solution)/shard_map/ppermute | solution.py:19
  233.7 8.9 %collective-permute-start.51 = (bf16[128,1024]{1,0:T(8,128)(2,1)S(1)}, bf16[128,1024]{1,0:T(8,128)(2,1)S(1)}, u32[]{:S(2)}, u32[]{:S(2)}) collective-permute-start(bf16[128,1024]{1,0:T(8,128)(2,1)S(1)} %get-tuple-element.125.refs_2_), channel_id=1, source_target_pairs={{0,16},{4,20},{8,24},{12,28},{16,0},{20,4},{24,8},{28,12},{1,17},{... | collective-permute-start | bytes 786440 | tf_op jit(solution)/shard_map/ppermute | solution.py:19
  243.3 14.9 %collective-permute-start.53 = (bf16[256,1024]{1,0:T(8,128)(2,1)S(1)}, bf16[256,1024]{1,0:T(8,128)(2,1)S(1)}, u32[]{:S(2)}, u32[]{:S(2)}) collective-permute-start(bf16[256,1024]{1,0:T(8,128)(2,1)S(1)} %get-tuple-element.109.refs_0_), channel_id=1, source_target_pairs={{0,8},{4,12},{8,0},{12,4},{16,24},{20,28},{24,16},{28,20},{1,9},{5... | collective-permute-start | bytes 1572872 | tf_op jit(solution)/shard_map/ppermute | solution.py:19
  244.4 14.9 %collective-permute-start.54 = (bf16[256,1024]{1,0:T(8,128)(2,1)S(1)}, bf16[256,1024]{1,0:T(8,128)(2,1)S(1)}, u32[]{:S(2)}, u32[]{:S(2)}) collective-permute-start(bf16[256,1024]{1,0:T(8,128)(2,1)S(1)} %get-tuple-element.110.refs_1_), channel_id=1, source_target_pairs={{0,16},{4,20},{8,24},{12,28},{16,0},{20,4},{24,8},{28,12},{1,17},{... | collective-permute-start | bytes 1572872 | tf_op jit(solution)/shard_map/ppermute | solution.py:19
  245.6 21.7 %collective-permute-start.55 = (bf16[256,1024]{1,0:T(8,128)(2,1)S(1)}, bf16[256,1024]{1,0:T(8,128)(2,1)S(1)}, u32[]{:S(2)}, u32[]{:S(2)}) collective-permute-start(bf16[256,1024]{1,0:T(8,128)(2,1)S(1)} %get-tuple-element.111.refs_2_), channel_id=1, source_target_pairs={{0,8},{4,12},{8,0},{12,4},{16,24},{20,28},{24,16},{28,20},{1,9},{5... | collective-permute-start | bytes 1572872 | tf_op jit(solution)/shard_map/ppermute | solution.py:19
  246.4 21.8 %collective-permute-start.56 = (bf16[256,1024]{1,0:T(8,128)(2,1)S(1)}, bf16[256,1024]{1,0:T(8,128)(2,1)S(1)}, u32[]{:S(2)}, u32[]{:S(2)}) collective-permute-start(bf16[256,1024]{1,0:T(8,128)(2,1)S(1)} %get-tuple-element.112.refs_3_), channel_id=1, source_target_pairs={{0,16},{4,20},{8,24},{12,28},{16,0},{20,4},{24,8},{28,12},{1,17},{... | collective-permute-start | bytes 1572872 | tf_op jit(solution)/shard_map/ppermute | solution.py:19
  (34 other events, 271.7 us)

commit v9 on v8

--- a/solution.py
+++ b/solution.py
@@ -124,7 +124,7 @@
             pl.BlockSpec((step, depth), lambda k, j, c: (jnp.where(k == 1, j, 0), 0)),
             pl.BlockSpec((16, 128), lambda k, j, c: (0, 0)),
         ],
-        grid=(2, 2 * steps), after=after, flops=2 * depth * width, moved=6 * depth * width, limit=16, name="turn_weight",
+        grid=(2, 2 * steps), after=after, flops=2 * depth * width, moved=6 * depth * width, limit=54, name="turn_weight",
     )
 
 
@@ -145,14 +145,20 @@
     return [first], [low, high]
 
 
-def go_round(parts):
+def relay(value, after):
+    def body(_, value_ref, out_ref):
+        out_ref[...] = value_ref[...]
+
+    (out,) = run(
+        body, jnp.zeros((1,), jnp.int32), [value], [whole(value)], [like(value.shape, BF16)],
+        [whole(value)], after=after, moved=4 * value.size, limit=8, name="relay",
+    )
+    return out
+
+
+def ring_step(share):
     n_feat = lax.axis_size("feat")
-    ring = [(i, (i + 1) % n_feat) for i in range(n_feat)]
-    lists = [[part] for part in parts]
-    for _ in range(1, n_feat):
-        for shares in lists:
-            shares.append(lax.ppermute(shares[-1], "feat", ring))
-    return lists
+    return lax.ppermute(share, "feat", [(i, (i + 1) % n_feat) for i in range(n_feat)])
 
 
 def choose(shares, n_chip, after=()):
@@ -265,7 +271,7 @@
         body, bits, [turned_own, turned_other, turned_own, turned_other, columns],
         [of_path(0), of_path(0), of_path(1), of_path(1), whole(columns)],
         [like((out_rows, batch), BF16)] * 2, [out_spec] * 2, grid=(steps,), after=after,
-        flops=8 * out_rows * depth * batch, moved=8 * out_rows * depth + 4 * batch * depth, limit=22, name="forward",
+        flops=8 * out_rows * depth * batch, moved=8 * out_rows * depth + 4 * batch * depth, name="forward",
     )
 
 
@@ -511,25 +517,37 @@
     def bits_at(level):
         return jnp.stack([bit_value("dp", order[level]) for order in orders])
 
-    shares = [go_round(parts) for parts in shares_of(view_features)]
+    shares = [[[part] for part in parts] for parts in shares_of(view_features)]
+    for step in range(1, n_feat):
+        if step == 2:
+            sent, turned_own, weight_squares = turn_weight(weight, core, after=[shares[1][0][-1]])
+            shares[1][0][-1] = relay(shares[1][0][-1], [turned_own])
+        for part in shares[1] + shares[0]:
+            part.append(ring_step(part[-1]))
+    turned_other = swap(sent, "dp", 1)
+
     def cross_plane(part, after=()):
         own = list(choose(part, n_chip, after=after))
         for mask in range(1, n_chip):
             own[mask] = swap(own[mask], "dp", 2 * mask)
         return own
 
-    def both_cores(images):
-        return assemble(place, images, swap(images, "dp", 1), view_features.shape[1])
+    def both_cores(own, collect_after=(), after=()):
+        images = collect(place, own, after=collect_after)
+        other = swap(images, "dp", 1)
+        return assemble(place, images, other, view_features.shape[1], after=after)
 
     def send_on(v, level, send):
         return [swap(send[p], "dp", 1 << orders[p][level]) for p in range(2)]
 
-    def sum_plane(rows, after=()):
-        others = [swap(rows[mask], "dp", 2 * mask) for mask in range(1, n_chip)]
-        return add_up([rows[0], *others], after=after)
-
-    def sum_line(total, bit, after=()):
-        return add_up([total, swap(total, "feat", 1 << bit)], after=after)
+    def sum_plane(rows):
+        total = rows[0].astype(F32)
+        for mask in range(1, n_chip):
+            total += swap(rows[mask], "dp", 2 * mask).astype(F32)
+        return total.astype(BF16)
+
+    def sum_line(total, bit):
+        return (total.astype(F32) + swap(total, "feat", 1 << bit).astype(F32)).astype(BF16)
 
     def spread_gram(total, after=()):
         parts = [total] + [swap(total, "dp", 2 * mask) for mask in range(1, n_chip)]
@@ -541,48 +559,46 @@
         other = [swap(part, "dp", 1 << bit) for part, bit in zip(parts, bits)]
         return join_all(parts, other, [bit_value("dp", bit) for bit in bits], after=after)
 
-    def with_swapped(parts):
-        return [one for own in parts for one in (own, swap(own, "dp", 1))]
-
     columns, turned, send, keep, got, gram, normed, half, inverse, rows = (
         [None] * 2 for _ in range(10)
     )
     bits = bits_at(0)
     line_bits = range(n_feat.bit_length() - 1)
     pieces = [cross_plane(part) for part in shares[1]]
-    sent, turned_own, weight_squares = turn_weight(weight, core, after=[pieces[1][0]])
-    turned_other = swap(sent, "dp", 1)
-    images = collect(place, pieces, after=[turned_own, shares[0][0][-2]])
-    columns[1] = both_cores(images)
+    columns[1] = both_cores(pieces, collect_after=[turned_own, shares[0][0][-2]])
     turned[1] = turn_columns(columns[1])
-    images = collect(place, [cross_plane(part, [images]) for part in shares[0]])
-    send[1] = forward(1 - bits, turned_own, turned_other, columns[1], after=[images])
+    send[1] = forward(1 - bits, turned_own, turned_other, columns[1])
     got[1] = send_on(1, 0, send[1])
+    pieces = [cross_plane(part, [send[1][0]]) for part in shares[0]]
     keep[1] = forward(bits, turned_own, turned_other, columns[1], after=[turned[1], send[1][0]])
-    columns[0] = both_cores(images)
+    for level in range(1, len(high)):
+        send[1], keep[1] = add_halves(bits_at(level), keep[1], got[1])
+        got[1] = send_on(1, level, send[1])
+    columns[0] = both_cores(pieces, [send[1][0]])
     turned[0] = turn_columns(columns[0])
-    send[0] = forward(1 - bits, turned_own, turned_other, columns[0], after=[keep[1][0]])
+    send[0] = forward(1 - bits, turned_own, turned_other, columns[0])
+    ahead = [send[0][0]]
     got[0] = send_on(0, 0, send[0])
-    keep[0] = forward(bits, turned_own, turned_other, columns[0], after=[turned[0], send[0][0]])
-    ahead = [keep[0][0]]
-    for level in range(1, len(high)):
-        for v in (1, 0):
-            send[v], keep[v] = add_halves(bits_at(level), keep[v], got[v], after=ahead)
-            got[v] = send_on(v, level, send[v])
-            ahead = [send[v][0]]
     normed[1], half[1], inverse[1] = normalise(keep[1], got[1], after=ahead)
     rows[1] = list(gram_rows(place, half[1], swap(half[1], "dp", 1), n_chip))
-    normed[0], half[0], inverse[0] = normalise(keep[0], got[0], after=[rows[1][0]])
+    keep[0] = forward(bits, turned_own, turned_other, columns[0], after=[turned[0], send[1][0]])
+    for level in range(1, len(high)):
+        send[0], keep[0] = add_halves(bits_at(level), keep[0], got[0], after=[rows[1][0]])
+        got[0] = send_on(0, level, send[0])
+    gram[1] = sum_plane(rows[1])
+    normed[0], half[0], inverse[0] = normalise(keep[0], got[0], after=[gram[1]])
     rows[0] = list(gram_rows(place, half[0], swap(half[0], "dp", 1), n_chip))
-    gram[1] = sum_plane(rows[1], after=[rows[0][0]])
-    gram[0] = sum_plane(rows[0], after=[gram[1]])
     for bit in line_bits:
-        gram[1] = sum_line(gram[1], bit, after=[gram[0]])
-        gram[0] = sum_line(gram[0], bit, after=[gram[1]])
-    gram[0] = spread_gram(gram[0])
-    gram[1] = spread_gram(gram[1], after=[gram[0][0]])
+        gram[1] = sum_line(gram[1], bit)
+    gram[1] = spread_gram(gram[1])
+    gram[0] = sum_plane(rows[0])
+    for bit in line_bits:
+        gram[0] = sum_line(gram[0], bit)
     out_grad = [None] * 2
-    out_grad[0] = out_grad_of(place, *gram[1], normed[0], half[0], half[1], inverse[0])
+    out_grad[0] = out_grad_of(
+        place, *gram[1], normed[0], half[0], half[1], inverse[0], after=[gram[0]]
+    )
+    gram[0] = spread_gram(gram[0], after=[out_grad[0]])
     share = out_grad[0].shape[0] // 2
     out_grad[1] = out_grad_of(place, *gram[0], normed[1], half[1], half[0], inverse[1])
     parts = [one for grad in out_grad for one in (grad[:share], grad[share:])]

time: 304 us -> 286 us (0.941)
  waiting for transfers between devices: 155 us -> 136 us
    ppermute x9, waiting for transfers between devices: 49.2 us -> 27.9 us  [ring_step(): lax.ppermute(share, 'feat', [(i, (i + 1) % n_feat) for i in range(n_feat)])]
    pallas_call x36 -> x31, Pallas kernels: 70.9 us -> 70.6 us  [run(): pl.pallas_call(kernel, grid_spec=pltpu.PrefetchScalarGridSpec(num_scalar_...]
  transfers between devices with their start and end apart: 68 -> 68, of which waited for: 40 -> 45; matrix products, arithmetic and copies ran while one was open for 0% -> 0% of each run, Pallas kernels for 18% -> 18%
where the time goes in v9:
time: 286 us; the launch traced here: 285 us
  waiting for transfers between devices  136 us (48%)
  Pallas kernels  70.6 us (25%)
  starting transfers between devices  69.9 us (24%)
  local copies, waits for them, and re-layouts  6.91 us (2%)
    ppermute x52, waiting for transfers between devices, swap(): lax.ppermute(value, axis, [(i, i ^ mask) for i in range(lax.axis_size(axi...  99.2 us
    pallas_call x31, Pallas kernels, run(): pl.pallas_call(kernel, grid_spec=pltpu.PrefetchScalarGridSpec(num_scalar_...  70.6 us
    ppermute x52, starting transfers between devices, swap(): lax.ppermute(value, axis, [(i, i ^ mask) for i in range(lax.axis_size(axi...  52.8 us
    ppermute x9, waiting for transfers between devices, ring_step(): lax.ppermute(share, 'feat', [(i, (i + 1) % n_feat) for i in range(n_feat)])  27.9 us
    ppermute x9, starting transfers between devices, ring_step(): lax.ppermute(share, 'feat', [(i, (i + 1) % n_feat) for i in range(n_feat)])  9.32 us
    ppermute x7, waiting for transfers between devices, sum_everywhere(): lax.ppermute(value, axes, [(i, i ^ mask) for i in range(count)])  8.77 us
    ppermute x7, starting transfers between devices, sum_everywhere(): lax.ppermute(value, axes, [(i, i ^ mask) for i in range(count)])  7.83 us
    unnamed x28, local copies, waits for them, and re-layouts  6.84 us
  transfers between devices with their start and end apart: 68, of which 45 were waited for; matrix products, arithmetic and copies ran while one was open for 0% of the time, Pallas kernels for 18%

profile of v9, /device:TPU:0, one launch (start us, length us, event | category | flops | bytes accessed | tf_op | source)
XLA Modules:
  0.0 285.2 jit_solution(1576147439074050417)
XLA Ops:
  1.9 3.1 %collective-permute-start.10 = (bf16[64,2048]{1,0:T(8,128)(2,1)S(1)}, bf16[64,2048]{1,0:T(8,128)(2,1)}, u32[]{:S(2)}, u32[]{:S(2)}) collective-permute-start(bf16[64,2048]{1,0:T(8,128)(2,1)S(1)} %get-tuple-element.70.refs_0_), channel_id=1, source_target_pairs={{0,1},{1,2},{2,3},{3,0},{4,5},{5,6},{6,7},{7,4},{8,9},{9,10},{10,1... | collective-permute-start | bytes 786440 | tf_op jit(solution)/shard_map/ppermute | solution.py:161
  8.0 6.3 %collective-permute-done.10.refs_1_ = bf16[64,2048]{1,0:T(8,128)(2,1)} collective-permute-done((bf16[64,2048]{1,0:T(8,128)(2,1)S(1)}, bf16[64,2048]{1,0:T(8,128)(2,1)}, u32[]{:S(2)}, u32[]{:S(2)}) %collective-permute-start.10) | collective-permute-done | bytes 262176 | tf_op jit(solution)/shard_map/ppermute | solution.py:161
  15.9 3.9 %collective-permute-done.3.refs_1_.refs_0_ = bf16[64,2048]{1,0:T(8,128)(2,1)S(1)} collective-permute-done((bf16[64,2048]{1,0:T(8,128)(2,1)S(1)}, bf16[64,2048]{1,0:T(8,128)(2,1)S(1)}, u32[]{:S(2)}, u32[]{:S(2)}) %collective-permute-start.3) | collective-permute-done | bytes 262176 | tf_op jit(solution)/shard_map/ppermute | solution.py:161
  20.5 8.5 %turn_weight.1 = (bf16[1024,1024]{1,0:T(8,128)(2,1)}, bf16[1024,1024]{1,0:T(8,128)(2,1)}, f32[16,128]{1,0:T(8,128)}) custom-call(s32[1]{0:T(128)} %bitcast.1.scalars_ref, f32[1024,2048]{1,0:T(8,128)} %refs_2_.1, bf16[64,2048]{1,0:T(8,128)(2,1)} %copy-done.3), custom_call_target="tpu_custom_call" | custom-call | flops 4194304 | bytes 12582912 | tf_op jit(solution)/shard_map/turn_weight/pallas_call | solution.py:61
  33.3 9.5 %collective-permute-done.5.refs_2_ = bf16[64,2048]{1,0:T(8,128)(2,1)} collective-permute-done((bf16[64,2048]{1,0:T(8,128)(2,1)S(1)}, bf16[64,2048]{1,0:T(8,128)(2,1)}, u32[]{:S(2)}, u32[]{:S(2)}) %collective-permute-start.5) | collective-permute-done | bytes 262176 | tf_op jit(solution)/shard_map/ppermute | solution.py:161
  42.7 5.5 %collective-permute-done.12.refs_3_ = bf16[64,2048]{1,0:T(8,128)(2,1)S(1)} collective-permute-done((bf16[64,2048]{1,0:T(8,128)(2,1)}, bf16[64,2048]{1,0:T(8,128)(2,1)S(1)}, u32[]{:S(2)}, u32[]{:S(2)}) %collective-permute-start.12) | collective-permute-done | bytes 262176 | tf_op jit(solution)/shard_map/ppermute | solution.py:161
  50.0 1.8 collective-permute-start.13
  56.2 1.8 collective-permute-start.7
  59.3 1.8 collective-permute-start.8
  63.8 2.5 collective-permute-done.15.refs_7_
  66.3 3.8 %collective-permute-done.7.refs_1_ = bf16[64,2048]{1,0:T(8,128)(2,1)S(1)} collective-permute-done((bf16[64,2048]{1,0:T(8,128)(2,1)S(1)}, bf16[64,2048]{1,0:T(8,128)(2,1)S(1)}, u32[]{:S(2)}, u32[]{:S(2)}) %collective-permute-start.7) | collective-permute-done | bytes 262176 | tf_op jit(solution)/shard_map/ppermute | solution.py:19
  70.1 3.7 %collective-permute-done.8.refs_2_ = bf16[64,2048]{1,0:T(8,128)(2,1)S(1)} collective-permute-done((bf16[64,2048]{1,0:T(8,128)(2,1)S(1)}, bf16[64,2048]{1,0:T(8,128)(2,1)S(1)}, u32[]{:S(2)}, u32[]{:S(2)}) %collective-permute-start.8) | collective-permute-done | bytes 262176 | tf_op jit(solution)/shard_map/ppermute | solution.py:19
  73.8 2.0 collect.2.refs_0_
  77.8 2.5 collective-permute-done.16.refs_1_
  80.3 3.0 %assemble.2.refs_4_.refs_0_ = bf16[1024,2048]{1,0:T(8,128)(2,1)S(1)} custom-call(s32[2]{0:T(128)S(1)} %pad_add_fusion.scalars_ref, bf16[512,2048]{1,0:T(8,128)(2,1)} %collect.2.refs_0_, bf16[512,2048]{1,0:T(8,128)(2,1)} %collective-permute-done.16.refs_1_), custom_call_target="tpu_custom_call" | custom-call | bytes 8388608 | tf_op jit(solution)/shard_map/assemble/pallas_call | solution.py:61
  83.3 4.2 %forward.4 = (bf16[256,1024]{1,0:T(8,128)(2,1)S(1)}, bf16[256,1024]{1,0:T(8,128)(2,1)S(1)}) custom-call(s32[2]{0:T(128)S(1)} %get-tuple-element.122.scalars_ref, bf16[1024,1024]{1,0:T(8,128)(2,1)S(1)} %copy-done.1, bf16[1024,1024]{1,0:T(8,128)(2,1)} %collective-permute-done.4.refs_1_.refs_3_, bf16[1024,1024]{1,0:T(8,128)(2,1)S(1)} %copy-done.1, ...), custom_call_target="tpu_custom_call" | custom-call | flops 2147483648 | bytes 6291456 | tf_op jit(solution)/shard_map/forward/pallas_call | solution.py:61
  89.7 2.8 collective-permute-done.2.refs_3_
  92.4 2.2 choose.5
  96.4 1.8 collective-permute-start.19
  99.5 4.2 %forward.5 = (bf16[256,1024]{1,0:T(8,128)(2,1)S(1)}, bf16[256,1024]{1,0:T(8,128)(2,1)S(1)}) custom-call(s32[2]{0:T(128)S(1)} %get-tuple-element.123.scalars_ref, bf16[1024,1024]{1,0:T(8,128)(2,1)S(1)} %copy-done.1, bf16[1024,1024]{1,0:T(8,128)(2,1)} %collective-permute-done.4.refs_1_.refs_3_, bf16[1024,1024]{1,0:T(8,128)(2,1)S(1)} %copy-done.1, ...), custom_call_target="tpu_custom_call" | custom-call | flops 2147483648 | bytes 6291456 | tf_op jit(solution)/shard_map/forward/pallas_call | solution.py:61
  104.7 10.4 %collective-permute-done.17.refs_1_ = bf16[128,2048]{1,0:T(8,128)(2,1)S(1)} collective-permute-done((bf16[128,2048]{1,0:T(8,128)(2,1)S(1)}, bf16[128,2048]{1,0:T(8,128)(2,1)S(1)}, u32[]{:S(2)}, u32[]{:S(2)}) %collective-permute-start.17) | collective-permute-done | bytes 524320 | tf_op jit(solution)/shard_map/ppermute | solution.py:19
  115.2 10.0 %collective-permute-done.19.refs_3_ = bf16[128,2048]{1,0:T(8,128)(2,1)S(1)} collective-permute-done((bf16[128,2048]{1,0:T(8,128)(2,1)S(1)}, bf16[128,2048]{1,0:T(8,128)(2,1)S(1)}, u32[]{:S(2)}, u32[]{:S(2)}) %collective-permute-start.19) | collective-permute-done | bytes 524320 | tf_op jit(solution)/shard_map/ppermute | solution.py:19
  128.1 2.0 collective-permute-done.22.refs_1_
  131.0 4.2 %forward.6 = (bf16[256,1024]{1,0:T(8,128)(2,1)S(1)}, bf16[256,1024]{1,0:T(8,128)(2,1)S(1)}) custom-call(s32[2]{0:T(128)S(1)} %get-tuple-element.122.scalars_ref, bf16[1024,1024]{1,0:T(8,128)(2,1)S(1)} %copy-done.1, bf16[1024,1024]{1,0:T(8,128)(2,1)} %collective-permute-done.4.refs_1_.refs_3_, bf16[1024,1024]{1,0:T(8,128)(2,1)S(1)} %copy-done.1, ...), custom_call_target="tpu_custom_call" | custom-call | flops 2147483648 | bytes 6291456 | tf_op jit(solution)/shard_map/forward/pallas_call | solution.py:61
  143.2 1.7 collective-permute-start.28
  144.9 4.2 %forward.7 = (bf16[256,1024]{1,0:T(8,128)(2,1)S(1)}, bf16[256,1024]{1,0:T(8,128)(2,1)S(1)}) custom-call(s32[2]{0:T(128)S(1)} %get-tuple-element.123.scalars_ref, bf16[1024,1024]{1,0:T(8,128)(2,1)S(1)} %copy-done.1, bf16[1024,1024]{1,0:T(8,128)(2,1)} %collective-permute-done.4.refs_1_.refs_3_, bf16[1024,1024]{1,0:T(8,128)(2,1)S(1)} %copy-done.1, ...), custom_call_target="tpu_custom_call" | custom-call | flops 2147483648 | bytes 6291456 | tf_op jit(solution)/shard_map/forward/pallas_call | solution.py:61
  149.1 1.8 collective-permute-done.36.refs_3_
  155.6 3.9 %collective-permute-done.28 = bf16[128,640]{1,0:T(8,128)(2,1)S(1)} collective-permute-done((bf16[128,640]{1,0:T(8,128)(2,1)S(1)}, bf16[128,640]{1,0:T(8,128)(2,1)S(1)}, u32[]{:S(2)}, u32[]{:S(2)}) %collective-permute-start.28) | collective-permute-done | bytes 163872 | tf_op jit(solution)/shard_map/ppermute | solution.py:19
  160.7 2.5 collective-permute-done.37.refs_1_
  165.1 2.1 collective-permute-start.30
  172.1 3.4 %collective-permute-done.30 = bf16[128,640]{1,0:T(8,128)(2,1)S(1)} collective-permute-done((bf16[128,640]{1,0:T(8,128)(2,1)S(1)}, bf16[128,640]{1,0:T(8,128)(2,1)S(1)}, u32[]{:S(2)}, u32[]{:S(2)}) %collective-permute-start.30) | collective-permute-done | bytes 163872 | tf_op jit(solution)/shard_map/ppermute | solution.py:19
  179.1 3.5 %collective-permute-done.41 = bf16[128,640]{1,0:T(8,128)(2,1)S(1)} collective-permute-done((bf16[128,640]{1,0:T(8,128)(2,1)S(1)}, bf16[128,640]{1,0:T(8,128)(2,1)S(1)}, u32[]{:S(2)}, u32[]{:S(2)}) %collective-permute-start.41) | collective-permute-done | bytes 163872 | tf_op jit(solution)/shard_map/ppermute | solution.py:19
  182.7 2.8 collective-permute-start.43
  186.2 2.6 collective-permute-done.43
  188.9 1.8 collective-permute-start.44
  190.6 6.7 %collective-permute-done.44 = bf16[128,640]{1,0:T(8,128)(2,1)S(1)} collective-permute-done((bf16[128,640]{1,0:T(8,128)(2,1)S(1)}, bf16[128,640]{1,0:T(8,128)(2,1)S(1)}, u32[]{:S(2)}, u32[]{:S(2)}) %collective-permute-start.44) | collective-permute-done | bytes 163872 | tf_op jit(solution)/shard_map/ppermute | solution.py:19
  201.0 2.3 out_grad_of.2.refs_4_
  208.3 2.4 out_grad_of.3
  212.9 2.5 collective-permute-done.50.refs_5_
  216.5 4.1 %collective-permute-done.52.refs_7_ = bf16[128,1024]{1,0:T(8,128)(2,1)S(1)} collective-permute-done((bf16[128,1024]{1,0:T(8,128)(2,1)S(1)}, bf16[128,1024]{1,0:T(8,128)(2,1)S(1)}, u32[]{:S(2)}, u32[]{:S(2)}) %collective-permute-start.52) | collective-permute-done | bytes 262176 | tf_op jit(solution)/shard_map/ppermute | solution.py:19
  226.3 10.7 %collective-permute-done.53.refs_4_ = bf16[256,1024]{1,0:T(8,128)(2,1)S(1)} collective-permute-done((bf16[256,1024]{1,0:T(8,128)(2,1)S(1)}, bf16[256,1024]{1,0:T(8,128)(2,1)S(1)}, u32[]{:S(2)}, u32[]{:S(2)}) %collective-permute-start.53) | collective-permute-done | bytes 524320 | tf_op jit(solution)/shard_map/ppermute | solution.py:19
  238.0 8.6 %collective-permute-done.55.refs_6_ = bf16[256,1024]{1,0:T(8,128)(2,1)S(1)} collective-permute-done((bf16[256,1024]{1,0:T(8,128)(2,1)S(1)}, bf16[256,1024]{1,0:T(8,128)(2,1)S(1)}, u32[]{:S(2)}, u32[]{:S(2)}) %collective-permute-start.55) | collective-permute-done | bytes 524320 | tf_op jit(solution)/shard_map/ppermute | solution.py:19
  249.2 5.9 %weight_grad_of.2 = (f32[1024,2048]{1,0:T(8,128)S(1)}, f32[16,128]{1,0:T(8,128)S(1)}) custom-call(s32[2]{0:T(128)S(1)} %pad_add_fusion.scalars_ref, bf16[1024,1024]{1,0:T(8,128)(2,1)S(1)} %turn_columns.3.refs_5_.refs_0_, bf16[1024,1024]{1,0:T(8,128)(2,1)S(1)} %turn_columns.2.refs_5_.refs_1_, bf16[512,1024]{1,0:T(8,128)(2,1)S(1)} %get-tuple-element.113.refs_2_, ...), custom_call_target="tpu_custom_call" | custom-call | flops 4294967296 | bytes 4194304 | tf_op jit(solution)/shard_map/weight_grad_of/pallas_call | solution.py:61
  255.3 5.6 %weight_grad_of.3 = (f32[1024,2048]{1,0:T(8,128)S(1)}, f32[16,128]{1,0:T(8,128)S(1)}) custom-call(s32[2]{0:T(128)S(1)} %pad_add_fusion.scalars_ref, bf16[1024,1024]{1,0:T(8,128)(2,1)S(1)} %turn_columns.3.refs_5_.refs_0_, bf16[1024,1024]{1,0:T(8,128)(2,1)S(1)} %turn_columns.2.refs_5_.refs_1_, ...), custom_call_target="tpu_custom_call", output_to_operand_aliasing={{0}: (8, {})} | custom-call | flops 4294967296 | bytes 4194304 | tf_op jit(solution)/shard_map/weight_grad_of/pallas_call | solution.py:61
  261.0 4.5 %collective-permute-start.63 = (f32[16,128]{1,0:T(8,128)S(1)}, f32[16,128]{1,0:T(8,128)S(1)}, u32[]{:S(2)}, u32[]{:S(2)}) collective-permute-start(f32[16,128]{1,0:T(8,128)S(1)} %get-tuple-element.120), channel_id=1, source_target_pairs={{0,3},{1,2},{2,1},{3,0},{4,7},{5,6},{6,5},{7,4},{8,11},{9,10},{10,... | collective-permute-start | bytes 24584 | tf_op jit(solution)/shard_map/ppermute | solution.py:40
  267.2 2.9 %collective-permute-done.62 = f32[16,128]{1,0:T(8,128)S(1)} collective-permute-done((f32[16,128]{1,0:T(8,128)S(1)}, f32[16,128]{1,0:T(8,128)S(1)}, u32[]{:S(2)}, u32[]{:S(2)}) %collective-permute-start.62) | collective-permute-done | bytes 8224 | tf_op jit(solution)/shard_map/ppermute | solution.py:40
  274.7 3.0 %collective-permute-done.67.refs_1_ = f32[16,128]{1,0:T(8,128)S(1)} collective-permute-done((f32[16,128]{1,0:T(8,128)S(1)}, f32[16,128]{1,0:T(8,128)S(1)}, u32[]{:S(2)}, u32[]{:S(2)}) %collective-permute-start.67) | collective-permute-done | bytes 8224 | tf_op jit(solution)/shard_map/ppermute | solution.py:40
  277.7 7.5 %update.1 = (f32[1024,2048]{1,0:T(8,128)}, f32[1024,2048]{1,0:T(8,128)}) custom-call(s32[1]{0:T(128)} %constant.21.clone.1.scalars_ref, f32[16,128]{1,0:T(8,128)S(1)} %add_add_fusion.refs_0_, f32[16,128]{1,0:T(8,128)S(1)} %collective-permute-done.67.refs_1_, f32[1024,2048]{1,0:T(8,128)S(1)} %bitcast.9, f32[1024,2048]{1,0:T(8,128)S(1)} %bitcast.11, ...), custom_call_target="tpu_custom_call" | custom-call | flops 8388608 | bytes 41943040 | tf_op jit(solution)/shard_map/update/pallas_call | solution.py:61
  (165 shorter events, 85.5 us)
Async XLA Ops:
  1.9 12.3 %collective-permute-start.10 = (bf16[64,2048]{1,0:T(8,128)(2,1)S(1)}, bf16[64,2048]{1,0:T(8,128)(2,1)}, u32[]{:S(2)}, u32[]{:S(2)}) collective-permute-start(bf16[64,2048]{1,0:T(8,128)(2,1)S(1)} %get-tuple-element.70.refs_0_), channel_id=1, source_target_pairs={{0,1},{1,2},{2,3},{3,0},{4,5},{5,6},{6,7},{7,4},{8,9},{9,10},{10,1... | collective-permute-start | bytes 786440 | tf_op jit(solution)/shard_map/ppermute | solution.py:161
  5.7 14.1 %collective-permute-start.3 = (bf16[64,2048]{1,0:T(8,128)(2,1)S(1)}, bf16[64,2048]{1,0:T(8,128)(2,1)S(1)}, u32[]{:S(2)}, u32[]{:S(2)}) collective-permute-start(bf16[64,2048]{1,0:T(8,128)(2,1)S(1)} %get-tuple-element.63.refs_0_), channel_id=1, source_target_pairs={{0,1},{1,2},{2,3},{3,0},{4,5},{5,6},{6,7},{7,4},{8,9},{9,10},{10,1... | collective-permute-start | bytes 786440 | tf_op jit(solution)/shard_map/ppermute | solution.py:161
  14.3 17.4 %collective-permute-start.11 = (bf16[64,2048]{1,0:T(8,128)(2,1)}, bf16[64,2048]{1,0:T(8,128)(2,1)}, u32[]{:S(2)}, u32[]{:S(2)}) collective-permute-start(bf16[64,2048]{1,0:T(8,128)(2,1)} %collective-permute-done.10.refs_1_), channel_id=1, source_target_pairs={{0,1},{1,2},{2,3},{3,0},{4,5},{5,6},{6,7},{7,4},{8,9},{9,10},{10,1... | collective-permute-start | bytes 786440 | tf_op jit(solution)/shard_map/ppermute | solution.py:161
  14.3 37.5 %collective-permute-start = (bf16[128,2048]{1,0:T(8,128)(2,1)S(1)}, bf16[128,2048]{1,0:T(8,128)(2,1)}, u32[]{:S(2)}, u32[]{:S(2)}) collective-permute-start(bf16[128,2048]{1,0:T(8,128)(2,1)S(1)} %get-tuple-element.62.refs_0_), channel_id=1, source_target_pairs={{0,1},{1,2},{2,3},{3,0},{4,5},{5,6},{6,7},{7,4},{8,9},{9,10},{10,1... | collective-permute-start | bytes 1572872 | tf_op jit(solution)/shard_map/ppermute | solution.py:161
  31.5 11.2 %collective-permute-start.5 = (bf16[64,2048]{1,0:T(8,128)(2,1)S(1)}, bf16[64,2048]{1,0:T(8,128)(2,1)}, u32[]{:S(2)}, u32[]{:S(2)}) collective-permute-start(bf16[64,2048]{1,0:T(8,128)(2,1)S(1)} %relay.1.refs_1_), channel_id=1, source_target_pairs={{0,1},{1,2},{2,3},{3,0},{4,5},{5,6},{6,7},{7,4},{8,9},{9,10},{10,1... | collective-permute-start | bytes 786440 | tf_op jit(solution)/shard_map/ppermute | solution.py:161
  31.6 16.6 %collective-permute-start.12 = (bf16[64,2048]{1,0:T(8,128)(2,1)}, bf16[64,2048]{1,0:T(8,128)(2,1)S(1)}, u32[]{:S(2)}, u32[]{:S(2)}) collective-permute-start(bf16[64,2048]{1,0:T(8,128)(2,1)} %collective-permute-done.11.refs_2_), channel_id=1, source_target_pairs={{0,1},{1,2},{2,3},{3,0},{4,5},{5,6},{6,7},{7,4},{8,9},{9,10},{10,1... | collective-permute-start | bytes 786440 | tf_op jit(solution)/shard_map/ppermute | solution.py:161
  42.7 10.8 %collective-permute-start.6 = (bf16[64,2048]{1,0:T(8,128)(2,1)}, bf16[64,2048]{1,0:T(8,128)(2,1)S(1)}, u32[]{:S(2)}, u32[]{:S(2)}) collective-permute-start(bf16[64,2048]{1,0:T(8,128)(2,1)} %collective-permute-done.5.refs_2_), channel_id=1, source_target_pairs={{0,1},{1,2},{2,3},{3,0},{4,5},{5,6},{6,7},{7,4},{8,9},{9,10},{10,1... | collective-permute-start | bytes 786440 | tf_op jit(solution)/shard_map/ppermute | solution.py:161
  50.0 9.3 %collective-permute-start.13 = (bf16[64,2048]{1,0:T(8,128)(2,1)S(1)}, bf16[64,2048]{1,0:T(8,128)(2,1)S(1)}, u32[]{:S(2)}, u32[]{:S(2)}) collective-permute-start(bf16[64,2048]{1,0:T(8,128)(2,1)S(1)} %get-tuple-element.72), channel_id=1, source_target_pairs={{0,8},{4,12},{8,0},{12,4},{16,24},{20,28},{24,16},{28,20},{1,9},{5... | collective-permute-start | bytes 786440 | tf_op jit(solution)/shard_map/ppermute | solution.py:19
  51.8 14.5 %collective-permute-start.1 = (bf16[128,2048]{1,0:T(8,128)(2,1)}, bf16[128,2048]{1,0:T(8,128)(2,1)S(1)}, u32[]{:S(2)}, u32[]{:S(2)}) collective-permute-start(bf16[128,2048]{1,0:T(8,128)(2,1)} %collective-permute-done.refs_1_), channel_id=1, source_target_pairs={{0,1},{1,2},{2,3},{3,0},{4,5},{5,6},{6,7},{7,4},{8,9},{9,10},{10,1... | collective-permute-start | bytes 1572872 | tf_op jit(solution)/shard_map/ppermute | solution.py:161
  51.8 10.5 %collective-permute-start.14 = (bf16[64,2048]{1,0:T(8,128)(2,1)S(1)}, bf16[64,2048]{1,0:T(8,128)(2,1)S(1)}, u32[]{:S(2)}, u32[]{:S(2)}) collective-permute-start(bf16[64,2048]{1,0:T(8,128)(2,1)S(1)} %get-tuple-element.73), channel_id=1, source_target_pairs={{0,16},{4,20},{8,24},{12,28},{16,0},{20,4},{24,8},{28,12},{1,17},{... | collective-permute-start | bytes 786440 | tf_op jit(solution)/shard_map/ppermute | solution.py:19
  53.3 12.9 %collective-permute-start.15 = (bf16[64,2048]{1,0:T(8,128)(2,1)S(1)}, bf16[64,2048]{1,0:T(8,128)(2,1)S(1)}, u32[]{:S(2)}, u32[]{:S(2)}) collective-permute-start(bf16[64,2048]{1,0:T(8,128)(2,1)S(1)} %get-tuple-element.74), channel_id=1, source_target_pairs={{0,24},{4,28},{8,16},{12,20},{16,8},{20,12},{24,0},{28,4},{1,25},{... | collective-permute-start | bytes 786440 | tf_op jit(solution)/shard_map/ppermute | solution.py:19
  56.2 13.9 %collective-permute-start.7 = (bf16[64,2048]{1,0:T(8,128)(2,1)S(1)}, bf16[64,2048]{1,0:T(8,128)(2,1)S(1)}, u32[]{:S(2)}, u32[]{:S(2)}) collective-permute-start(bf16[64,2048]{1,0:T(8,128)(2,1)S(1)} %get-tuple-element.67), channel_id=1, source_target_pairs={{0,8},{4,12},{8,0},{12,4},{16,24},{20,28},{24,16},{28,20},{1,9},{5... | collective-permute-start | bytes 786440 | tf_op jit(solution)/shard_map/ppermute | solution.py:19
  59.3 14.5 %collective-permute-start.8 = (bf16[64,2048]{1,0:T(8,128)(2,1)S(1)}, bf16[64,2048]{1,0:T(8,128)(2,1)S(1)}, u32[]{:S(2)}, u32[]{:S(2)}) collective-permute-start(bf16[64,2048]{1,0:T(8,128)(2,1)S(1)} %get-tuple-element.68), channel_id=1, source_target_pairs={{0,16},{4,20},{8,24},{12,28},{16,0},{20,4},{24,8},{28,12},{1,17},{... | collective-permute-start | bytes 786440 | tf_op jit(solution)/shard_map/ppermute | solution.py:19
  62.3 11.5 %collective-permute-start.9 = (bf16[64,2048]{1,0:T(8,128)(2,1)S(1)}, bf16[64,2048]{1,0:T(8,128)(2,1)S(1)}, u32[]{:S(2)}, u32[]{:S(2)}) collective-permute-start(bf16[64,2048]{1,0:T(8,128)(2,1)S(1)} %get-tuple-element.69), channel_id=1, source_target_pairs={{0,24},{4,28},{8,16},{12,20},{16,8},{20,12},{24,0},{28,4},{1,25},{... | collective-permute-start | bytes 786440 | tf_op jit(solution)/shard_map/ppermute | solution.py:19
  75.8 7.5 %collective-permute-start.4 = (bf16[1024,1024]{1,0:T(8,128)(2,1)}, bf16[1024,1024]{1,0:T(8,128)(2,1)}, u32[]{:S(2)}, u32[]{:S(2)}) collective-permute-start(bf16[1024,1024]{1,0:T(8,128)(2,1)} %get-tuple-element.65), channel_id=1, source_target_pairs={{0,4},{4,0},{8,12},{12,8},{16,20},{20,16},{24,28},{28,24},{1,5},{5... | collective-permute-start | bytes 6291464 | tf_op jit(solution)/shard_map/ppermute | solution.py:19
  76.3 16.1 %collective-permute-start.2 = (bf16[128,2048]{1,0:T(8,128)(2,1)S(1)}, bf16[128,2048]{1,0:T(8,128)(2,1)}, u32[]{:S(2)}, u32[]{:S(2)}) collective-permute-start(bf16[128,2048]{1,0:T(8,128)(2,1)S(1)} %collective-permute-done.1.refs_9_.refs_2_), channel_id=1, source_target_pairs={{0,1},{1,2},{2,3},{3,0},{4,5},{5,6},{6,7},{7,4},{8,9},{9,10},{10,1... | collective-permute-start | bytes 1572872 | tf_op jit(solution)/shard_map/ppermute | solution.py:161
  87.5 16.2 %collective-permute-start.21 = (bf16[256,1024]{1,0:T(8,128)(2,1)S(1)}, bf16[256,1024]{1,0:T(8,128)(2,1)S(1)}, u32[]{:S(2)}, u32[]{:S(2)}) collective-permute-start(bf16[256,1024]{1,0:T(8,128)(2,1)S(1)} %get-tuple-element.82), channel_id=1, source_target_pairs={{0,16},{4,20},{8,24},{12,28},{16,0},{20,4},{24,8},{28,12},{1,17},{... | collective-permute-start | bytes 1572872 | tf_op jit(solution)/shard_map/ppermute | solution.py:19
  89.1 14.8 %collective-permute-start.20 = (bf16[256,1024]{1,0:T(8,128)(2,1)S(1)}, bf16[256,1024]{1,0:T(8,128)(2,1)S(1)}, u32[]{:S(2)}, u32[]{:S(2)}) collective-permute-start(bf16[256,1024]{1,0:T(8,128)(2,1)S(1)} %get-tuple-element.75.refs_4_.refs_6_), channel_id=1, source_target_pairs={{0,8},{4,12},{8,0},{12,4},{16,24},{20,28},{24,16},{28,20},{1,9},{5... | collective-permute-start | bytes 1572872 | tf_op jit(solution)/shard_map/ppermute | solution.py:19
  94.6 20.6 %collective-permute-start.17 = (bf16[128,2048]{1,0:T(8,128)(2,1)S(1)}, bf16[128,2048]{1,0:T(8,128)(2,1)S(1)}, u32[]{:S(2)}, u32[]{:S(2)}) collective-permute-start(bf16[128,2048]{1,0:T(8,128)(2,1)S(1)} %get-tuple-element.77), channel_id=1, source_target_pairs={{0,8},{4,12},{8,0},{12,4},{16,24},{20,28},{24,16},{28,20},{1,9},{5... | collective-permute-start | bytes 1572872 | tf_op jit(solution)/shard_map/ppermute | solution.py:19
  95.5 19.7 %collective-permute-start.18 = (bf16[128,2048]{1,0:T(8,128)(2,1)S(1)}, bf16[128,2048]{1,0:T(8,128)(2,1)S(1)}, u32[]{:S(2)}, u32[]{:S(2)}) collective-permute-start(bf16[128,2048]{1,0:T(8,128)(2,1)S(1)} %get-tuple-element.78), channel_id=1, source_target_pairs={{0,16},{4,20},{8,24},{12,28},{16,0},{20,4},{24,8},{28,12},{1,17},{... | collective-permute-start | bytes 1572872 | tf_op jit(solution)/shard_map/ppermute | solution.py:19
  96.4 28.9 %collective-permute-start.19 = (bf16[128,2048]{1,0:T(8,128)(2,1)S(1)}, bf16[128,2048]{1,0:T(8,128)(2,1)S(1)}, u32[]{:S(2)}, u32[]{:S(2)}) collective-permute-start(bf16[128,2048]{1,0:T(8,128)(2,1)S(1)} %get-tuple-element.79), channel_id=1, source_target_pairs={{0,24},{4,28},{8,16},{12,20},{16,8},{20,12},{24,0},{28,4},{1,25},{... | collective-permute-start | bytes 1572872 | tf_op jit(solution)/shard_map/ppermute | solution.py:19
  126.0 9.2 %collective-permute-start.24 = (bf16[128,1024]{1,0:T(8,128)(2,1)S(1)}, bf16[128,1024]{1,0:T(8,128)(2,1)S(1)}, u32[]{:S(2)}, u32[]{:S(2)}) collective-permute-start(bf16[128,1024]{1,0:T(8,128)(2,1)S(1)} %get-tuple-element.86), channel_id=1, source_target_pairs={{0,8},{4,12},{8,0},{12,4},{16,24},{20,28},{24,16},{28,20},{1,9},{5... | collective-permute-start | bytes 786440 | tf_op jit(solution)/shard_map/ppermute | solution.py:19
  127.3 8.4 %collective-permute-start.23 = (bf16[128,1024]{1,0:T(8,128)(2,1)S(1)}, bf16[128,1024]{1,0:T(8,128)(2,1)S(1)}, u32[]{:S(2)}, u32[]{:S(2)}) collective-permute-start(bf16[128,1024]{1,0:T(8,128)(2,1)S(1)} %get-tuple-element.83.refs_4_.refs_6_), channel_id=1, source_target_pairs={{0,16},{4,20},{8,24},{12,28},{16,0},{20,4},{24,8},{28,12},{1,17},{... | collective-permute-start | bytes 786440 | tf_op jit(solution)/shard_map/ppermute | solution.py:19
  136.2 14.8 %collective-permute-start.36 = (bf16[256,1024]{1,0:T(8,128)(2,1)S(1)}, bf16[256,1024]{1,0:T(8,128)(2,1)S(1)}, u32[]{:S(2)}, u32[]{:S(2)}) collective-permute-start(bf16[256,1024]{1,0:T(8,128)(2,1)S(1)} %get-tuple-element.95), channel_id=1, source_target_pairs={{0,16},{4,20},{8,24},{12,28},{16,0},{20,4},{24,8},{28,12},{1,17},{... | collective-permute-start | bytes 1572872 | tf_op jit(solution)/shard_map/ppermute | solution.py:19
  137.3 14.8 %collective-permute-start.35 = (bf16[256,1024]{1,0:T(8,128)(2,1)S(1)}, bf16[256,1024]{1,0:T(8,128)(2,1)S(1)}, u32[]{:S(2)}, u32[]{:S(2)}) collective-permute-start(bf16[256,1024]{1,0:T(8,128)(2,1)S(1)} %get-tuple-element.87.refs_4_), channel_id=1, source_target_pairs={{0,8},{4,12},{8,0},{12,4},{16,24},{20,28},{24,16},{28,20},{1,9},{5... | collective-permute-start | bytes 1572872 | tf_op jit(solution)/shard_map/ppermute | solution.py:19
  141.4 14.2 %collective-permute-start.26 = (bf16[128,640]{1,0:T(8,128)(2,1)S(1)}, bf16[128,640]{1,0:T(8,128)(2,1)S(1)}, u32[]{:S(2)}, u32[]{:S(2)}) collective-permute-start(bf16[128,640]{1,0:T(8,128)(2,1)S(1)} %get-tuple-element.90), channel_id=1, source_target_pairs={{0,8},{4,12},{8,0},{12,4},{16,24},{20,28},{24,16},{28,20},{1,9},{5... | collective-permute-start | bytes 491528 | tf_op jit(solution)/shard_map/ppermute | solution.py:19
  142.2 13.4 %collective-permute-start.27 = (bf16[128,640]{1,0:T(8,128)(2,1)S(1)}, bf16[128,640]{1,0:T(8,128)(2,1)S(1)}, u32[]{:S(2)}, u32[]{:S(2)}) collective-permute-start(bf16[128,640]{1,0:T(8,128)(2,1)S(1)} %get-tuple-element.91), channel_id=1, source_target_pairs={{0,16},{4,20},{8,24},{12,28},{16,0},{20,4},{24,8},{28,12},{1,17},{... | collective-permute-start | bytes 491528 | tf_op jit(solution)/shard_map/ppermute | solution.py:19
  143.2 16.4 %collective-permute-start.28 = (bf16[128,640]{1,0:T(8,128)(2,1)S(1)}, bf16[128,640]{1,0:T(8,128)(2,1)S(1)}, u32[]{:S(2)}, u32[]{:S(2)}) collective-permute-start(bf16[128,640]{1,0:T(8,128)(2,1)S(1)} %get-tuple-element.92), channel_id=1, source_target_pairs={{0,24},{4,28},{8,16},{12,20},{16,8},{20,12},{24,0},{28,4},{1,25},{... | collective-permute-start | bytes 491528 | tf_op jit(solution)/shard_map/ppermute | solution.py:19
  152.9 10.3 %collective-permute-start.37 = (bf16[128,1024]{1,0:T(8,128)(2,1)S(1)}, bf16[128,1024]{1,0:T(8,128)(2,1)S(1)}, u32[]{:S(2)}, u32[]{:S(2)}) collective-permute-start(bf16[128,1024]{1,0:T(8,128)(2,1)S(1)} %get-tuple-element.97), channel_id=1, source_target_pairs={{0,16},{4,20},{8,24},{12,28},{16,0},{20,4},{24,8},{28,12},{1,17},{... | collective-permute-start | bytes 786440 | tf_op jit(solution)/shard_map/ppermute | solution.py:19
  153.9 10.0 %collective-permute-start.38 = (bf16[128,1024]{1,0:T(8,128)(2,1)S(1)}, bf16[128,1024]{1,0:T(8,128)(2,1)S(1)}, u32[]{:S(2)}, u32[]{:S(2)}) collective-permute-start(bf16[128,1024]{1,0:T(8,128)(2,1)S(1)} %get-tuple-element.99), channel_id=1, source_target_pairs={{0,8},{4,12},{8,0},{12,4},{16,24},{20,28},{24,16},{28,20},{1,9},{5... | collective-permute-start | bytes 786440 | tf_op jit(solution)/shard_map/ppermute | solution.py:19
  165.1 10.5 %collective-permute-start.30 = (bf16[128,640]{1,0:T(8,128)(2,1)S(1)}, bf16[128,640]{1,0:T(8,128)(2,1)S(1)}, u32[]{:S(2)}, u32[]{:S(2)}) collective-permute-start(bf16[128,640]{1,0:T(8,128)(2,1)S(1)} %add_convert_fusion.4), channel_id=1, source_target_pairs={{0,2},{1,3},{2,0},{3,1},{4,6},{5,7},{6,4},{7,5},{8,10},{9,11},{10,... | collective-permute-start | bytes 491528 | tf_op jit(solution)/shard_map/ppermute | solution.py:19
  168.5 9.8 %collective-permute-start.40 = (bf16[128,640]{1,0:T(8,128)(2,1)S(1)}, bf16[128,640]{1,0:T(8,128)(2,1)S(1)}, u32[]{:S(2)}, u32[]{:S(2)}) collective-permute-start(bf16[128,640]{1,0:T(8,128)(2,1)S(1)} %get-tuple-element.104), channel_id=1, source_target_pairs={{0,8},{4,12},{8,0},{12,4},{16,24},{20,28},{24,16},{28,20},{1,9},{5... | collective-permute-start | bytes 491528 | tf_op jit(solution)/shard_map/ppermute | solution.py:19
  169.8 12.8 %collective-permute-start.41 = (bf16[128,640]{1,0:T(8,128)(2,1)S(1)}, bf16[128,640]{1,0:T(8,128)(2,1)S(1)}, u32[]{:S(2)}, u32[]{:S(2)}) collective-permute-start(bf16[128,640]{1,0:T(8,128)(2,1)S(1)} %get-tuple-element.105), channel_id=1, source_target_pairs={{0,16},{4,20},{8,24},{12,28},{16,0},{20,4},{24,8},{28,12},{1,17},{... | collective-permute-start | bytes 491528 | tf_op jit(solution)/shard_map/ppermute | solution.py:19
  171.2 11.3 %collective-permute-start.42 = (bf16[128,640]{1,0:T(8,128)(2,1)S(1)}, bf16[128,640]{1,0:T(8,128)(2,1)S(1)}, u32[]{:S(2)}, u32[]{:S(2)}) collective-permute-start(bf16[128,640]{1,0:T(8,128)(2,1)S(1)} %get-tuple-element.106), channel_id=1, source_target_pairs={{0,24},{4,28},{8,16},{12,20},{16,8},{20,12},{24,0},{28,4},{1,25},{... | collective-permute-start | bytes 491528 | tf_op jit(solution)/shard_map/ppermute | solution.py:19
  175.6 9.9 %collective-permute-start.33 = (bf16[128,640]{1,0:T(8,128)(2,1)S(1)}, bf16[128,640]{1,0:T(8,128)(2,1)S(1)}, u32[]{:S(2)}, u32[]{:S(2)}) collective-permute-start(bf16[128,640]{1,0:T(8,128)(2,1)S(1)} %add_convert_fusion.3.refs_0_), channel_id=1, source_target_pairs={{0,24},{4,28},{8,16},{12,20},{16,8},{20,12},{24,0},{28,4},{1,25},{... | collective-permute-start | bytes 491528 | tf_op jit(solution)/shard_map/ppermute | solution.py:19
  176.8 9.2 %collective-permute-start.32 = (bf16[128,640]{1,0:T(8,128)(2,1)S(1)}, bf16[128,640]{1,0:T(8,128)(2,1)S(1)}, u32[]{:S(2)}, u32[]{:S(2)}) collective-permute-start(bf16[128,640]{1,0:T(8,128)(2,1)S(1)} %add_convert_fusion.3.refs_0_), channel_id=1, source_target_pairs={{0,16},{4,20},{8,24},{12,28},{16,0},{20,4},{24,8},{28,12},{1,17},{... | collective-permute-start | bytes 491528 | tf_op jit(solution)/shard_map/ppermute | solution.py:19
  178.4 7.7 %collective-permute-start.31 = (bf16[128,640]{1,0:T(8,128)(2,1)S(1)}, bf16[128,640]{1,0:T(8,128)(2,1)S(1)}, u32[]{:S(2)}, u32[]{:S(2)}) collective-permute-start(bf16[128,640]{1,0:T(8,128)(2,1)S(1)} %add_convert_fusion.3.refs_0_), channel_id=1, source_target_pairs={{0,8},{4,12},{8,0},{12,4},{16,24},{20,28},{24,16},{28,20},{1,9},{5... | collective-permute-start | bytes 491528 | tf_op jit(solution)/shard_map/ppermute | solution.py:19
  186.1 14.8 %collective-permute-start.34 = (bf16[4,128,640]{2,1,0:T(8,128)(2,1)S(1)}, bf16[4,128,640]{2,1,0:T(8,128)(2,1)S(1)}, u32[]{:S(2)}, u32[]{:S(2)}) collective-permute-start(bf16[4,128,640]{2,1,0:T(8,128)(2,1)S(1)} %pile.2.refs_0_), channel_id=1, source_target_pairs={{0,4},{4,0},{8,12},{12,8},{16,20},{20,16},{24,28},{28,24},{1,5},{5... | collective-permute-start | bytes 1966088 | tf_op jit(solution)/shard_map/ppermute | solution.py:19
  188.9 8.5 %collective-permute-start.44 = (bf16[128,640]{1,0:T(8,128)(2,1)S(1)}, bf16[128,640]{1,0:T(8,128)(2,1)S(1)}, u32[]{:S(2)}, u32[]{:S(2)}) collective-permute-start(bf16[128,640]{1,0:T(8,128)(2,1)S(1)} %add_convert_fusion.1), channel_id=1, source_target_pairs={{0,2},{1,3},{2,0},{3,1},{4,6},{5,7},{6,4},{7,5},{8,10},{9,11},{10,... | collective-permute-start | bytes 491528 | tf_op jit(solution)/shard_map/ppermute | solution.py:19
  197.4 7.2 %collective-permute-start.47 = (bf16[128,640]{1,0:T(8,128)(2,1)S(1)}, bf16[128,640]{1,0:T(8,128)(2,1)S(1)}, u32[]{:S(2)}, u32[]{:S(2)}) collective-permute-start(bf16[128,640]{1,0:T(8,128)(2,1)S(1)} %add_convert_fusion.refs_6_.refs_0_), channel_id=1, source_target_pairs={{0,24},{4,28},{8,16},{12,20},{16,8},{20,12},{24,0},{28,4},{1,25},{... | collective-permute-start | bytes 491528 | tf_op jit(solution)/shard_map/ppermute | solution.py:19
  206.2 9.2 %collective-permute-start.50 = (bf16[128,1024]{1,0:T(8,128)(2,1)S(1)}, bf16[128,1024]{1,0:T(8,128)(2,1)S(1)}, u32[]{:S(2)}, u32[]{:S(2)}) collective-permute-start(bf16[128,1024]{1,0:T(8,128)(2,1)S(1)} %get-tuple-element.126.refs_1_), channel_id=1, source_target_pairs={{0,8},{4,12},{8,0},{12,4},{16,24},{20,28},{24,16},{28,20},{1,9},{5... | collective-permute-start | bytes 786440 | tf_op jit(solution)/shard_map/ppermute | solution.py:19
  207.4 9.1 %collective-permute-start.49 = (bf16[128,1024]{1,0:T(8,128)(2,1)S(1)}, bf16[128,1024]{1,0:T(8,128)(2,1)S(1)}, u32[]{:S(2)}, u32[]{:S(2)}) collective-permute-start(bf16[128,1024]{1,0:T(8,128)(2,1)S(1)} %get-tuple-element.127.refs_0_), channel_id=1, source_target_pairs={{0,16},{4,20},{8,24},{12,28},{16,0},{20,4},{24,8},{28,12},{1,17},{... | collective-permute-start | bytes 786440 | tf_op jit(solution)/shard_map/ppermute | solution.py:19
  210.7 9.9 %collective-permute-start.52 = (bf16[128,1024]{1,0:T(8,128)(2,1)S(1)}, bf16[128,1024]{1,0:T(8,128)(2,1)S(1)}, u32[]{:S(2)}, u32[]{:S(2)}) collective-permute-start(bf16[128,1024]{1,0:T(8,128)(2,1)S(1)} %get-tuple-element.124.refs_3_), channel_id=1, source_target_pairs={{0,8},{4,12},{8,0},{12,4},{16,24},{20,28},{24,16},{28,20},{1,9},{5... | collective-permute-start | bytes 786440 | tf_op jit(solution)/shard_map/ppermute | solution.py:19
  211.8 9.6 %collective-permute-start.51 = (bf16[128,1024]{1,0:T(8,128)(2,1)S(1)}, bf16[128,1024]{1,0:T(8,128)(2,1)S(1)}, u32[]{:S(2)}, u32[]{:S(2)}) collective-permute-start(bf16[128,1024]{1,0:T(8,128)(2,1)S(1)} %get-tuple-element.125.refs_2_), channel_id=1, source_target_pairs={{0,16},{4,20},{8,24},{12,28},{16,0},{20,4},{24,8},{28,12},{1,17},{... | collective-permute-start | bytes 786440 | tf_op jit(solution)/shard_map/ppermute | solution.py:19
  222.1 14.9 %collective-permute-start.53 = (bf16[256,1024]{1,0:T(8,128)(2,1)S(1)}, bf16[256,1024]{1,0:T(8,128)(2,1)S(1)}, u32[]{:S(2)}, u32[]{:S(2)}) collective-permute-start(bf16[256,1024]{1,0:T(8,128)(2,1)S(1)} %get-tuple-element.109.refs_0_), channel_id=1, source_target_pairs={{0,8},{4,12},{8,0},{12,4},{16,24},{20,28},{24,16},{28,20},{1,9},{5... | collective-permute-start | bytes 1572872 | tf_op jit(solution)/shard_map/ppermute | solution.py:19
  223.1 14.9 %collective-permute-start.54 = (bf16[256,1024]{1,0:T(8,128)(2,1)S(1)}, bf16[256,1024]{1,0:T(8,128)(2,1)S(1)}, u32[]{:S(2)}, u32[]{:S(2)}) collective-permute-start(bf16[256,1024]{1,0:T(8,128)(2,1)S(1)} %get-tuple-element.110.refs_1_), channel_id=1, source_target_pairs={{0,16},{4,20},{8,24},{12,28},{16,0},{20,4},{24,8},{28,12},{1,17},{... | collective-permute-start | bytes 1572872 | tf_op jit(solution)/shard_map/ppermute | solution.py:19
  224.1 22.5 %collective-permute-start.55 = (bf16[256,1024]{1,0:T(8,128)(2,1)S(1)}, bf16[256,1024]{1,0:T(8,128)(2,1)S(1)}, u32[]{:S(2)}, u32[]{:S(2)}) collective-permute-start(bf16[256,1024]{1,0:T(8,128)(2,1)S(1)} %get-tuple-element.111.refs_2_), channel_id=1, source_target_pairs={{0,8},{4,12},{8,0},{12,4},{16,24},{20,28},{24,16},{28,20},{1,9},{5... | collective-permute-start | bytes 1572872 | tf_op jit(solution)/shard_map/ppermute | solution.py:19
  225.1 22.2 %collective-permute-start.56 = (bf16[256,1024]{1,0:T(8,128)(2,1)S(1)}, bf16[256,1024]{1,0:T(8,128)(2,1)S(1)}, u32[]{:S(2)}, u32[]{:S(2)}) collective-permute-start(bf16[256,1024]{1,0:T(8,128)(2,1)S(1)} %get-tuple-element.112.refs_3_), channel_id=1, source_target_pairs={{0,16},{4,20},{8,24},{12,28},{16,0},{20,4},{24,8},{28,12},{1,17},{... | collective-permute-start | bytes 1572872 | tf_op jit(solution)/shard_map/ppermute | solution.py:19
  (34 other events, 282.1 us)

commit v10 on v9

--- a/solution.py
+++ b/solution.py
@@ -43,36 +43,46 @@
 
 
 def whole(array):
-    zeros = (0,) * array.ndim
-    return pl.BlockSpec(array.shape, lambda *_: zeros, pipeline_mode=pl.Buffered(1))
+    return None
 
 
 def like(shape, kind):
     return jax.ShapeDtypeStruct(shape, kind)
 
 
-def run(body, scalars, operands, in_specs, outs, out_specs, grid=(1,), scratch=(), after=(),
+def run(body, scalars, operands, in_specs, outs, out_specs, grid=None, scratch=(), after=(),
         flops=0, moved=0, limit=32, name=None, aliases=None):
     n_in, n_after = len(operands), len(after)
-
-    def kernel(scalars_ref, *refs):
-        body(scalars_ref, *refs[:n_in], *refs[n_in + n_after :])
-
-    return pl.pallas_call(
-        kernel,
-        grid_spec=pltpu.PrefetchScalarGridSpec(
-            num_scalar_prefetch=1,
-            grid=grid,
-            in_specs=list(in_specs) + [pl.BlockSpec(memory_space=pl.ANY)] * n_after,
-            out_specs=list(out_specs),
-            scratch_shapes=list(scratch),
-        ),
+    unread = [pl.BlockSpec(memory_space=pl.ANY)] * n_after
+    options = dict(
         out_shape=list(outs),
         compiler_params=pltpu.CompilerParams(vmem_limit_bytes=limit * MIB),
         cost_estimate=pl.CostEstimate(flops=flops, bytes_accessed=moved, transcendentals=0),
+        input_output_aliases=aliases or {},
         name=name,
-        input_output_aliases=aliases or {},
-    )(scalars, *operands, *after)
+    )
+
+    def kernel(scalars_ref, *refs):
+        body(scalars_ref, *refs[:n_in], *refs[n_in + n_after :])
+
+    if grid is None:
+        inside = pl.BlockSpec(memory_space=pltpu.VMEM)
+        in_specs = [spec or inside for spec in in_specs]
+        out_specs = [spec or inside for spec in out_specs]
+        call = pl.pallas_call(
+            kernel, in_specs=[pl.BlockSpec(memory_space=pltpu.SMEM), *in_specs, *unread],
+            out_specs=out_specs, scratch_shapes=list(scratch), **options,
+        )
+    else:
+        call = pl.pallas_call(
+            kernel,
+            grid_spec=pltpu.PrefetchScalarGridSpec(
+                num_scalar_prefetch=1, grid=grid, in_specs=list(in_specs) + unread,
+                out_specs=list(out_specs), scratch_shapes=list(scratch),
+            ),
+            **options,
+        )
+    return call(scalars, *operands, *after)
 
 
 def fold(square):
@@ -124,7 +134,7 @@
             pl.BlockSpec((step, depth), lambda k, j, c: (jnp.where(k == 1, j, 0), 0)),
             pl.BlockSpec((16, 128), lambda k, j, c: (0, 0)),
         ],
-        grid=(2, 2 * steps), after=after, flops=2 * depth * width, moved=6 * depth * width, limit=54, name="turn_weight",
+        grid=(2, 2 * steps), after=after, flops=2 * depth * width, moved=6 * depth * width, limit=16, name="turn_weight",
     )
 
 
@@ -247,12 +257,11 @@
     rows, depth = turned_own.shape
     batch = columns.shape[0]
     out_rows = rows // 4
-    step = min(256, out_rows)
-    steps = out_rows // step
-
-    def body(bits_ref, own_a, other_a, own_b, other_b, columns_ref, out_a, out_b):
-        own = jnp.concatenate([own_a[...], own_b[...]], 0)
-        other = jnp.concatenate([other_a[...], other_b[...]], 0)
+
+    def body(bits_ref, own_ref, other_ref, columns_ref, out_a, out_b):
+        starts = [pl.multiple_of((2 * p + bits_ref[p]) * out_rows, out_rows) for p in range(2)]
+        own = jnp.concatenate([own_ref[pl.ds(start, out_rows), :] for start in starts], 0)
+        other = jnp.concatenate([other_ref[pl.ds(start, out_rows), :] for start in starts], 0)
         block = lax.dot_general(
             own, columns_ref[:, :depth], ROWS_BY_ROWS, preferred_element_type=F32
         )
@@ -260,18 +269,14 @@
             other, columns_ref[:, depth:], ROWS_BY_ROWS, preferred_element_type=F32
         )
         block = (block - jnp.mean(block, 1, keepdims=True)).astype(BF16)
-        out_a[...] = block[:step]
-        out_b[...] = block[step:]
-
-    def of_path(path):
-        return pl.BlockSpec((step, depth), lambda i, b: ((2 * path + b[path]) * steps + i, 0))
-
-    out_spec = pl.BlockSpec((step, batch), lambda i, b: (i, 0))
-    return run(
-        body, bits, [turned_own, turned_other, turned_own, turned_other, columns],
-        [of_path(0), of_path(0), of_path(1), of_path(1), whole(columns)],
-        [like((out_rows, batch), BF16)] * 2, [out_spec] * 2, grid=(steps,), after=after,
-        flops=8 * out_rows * depth * batch, moved=8 * out_rows * depth + 4 * batch * depth, name="forward",
+        out_a[...] = block[:out_rows]
+        out_b[...] = block[out_rows:]
+
+    return run(
+        body, bits, [turned_own, turned_other, columns], [None] * 3,
+        [like((out_rows, batch), BF16)] * 2, [None] * 2, after=after,
+        flops=8 * out_rows * depth * batch, moved=8 * out_rows * depth + 4 * batch * depth,
+        limit=16, name="forward",
     )
 
 
@@ -446,36 +451,38 @@
 
     def body(place_ref, first_ref, second_ref, *refs):
         square_in_ref = refs[len(pieces)]
-        out_ref, square_ref = refs[-2:]
+        out_ref, square_ref, total_ref, sems = refs[-4:]
+        core = place_ref[1]
+        square_ref[...] = square_in_ref[...]
+        copies = []
         for path in range(n_path):
-
-            @pl.when(pl.program_id(0) == path)
-            def _():
-                total = lax.dot_general(
-                    first_ref[...], refs[path][...], ROWS_BY_ROWS, preferred_element_type=F32
+            total = lax.dot_general(
+                first_ref[...], refs[path][...], ROWS_BY_ROWS, preferred_element_type=F32
+            )
+            total += lax.dot_general(
+                second_ref[...], refs[n_path + path][...], ROWS_BY_ROWS,
+                preferred_element_type=F32,
+            )
+            total_ref[path] = total
+            start = pl.multiple_of((2 * path + (core ^ flip)) * cols, cols)
+            copies.append(
+                pltpu.make_async_copy(
+                    total_ref.at[path], out_ref.at[:, pl.ds(start, cols)], sems.at[path]
                 )
-                total += lax.dot_general(
-                    second_ref[...], refs[n_path + path][...], ROWS_BY_ROWS,
-                    preferred_element_type=F32,
-                )
-                if path == 0:
-                    square_ref[...] = square_in_ref[...]
-                square_ref[:8, :] += fold(total * total)
-                out_ref[...] = total
+            )
+            copies[-1].start()
+            square_ref[:8, :] += fold(total * total)
+        for copy in copies:
+            copy.wait()
 
     operands = [*turned, *pieces, squares] + ([] if done is None else [done])
-    specs = [whole(one) for one in [*turned, *pieces, squares]]
-    if done is not None:
-        specs.append(pl.BlockSpec(memory_space=pl.ANY))
-    return run(
-        body, place, operands, specs,
-        [like((depth, 2 * n_path * cols), F32), like(squares.shape, F32)],
-        [
-            pl.BlockSpec((depth, cols), lambda j, s: (0, 2 * j + (s[1] ^ flip))),
-            pl.BlockSpec(squares.shape, lambda j, s: (0, 0)),
-        ],
-        grid=(n_path,), flops=4 * n_path * cols * batch * depth, moved=4 * n_path * depth * cols,
-        limit=22, aliases={len(operands): 0} if done is not None else {}, name="weight_grad_of",
+    hbm = pl.BlockSpec(memory_space=pl.ANY)
+    return run(
+        body, place, operands, [None] * (3 + len(pieces)) + ([] if done is None else [hbm]),
+        [like((depth, 2 * n_path * cols), F32), like(squares.shape, F32)], [hbm, None],
+        scratch=[pltpu.VMEM((n_path, depth, cols), F32), pltpu.SemaphoreType.DMA((n_path,))],
+        flops=4 * n_path * cols * batch * depth, moved=4 * n_path * depth * cols,
+        limit=20, aliases={len(operands): 0} if done is not None else {}, name="weight_grad_of",
     )
 
 
@@ -500,7 +507,7 @@
     out = like((depth, width), F32)
     return run(
         body, jnp.zeros((1,), jnp.int32), [*sums, weight, velocity, weight_grad],
-        [whole(one) for one in sums] + [tile] * 3, [out, out], [tile, tile],
+        [pl.BlockSpec(one.shape, lambda i, s: (0, 0)) for one in sums] + [tile] * 3, [out, out], [tile, tile],
         grid=(depth // step,), flops=4 * depth * width, moved=20 * depth * width, limit=16, name="update",
     )
 

time: 286 us -> 285 us (level)
  waiting for transfers between devices: 136 us -> 142 us
  Pallas kernels: 70.6 us -> 65 us
    pallas_call x31, Pallas kernels: 70.6 us -> 65 us  [run(): return call(scalars, *operands, *after)]
    ppermute x9, waiting for transfers between devices: 27.9 us -> 32.8 us  [ring_step(): lax.ppermute(share, 'feat', [(i, (i + 1) % n_feat) for i in range(n_feat)])]
    unnamed x28 -> x20, local copies, waits for them, and re-layouts: 6.84 us -> 5.59 us
  transfers between devices with their start and end apart: 68 -> 68, of which waited for: 45 -> 44; matrix products, arithmetic and copies ran while one was open for 0% -> 0% of each run, Pallas kernels for 18% -> 16%
where the time goes in v10:
time: 285 us; the launch traced here: 284 us
  waiting for transfers between devices  142 us (50%)
  starting transfers between devices  69.8 us (24%)
  Pallas kernels  65 us (23%)
  local copies, waits for them, and re-layouts  5.66 us (2%)
    ppermute x52, waiting for transfers between devices, swap(): lax.ppermute(value, axis, [(i, i ^ mask) for i in range(lax.axis_size(axi...  101 us
    pallas_call x31, Pallas kernels, run(): return call(scalars, *operands, *after)  65 us
    ppermute x52, starting transfers between devices, swap(): lax.ppermute(value, axis, [(i, i ^ mask) for i in range(lax.axis_size(axi...  52.8 us
    ppermute x9, waiting for transfers between devices, ring_step(): lax.ppermute(share, 'feat', [(i, (i + 1) % n_feat) for i in range(n_feat)])  32.8 us
    ppermute x9, starting transfers between devices, ring_step(): lax.ppermute(share, 'feat', [(i, (i + 1) % n_feat) for i in range(n_feat)])  9.07 us
    ppermute x7, waiting for transfers between devices, sum_everywhere(): lax.ppermute(value, axes, [(i, i ^ mask) for i in range(count)])  8.01 us
    ppermute x7, starting transfers between devices, sum_everywhere(): lax.ppermute(value, axes, [(i, i ^ mask) for i in range(count)])  7.95 us
  transfers between devices with their start and end apart: 68, of which 44 were waited for; matrix products, arithmetic and copies ran while one was open for 0% of the time, Pallas kernels for 16%

profile of v10, /device:TPU:0, one launch (start us, length us, event | category | flops | bytes accessed | tf_op | source)
XLA Modules:
  0.0 284.4 jit_solution(15075880165121145080)
XLA Ops:
  1.9 3.1 %collective-permute-start.10 = (bf16[64,2048]{1,0:T(8,128)(2,1)S(1)}, bf16[64,2048]{1,0:T(8,128)(2,1)}, u32[]{:S(2)}, u32[]{:S(2)}) collective-permute-start(bf16[64,2048]{1,0:T(8,128)(2,1)S(1)} %get-tuple-element.70.refs_0_), channel_id=1, source_target_pairs={{0,1},{1,2},{2,3},{3,0},{4,5},{5,6},{6,7},{7,4},{8,9},{9,10},{10,1... | collective-permute-start | bytes 786440 | tf_op jit(solution)/shard_map/ppermute | solution.py:171
  6.6 7.7 %collective-permute-done.10.refs_1_ = bf16[64,2048]{1,0:T(8,128)(2,1)} collective-permute-done((bf16[64,2048]{1,0:T(8,128)(2,1)S(1)}, bf16[64,2048]{1,0:T(8,128)(2,1)}, u32[]{:S(2)}, u32[]{:S(2)}) %collective-permute-start.10) | collective-permute-done | bytes 262176 | tf_op jit(solution)/shard_map/ppermute | solution.py:171
  15.9 3.9 %collective-permute-done.3.refs_1_.refs_0_ = bf16[64,2048]{1,0:T(8,128)(2,1)S(1)} collective-permute-done((bf16[64,2048]{1,0:T(8,128)(2,1)S(1)}, bf16[64,2048]{1,0:T(8,128)(2,1)S(1)}, u32[]{:S(2)}, u32[]{:S(2)}) %collective-permute-start.3) | collective-permute-done | bytes 262176 | tf_op jit(solution)/shard_map/ppermute | solution.py:171
  19.8 3.4 %copy-done = f32[1024,2048]{1,0:T(8,128)S(1)} copy-done((f32[1024,2048]{1,0:T(8,128)S(1)}, f32[1024,2048]{1,0:T(8,128)}, u32[]{:S(2)}) %copy-start) | copy-done | bytes 8388632
  23.2 4.6 %turn_weight.1 = (bf16[1024,1024]{1,0:T(8,128)(2,1)}, bf16[1024,1024]{1,0:T(8,128)(2,1)S(1)}, f32[16,128]{1,0:T(8,128)S(1)}) custom-call(s32[1]{0:T(128)} %bitcast.1.scalars_ref, f32[1024,2048]{1,0:T(8,128)S(1)} %copy-done, bf16[64,2048]{1,0:T(8,128)(2,1)S(1)} %collective-permute-done.3.refs_1_.refs_0_), custom_call_target="tpu_custom_call" | custom-call | flops 4194304 | bytes 12582912 | tf_op jit(solution)/shard_map/turn_weight/pallas_call | solution.py:85
  29.6 12.9 %collective-permute-done.5.refs_2_ = bf16[64,2048]{1,0:T(8,128)(2,1)} collective-permute-done((bf16[64,2048]{1,0:T(8,128)(2,1)S(1)}, bf16[64,2048]{1,0:T(8,128)(2,1)}, u32[]{:S(2)}, u32[]{:S(2)}) %collective-permute-start.5) | collective-permute-done | bytes 262176 | tf_op jit(solution)/shard_map/ppermute | solution.py:171
  42.5 5.5 %collective-permute-done.12.refs_3_ = bf16[64,2048]{1,0:T(8,128)(2,1)S(1)} collective-permute-done((bf16[64,2048]{1,0:T(8,128)(2,1)}, bf16[64,2048]{1,0:T(8,128)(2,1)S(1)}, u32[]{:S(2)}, u32[]{:S(2)}) %collective-permute-start.12) | collective-permute-done | bytes 262176 | tf_op jit(solution)/shard_map/ppermute | solution.py:171
  49.2 1.8 collective-permute-start.13
  54.9 1.8 collective-permute-start.7
  56.7 1.8 collective-permute-done.13.refs_5_
  58.5 1.8 collective-permute-start.8
  60.3 1.7 collective-permute-done.14.refs_6_
  63.6 1.8 collective-permute-done.15.refs_7_
  65.5 4.3 %collective-permute-done.7.refs_1_ = bf16[64,2048]{1,0:T(8,128)(2,1)S(1)} collective-permute-done((bf16[64,2048]{1,0:T(8,128)(2,1)S(1)}, bf16[64,2048]{1,0:T(8,128)(2,1)S(1)}, u32[]{:S(2)}, u32[]{:S(2)}) %collective-permute-start.7) | collective-permute-done | bytes 262176 | tf_op jit(solution)/shard_map/ppermute | solution.py:19
  69.8 3.8 %collective-permute-done.8.refs_2_ = bf16[64,2048]{1,0:T(8,128)(2,1)S(1)} collective-permute-done((bf16[64,2048]{1,0:T(8,128)(2,1)S(1)}, bf16[64,2048]{1,0:T(8,128)(2,1)S(1)}, u32[]{:S(2)}, u32[]{:S(2)}) %collective-permute-start.8) | collective-permute-done | bytes 262176 | tf_op jit(solution)/shard_map/ppermute | solution.py:19
  73.6 2.0 collect.2.refs_0_
  77.3 2.8 collective-permute-done.16.refs_1_
  80.1 2.5 assemble.2.refs_2_.refs_0_
  83.1 4.1 %forward.4 = (bf16[256,1024]{1,0:T(8,128)(2,1)S(1)}, bf16[256,1024]{1,0:T(8,128)(2,1)S(1)}) custom-call(s32[2]{0:T(128)S(1)} %get-tuple-element.122.scalars_ref, bf16[1024,1024]{1,0:T(8,128)(2,1)S(1)} %get-tuple-element.64.refs_1_.refs_8_.refs_0_, bf16[1024,1024]{1,0:T(8,128)(2,1)} %collective-permute-done.4.refs_1_, ...), custom_call_target="tpu_custom_call" | custom-call | flops 2147483648 | bytes 6291456 | tf_op jit(solution)/shard_map/forward/pallas_call | solution.py:85
  89.2 2.7 collective-permute-done.2.refs_3_
  98.5 4.1 %forward.5 = (bf16[256,1024]{1,0:T(8,128)(2,1)S(1)}, bf16[256,1024]{1,0:T(8,128)(2,1)S(1)}) custom-call(s32[2]{0:T(128)S(1)} %get-tuple-element.123.scalars_ref, bf16[1024,1024]{1,0:T(8,128)(2,1)S(1)} %get-tuple-element.64.refs_1_.refs_8_.refs_0_, bf16[1024,1024]{1,0:T(8,128)(2,1)} %collective-permute-done.4.refs_1_, ...), custom_call_target="tpu_custom_call" | custom-call | flops 2147483648 | bytes 6291456 | tf_op jit(solution)/shard_map/forward/pallas_call | solution.py:85
  104.3 10.4 %collective-permute-done.17.refs_1_ = bf16[128,2048]{1,0:T(8,128)(2,1)S(1)} collective-permute-done((bf16[128,2048]{1,0:T(8,128)(2,1)S(1)}, bf16[128,2048]{1,0:T(8,128)(2,1)S(1)}, u32[]{:S(2)}, u32[]{:S(2)}) %collective-permute-start.17) | collective-permute-done | bytes 524320 | tf_op jit(solution)/shard_map/ppermute | solution.py:19
  114.8 10.0 %collective-permute-done.19.refs_3_ = bf16[128,2048]{1,0:T(8,128)(2,1)S(1)} collective-permute-done((bf16[128,2048]{1,0:T(8,128)(2,1)S(1)}, bf16[128,2048]{1,0:T(8,128)(2,1)S(1)}, u32[]{:S(2)}, u32[]{:S(2)}) %collective-permute-start.19) | collective-permute-done | bytes 524320 | tf_op jit(solution)/shard_map/ppermute | solution.py:19
  127.7 2.0 collective-permute-done.22.refs_1_
  130.5 4.1 %forward.6 = (bf16[256,1024]{1,0:T(8,128)(2,1)S(1)}, bf16[256,1024]{1,0:T(8,128)(2,1)S(1)}) custom-call(s32[2]{0:T(128)S(1)} %get-tuple-element.122.scalars_ref, bf16[1024,1024]{1,0:T(8,128)(2,1)S(1)} %get-tuple-element.64.refs_1_.refs_8_.refs_0_, bf16[1024,1024]{1,0:T(8,128)(2,1)} %collective-permute-done.4.refs_1_, ...), custom_call_target="tpu_custom_call" | custom-call | flops 2147483648 | bytes 6291456 | tf_op jit(solution)/shard_map/forward/pallas_call | solution.py:85
  142.8 1.7 collective-permute-start.28
  144.5 4.1 %forward.7 = (bf16[256,1024]{1,0:T(8,128)(2,1)S(1)}, bf16[256,1024]{1,0:T(8,128)(2,1)S(1)}) custom-call(s32[2]{0:T(128)S(1)} %get-tuple-element.123.scalars_ref, bf16[1024,1024]{1,0:T(8,128)(2,1)S(1)} %get-tuple-element.64.refs_1_.refs_8_.refs_0_, bf16[1024,1024]{1,0:T(8,128)(2,1)} %collective-permute-done.4.refs_1_, ...), custom_call_target="tpu_custom_call" | custom-call | flops 2147483648 | bytes 6291456 | tf_op jit(solution)/shard_map/forward/pallas_call | solution.py:85
  148.6 2.0 collective-permute-done.36.refs_3_
  155.0 4.1 %collective-permute-done.28 = bf16[128,640]{1,0:T(8,128)(2,1)S(1)} collective-permute-done((bf16[128,640]{1,0:T(8,128)(2,1)S(1)}, bf16[128,640]{1,0:T(8,128)(2,1)S(1)}, u32[]{:S(2)}, u32[]{:S(2)}) %collective-permute-start.28) | collective-permute-done | bytes 163872 | tf_op jit(solution)/shard_map/ppermute | solution.py:19
  159.8 2.9 %collective-permute-done.37.refs_1_ = bf16[128,1024]{1,0:T(8,128)(2,1)S(1)} collective-permute-done((bf16[128,1024]{1,0:T(8,128)(2,1)S(1)}, bf16[128,1024]{1,0:T(8,128)(2,1)S(1)}, u32[]{:S(2)}, u32[]{:S(2)}) %collective-permute-start.37) | collective-permute-done | bytes 262176 | tf_op jit(solution)/shard_map/ppermute | solution.py:19
  164.6 1.9 collective-permute-start.30
  171.4 3.5 %collective-permute-done.30 = bf16[128,640]{1,0:T(8,128)(2,1)S(1)} collective-permute-done((bf16[128,640]{1,0:T(8,128)(2,1)S(1)}, bf16[128,640]{1,0:T(8,128)(2,1)S(1)}, u32[]{:S(2)}, u32[]{:S(2)}) %collective-permute-start.30) | collective-permute-done | bytes 163872 | tf_op jit(solution)/shard_map/ppermute | solution.py:19
  178.5 3.0 %collective-permute-done.41 = bf16[128,640]{1,0:T(8,128)(2,1)S(1)} collective-permute-done((bf16[128,640]{1,0:T(8,128)(2,1)S(1)}, bf16[128,640]{1,0:T(8,128)(2,1)S(1)}, u32[]{:S(2)}, u32[]{:S(2)}) %collective-permute-start.41) | collective-permute-done | bytes 163872 | tf_op jit(solution)/shard_map/ppermute | solution.py:19
  181.6 3.7 %collective-permute-start.43 = (bf16[128,640]{1,0:T(8,128)(2,1)S(1)}, bf16[128,640]{1,0:T(8,128)(2,1)S(1)}, u32[]{:S(2)}, u32[]{:S(2)}) collective-permute-start(bf16[128,640]{1,0:T(8,128)(2,1)S(1)} %add_convert_fusion.2), channel_id=1, source_target_pairs={{0,1},{1,0},{2,3},{3,2},{4,5},{5,4},{6,7},{7,6},{8,9},{9,8},{10,11... | collective-permute-start | bytes 491528 | tf_op jit(solution)/shard_map/ppermute | solution.py:19
  185.5 3.1 %collective-permute-done.43 = bf16[128,640]{1,0:T(8,128)(2,1)S(1)} collective-permute-done((bf16[128,640]{1,0:T(8,128)(2,1)S(1)}, bf16[128,640]{1,0:T(8,128)(2,1)S(1)}, u32[]{:S(2)}, u32[]{:S(2)}) %collective-permute-start.43) | collective-permute-done | bytes 163872 | tf_op jit(solution)/shard_map/ppermute | solution.py:19
  190.1 6.7 %collective-permute-done.44 = bf16[128,640]{1,0:T(8,128)(2,1)S(1)} collective-permute-done((bf16[128,640]{1,0:T(8,128)(2,1)S(1)}, bf16[128,640]{1,0:T(8,128)(2,1)S(1)}, u32[]{:S(2)}, u32[]{:S(2)}) %collective-permute-start.44) | collective-permute-done | bytes 163872 | tf_op jit(solution)/shard_map/ppermute | solution.py:19
  200.4 2.4 out_grad_of.2.refs_4_
  207.5 2.4 out_grad_of.3
  212.0 2.5 collective-permute-done.50.refs_5_
  215.8 4.0 %collective-permute-done.52.refs_7_ = bf16[128,1024]{1,0:T(8,128)(2,1)S(1)} collective-permute-done((bf16[128,1024]{1,0:T(8,128)(2,1)S(1)}, bf16[128,1024]{1,0:T(8,128)(2,1)S(1)}, u32[]{:S(2)}, u32[]{:S(2)}) %collective-permute-start.52) | collective-permute-done | bytes 262176 | tf_op jit(solution)/shard_map/ppermute | solution.py:19
  225.5 10.7 %collective-permute-done.53.refs_4_ = bf16[256,1024]{1,0:T(8,128)(2,1)S(1)} collective-permute-done((bf16[256,1024]{1,0:T(8,128)(2,1)S(1)}, bf16[256,1024]{1,0:T(8,128)(2,1)S(1)}, u32[]{:S(2)}, u32[]{:S(2)}) %collective-permute-start.53) | collective-permute-done | bytes 524320 | tf_op jit(solution)/shard_map/ppermute | solution.py:19
  237.1 8.8 %collective-permute-done.55.refs_6_ = bf16[256,1024]{1,0:T(8,128)(2,1)S(1)} collective-permute-done((bf16[256,1024]{1,0:T(8,128)(2,1)S(1)}, bf16[256,1024]{1,0:T(8,128)(2,1)S(1)}, u32[]{:S(2)}, u32[]{:S(2)}) %collective-permute-start.55) | collective-permute-done | bytes 524320 | tf_op jit(solution)/shard_map/ppermute | solution.py:19
  248.3 6.3 %weight_grad_of.2 = (f32[1024,2048]{1,0:T(8,128)S(1)}, f32[16,128]{1,0:T(8,128)S(1)}) custom-call(s32[2]{0:T(128)S(1)} %pad_add_fusion.scalars_ref, bf16[1024,1024]{1,0:T(8,128)(2,1)S(1)} %turn_columns.3.refs_3_.refs_0_, bf16[1024,1024]{1,0:T(8,128)(2,1)S(1)} %turn_columns.2.refs_3_.refs_1_, bf16[512,1024]{1,0:T(8,128)(2,1)S(1)} %get-tuple-element.113.refs_2_, ...), custom_call_target="tpu_custom_call" | custom-call | flops 4294967296 | bytes 4194304 | tf_op jit(solution)/shard_map/weight_grad_of/pallas_call | solution.py:85
  254.7 6.1 %weight_grad_of.3 = (f32[1024,2048]{1,0:T(8,128)S(1)}, f32[16,128]{1,0:T(8,128)S(1)}) custom-call(s32[2]{0:T(128)S(1)} %pad_add_fusion.scalars_ref, bf16[1024,1024]{1,0:T(8,128)(2,1)S(1)} %turn_columns.3.refs_3_.refs_0_, bf16[1024,1024]{1,0:T(8,128)(2,1)S(1)} %turn_columns.2.refs_3_.refs_1_, ...), custom_call_target="tpu_custom_call", output_to_operand_aliasing={{0}: (8, {})} | custom-call | flops 4294967296 | bytes 4194304 | tf_op jit(solution)/shard_map/weight_grad_of/pallas_call | solution.py:85
  260.8 3.9 %collective-permute-start.63 = (f32[16,128]{1,0:T(8,128)S(1)}, f32[16,128]{1,0:T(8,128)S(1)}, u32[]{:S(2)}, u32[]{:S(2)}) collective-permute-start(f32[16,128]{1,0:T(8,128)S(1)} %get-tuple-element.120), channel_id=1, source_target_pairs={{0,3},{1,2},{2,1},{3,0},{4,7},{5,6},{6,5},{7,4},{8,11},{9,10},{10,... | collective-permute-start | bytes 24584 | tf_op jit(solution)/shard_map/ppermute | solution.py:40
  266.4 2.9 %collective-permute-done.62 = f32[16,128]{1,0:T(8,128)S(1)} collective-permute-done((f32[16,128]{1,0:T(8,128)S(1)}, f32[16,128]{1,0:T(8,128)S(1)}, u32[]{:S(2)}, u32[]{:S(2)}) %collective-permute-start.62) | collective-permute-done | bytes 8224 | tf_op jit(solution)/shard_map/ppermute | solution.py:40
  274.6 2.2 collective-permute-done.67.refs_1_
  276.9 7.5 %update.1 = (f32[1024,2048]{1,0:T(8,128)}, f32[1024,2048]{1,0:T(8,128)}) custom-call(s32[1]{0:T(128)} %constant.21.clone.1.scalars_ref, f32[16,128]{1,0:T(8,128)S(1)} %add_add_fusion.refs_0_, f32[16,128]{1,0:T(8,128)S(1)} %collective-permute-done.67.refs_1_, f32[1024,2048]{1,0:T(8,128)S(1)} %bitcast.9, f32[1024,2048]{1,0:T(8,128)S(1)} %bitcast.11, ...), custom_call_target="tpu_custom_call" | custom-call | flops 8388608 | bytes 41943040 | tf_op jit(solution)/shard_map/update/pallas_call | solution.py:85
  (157 shorter events, 82.3 us)
Async XLA Ops:
  1.9 12.3 %collective-permute-start.10 = (bf16[64,2048]{1,0:T(8,128)(2,1)S(1)}, bf16[64,2048]{1,0:T(8,128)(2,1)}, u32[]{:S(2)}, u32[]{:S(2)}) collective-permute-start(bf16[64,2048]{1,0:T(8,128)(2,1)S(1)} %get-tuple-element.70.refs_0_), channel_id=1, source_target_pairs={{0,1},{1,2},{2,3},{3,0},{4,5},{5,6},{6,7},{7,4},{8,9},{9,10},{10,1... | collective-permute-start | bytes 786440 | tf_op jit(solution)/shard_map/ppermute | solution.py:171
  5.0 14.8 %collective-permute-start.3 = (bf16[64,2048]{1,0:T(8,128)(2,1)S(1)}, bf16[64,2048]{1,0:T(8,128)(2,1)S(1)}, u32[]{:S(2)}, u32[]{:S(2)}) collective-permute-start(bf16[64,2048]{1,0:T(8,128)(2,1)S(1)} %get-tuple-element.63.refs_0_), channel_id=1, source_target_pairs={{0,1},{1,2},{2,3},{3,0},{4,5},{5,6},{6,7},{7,4},{8,9},{9,10},{10,1... | collective-permute-start | bytes 786440 | tf_op jit(solution)/shard_map/ppermute | solution.py:171
  14.3 13.6 %collective-permute-start.11 = (bf16[64,2048]{1,0:T(8,128)(2,1)}, bf16[64,2048]{1,0:T(8,128)(2,1)}, u32[]{:S(2)}, u32[]{:S(2)}) collective-permute-start(bf16[64,2048]{1,0:T(8,128)(2,1)} %collective-permute-done.10.refs_1_), channel_id=1, source_target_pairs={{0,1},{1,2},{2,3},{3,0},{4,5},{5,6},{6,7},{7,4},{8,9},{9,10},{10,1... | collective-permute-start | bytes 786440 | tf_op jit(solution)/shard_map/ppermute | solution.py:171
  14.3 36.7 %collective-permute-start = (bf16[128,2048]{1,0:T(8,128)(2,1)S(1)}, bf16[128,2048]{1,0:T(8,128)(2,1)}, u32[]{:S(2)}, u32[]{:S(2)}) collective-permute-start(bf16[128,2048]{1,0:T(8,128)(2,1)S(1)} %get-tuple-element.62.refs_0_), channel_id=1, source_target_pairs={{0,1},{1,2},{2,3},{3,0},{4,5},{5,6},{6,7},{7,4},{8,9},{9,10},{10,1... | collective-permute-start | bytes 1572872 | tf_op jit(solution)/shard_map/ppermute | solution.py:171
  27.8 14.7 %collective-permute-start.5 = (bf16[64,2048]{1,0:T(8,128)(2,1)S(1)}, bf16[64,2048]{1,0:T(8,128)(2,1)}, u32[]{:S(2)}, u32[]{:S(2)}) collective-permute-start(bf16[64,2048]{1,0:T(8,128)(2,1)S(1)} %relay.1.refs_1_), channel_id=1, source_target_pairs={{0,1},{1,2},{2,3},{3,0},{4,5},{5,6},{6,7},{7,4},{8,9},{9,10},{10,1... | collective-permute-start | bytes 786440 | tf_op jit(solution)/shard_map/ppermute | solution.py:171
  27.9 20.1 %collective-permute-start.12 = (bf16[64,2048]{1,0:T(8,128)(2,1)}, bf16[64,2048]{1,0:T(8,128)(2,1)S(1)}, u32[]{:S(2)}, u32[]{:S(2)}) collective-permute-start(bf16[64,2048]{1,0:T(8,128)(2,1)} %collective-permute-done.11.refs_2_), channel_id=1, source_target_pairs={{0,1},{1,2},{2,3},{3,0},{4,5},{5,6},{6,7},{7,4},{8,9},{9,10},{10,1... | collective-permute-start | bytes 786440 | tf_op jit(solution)/shard_map/ppermute | solution.py:171
  42.5 10.3 %collective-permute-start.6 = (bf16[64,2048]{1,0:T(8,128)(2,1)}, bf16[64,2048]{1,0:T(8,128)(2,1)S(1)}, u32[]{:S(2)}, u32[]{:S(2)}) collective-permute-start(bf16[64,2048]{1,0:T(8,128)(2,1)} %collective-permute-done.5.refs_2_), channel_id=1, source_target_pairs={{0,1},{1,2},{2,3},{3,0},{4,5},{5,6},{6,7},{7,4},{8,9},{9,10},{10,1... | collective-permute-start | bytes 786440 | tf_op jit(solution)/shard_map/ppermute | solution.py:171
  49.2 9.3 %collective-permute-start.13 = (bf16[64,2048]{1,0:T(8,128)(2,1)S(1)}, bf16[64,2048]{1,0:T(8,128)(2,1)S(1)}, u32[]{:S(2)}, u32[]{:S(2)}) collective-permute-start(bf16[64,2048]{1,0:T(8,128)(2,1)S(1)} %get-tuple-element.72), channel_id=1, source_target_pairs={{0,8},{4,12},{8,0},{12,4},{16,24},{20,28},{24,16},{28,20},{1,9},{5... | collective-permute-start | bytes 786440 | tf_op jit(solution)/shard_map/ppermute | solution.py:19
  51.0 14.4 %collective-permute-start.1 = (bf16[128,2048]{1,0:T(8,128)(2,1)}, bf16[128,2048]{1,0:T(8,128)(2,1)S(1)}, u32[]{:S(2)}, u32[]{:S(2)}) collective-permute-start(bf16[128,2048]{1,0:T(8,128)(2,1)} %collective-permute-done.refs_1_), channel_id=1, source_target_pairs={{0,1},{1,2},{2,3},{3,0},{4,5},{5,6},{6,7},{7,4},{8,9},{9,10},{10,1... | collective-permute-start | bytes 1572872 | tf_op jit(solution)/shard_map/ppermute | solution.py:171
  51.1 11.0 %collective-permute-start.14 = (bf16[64,2048]{1,0:T(8,128)(2,1)S(1)}, bf16[64,2048]{1,0:T(8,128)(2,1)S(1)}, u32[]{:S(2)}, u32[]{:S(2)}) collective-permute-start(bf16[64,2048]{1,0:T(8,128)(2,1)S(1)} %get-tuple-element.73), channel_id=1, source_target_pairs={{0,16},{4,20},{8,24},{12,28},{16,0},{20,4},{24,8},{28,12},{1,17},{... | collective-permute-start | bytes 786440 | tf_op jit(solution)/shard_map/ppermute | solution.py:19
  52.6 12.9 %collective-permute-start.15 = (bf16[64,2048]{1,0:T(8,128)(2,1)S(1)}, bf16[64,2048]{1,0:T(8,128)(2,1)S(1)}, u32[]{:S(2)}, u32[]{:S(2)}) collective-permute-start(bf16[64,2048]{1,0:T(8,128)(2,1)S(1)} %get-tuple-element.74), channel_id=1, source_target_pairs={{0,24},{4,28},{8,16},{12,20},{16,8},{20,12},{24,0},{28,4},{1,25},{... | collective-permute-start | bytes 786440 | tf_op jit(solution)/shard_map/ppermute | solution.py:19
  54.9 14.9 %collective-permute-start.7 = (bf16[64,2048]{1,0:T(8,128)(2,1)S(1)}, bf16[64,2048]{1,0:T(8,128)(2,1)S(1)}, u32[]{:S(2)}, u32[]{:S(2)}) collective-permute-start(bf16[64,2048]{1,0:T(8,128)(2,1)S(1)} %get-tuple-element.67), channel_id=1, source_target_pairs={{0,8},{4,12},{8,0},{12,4},{16,24},{20,28},{24,16},{28,20},{1,9},{5... | collective-permute-start | bytes 786440 | tf_op jit(solution)/shard_map/ppermute | solution.py:19
  58.5 15.0 %collective-permute-start.8 = (bf16[64,2048]{1,0:T(8,128)(2,1)S(1)}, bf16[64,2048]{1,0:T(8,128)(2,1)S(1)}, u32[]{:S(2)}, u32[]{:S(2)}) collective-permute-start(bf16[64,2048]{1,0:T(8,128)(2,1)S(1)} %get-tuple-element.68), channel_id=1, source_target_pairs={{0,16},{4,20},{8,24},{12,28},{16,0},{20,4},{24,8},{28,12},{1,17},{... | collective-permute-start | bytes 786440 | tf_op jit(solution)/shard_map/ppermute | solution.py:19
  62.0 11.5 %collective-permute-start.9 = (bf16[64,2048]{1,0:T(8,128)(2,1)S(1)}, bf16[64,2048]{1,0:T(8,128)(2,1)S(1)}, u32[]{:S(2)}, u32[]{:S(2)}) collective-permute-start(bf16[64,2048]{1,0:T(8,128)(2,1)S(1)} %get-tuple-element.69), channel_id=1, source_target_pairs={{0,24},{4,28},{8,16},{12,20},{16,8},{20,12},{24,0},{28,4},{1,25},{... | collective-permute-start | bytes 786440 | tf_op jit(solution)/shard_map/ppermute | solution.py:19
  75.6 7.5 %collective-permute-start.4 = (bf16[1024,1024]{1,0:T(8,128)(2,1)}, bf16[1024,1024]{1,0:T(8,128)(2,1)}, u32[]{:S(2)}, u32[]{:S(2)}) collective-permute-start(bf16[1024,1024]{1,0:T(8,128)(2,1)} %get-tuple-element.65), channel_id=1, source_target_pairs={{0,4},{4,0},{8,12},{12,8},{16,20},{20,16},{24,28},{28,24},{1,5},{5... | collective-permute-start | bytes 6291464 | tf_op jit(solution)/shard_map/ppermute | solution.py:19
  76.1 15.9 %collective-permute-start.2 = (bf16[128,2048]{1,0:T(8,128)(2,1)S(1)}, bf16[128,2048]{1,0:T(8,128)(2,1)}, u32[]{:S(2)}, u32[]{:S(2)}) collective-permute-start(bf16[128,2048]{1,0:T(8,128)(2,1)S(1)} %collective-permute-done.1.refs_9_.refs_2_), channel_id=1, source_target_pairs={{0,1},{1,2},{2,3},{3,0},{4,5},{5,6},{6,7},{7,4},{8,9},{9,10},{10,1... | collective-permute-start | bytes 1572872 | tf_op jit(solution)/shard_map/ppermute | solution.py:171
  87.1 15.5 %collective-permute-start.21 = (bf16[256,1024]{1,0:T(8,128)(2,1)S(1)}, bf16[256,1024]{1,0:T(8,128)(2,1)S(1)}, u32[]{:S(2)}, u32[]{:S(2)}) collective-permute-start(bf16[256,1024]{1,0:T(8,128)(2,1)S(1)} %get-tuple-element.82), channel_id=1, source_target_pairs={{0,16},{4,20},{8,24},{12,28},{16,0},{20,4},{24,8},{28,12},{1,17},{... | collective-permute-start | bytes 1572872 | tf_op jit(solution)/shard_map/ppermute | solution.py:19
  88.7 14.8 %collective-permute-start.20 = (bf16[256,1024]{1,0:T(8,128)(2,1)S(1)}, bf16[256,1024]{1,0:T(8,128)(2,1)S(1)}, u32[]{:S(2)}, u32[]{:S(2)}) collective-permute-start(bf16[256,1024]{1,0:T(8,128)(2,1)S(1)} %get-tuple-element.75.refs_4_), channel_id=1, source_target_pairs={{0,8},{4,12},{8,0},{12,4},{16,24},{20,28},{24,16},{28,20},{1,9},{5... | collective-permute-start | bytes 1572872 | tf_op jit(solution)/shard_map/ppermute | solution.py:19
  93.6 21.1 %collective-permute-start.17 = (bf16[128,2048]{1,0:T(8,128)(2,1)S(1)}, bf16[128,2048]{1,0:T(8,128)(2,1)S(1)}, u32[]{:S(2)}, u32[]{:S(2)}) collective-permute-start(bf16[128,2048]{1,0:T(8,128)(2,1)S(1)} %get-tuple-element.77), channel_id=1, source_target_pairs={{0,8},{4,12},{8,0},{12,4},{16,24},{20,28},{24,16},{28,20},{1,9},{5... | collective-permute-start | bytes 1572872 | tf_op jit(solution)/shard_map/ppermute | solution.py:19
  94.8 20.0 %collective-permute-start.18 = (bf16[128,2048]{1,0:T(8,128)(2,1)S(1)}, bf16[128,2048]{1,0:T(8,128)(2,1)S(1)}, u32[]{:S(2)}, u32[]{:S(2)}) collective-permute-start(bf16[128,2048]{1,0:T(8,128)(2,1)S(1)} %get-tuple-element.78), channel_id=1, source_target_pairs={{0,16},{4,20},{8,24},{12,28},{16,0},{20,4},{24,8},{28,12},{1,17},{... | collective-permute-start | bytes 1572872 | tf_op jit(solution)/shard_map/ppermute | solution.py:19
  95.6 29.2 %collective-permute-start.19 = (bf16[128,2048]{1,0:T(8,128)(2,1)S(1)}, bf16[128,2048]{1,0:T(8,128)(2,1)S(1)}, u32[]{:S(2)}, u32[]{:S(2)}) collective-permute-start(bf16[128,2048]{1,0:T(8,128)(2,1)S(1)} %get-tuple-element.79), channel_id=1, source_target_pairs={{0,24},{4,28},{8,16},{12,20},{16,8},{20,12},{24,0},{28,4},{1,25},{... | collective-permute-start | bytes 1572872 | tf_op jit(solution)/shard_map/ppermute | solution.py:19
  125.6 9.0 %collective-permute-start.24 = (bf16[128,1024]{1,0:T(8,128)(2,1)S(1)}, bf16[128,1024]{1,0:T(8,128)(2,1)S(1)}, u32[]{:S(2)}, u32[]{:S(2)}) collective-permute-start(bf16[128,1024]{1,0:T(8,128)(2,1)S(1)} %get-tuple-element.86), channel_id=1, source_target_pairs={{0,8},{4,12},{8,0},{12,4},{16,24},{20,28},{24,16},{28,20},{1,9},{5... | collective-permute-start | bytes 786440 | tf_op jit(solution)/shard_map/ppermute | solution.py:19
  126.9 8.4 %collective-permute-start.23 = (bf16[128,1024]{1,0:T(8,128)(2,1)S(1)}, bf16[128,1024]{1,0:T(8,128)(2,1)S(1)}, u32[]{:S(2)}, u32[]{:S(2)}) collective-permute-start(bf16[128,1024]{1,0:T(8,128)(2,1)S(1)} %get-tuple-element.83.refs_4_), channel_id=1, source_target_pairs={{0,16},{4,20},{8,24},{12,28},{16,0},{20,4},{24,8},{28,12},{1,17},{... | collective-permute-start | bytes 786440 | tf_op jit(solution)/shard_map/ppermute | solution.py:19
  135.8 14.8 %collective-permute-start.36 = (bf16[256,1024]{1,0:T(8,128)(2,1)S(1)}, bf16[256,1024]{1,0:T(8,128)(2,1)S(1)}, u32[]{:S(2)}, u32[]{:S(2)}) collective-permute-start(bf16[256,1024]{1,0:T(8,128)(2,1)S(1)} %get-tuple-element.95), channel_id=1, source_target_pairs={{0,16},{4,20},{8,24},{12,28},{16,0},{20,4},{24,8},{28,12},{1,17},{... | collective-permute-start | bytes 1572872 | tf_op jit(solution)/shard_map/ppermute | solution.py:19
  136.8 14.8 %collective-permute-start.35 = (bf16[256,1024]{1,0:T(8,128)(2,1)S(1)}, bf16[256,1024]{1,0:T(8,128)(2,1)S(1)}, u32[]{:S(2)}, u32[]{:S(2)}) collective-permute-start(bf16[256,1024]{1,0:T(8,128)(2,1)S(1)} %get-tuple-element.87.refs_4_), channel_id=1, source_target_pairs={{0,8},{4,12},{8,0},{12,4},{16,24},{20,28},{24,16},{28,20},{1,9},{5... | collective-permute-start | bytes 1572872 | tf_op jit(solution)/shard_map/ppermute | solution.py:19
  141.0 14.1 %collective-permute-start.26 = (bf16[128,640]{1,0:T(8,128)(2,1)S(1)}, bf16[128,640]{1,0:T(8,128)(2,1)S(1)}, u32[]{:S(2)}, u32[]{:S(2)}) collective-permute-start(bf16[128,640]{1,0:T(8,128)(2,1)S(1)} %get-tuple-element.90), channel_id=1, source_target_pairs={{0,8},{4,12},{8,0},{12,4},{16,24},{20,28},{24,16},{28,20},{1,9},{5... | collective-permute-start | bytes 491528 | tf_op jit(solution)/shard_map/ppermute | solution.py:19
  141.7 13.4 %collective-permute-start.27 = (bf16[128,640]{1,0:T(8,128)(2,1)S(1)}, bf16[128,640]{1,0:T(8,128)(2,1)S(1)}, u32[]{:S(2)}, u32[]{:S(2)}) collective-permute-start(bf16[128,640]{1,0:T(8,128)(2,1)S(1)} %get-tuple-element.91), channel_id=1, source_target_pairs={{0,16},{4,20},{8,24},{12,28},{16,0},{20,4},{24,8},{28,12},{1,17},{... | collective-permute-start | bytes 491528 | tf_op jit(solution)/shard_map/ppermute | solution.py:19
  142.8 16.4 %collective-permute-start.28 = (bf16[128,640]{1,0:T(8,128)(2,1)S(1)}, bf16[128,640]{1,0:T(8,128)(2,1)S(1)}, u32[]{:S(2)}, u32[]{:S(2)}) collective-permute-start(bf16[128,640]{1,0:T(8,128)(2,1)S(1)} %get-tuple-element.92), channel_id=1, source_target_pairs={{0,24},{4,28},{8,16},{12,20},{16,8},{20,12},{24,0},{28,4},{1,25},{... | collective-permute-start | bytes 491528 | tf_op jit(solution)/shard_map/ppermute | solution.py:19
  152.3 10.4 %collective-permute-start.37 = (bf16[128,1024]{1,0:T(8,128)(2,1)S(1)}, bf16[128,1024]{1,0:T(8,128)(2,1)S(1)}, u32[]{:S(2)}, u32[]{:S(2)}) collective-permute-start(bf16[128,1024]{1,0:T(8,128)(2,1)S(1)} %get-tuple-element.97), channel_id=1, source_target_pairs={{0,16},{4,20},{8,24},{12,28},{16,0},{20,4},{24,8},{28,12},{1,17},{... | collective-permute-start | bytes 786440 | tf_op jit(solution)/shard_map/ppermute | solution.py:19
  153.5 9.9 %collective-permute-start.38 = (bf16[128,1024]{1,0:T(8,128)(2,1)S(1)}, bf16[128,1024]{1,0:T(8,128)(2,1)S(1)}, u32[]{:S(2)}, u32[]{:S(2)}) collective-permute-start(bf16[128,1024]{1,0:T(8,128)(2,1)S(1)} %get-tuple-element.99), channel_id=1, source_target_pairs={{0,8},{4,12},{8,0},{12,4},{16,24},{20,28},{24,16},{28,20},{1,9},{5... | collective-permute-start | bytes 786440 | tf_op jit(solution)/shard_map/ppermute | solution.py:19
  164.6 10.3 %collective-permute-start.30 = (bf16[128,640]{1,0:T(8,128)(2,1)S(1)}, bf16[128,640]{1,0:T(8,128)(2,1)S(1)}, u32[]{:S(2)}, u32[]{:S(2)}) collective-permute-start(bf16[128,640]{1,0:T(8,128)(2,1)S(1)} %add_convert_fusion.4), channel_id=1, source_target_pairs={{0,2},{1,3},{2,0},{3,1},{4,6},{5,7},{6,4},{7,5},{8,10},{9,11},{10,... | collective-permute-start | bytes 491528 | tf_op jit(solution)/shard_map/ppermute | solution.py:19
  167.9 10.1 %collective-permute-start.40 = (bf16[128,640]{1,0:T(8,128)(2,1)S(1)}, bf16[128,640]{1,0:T(8,128)(2,1)S(1)}, u32[]{:S(2)}, u32[]{:S(2)}) collective-permute-start(bf16[128,640]{1,0:T(8,128)(2,1)S(1)} %get-tuple-element.104), channel_id=1, source_target_pairs={{0,8},{4,12},{8,0},{12,4},{16,24},{20,28},{24,16},{28,20},{1,9},{5... | collective-permute-start | bytes 491528 | tf_op jit(solution)/shard_map/ppermute | solution.py:19
  169.2 12.3 %collective-permute-start.41 = (bf16[128,640]{1,0:T(8,128)(2,1)S(1)}, bf16[128,640]{1,0:T(8,128)(2,1)S(1)}, u32[]{:S(2)}, u32[]{:S(2)}) collective-permute-start(bf16[128,640]{1,0:T(8,128)(2,1)S(1)} %get-tuple-element.105), channel_id=1, source_target_pairs={{0,16},{4,20},{8,24},{12,28},{16,0},{20,4},{24,8},{28,12},{1,17},{... | collective-permute-start | bytes 491528 | tf_op jit(solution)/shard_map/ppermute | solution.py:19
  170.9 10.6 %collective-permute-start.42 = (bf16[128,640]{1,0:T(8,128)(2,1)S(1)}, bf16[128,640]{1,0:T(8,128)(2,1)S(1)}, u32[]{:S(2)}, u32[]{:S(2)}) collective-permute-start(bf16[128,640]{1,0:T(8,128)(2,1)S(1)} %get-tuple-element.106), channel_id=1, source_target_pairs={{0,24},{4,28},{8,16},{12,20},{16,8},{20,12},{24,0},{28,4},{1,25},{... | collective-permute-start | bytes 491528 | tf_op jit(solution)/shard_map/ppermute | solution.py:19
  175.0 10.3 %collective-permute-start.33 = (bf16[128,640]{1,0:T(8,128)(2,1)S(1)}, bf16[128,640]{1,0:T(8,128)(2,1)S(1)}, u32[]{:S(2)}, u32[]{:S(2)}) collective-permute-start(bf16[128,640]{1,0:T(8,128)(2,1)S(1)} %add_convert_fusion.3.refs_0_), channel_id=1, source_target_pairs={{0,24},{4,28},{8,16},{12,20},{16,8},{20,12},{24,0},{28,4},{1,25},{... | collective-permute-start | bytes 491528 | tf_op jit(solution)/shard_map/ppermute | solution.py:19
  176.4 9.0 %collective-permute-start.32 = (bf16[128,640]{1,0:T(8,128)(2,1)S(1)}, bf16[128,640]{1,0:T(8,128)(2,1)S(1)}, u32[]{:S(2)}, u32[]{:S(2)}) collective-permute-start(bf16[128,640]{1,0:T(8,128)(2,1)S(1)} %add_convert_fusion.3.refs_0_), channel_id=1, source_target_pairs={{0,16},{4,20},{8,24},{12,28},{16,0},{20,4},{24,8},{28,12},{1,17},{... | collective-permute-start | bytes 491528 | tf_op jit(solution)/shard_map/ppermute | solution.py:19
  177.9 7.5 %collective-permute-start.31 = (bf16[128,640]{1,0:T(8,128)(2,1)S(1)}, bf16[128,640]{1,0:T(8,128)(2,1)S(1)}, u32[]{:S(2)}, u32[]{:S(2)}) collective-permute-start(bf16[128,640]{1,0:T(8,128)(2,1)S(1)} %add_convert_fusion.3.refs_0_), channel_id=1, source_target_pairs={{0,8},{4,12},{8,0},{12,4},{16,24},{20,28},{24,16},{28,20},{1,9},{5... | collective-permute-start | bytes 491528 | tf_op jit(solution)/shard_map/ppermute | solution.py:19
  185.4 15.0 %collective-permute-start.34 = (bf16[4,128,640]{2,1,0:T(8,128)(2,1)S(1)}, bf16[4,128,640]{2,1,0:T(8,128)(2,1)S(1)}, u32[]{:S(2)}, u32[]{:S(2)}) collective-permute-start(bf16[4,128,640]{2,1,0:T(8,128)(2,1)S(1)} %pile.2.refs_0_), channel_id=1, source_target_pairs={{0,4},{4,0},{8,12},{12,8},{16,20},{20,16},{24,28},{28,24},{1,5},{5... | collective-permute-start | bytes 1966088 | tf_op jit(solution)/shard_map/ppermute | solution.py:19
  188.7 8.2 %collective-permute-start.44 = (bf16[128,640]{1,0:T(8,128)(2,1)S(1)}, bf16[128,640]{1,0:T(8,128)(2,1)S(1)}, u32[]{:S(2)}, u32[]{:S(2)}) collective-permute-start(bf16[128,640]{1,0:T(8,128)(2,1)S(1)} %add_convert_fusion.1), channel_id=1, source_target_pairs={{0,2},{1,3},{2,0},{3,1},{4,6},{5,7},{6,4},{7,5},{8,10},{9,11},{10,... | collective-permute-start | bytes 491528 | tf_op jit(solution)/shard_map/ppermute | solution.py:19
  205.3 9.2 %collective-permute-start.50 = (bf16[128,1024]{1,0:T(8,128)(2,1)S(1)}, bf16[128,1024]{1,0:T(8,128)(2,1)S(1)}, u32[]{:S(2)}, u32[]{:S(2)}) collective-permute-start(bf16[128,1024]{1,0:T(8,128)(2,1)S(1)} %get-tuple-element.126.refs_1_), channel_id=1, source_target_pairs={{0,8},{4,12},{8,0},{12,4},{16,24},{20,28},{24,16},{28,20},{1,9},{5... | collective-permute-start | bytes 786440 | tf_op jit(solution)/shard_map/ppermute | solution.py:19
  206.6 9.1 %collective-permute-start.49 = (bf16[128,1024]{1,0:T(8,128)(2,1)S(1)}, bf16[128,1024]{1,0:T(8,128)(2,1)S(1)}, u32[]{:S(2)}, u32[]{:S(2)}) collective-permute-start(bf16[128,1024]{1,0:T(8,128)(2,1)S(1)} %get-tuple-element.127.refs_0_), channel_id=1, source_target_pairs={{0,16},{4,20},{8,24},{12,28},{16,0},{20,4},{24,8},{28,12},{1,17},{... | collective-permute-start | bytes 786440 | tf_op jit(solution)/shard_map/ppermute | solution.py:19
  209.9 9.8 %collective-permute-start.52 = (bf16[128,1024]{1,0:T(8,128)(2,1)S(1)}, bf16[128,1024]{1,0:T(8,128)(2,1)S(1)}, u32[]{:S(2)}, u32[]{:S(2)}) collective-permute-start(bf16[128,1024]{1,0:T(8,128)(2,1)S(1)} %get-tuple-element.124.refs_3_), channel_id=1, source_target_pairs={{0,8},{4,12},{8,0},{12,4},{16,24},{20,28},{24,16},{28,20},{1,9},{5... | collective-permute-start | bytes 786440 | tf_op jit(solution)/shard_map/ppermute | solution.py:19
  211.1 9.6 %collective-permute-start.51 = (bf16[128,1024]{1,0:T(8,128)(2,1)S(1)}, bf16[128,1024]{1,0:T(8,128)(2,1)S(1)}, u32[]{:S(2)}, u32[]{:S(2)}) collective-permute-start(bf16[128,1024]{1,0:T(8,128)(2,1)S(1)} %get-tuple-element.125.refs_2_), channel_id=1, source_target_pairs={{0,16},{4,20},{8,24},{12,28},{16,0},{20,4},{24,8},{28,12},{1,17},{... | collective-permute-start | bytes 786440 | tf_op jit(solution)/shard_map/ppermute | solution.py:19
  221.3 14.9 %collective-permute-start.53 = (bf16[256,1024]{1,0:T(8,128)(2,1)S(1)}, bf16[256,1024]{1,0:T(8,128)(2,1)S(1)}, u32[]{:S(2)}, u32[]{:S(2)}) collective-permute-start(bf16[256,1024]{1,0:T(8,128)(2,1)S(1)} %get-tuple-element.109.refs_0_), channel_id=1, source_target_pairs={{0,8},{4,12},{8,0},{12,4},{16,24},{20,28},{24,16},{28,20},{1,9},{5... | collective-permute-start | bytes 1572872 | tf_op jit(solution)/shard_map/ppermute | solution.py:19
  222.2 14.9 %collective-permute-start.54 = (bf16[256,1024]{1,0:T(8,128)(2,1)S(1)}, bf16[256,1024]{1,0:T(8,128)(2,1)S(1)}, u32[]{:S(2)}, u32[]{:S(2)}) collective-permute-start(bf16[256,1024]{1,0:T(8,128)(2,1)S(1)} %get-tuple-element.110.refs_1_), channel_id=1, source_target_pairs={{0,16},{4,20},{8,24},{12,28},{16,0},{20,4},{24,8},{28,12},{1,17},{... | collective-permute-start | bytes 1572872 | tf_op jit(solution)/shard_map/ppermute | solution.py:19
  223.1 22.7 %collective-permute-start.55 = (bf16[256,1024]{1,0:T(8,128)(2,1)S(1)}, bf16[256,1024]{1,0:T(8,128)(2,1)S(1)}, u32[]{:S(2)}, u32[]{:S(2)}) collective-permute-start(bf16[256,1024]{1,0:T(8,128)(2,1)S(1)} %get-tuple-element.111.refs_2_), channel_id=1, source_target_pairs={{0,8},{4,12},{8,0},{12,4},{16,24},{20,28},{24,16},{28,20},{1,9},{5... | collective-permute-start | bytes 1572872 | tf_op jit(solution)/shard_map/ppermute | solution.py:19
  224.3 22.1 %collective-permute-start.56 = (bf16[256,1024]{1,0:T(8,128)(2,1)S(1)}, bf16[256,1024]{1,0:T(8,128)(2,1)S(1)}, u32[]{:S(2)}, u32[]{:S(2)}) collective-permute-start(bf16[256,1024]{1,0:T(8,128)(2,1)S(1)} %get-tuple-element.112.refs_3_), channel_id=1, source_target_pairs={{0,16},{4,20},{8,24},{12,28},{16,0},{20,4},{24,8},{28,12},{1,17},{... | collective-permute-start | bytes 1572872 | tf_op jit(solution)/shard_map/ppermute | solution.py:19
  247.2 7.4 %collective-permute-start.57 = (bf16[512,1024]{1,0:T(8,128)(2,1)S(1)}, bf16[512,1024]{1,0:T(8,128)(2,1)S(1)}, u32[]{:S(2)}, u32[]{:S(2)}) collective-permute-start(bf16[512,1024]{1,0:T(8,128)(2,1)S(1)} %get-tuple-element.113.refs_2_), channel_id=1, source_target_pairs={{0,4},{4,0},{8,12},{12,8},{16,20},{20,16},{24,28},{28,24},{1,5},{5... | collective-permute-start | bytes 3145736 | tf_op jit(solution)/shard_map/ppermute | solution.py:19
  (30 other events, 270.6 us)

commit v11 on v10

--- a/solution.py
+++ b/solution.py
@@ -451,10 +451,9 @@
 
     def body(place_ref, first_ref, second_ref, *refs):
         square_in_ref = refs[len(pieces)]
-        out_ref, square_ref, total_ref, sems = refs[-4:]
+        out_ref, square_ref = refs[-2:]
         core = place_ref[1]
         square_ref[...] = square_in_ref[...]
-        copies = []
         for path in range(n_path):
             total = lax.dot_general(
                 first_ref[...], refs[path][...], ROWS_BY_ROWS, preferred_element_type=F32
@@ -463,26 +462,16 @@
                 second_ref[...], refs[n_path + path][...], ROWS_BY_ROWS,
                 preferred_element_type=F32,
             )
-            total_ref[path] = total
             start = pl.multiple_of((2 * path + (core ^ flip)) * cols, cols)
-            copies.append(
-                pltpu.make_async_copy(
-                    total_ref.at[path], out_ref.at[:, pl.ds(start, cols)], sems.at[path]
-                )
-            )
-            copies[-1].start()
+            out_ref[:, pl.ds(start, cols)] = total
             square_ref[:8, :] += fold(total * total)
-        for copy in copies:
-            copy.wait()
 
     operands = [*turned, *pieces, squares] + ([] if done is None else [done])
-    hbm = pl.BlockSpec(memory_space=pl.ANY)
-    return run(
-        body, place, operands, [None] * (3 + len(pieces)) + ([] if done is None else [hbm]),
-        [like((depth, 2 * n_path * cols), F32), like(squares.shape, F32)], [hbm, None],
-        scratch=[pltpu.VMEM((n_path, depth, cols), F32), pltpu.SemaphoreType.DMA((n_path,))],
+    return run(
+        body, place, operands, [None] * len(operands),
+        [like((depth, 2 * n_path * cols), F32), like(squares.shape, F32)], [None, None],
         flops=4 * n_path * cols * batch * depth, moved=4 * n_path * depth * cols,
-        limit=20, aliases={len(operands): 0} if done is not None else {}, name="weight_grad_of",
+        limit=16, aliases={len(operands): 0} if done is not None else {}, name="weight_grad_of",
     )
 
 

time: 285 us -> 283 us (level)
  transfers between devices with their start and end apart: 68 -> 68, of which waited for: 44 -> 45; matrix products, arithmetic and copies ran while one was open for 0% -> 0% of each run, Pallas kernels for 16% -> 16%
where the time goes in v11:
time: 283 us
  waiting for transfers between devices  143 us (51%)
  starting transfers between devices  69.8 us (25%)
  Pallas kernels  63 us (22%)
  local copies, waits for them, and re-layouts  5.65 us (2%)
    ppermute x52, waiting for transfers between devices, swap(): lax.ppermute(value, axis, [(i, i ^ mask) for i in range(lax.axis_size(axi...  102 us
    pallas_call x31, Pallas kernels, run(): return call(scalars, *operands, *after)  63 us
    ppermute x52, starting transfers between devices, swap(): lax.ppermute(value, axis, [(i, i ^ mask) for i in range(lax.axis_size(axi...  52.8 us
    ppermute x9, waiting for transfers between devices, ring_step(): lax.ppermute(share, 'feat', [(i, (i + 1) % n_feat) for i in range(n_feat)])  32.8 us
    ppermute x9, starting transfers between devices, ring_step(): lax.ppermute(share, 'feat', [(i, (i + 1) % n_feat) for i in range(n_feat)])  9.07 us
    ppermute x7, waiting for transfers between devices, sum_everywhere(): lax.ppermute(value, axes, [(i, i ^ mask) for i in range(count)])  8.02 us
    ppermute x7, starting transfers between devices, sum_everywhere(): lax.ppermute(value, axes, [(i, i ^ mask) for i in range(count)])  7.93 us
  transfers between devices with their start and end apart: 68, of which 45 were waited for; matrix products, arithmetic and copies ran while one was open for 0% of the time, Pallas kernels for 16%

profile of v11, /device:TPU:0, one launch (start us, length us, event | category | flops | bytes accessed | tf_op | source)
XLA Modules:
  0.0 283.0 jit_solution(2335602605852245338)
XLA Ops:
  1.9 3.1 %collective-permute-start.10 = (bf16[64,2048]{1,0:T(8,128)(2,1)S(1)}, bf16[64,2048]{1,0:T(8,128)(2,1)}, u32[]{:S(2)}, u32[]{:S(2)}) collective-permute-start(bf16[64,2048]{1,0:T(8,128)(2,1)S(1)} %get-tuple-element.70.refs_0_), channel_id=1, source_target_pairs={{0,1},{1,2},{2,3},{3,0},{4,5},{5,6},{6,7},{7,4},{8,9},{9,10},{10,1... | collective-permute-start | bytes 786440 | tf_op jit(solution)/shard_map/ppermute | solution.py:171
  6.6 7.7 %collective-permute-done.10.refs_1_ = bf16[64,2048]{1,0:T(8,128)(2,1)} collective-permute-done((bf16[64,2048]{1,0:T(8,128)(2,1)S(1)}, bf16[64,2048]{1,0:T(8,128)(2,1)}, u32[]{:S(2)}, u32[]{:S(2)}) %collective-permute-start.10) | collective-permute-done | bytes 262176 | tf_op jit(solution)/shard_map/ppermute | solution.py:171
  15.9 3.9 %collective-permute-done.3.refs_1_.refs_0_ = bf16[64,2048]{1,0:T(8,128)(2,1)S(1)} collective-permute-done((bf16[64,2048]{1,0:T(8,128)(2,1)S(1)}, bf16[64,2048]{1,0:T(8,128)(2,1)S(1)}, u32[]{:S(2)}, u32[]{:S(2)}) %collective-permute-start.3) | collective-permute-done | bytes 262176 | tf_op jit(solution)/shard_map/ppermute | solution.py:171
  19.8 3.4 %copy-done = f32[1024,2048]{1,0:T(8,128)S(1)} copy-done((f32[1024,2048]{1,0:T(8,128)S(1)}, f32[1024,2048]{1,0:T(8,128)}, u32[]{:S(2)}) %copy-start) | copy-done | bytes 8388632
  23.2 4.6 %turn_weight.1 = (bf16[1024,1024]{1,0:T(8,128)(2,1)}, bf16[1024,1024]{1,0:T(8,128)(2,1)S(1)}, f32[16,128]{1,0:T(8,128)S(1)}) custom-call(s32[1]{0:T(128)} %bitcast.1.scalars_ref, f32[1024,2048]{1,0:T(8,128)S(1)} %copy-done, bf16[64,2048]{1,0:T(8,128)(2,1)S(1)} %collective-permute-done.3.refs_1_.refs_0_), custom_call_target="tpu_custom_call" | custom-call | flops 4194304 | bytes 12582912 | tf_op jit(solution)/shard_map/turn_weight/pallas_call | solution.py:85
  29.6 12.9 %collective-permute-done.5.refs_2_ = bf16[64,2048]{1,0:T(8,128)(2,1)} collective-permute-done((bf16[64,2048]{1,0:T(8,128)(2,1)S(1)}, bf16[64,2048]{1,0:T(8,128)(2,1)}, u32[]{:S(2)}, u32[]{:S(2)}) %collective-permute-start.5) | collective-permute-done | bytes 262176 | tf_op jit(solution)/shard_map/ppermute | solution.py:171
  42.5 5.5 %collective-permute-done.12.refs_3_ = bf16[64,2048]{1,0:T(8,128)(2,1)S(1)} collective-permute-done((bf16[64,2048]{1,0:T(8,128)(2,1)}, bf16[64,2048]{1,0:T(8,128)(2,1)S(1)}, u32[]{:S(2)}, u32[]{:S(2)}) %collective-permute-start.12) | collective-permute-done | bytes 262176 | tf_op jit(solution)/shard_map/ppermute | solution.py:171
  49.2 1.8 collective-permute-start.13
  54.9 1.8 collective-permute-start.7
  56.7 1.8 collective-permute-done.13.refs_5_
  58.5 1.8 collective-permute-start.8
  60.3 1.7 collective-permute-done.14.refs_6_
  63.6 1.8 collective-permute-done.15.refs_7_
  65.5 4.3 %collective-permute-done.7.refs_1_ = bf16[64,2048]{1,0:T(8,128)(2,1)S(1)} collective-permute-done((bf16[64,2048]{1,0:T(8,128)(2,1)S(1)}, bf16[64,2048]{1,0:T(8,128)(2,1)S(1)}, u32[]{:S(2)}, u32[]{:S(2)}) %collective-permute-start.7) | collective-permute-done | bytes 262176 | tf_op jit(solution)/shard_map/ppermute | solution.py:19
  69.8 3.8 %collective-permute-done.8.refs_2_ = bf16[64,2048]{1,0:T(8,128)(2,1)S(1)} collective-permute-done((bf16[64,2048]{1,0:T(8,128)(2,1)S(1)}, bf16[64,2048]{1,0:T(8,128)(2,1)S(1)}, u32[]{:S(2)}, u32[]{:S(2)}) %collective-permute-start.8) | collective-permute-done | bytes 262176 | tf_op jit(solution)/shard_map/ppermute | solution.py:19
  73.6 2.0 collect.2.refs_0_
  77.3 2.8 collective-permute-done.16.refs_1_
  80.1 2.5 assemble.2.refs_2_.refs_0_
  83.1 4.1 %forward.4 = (bf16[256,1024]{1,0:T(8,128)(2,1)S(1)}, bf16[256,1024]{1,0:T(8,128)(2,1)S(1)}) custom-call(s32[2]{0:T(128)S(1)} %get-tuple-element.122.scalars_ref, bf16[1024,1024]{1,0:T(8,128)(2,1)S(1)} %get-tuple-element.64.refs_1_.refs_8_.refs_0_, bf16[1024,1024]{1,0:T(8,128)(2,1)} %collective-permute-done.4.refs_1_, ...), custom_call_target="tpu_custom_call" | custom-call | flops 2147483648 | bytes 6291456 | tf_op jit(solution)/shard_map/forward/pallas_call | solution.py:85
  89.2 2.7 collective-permute-done.2.refs_3_
  98.5 4.1 %forward.5 = (bf16[256,1024]{1,0:T(8,128)(2,1)S(1)}, bf16[256,1024]{1,0:T(8,128)(2,1)S(1)}) custom-call(s32[2]{0:T(128)S(1)} %get-tuple-element.123.scalars_ref, bf16[1024,1024]{1,0:T(8,128)(2,1)S(1)} %get-tuple-element.64.refs_1_.refs_8_.refs_0_, bf16[1024,1024]{1,0:T(8,128)(2,1)} %collective-permute-done.4.refs_1_, ...), custom_call_target="tpu_custom_call" | custom-call | flops 2147483648 | bytes 6291456 | tf_op jit(solution)/shard_map/forward/pallas_call | solution.py:85
  104.3 10.4 %collective-permute-done.17.refs_1_ = bf16[128,2048]{1,0:T(8,128)(2,1)S(1)} collective-permute-done((bf16[128,2048]{1,0:T(8,128)(2,1)S(1)}, bf16[128,2048]{1,0:T(8,128)(2,1)S(1)}, u32[]{:S(2)}, u32[]{:S(2)}) %collective-permute-start.17) | collective-permute-done | bytes 524320 | tf_op jit(solution)/shard_map/ppermute | solution.py:19
  114.8 10.0 %collective-permute-done.19.refs_3_ = bf16[128,2048]{1,0:T(8,128)(2,1)S(1)} collective-permute-done((bf16[128,2048]{1,0:T(8,128)(2,1)S(1)}, bf16[128,2048]{1,0:T(8,128)(2,1)S(1)}, u32[]{:S(2)}, u32[]{:S(2)}) %collective-permute-start.19) | collective-permute-done | bytes 524320 | tf_op jit(solution)/shard_map/ppermute | solution.py:19
  127.7 2.0 collective-permute-done.22.refs_1_
  130.5 4.1 %forward.6 = (bf16[256,1024]{1,0:T(8,128)(2,1)S(1)}, bf16[256,1024]{1,0:T(8,128)(2,1)S(1)}) custom-call(s32[2]{0:T(128)S(1)} %get-tuple-element.122.scalars_ref, bf16[1024,1024]{1,0:T(8,128)(2,1)S(1)} %get-tuple-element.64.refs_1_.refs_8_.refs_0_, bf16[1024,1024]{1,0:T(8,128)(2,1)} %collective-permute-done.4.refs_1_, ...), custom_call_target="tpu_custom_call" | custom-call | flops 2147483648 | bytes 6291456 | tf_op jit(solution)/shard_map/forward/pallas_call | solution.py:85
  142.8 1.7 collective-permute-start.28
  144.5 4.1 %forward.7 = (bf16[256,1024]{1,0:T(8,128)(2,1)S(1)}, bf16[256,1024]{1,0:T(8,128)(2,1)S(1)}) custom-call(s32[2]{0:T(128)S(1)} %get-tuple-element.123.scalars_ref, bf16[1024,1024]{1,0:T(8,128)(2,1)S(1)} %get-tuple-element.64.refs_1_.refs_8_.refs_0_, bf16[1024,1024]{1,0:T(8,128)(2,1)} %collective-permute-done.4.refs_1_, ...), custom_call_target="tpu_custom_call" | custom-call | flops 2147483648 | bytes 6291456 | tf_op jit(solution)/shard_map/forward/pallas_call | solution.py:85
  148.6 2.0 collective-permute-done.36.refs_3_
  155.0 4.1 %collective-permute-done.28 = bf16[128,640]{1,0:T(8,128)(2,1)S(1)} collective-permute-done((bf16[128,640]{1,0:T(8,128)(2,1)S(1)}, bf16[128,640]{1,0:T(8,128)(2,1)S(1)}, u32[]{:S(2)}, u32[]{:S(2)}) %collective-permute-start.28) | collective-permute-done | bytes 163872 | tf_op jit(solution)/shard_map/ppermute | solution.py:19
  159.8 2.9 %collective-permute-done.37.refs_1_ = bf16[128,1024]{1,0:T(8,128)(2,1)S(1)} collective-permute-done((bf16[128,1024]{1,0:T(8,128)(2,1)S(1)}, bf16[128,1024]{1,0:T(8,128)(2,1)S(1)}, u32[]{:S(2)}, u32[]{:S(2)}) %collective-permute-start.37) | collective-permute-done | bytes 262176 | tf_op jit(solution)/shard_map/ppermute | solution.py:19
  164.6 1.9 collective-permute-start.30
  171.4 3.5 %collective-permute-done.30 = bf16[128,640]{1,0:T(8,128)(2,1)S(1)} collective-permute-done((bf16[128,640]{1,0:T(8,128)(2,1)S(1)}, bf16[128,640]{1,0:T(8,128)(2,1)S(1)}, u32[]{:S(2)}, u32[]{:S(2)}) %collective-permute-start.30) | collective-permute-done | bytes 163872 | tf_op jit(solution)/shard_map/ppermute | solution.py:19
  178.6 3.0 %collective-permute-done.41 = bf16[128,640]{1,0:T(8,128)(2,1)S(1)} collective-permute-done((bf16[128,640]{1,0:T(8,128)(2,1)S(1)}, bf16[128,640]{1,0:T(8,128)(2,1)S(1)}, u32[]{:S(2)}, u32[]{:S(2)}) %collective-permute-start.41) | collective-permute-done | bytes 163872 | tf_op jit(solution)/shard_map/ppermute | solution.py:19
  181.6 3.7 %collective-permute-start.43 = (bf16[128,640]{1,0:T(8,128)(2,1)S(1)}, bf16[128,640]{1,0:T(8,128)(2,1)S(1)}, u32[]{:S(2)}, u32[]{:S(2)}) collective-permute-start(bf16[128,640]{1,0:T(8,128)(2,1)S(1)} %add_convert_fusion.2), channel_id=1, source_target_pairs={{0,1},{1,0},{2,3},{3,2},{4,5},{5,4},{6,7},{7,6},{8,9},{9,8},{10,11... | collective-permute-start | bytes 491528 | tf_op jit(solution)/shard_map/ppermute | solution.py:19
  185.5 3.1 %collective-permute-done.43 = bf16[128,640]{1,0:T(8,128)(2,1)S(1)} collective-permute-done((bf16[128,640]{1,0:T(8,128)(2,1)S(1)}, bf16[128,640]{1,0:T(8,128)(2,1)S(1)}, u32[]{:S(2)}, u32[]{:S(2)}) %collective-permute-start.43) | collective-permute-done | bytes 163872 | tf_op jit(solution)/shard_map/ppermute | solution.py:19
  190.1 6.8 %collective-permute-done.44 = bf16[128,640]{1,0:T(8,128)(2,1)S(1)} collective-permute-done((bf16[128,640]{1,0:T(8,128)(2,1)S(1)}, bf16[128,640]{1,0:T(8,128)(2,1)S(1)}, u32[]{:S(2)}, u32[]{:S(2)}) %collective-permute-start.44) | collective-permute-done | bytes 163872 | tf_op jit(solution)/shard_map/ppermute | solution.py:19
  200.4 2.4 out_grad_of.2.refs_4_
  207.5 2.4 out_grad_of.3
  212.0 2.5 collective-permute-done.50.refs_5_
  215.8 4.0 %collective-permute-done.52.refs_7_ = bf16[128,1024]{1,0:T(8,128)(2,1)S(1)} collective-permute-done((bf16[128,1024]{1,0:T(8,128)(2,1)S(1)}, bf16[128,1024]{1,0:T(8,128)(2,1)S(1)}, u32[]{:S(2)}, u32[]{:S(2)}) %collective-permute-start.52) | collective-permute-done | bytes 262176 | tf_op jit(solution)/shard_map/ppermute | solution.py:19
  225.5 10.7 %collective-permute-done.53.refs_4_ = bf16[256,1024]{1,0:T(8,128)(2,1)S(1)} collective-permute-done((bf16[256,1024]{1,0:T(8,128)(2,1)S(1)}, bf16[256,1024]{1,0:T(8,128)(2,1)S(1)}, u32[]{:S(2)}, u32[]{:S(2)}) %collective-permute-start.53) | collective-permute-done | bytes 524320 | tf_op jit(solution)/shard_map/ppermute | solution.py:19
  237.1 8.8 %collective-permute-done.55.refs_6_ = bf16[256,1024]{1,0:T(8,128)(2,1)S(1)} collective-permute-done((bf16[256,1024]{1,0:T(8,128)(2,1)S(1)}, bf16[256,1024]{1,0:T(8,128)(2,1)S(1)}, u32[]{:S(2)}, u32[]{:S(2)}) %collective-permute-start.55) | collective-permute-done | bytes 524320 | tf_op jit(solution)/shard_map/ppermute | solution.py:19
  248.3 5.3 %weight_grad_of.2 = (f32[1024,2048]{1,0:T(8,128)S(1)}, f32[16,128]{1,0:T(8,128)S(1)}) custom-call(s32[2]{0:T(128)S(1)} %pad_add_fusion.scalars_ref, bf16[1024,1024]{1,0:T(8,128)(2,1)S(1)} %turn_columns.3.refs_3_.refs_0_, bf16[1024,1024]{1,0:T(8,128)(2,1)S(1)} %turn_columns.2.refs_3_.refs_1_, bf16[512,1024]{1,0:T(8,128)(2,1)S(1)} %get-tuple-element.113.refs_2_, ...), custom_call_target="tpu_custom_call" | custom-call | flops 4294967296 | bytes 4194304 | tf_op jit(solution)/shard_map/weight_grad_of/pallas_call | solution.py:85
  254.5 5.1 %weight_grad_of.3 = (f32[1024,2048]{1,0:T(8,128)S(1)}, f32[16,128]{1,0:T(8,128)S(1)}) custom-call(s32[2]{0:T(128)S(1)} %pad_add_fusion.scalars_ref, bf16[1024,1024]{1,0:T(8,128)(2,1)S(1)} %turn_columns.3.refs_3_.refs_0_, bf16[1024,1024]{1,0:T(8,128)(2,1)S(1)} %turn_columns.2.refs_3_.refs_1_, ...), custom_call_target="tpu_custom_call", output_to_operand_aliasing={{0}: (8, {})} | custom-call | flops 4294967296 | bytes 4194304 | tf_op jit(solution)/shard_map/weight_grad_of/pallas_call | solution.py:85
  259.5 3.9 %collective-permute-start.63 = (f32[16,128]{1,0:T(8,128)S(1)}, f32[16,128]{1,0:T(8,128)S(1)}, u32[]{:S(2)}, u32[]{:S(2)}) collective-permute-start(f32[16,128]{1,0:T(8,128)S(1)} %get-tuple-element.120), channel_id=1, source_target_pairs={{0,3},{1,2},{2,1},{3,0},{4,7},{5,6},{6,5},{7,4},{8,11},{9,10},{10,... | collective-permute-start | bytes 24584 | tf_op jit(solution)/shard_map/ppermute | solution.py:40
  265.1 2.9 %collective-permute-done.62 = f32[16,128]{1,0:T(8,128)S(1)} collective-permute-done((f32[16,128]{1,0:T(8,128)S(1)}, f32[16,128]{1,0:T(8,128)S(1)}, u32[]{:S(2)}, u32[]{:S(2)}) %collective-permute-start.62) | collective-permute-done | bytes 8224 | tf_op jit(solution)/shard_map/ppermute | solution.py:40
  273.3 2.2 collective-permute-done.67.refs_1_
  275.6 7.5 %update.1 = (f32[1024,2048]{1,0:T(8,128)}, f32[1024,2048]{1,0:T(8,128)}) custom-call(s32[1]{0:T(128)} %constant.21.clone.1.scalars_ref, f32[16,128]{1,0:T(8,128)S(1)} %add_add_fusion.refs_0_, f32[16,128]{1,0:T(8,128)S(1)} %collective-permute-done.67.refs_1_, f32[1024,2048]{1,0:T(8,128)S(1)} %bitcast.9, f32[1024,2048]{1,0:T(8,128)S(1)} %bitcast.11, ...), custom_call_target="tpu_custom_call" | custom-call | flops 8388608 | bytes 41943040 | tf_op jit(solution)/shard_map/update/pallas_call | solution.py:85
  (157 shorter events, 83.0 us)
Async XLA Ops:
  1.9 12.3 %collective-permute-start.10 = (bf16[64,2048]{1,0:T(8,128)(2,1)S(1)}, bf16[64,2048]{1,0:T(8,128)(2,1)}, u32[]{:S(2)}, u32[]{:S(2)}) collective-permute-start(bf16[64,2048]{1,0:T(8,128)(2,1)S(1)} %get-tuple-element.70.refs_0_), channel_id=1, source_target_pairs={{0,1},{1,2},{2,3},{3,0},{4,5},{5,6},{6,7},{7,4},{8,9},{9,10},{10,1... | collective-permute-start | bytes 786440 | tf_op jit(solution)/shard_map/ppermute | solution.py:171
  5.0 14.8 %collective-permute-start.3 = (bf16[64,2048]{1,0:T(8,128)(2,1)S(1)}, bf16[64,2048]{1,0:T(8,128)(2,1)S(1)}, u32[]{:S(2)}, u32[]{:S(2)}) collective-permute-start(bf16[64,2048]{1,0:T(8,128)(2,1)S(1)} %get-tuple-element.63.refs_0_), channel_id=1, source_target_pairs={{0,1},{1,2},{2,3},{3,0},{4,5},{5,6},{6,7},{7,4},{8,9},{9,10},{10,1... | collective-permute-start | bytes 786440 | tf_op jit(solution)/shard_map/ppermute | solution.py:171
  14.3 13.6 %collective-permute-start.11 = (bf16[64,2048]{1,0:T(8,128)(2,1)}, bf16[64,2048]{1,0:T(8,128)(2,1)}, u32[]{:S(2)}, u32[]{:S(2)}) collective-permute-start(bf16[64,2048]{1,0:T(8,128)(2,1)} %collective-permute-done.10.refs_1_), channel_id=1, source_target_pairs={{0,1},{1,2},{2,3},{3,0},{4,5},{5,6},{6,7},{7,4},{8,9},{9,10},{10,1... | collective-permute-start | bytes 786440 | tf_op jit(solution)/shard_map/ppermute | solution.py:171
  14.3 36.7 %collective-permute-start = (bf16[128,2048]{1,0:T(8,128)(2,1)S(1)}, bf16[128,2048]{1,0:T(8,128)(2,1)}, u32[]{:S(2)}, u32[]{:S(2)}) collective-permute-start(bf16[128,2048]{1,0:T(8,128)(2,1)S(1)} %get-tuple-element.62.refs_0_), channel_id=1, source_target_pairs={{0,1},{1,2},{2,3},{3,0},{4,5},{5,6},{6,7},{7,4},{8,9},{9,10},{10,1... | collective-permute-start | bytes 1572872 | tf_op jit(solution)/shard_map/ppermute | solution.py:171
  27.8 14.7 %collective-permute-start.5 = (bf16[64,2048]{1,0:T(8,128)(2,1)S(1)}, bf16[64,2048]{1,0:T(8,128)(2,1)}, u32[]{:S(2)}, u32[]{:S(2)}) collective-permute-start(bf16[64,2048]{1,0:T(8,128)(2,1)S(1)} %relay.1.refs_1_), channel_id=1, source_target_pairs={{0,1},{1,2},{2,3},{3,0},{4,5},{5,6},{6,7},{7,4},{8,9},{9,10},{10,1... | collective-permute-start | bytes 786440 | tf_op jit(solution)/shard_map/ppermute | solution.py:171
  27.9 20.1 %collective-permute-start.12 = (bf16[64,2048]{1,0:T(8,128)(2,1)}, bf16[64,2048]{1,0:T(8,128)(2,1)S(1)}, u32[]{:S(2)}, u32[]{:S(2)}) collective-permute-start(bf16[64,2048]{1,0:T(8,128)(2,1)} %collective-permute-done.11.refs_2_), channel_id=1, source_target_pairs={{0,1},{1,2},{2,3},{3,0},{4,5},{5,6},{6,7},{7,4},{8,9},{9,10},{10,1... | collective-permute-start | bytes 786440 | tf_op jit(solution)/shard_map/ppermute | solution.py:171
  42.5 10.3 %collective-permute-start.6 = (bf16[64,2048]{1,0:T(8,128)(2,1)}, bf16[64,2048]{1,0:T(8,128)(2,1)S(1)}, u32[]{:S(2)}, u32[]{:S(2)}) collective-permute-start(bf16[64,2048]{1,0:T(8,128)(2,1)} %collective-permute-done.5.refs_2_), channel_id=1, source_target_pairs={{0,1},{1,2},{2,3},{3,0},{4,5},{5,6},{6,7},{7,4},{8,9},{9,10},{10,1... | collective-permute-start | bytes 786440 | tf_op jit(solution)/shard_map/ppermute | solution.py:171
  49.2 9.3 %collective-permute-start.13 = (bf16[64,2048]{1,0:T(8,128)(2,1)S(1)}, bf16[64,2048]{1,0:T(8,128)(2,1)S(1)}, u32[]{:S(2)}, u32[]{:S(2)}) collective-permute-start(bf16[64,2048]{1,0:T(8,128)(2,1)S(1)} %get-tuple-element.72), channel_id=1, source_target_pairs={{0,8},{4,12},{8,0},{12,4},{16,24},{20,28},{24,16},{28,20},{1,9},{5... | collective-permute-start | bytes 786440 | tf_op jit(solution)/shard_map/ppermute | solution.py:19
  51.0 14.4 %collective-permute-start.1 = (bf16[128,2048]{1,0:T(8,128)(2,1)}, bf16[128,2048]{1,0:T(8,128)(2,1)S(1)}, u32[]{:S(2)}, u32[]{:S(2)}) collective-permute-start(bf16[128,2048]{1,0:T(8,128)(2,1)} %collective-permute-done.refs_1_), channel_id=1, source_target_pairs={{0,1},{1,2},{2,3},{3,0},{4,5},{5,6},{6,7},{7,4},{8,9},{9,10},{10,1... | collective-permute-start | bytes 1572872 | tf_op jit(solution)/shard_map/ppermute | solution.py:171
  51.1 11.0 %collective-permute-start.14 = (bf16[64,2048]{1,0:T(8,128)(2,1)S(1)}, bf16[64,2048]{1,0:T(8,128)(2,1)S(1)}, u32[]{:S(2)}, u32[]{:S(2)}) collective-permute-start(bf16[64,2048]{1,0:T(8,128)(2,1)S(1)} %get-tuple-element.73), channel_id=1, source_target_pairs={{0,16},{4,20},{8,24},{12,28},{16,0},{20,4},{24,8},{28,12},{1,17},{... | collective-permute-start | bytes 786440 | tf_op jit(solution)/shard_map/ppermute | solution.py:19
  52.6 12.9 %collective-permute-start.15 = (bf16[64,2048]{1,0:T(8,128)(2,1)S(1)}, bf16[64,2048]{1,0:T(8,128)(2,1)S(1)}, u32[]{:S(2)}, u32[]{:S(2)}) collective-permute-start(bf16[64,2048]{1,0:T(8,128)(2,1)S(1)} %get-tuple-element.74), channel_id=1, source_target_pairs={{0,24},{4,28},{8,16},{12,20},{16,8},{20,12},{24,0},{28,4},{1,25},{... | collective-permute-start | bytes 786440 | tf_op jit(solution)/shard_map/ppermute | solution.py:19
  54.9 14.9 %collective-permute-start.7 = (bf16[64,2048]{1,0:T(8,128)(2,1)S(1)}, bf16[64,2048]{1,0:T(8,128)(2,1)S(1)}, u32[]{:S(2)}, u32[]{:S(2)}) collective-permute-start(bf16[64,2048]{1,0:T(8,128)(2,1)S(1)} %get-tuple-element.67), channel_id=1, source_target_pairs={{0,8},{4,12},{8,0},{12,4},{16,24},{20,28},{24,16},{28,20},{1,9},{5... | collective-permute-start | bytes 786440 | tf_op jit(solution)/shard_map/ppermute | solution.py:19
  58.5 15.0 %collective-permute-start.8 = (bf16[64,2048]{1,0:T(8,128)(2,1)S(1)}, bf16[64,2048]{1,0:T(8,128)(2,1)S(1)}, u32[]{:S(2)}, u32[]{:S(2)}) collective-permute-start(bf16[64,2048]{1,0:T(8,128)(2,1)S(1)} %get-tuple-element.68), channel_id=1, source_target_pairs={{0,16},{4,20},{8,24},{12,28},{16,0},{20,4},{24,8},{28,12},{1,17},{... | collective-permute-start | bytes 786440 | tf_op jit(solution)/shard_map/ppermute | solution.py:19
  62.0 11.5 %collective-permute-start.9 = (bf16[64,2048]{1,0:T(8,128)(2,1)S(1)}, bf16[64,2048]{1,0:T(8,128)(2,1)S(1)}, u32[]{:S(2)}, u32[]{:S(2)}) collective-permute-start(bf16[64,2048]{1,0:T(8,128)(2,1)S(1)} %get-tuple-element.69), channel_id=1, source_target_pairs={{0,24},{4,28},{8,16},{12,20},{16,8},{20,12},{24,0},{28,4},{1,25},{... | collective-permute-start | bytes 786440 | tf_op jit(solution)/shard_map/ppermute | solution.py:19
  75.6 7.5 %collective-permute-start.4 = (bf16[1024,1024]{1,0:T(8,128)(2,1)}, bf16[1024,1024]{1,0:T(8,128)(2,1)}, u32[]{:S(2)}, u32[]{:S(2)}) collective-permute-start(bf16[1024,1024]{1,0:T(8,128)(2,1)} %get-tuple-element.65), channel_id=1, source_target_pairs={{0,4},{4,0},{8,12},{12,8},{16,20},{20,16},{24,28},{28,24},{1,5},{5... | collective-permute-start | bytes 6291464 | tf_op jit(solution)/shard_map/ppermute | solution.py:19
  76.1 15.9 %collective-permute-start.2 = (bf16[128,2048]{1,0:T(8,128)(2,1)S(1)}, bf16[128,2048]{1,0:T(8,128)(2,1)}, u32[]{:S(2)}, u32[]{:S(2)}) collective-permute-start(bf16[128,2048]{1,0:T(8,128)(2,1)S(1)} %collective-permute-done.1.refs_9_.refs_2_), channel_id=1, source_target_pairs={{0,1},{1,2},{2,3},{3,0},{4,5},{5,6},{6,7},{7,4},{8,9},{9,10},{10,1... | collective-permute-start | bytes 1572872 | tf_op jit(solution)/shard_map/ppermute | solution.py:171
  87.1 15.5 %collective-permute-start.21 = (bf16[256,1024]{1,0:T(8,128)(2,1)S(1)}, bf16[256,1024]{1,0:T(8,128)(2,1)S(1)}, u32[]{:S(2)}, u32[]{:S(2)}) collective-permute-start(bf16[256,1024]{1,0:T(8,128)(2,1)S(1)} %get-tuple-element.82), channel_id=1, source_target_pairs={{0,16},{4,20},{8,24},{12,28},{16,0},{20,4},{24,8},{28,12},{1,17},{... | collective-permute-start | bytes 1572872 | tf_op jit(solution)/shard_map/ppermute | solution.py:19
  88.7 14.8 %collective-permute-start.20 = (bf16[256,1024]{1,0:T(8,128)(2,1)S(1)}, bf16[256,1024]{1,0:T(8,128)(2,1)S(1)}, u32[]{:S(2)}, u32[]{:S(2)}) collective-permute-start(bf16[256,1024]{1,0:T(8,128)(2,1)S(1)} %get-tuple-element.75.refs_4_), channel_id=1, source_target_pairs={{0,8},{4,12},{8,0},{12,4},{16,24},{20,28},{24,16},{28,20},{1,9},{5... | collective-permute-start | bytes 1572872 | tf_op jit(solution)/shard_map/ppermute | solution.py:19
  93.6 21.1 %collective-permute-start.17 = (bf16[128,2048]{1,0:T(8,128)(2,1)S(1)}, bf16[128,2048]{1,0:T(8,128)(2,1)S(1)}, u32[]{:S(2)}, u32[]{:S(2)}) collective-permute-start(bf16[128,2048]{1,0:T(8,128)(2,1)S(1)} %get-tuple-element.77), channel_id=1, source_target_pairs={{0,8},{4,12},{8,0},{12,4},{16,24},{20,28},{24,16},{28,20},{1,9},{5... | collective-permute-start | bytes 1572872 | tf_op jit(solution)/shard_map/ppermute | solution.py:19
  94.8 20.0 %collective-permute-start.18 = (bf16[128,2048]{1,0:T(8,128)(2,1)S(1)}, bf16[128,2048]{1,0:T(8,128)(2,1)S(1)}, u32[]{:S(2)}, u32[]{:S(2)}) collective-permute-start(bf16[128,2048]{1,0:T(8,128)(2,1)S(1)} %get-tuple-element.78), channel_id=1, source_target_pairs={{0,16},{4,20},{8,24},{12,28},{16,0},{20,4},{24,8},{28,12},{1,17},{... | collective-permute-start | bytes 1572872 | tf_op jit(solution)/shard_map/ppermute | solution.py:19
  95.6 29.2 %collective-permute-start.19 = (bf16[128,2048]{1,0:T(8,128)(2,1)S(1)}, bf16[128,2048]{1,0:T(8,128)(2,1)S(1)}, u32[]{:S(2)}, u32[]{:S(2)}) collective-permute-start(bf16[128,2048]{1,0:T(8,128)(2,1)S(1)} %get-tuple-element.79), channel_id=1, source_target_pairs={{0,24},{4,28},{8,16},{12,20},{16,8},{20,12},{24,0},{28,4},{1,25},{... | collective-permute-start | bytes 1572872 | tf_op jit(solution)/shard_map/ppermute | solution.py:19
  125.6 9.0 %collective-permute-start.24 = (bf16[128,1024]{1,0:T(8,128)(2,1)S(1)}, bf16[128,1024]{1,0:T(8,128)(2,1)S(1)}, u32[]{:S(2)}, u32[]{:S(2)}) collective-permute-start(bf16[128,1024]{1,0:T(8,128)(2,1)S(1)} %get-tuple-element.86), channel_id=1, source_target_pairs={{0,8},{4,12},{8,0},{12,4},{16,24},{20,28},{24,16},{28,20},{1,9},{5... | collective-permute-start | bytes 786440 | tf_op jit(solution)/shard_map/ppermute | solution.py:19
  126.9 8.4 %collective-permute-start.23 = (bf16[128,1024]{1,0:T(8,128)(2,1)S(1)}, bf16[128,1024]{1,0:T(8,128)(2,1)S(1)}, u32[]{:S(2)}, u32[]{:S(2)}) collective-permute-start(bf16[128,1024]{1,0:T(8,128)(2,1)S(1)} %get-tuple-element.83.refs_4_), channel_id=1, source_target_pairs={{0,16},{4,20},{8,24},{12,28},{16,0},{20,4},{24,8},{28,12},{1,17},{... | collective-permute-start | bytes 786440 | tf_op jit(solution)/shard_map/ppermute | solution.py:19
  135.8 14.8 %collective-permute-start.36 = (bf16[256,1024]{1,0:T(8,128)(2,1)S(1)}, bf16[256,1024]{1,0:T(8,128)(2,1)S(1)}, u32[]{:S(2)}, u32[]{:S(2)}) collective-permute-start(bf16[256,1024]{1,0:T(8,128)(2,1)S(1)} %get-tuple-element.95), channel_id=1, source_target_pairs={{0,16},{4,20},{8,24},{12,28},{16,0},{20,4},{24,8},{28,12},{1,17},{... | collective-permute-start | bytes 1572872 | tf_op jit(solution)/shard_map/ppermute | solution.py:19
  136.8 14.8 %collective-permute-start.35 = (bf16[256,1024]{1,0:T(8,128)(2,1)S(1)}, bf16[256,1024]{1,0:T(8,128)(2,1)S(1)}, u32[]{:S(2)}, u32[]{:S(2)}) collective-permute-start(bf16[256,1024]{1,0:T(8,128)(2,1)S(1)} %get-tuple-element.87.refs_4_), channel_id=1, source_target_pairs={{0,8},{4,12},{8,0},{12,4},{16,24},{20,28},{24,16},{28,20},{1,9},{5... | collective-permute-start | bytes 1572872 | tf_op jit(solution)/shard_map/ppermute | solution.py:19
  141.0 14.1 %collective-permute-start.26 = (bf16[128,640]{1,0:T(8,128)(2,1)S(1)}, bf16[128,640]{1,0:T(8,128)(2,1)S(1)}, u32[]{:S(2)}, u32[]{:S(2)}) collective-permute-start(bf16[128,640]{1,0:T(8,128)(2,1)S(1)} %get-tuple-element.90), channel_id=1, source_target_pairs={{0,8},{4,12},{8,0},{12,4},{16,24},{20,28},{24,16},{28,20},{1,9},{5... | collective-permute-start | bytes 491528 | tf_op jit(solution)/shard_map/ppermute | solution.py:19
  141.7 13.4 %collective-permute-start.27 = (bf16[128,640]{1,0:T(8,128)(2,1)S(1)}, bf16[128,640]{1,0:T(8,128)(2,1)S(1)}, u32[]{:S(2)}, u32[]{:S(2)}) collective-permute-start(bf16[128,640]{1,0:T(8,128)(2,1)S(1)} %get-tuple-element.91), channel_id=1, source_target_pairs={{0,16},{4,20},{8,24},{12,28},{16,0},{20,4},{24,8},{28,12},{1,17},{... | collective-permute-start | bytes 491528 | tf_op jit(solution)/shard_map/ppermute | solution.py:19
  142.8 16.4 %collective-permute-start.28 = (bf16[128,640]{1,0:T(8,128)(2,1)S(1)}, bf16[128,640]{1,0:T(8,128)(2,1)S(1)}, u32[]{:S(2)}, u32[]{:S(2)}) collective-permute-start(bf16[128,640]{1,0:T(8,128)(2,1)S(1)} %get-tuple-element.92), channel_id=1, source_target_pairs={{0,24},{4,28},{8,16},{12,20},{16,8},{20,12},{24,0},{28,4},{1,25},{... | collective-permute-start | bytes 491528 | tf_op jit(solution)/shard_map/ppermute | solution.py:19
  152.3 10.4 %collective-permute-start.37 = (bf16[128,1024]{1,0:T(8,128)(2,1)S(1)}, bf16[128,1024]{1,0:T(8,128)(2,1)S(1)}, u32[]{:S(2)}, u32[]{:S(2)}) collective-permute-start(bf16[128,1024]{1,0:T(8,128)(2,1)S(1)} %get-tuple-element.97), channel_id=1, source_target_pairs={{0,16},{4,20},{8,24},{12,28},{16,0},{20,4},{24,8},{28,12},{1,17},{... | collective-permute-start | bytes 786440 | tf_op jit(solution)/shard_map/ppermute | solution.py:19
  153.5 9.9 %collective-permute-start.38 = (bf16[128,1024]{1,0:T(8,128)(2,1)S(1)}, bf16[128,1024]{1,0:T(8,128)(2,1)S(1)}, u32[]{:S(2)}, u32[]{:S(2)}) collective-permute-start(bf16[128,1024]{1,0:T(8,128)(2,1)S(1)} %get-tuple-element.99), channel_id=1, source_target_pairs={{0,8},{4,12},{8,0},{12,4},{16,24},{20,28},{24,16},{28,20},{1,9},{5... | collective-permute-start | bytes 786440 | tf_op jit(solution)/shard_map/ppermute | solution.py:19
  164.6 10.3 %collective-permute-start.30 = (bf16[128,640]{1,0:T(8,128)(2,1)S(1)}, bf16[128,640]{1,0:T(8,128)(2,1)S(1)}, u32[]{:S(2)}, u32[]{:S(2)}) collective-permute-start(bf16[128,640]{1,0:T(8,128)(2,1)S(1)} %add_convert_fusion.4), channel_id=1, source_target_pairs={{0,2},{1,3},{2,0},{3,1},{4,6},{5,7},{6,4},{7,5},{8,10},{9,11},{10,... | collective-permute-start | bytes 491528 | tf_op jit(solution)/shard_map/ppermute | solution.py:19
  167.9 10.1 %collective-permute-start.40 = (bf16[128,640]{1,0:T(8,128)(2,1)S(1)}, bf16[128,640]{1,0:T(8,128)(2,1)S(1)}, u32[]{:S(2)}, u32[]{:S(2)}) collective-permute-start(bf16[128,640]{1,0:T(8,128)(2,1)S(1)} %get-tuple-element.104), channel_id=1, source_target_pairs={{0,8},{4,12},{8,0},{12,4},{16,24},{20,28},{24,16},{28,20},{1,9},{5... | collective-permute-start | bytes 491528 | tf_op jit(solution)/shard_map/ppermute | solution.py:19
  169.2 12.3 %collective-permute-start.41 = (bf16[128,640]{1,0:T(8,128)(2,1)S(1)}, bf16[128,640]{1,0:T(8,128)(2,1)S(1)}, u32[]{:S(2)}, u32[]{:S(2)}) collective-permute-start(bf16[128,640]{1,0:T(8,128)(2,1)S(1)} %get-tuple-element.105), channel_id=1, source_target_pairs={{0,16},{4,20},{8,24},{12,28},{16,0},{20,4},{24,8},{28,12},{1,17},{... | collective-permute-start | bytes 491528 | tf_op jit(solution)/shard_map/ppermute | solution.py:19
  170.9 10.6 %collective-permute-start.42 = (bf16[128,640]{1,0:T(8,128)(2,1)S(1)}, bf16[128,640]{1,0:T(8,128)(2,1)S(1)}, u32[]{:S(2)}, u32[]{:S(2)}) collective-permute-start(bf16[128,640]{1,0:T(8,128)(2,1)S(1)} %get-tuple-element.106), channel_id=1, source_target_pairs={{0,24},{4,28},{8,16},{12,20},{16,8},{20,12},{24,0},{28,4},{1,25},{... | collective-permute-start | bytes 491528 | tf_op jit(solution)/shard_map/ppermute | solution.py:19
  175.0 10.3 %collective-permute-start.33 = (bf16[128,640]{1,0:T(8,128)(2,1)S(1)}, bf16[128,640]{1,0:T(8,128)(2,1)S(1)}, u32[]{:S(2)}, u32[]{:S(2)}) collective-permute-start(bf16[128,640]{1,0:T(8,128)(2,1)S(1)} %add_convert_fusion.3.refs_0_), channel_id=1, source_target_pairs={{0,24},{4,28},{8,16},{12,20},{16,8},{20,12},{24,0},{28,4},{1,25},{... | collective-permute-start | bytes 491528 | tf_op jit(solution)/shard_map/ppermute | solution.py:19
  176.4 9.0 %collective-permute-start.32 = (bf16[128,640]{1,0:T(8,128)(2,1)S(1)}, bf16[128,640]{1,0:T(8,128)(2,1)S(1)}, u32[]{:S(2)}, u32[]{:S(2)}) collective-permute-start(bf16[128,640]{1,0:T(8,128)(2,1)S(1)} %add_convert_fusion.3.refs_0_), channel_id=1, source_target_pairs={{0,16},{4,20},{8,24},{12,28},{16,0},{20,4},{24,8},{28,12},{1,17},{... | collective-permute-start | bytes 491528 | tf_op jit(solution)/shard_map/ppermute | solution.py:19
  177.9 7.5 %collective-permute-start.31 = (bf16[128,640]{1,0:T(8,128)(2,1)S(1)}, bf16[128,640]{1,0:T(8,128)(2,1)S(1)}, u32[]{:S(2)}, u32[]{:S(2)}) collective-permute-start(bf16[128,640]{1,0:T(8,128)(2,1)S(1)} %add_convert_fusion.3.refs_0_), channel_id=1, source_target_pairs={{0,8},{4,12},{8,0},{12,4},{16,24},{20,28},{24,16},{28,20},{1,9},{5... | collective-permute-start | bytes 491528 | tf_op jit(solution)/shard_map/ppermute | solution.py:19
  181.6 7.0 %collective-permute-start.43 = (bf16[128,640]{1,0:T(8,128)(2,1)S(1)}, bf16[128,640]{1,0:T(8,128)(2,1)S(1)}, u32[]{:S(2)}, u32[]{:S(2)}) collective-permute-start(bf16[128,640]{1,0:T(8,128)(2,1)S(1)} %add_convert_fusion.2), channel_id=1, source_target_pairs={{0,1},{1,0},{2,3},{3,2},{4,5},{5,4},{6,7},{7,6},{8,9},{9,8},{10,11... | collective-permute-start | bytes 491528 | tf_op jit(solution)/shard_map/ppermute | solution.py:19
  185.5 15.0 %collective-permute-start.34 = (bf16[4,128,640]{2,1,0:T(8,128)(2,1)S(1)}, bf16[4,128,640]{2,1,0:T(8,128)(2,1)S(1)}, u32[]{:S(2)}, u32[]{:S(2)}) collective-permute-start(bf16[4,128,640]{2,1,0:T(8,128)(2,1)S(1)} %pile.2.refs_0_), channel_id=1, source_target_pairs={{0,4},{4,0},{8,12},{12,8},{16,20},{20,16},{24,28},{28,24},{1,5},{5... | collective-permute-start | bytes 1966088 | tf_op jit(solution)/shard_map/ppermute | solution.py:19
  188.7 8.2 %collective-permute-start.44 = (bf16[128,640]{1,0:T(8,128)(2,1)S(1)}, bf16[128,640]{1,0:T(8,128)(2,1)S(1)}, u32[]{:S(2)}, u32[]{:S(2)}) collective-permute-start(bf16[128,640]{1,0:T(8,128)(2,1)S(1)} %add_convert_fusion.1), channel_id=1, source_target_pairs={{0,2},{1,3},{2,0},{3,1},{4,6},{5,7},{6,4},{7,5},{8,10},{9,11},{10,... | collective-permute-start | bytes 491528 | tf_op jit(solution)/shard_map/ppermute | solution.py:19
  205.3 9.2 %collective-permute-start.50 = (bf16[128,1024]{1,0:T(8,128)(2,1)S(1)}, bf16[128,1024]{1,0:T(8,128)(2,1)S(1)}, u32[]{:S(2)}, u32[]{:S(2)}) collective-permute-start(bf16[128,1024]{1,0:T(8,128)(2,1)S(1)} %get-tuple-element.126.refs_1_), channel_id=1, source_target_pairs={{0,8},{4,12},{8,0},{12,4},{16,24},{20,28},{24,16},{28,20},{1,9},{5... | collective-permute-start | bytes 786440 | tf_op jit(solution)/shard_map/ppermute | solution.py:19
  206.6 9.1 %collective-permute-start.49 = (bf16[128,1024]{1,0:T(8,128)(2,1)S(1)}, bf16[128,1024]{1,0:T(8,128)(2,1)S(1)}, u32[]{:S(2)}, u32[]{:S(2)}) collective-permute-start(bf16[128,1024]{1,0:T(8,128)(2,1)S(1)} %get-tuple-element.127.refs_0_), channel_id=1, source_target_pairs={{0,16},{4,20},{8,24},{12,28},{16,0},{20,4},{24,8},{28,12},{1,17},{... | collective-permute-start | bytes 786440 | tf_op jit(solution)/shard_map/ppermute | solution.py:19
  209.9 9.8 %collective-permute-start.52 = (bf16[128,1024]{1,0:T(8,128)(2,1)S(1)}, bf16[128,1024]{1,0:T(8,128)(2,1)S(1)}, u32[]{:S(2)}, u32[]{:S(2)}) collective-permute-start(bf16[128,1024]{1,0:T(8,128)(2,1)S(1)} %get-tuple-element.124.refs_3_), channel_id=1, source_target_pairs={{0,8},{4,12},{8,0},{12,4},{16,24},{20,28},{24,16},{28,20},{1,9},{5... | collective-permute-start | bytes 786440 | tf_op jit(solution)/shard_map/ppermute | solution.py:19
  211.1 9.6 %collective-permute-start.51 = (bf16[128,1024]{1,0:T(8,128)(2,1)S(1)}, bf16[128,1024]{1,0:T(8,128)(2,1)S(1)}, u32[]{:S(2)}, u32[]{:S(2)}) collective-permute-start(bf16[128,1024]{1,0:T(8,128)(2,1)S(1)} %get-tuple-element.125.refs_2_), channel_id=1, source_target_pairs={{0,16},{4,20},{8,24},{12,28},{16,0},{20,4},{24,8},{28,12},{1,17},{... | collective-permute-start | bytes 786440 | tf_op jit(solution)/shard_map/ppermute | solution.py:19
  221.3 14.9 %collective-permute-start.53 = (bf16[256,1024]{1,0:T(8,128)(2,1)S(1)}, bf16[256,1024]{1,0:T(8,128)(2,1)S(1)}, u32[]{:S(2)}, u32[]{:S(2)}) collective-permute-start(bf16[256,1024]{1,0:T(8,128)(2,1)S(1)} %get-tuple-element.109.refs_0_), channel_id=1, source_target_pairs={{0,8},{4,12},{8,0},{12,4},{16,24},{20,28},{24,16},{28,20},{1,9},{5... | collective-permute-start | bytes 1572872 | tf_op jit(solution)/shard_map/ppermute | solution.py:19
  222.2 14.9 %collective-permute-start.54 = (bf16[256,1024]{1,0:T(8,128)(2,1)S(1)}, bf16[256,1024]{1,0:T(8,128)(2,1)S(1)}, u32[]{:S(2)}, u32[]{:S(2)}) collective-permute-start(bf16[256,1024]{1,0:T(8,128)(2,1)S(1)} %get-tuple-element.110.refs_1_), channel_id=1, source_target_pairs={{0,16},{4,20},{8,24},{12,28},{16,0},{20,4},{24,8},{28,12},{1,17},{... | collective-permute-start | bytes 1572872 | tf_op jit(solution)/shard_map/ppermute | solution.py:19
  223.1 22.7 %collective-permute-start.55 = (bf16[256,1024]{1,0:T(8,128)(2,1)S(1)}, bf16[256,1024]{1,0:T(8,128)(2,1)S(1)}, u32[]{:S(2)}, u32[]{:S(2)}) collective-permute-start(bf16[256,1024]{1,0:T(8,128)(2,1)S(1)} %get-tuple-element.111.refs_2_), channel_id=1, source_target_pairs={{0,8},{4,12},{8,0},{12,4},{16,24},{20,28},{24,16},{28,20},{1,9},{5... | collective-permute-start | bytes 1572872 | tf_op jit(solution)/shard_map/ppermute | solution.py:19
  224.3 22.1 %collective-permute-start.56 = (bf16[256,1024]{1,0:T(8,128)(2,1)S(1)}, bf16[256,1024]{1,0:T(8,128)(2,1)S(1)}, u32[]{:S(2)}, u32[]{:S(2)}) collective-permute-start(bf16[256,1024]{1,0:T(8,128)(2,1)S(1)} %get-tuple-element.112.refs_3_), channel_id=1, source_target_pairs={{0,16},{4,20},{8,24},{12,28},{16,0},{20,4},{24,8},{28,12},{1,17},{... | collective-permute-start | bytes 1572872 | tf_op jit(solution)/shard_map/ppermute | solution.py:19
  (30 other events, 263.4 us)

commit v12 on v11

--- a/solution.py
+++ b/solution.py
@@ -444,33 +444,41 @@
     return out_grad
 
 
-def weight_grad_of(place, turned, pieces, flip, squares, done=None):
-    depth, batch = turned[0].shape
-    cols = pieces[0].shape[0]
-    n_path = len(pieces) // 2
-
-    def body(place_ref, first_ref, second_ref, *refs):
-        square_in_ref = refs[len(pieces)]
-        out_ref, square_ref = refs[-2:]
+def weight_grad_of(place, views, flip, squares=None, done=None, add=False):
+    depth, batch = views[0][0].shape
+    n_path = len(views[0][1])
+    cols = views[0][1][0].shape[0]
+    operands = [one for turned, pieces in views for one in (turned, *pieces)]
+    n_product = len(operands)
+
+    def body(place_ref, *refs):
+        n_out = 1 if squares is None else 2
+        out_ref = refs[-n_out]
         core = place_ref[1]
-        square_ref[...] = square_in_ref[...]
+        if squares is not None:
+            square_ref = refs[-1]
+            square_ref[...] = refs[n_product][...]
         for path in range(n_path):
-            total = lax.dot_general(
-                first_ref[...], refs[path][...], ROWS_BY_ROWS, preferred_element_type=F32
-            )
-            total += lax.dot_general(
-                second_ref[...], refs[n_path + path][...], ROWS_BY_ROWS,
-                preferred_element_type=F32,
-            )
             start = pl.multiple_of((2 * path + (core ^ flip)) * cols, cols)
-            out_ref[:, pl.ds(start, cols)] = total
-            square_ref[:8, :] += fold(total * total)
-
-    operands = [*turned, *pieces, squares] + ([] if done is None else [done])
-    return run(
-        body, place, operands, [None] * len(operands),
-        [like((depth, 2 * n_path * cols), F32), like(squares.shape, F32)], [None, None],
-        flops=4 * n_path * cols * batch * depth, moved=4 * n_path * depth * cols,
+            place_of = (slice(None), pl.ds(start, cols))
+            total = refs[-n_out - 1][place_of] if add else None
+            for first in range(0, n_product, n_path + 1):
+                product = lax.dot_general(
+                    refs[first][...], refs[first + 1 + path][...], ROWS_BY_ROWS,
+                    preferred_element_type=F32,
+                )
+                total = product if total is None else total + product
+            out_ref[place_of] = total
+            if squares is not None:
+                square_ref[:8, :] += fold(total * total)
+
+    operands += [one for one in (squares, done) if one is not None]
+    out = [like((depth, 2 * n_path * cols), F32)]
+    if squares is not None:
+        out.append(like(squares.shape, F32))
+    return run(
+        body, place, operands, [None] * len(operands), out, [None] * len(out),
+        flops=2 * len(views) * n_path * cols * batch * depth, moved=4 * n_path * depth * cols,
         limit=16, aliases={len(operands): 0} if done is not None else {}, name="weight_grad_of",
     )
 
@@ -598,11 +606,19 @@
     share = out_grad[0].shape[0] // 2
     out_grad[1] = out_grad_of(place, *gram[0], normed[1], half[1], half[0], inverse[1])
     parts = [one for grad in out_grad for one in (grad[:share], grad[share:])]
-    for step in range(len(high)):
+    for step in range(len(high) - 1):
         parts = gather_step(parts, step)
-    swapped = [swap(part, "dp", 1) for part in parts]
-    weight_grad, squares = weight_grad_of(place, turned, parts, 0, weight_squares)
-    weight_grad, squares = weight_grad_of(place, turned, swapped, 1, squares, weight_grad)
+    step = len(high) - 1
+    first_parts = gather_step(parts[:2], step)
+    (weight_grad,) = weight_grad_of(place, [(turned[0], first_parts)], 0)
+    second_parts = gather_step(parts[2:], step, after=[weight_grad])
+    swapped = [[swap(part, "dp", 1) for part in one] for one in (first_parts, second_parts)]
+    weight_grad, squares = weight_grad_of(
+        place, [(turned[1], second_parts)], 0, weight_squares, weight_grad, add=True
+    )
+    weight_grad, squares = weight_grad_of(
+        place, list(zip(turned, swapped)), 1, squares, weight_grad
+    )
     return update(sum_everywhere(squares), weight, velocity, weight_grad)
 
 

time: 283 us -> 281 us (level)
  waiting for transfers between devices: 143 us -> 138 us
    ppermute x52, waiting for transfers between devices: 102 us -> 97.3 us  [swap(): lax.ppermute(value, axis, [(i, i ^ mask) for i in range(lax.axis_size(axi...]
    pallas_call x31 -> x33, Pallas kernels: 63 us -> 64.5 us  [run(): return call(scalars, *operands, *after)]
  transfers between devices with their start and end apart: 68 -> 68, of which waited for: 45 -> 45; matrix products, arithmetic and copies ran while one was open for 0% -> 0% of each run, Pallas kernels for 16% -> 17%
where the time goes in v12:
time: 281 us
  waiting for transfers between devices  138 us (49%)
  starting transfers between devices  69.9 us (25%)
  Pallas kernels  64.5 us (23%)
  local copies, waits for them, and re-layouts  6.6 us (2%)
    ppermute x52, waiting for transfers between devices, swap(): lax.ppermute(value, axis, [(i, i ^ mask) for i in range(lax.axis_size(axi...  97.3 us
    pallas_call x33, Pallas kernels, run(): return call(scalars, *operands, *after)  64.5 us
    ppermute x52, starting transfers between devices, swap(): lax.ppermute(value, axis, [(i, i ^ mask) for i in range(lax.axis_size(axi...  52.8 us
    ppermute x9, waiting for transfers between devices, ring_step(): lax.ppermute(share, 'feat', [(i, (i + 1) % n_feat) for i in range(n_feat)])  32.8 us
    ppermute x9, starting transfers between devices, ring_step(): lax.ppermute(share, 'feat', [(i, (i + 1) % n_feat) for i in range(n_feat)])  9.07 us
    ppermute x7, waiting for transfers between devices, sum_everywhere(): lax.ppermute(value, axes, [(i, i ^ mask) for i in range(count)])  8.01 us
    ppermute x7, starting transfers between devices, sum_everywhere(): lax.ppermute(value, axes, [(i, i ^ mask) for i in range(count)])  7.95 us
    unnamed x20, local copies, waits for them, and re-layouts  6.53 us
  transfers between devices with their start and end apart: 68, of which 45 were waited for; matrix products, arithmetic and copies ran while one was open for 0% of the time, Pallas kernels for 17%

profile of v12, /device:TPU:0, one launch (start us, length us, event | category | flops | bytes accessed | tf_op | source)
XLA Modules:
  0.0 280.9 jit_solution(1187066560177221390)
XLA Ops:
  1.9 3.1 %collective-permute-start.10 = (bf16[64,2048]{1,0:T(8,128)(2,1)S(1)}, bf16[64,2048]{1,0:T(8,128)(2,1)}, u32[]{:S(2)}, u32[]{:S(2)}) collective-permute-start(bf16[64,2048]{1,0:T(8,128)(2,1)S(1)} %get-tuple-element.70.refs_0_), channel_id=1, source_target_pairs={{0,1},{1,2},{2,3},{3,0},{4,5},{5,6},{6,7},{7,4},{8,9},{9,10},{10,1... | collective-permute-start | bytes 786440 | tf_op jit(solution)/shard_map/ppermute | solution.py:171
  6.6 7.7 %collective-permute-done.10.refs_1_ = bf16[64,2048]{1,0:T(8,128)(2,1)} collective-permute-done((bf16[64,2048]{1,0:T(8,128)(2,1)S(1)}, bf16[64,2048]{1,0:T(8,128)(2,1)}, u32[]{:S(2)}, u32[]{:S(2)}) %collective-permute-start.10) | collective-permute-done | bytes 262176 | tf_op jit(solution)/shard_map/ppermute | solution.py:171
  15.9 3.9 %collective-permute-done.3.refs_1_.refs_0_ = bf16[64,2048]{1,0:T(8,128)(2,1)S(1)} collective-permute-done((bf16[64,2048]{1,0:T(8,128)(2,1)S(1)}, bf16[64,2048]{1,0:T(8,128)(2,1)S(1)}, u32[]{:S(2)}, u32[]{:S(2)}) %collective-permute-start.3) | collective-permute-done | bytes 262176 | tf_op jit(solution)/shard_map/ppermute | solution.py:171
  19.8 3.4 %copy-done = f32[1024,2048]{1,0:T(8,128)S(1)} copy-done((f32[1024,2048]{1,0:T(8,128)S(1)}, f32[1024,2048]{1,0:T(8,128)}, u32[]{:S(2)}) %copy-start) | copy-done | bytes 8388632
  23.2 4.6 %turn_weight.1 = (bf16[1024,1024]{1,0:T(8,128)(2,1)}, bf16[1024,1024]{1,0:T(8,128)(2,1)S(1)}, f32[16,128]{1,0:T(8,128)S(1)}) custom-call(s32[1]{0:T(128)} %bitcast.1.scalars_ref, f32[1024,2048]{1,0:T(8,128)S(1)} %copy-done, bf16[64,2048]{1,0:T(8,128)(2,1)S(1)} %collective-permute-done.3.refs_1_.refs_0_), custom_call_target="tpu_custom_call" | custom-call | flops 4194304 | bytes 12582912 | tf_op jit(solution)/shard_map/turn_weight/pallas_call | solution.py:85
  29.6 12.9 %collective-permute-done.5.refs_2_ = bf16[64,2048]{1,0:T(8,128)(2,1)} collective-permute-done((bf16[64,2048]{1,0:T(8,128)(2,1)S(1)}, bf16[64,2048]{1,0:T(8,128)(2,1)}, u32[]{:S(2)}, u32[]{:S(2)}) %collective-permute-start.5) | collective-permute-done | bytes 262176 | tf_op jit(solution)/shard_map/ppermute | solution.py:171
  42.5 5.5 %collective-permute-done.12.refs_3_ = bf16[64,2048]{1,0:T(8,128)(2,1)S(1)} collective-permute-done((bf16[64,2048]{1,0:T(8,128)(2,1)}, bf16[64,2048]{1,0:T(8,128)(2,1)S(1)}, u32[]{:S(2)}, u32[]{:S(2)}) %collective-permute-start.12) | collective-permute-done | bytes 262176 | tf_op jit(solution)/shard_map/ppermute | solution.py:171
  50.2 1.8 collective-permute-start.13
  55.8 1.8 collective-permute-start.7
  57.7 1.8 collective-permute-done.13.refs_5_
  59.5 1.8 collective-permute-start.8
  61.3 2.7 collective-permute-done.14.refs_6_
  66.4 4.3 %collective-permute-done.7.refs_1_ = bf16[64,2048]{1,0:T(8,128)(2,1)S(1)} collective-permute-done((bf16[64,2048]{1,0:T(8,128)(2,1)S(1)}, bf16[64,2048]{1,0:T(8,128)(2,1)S(1)}, u32[]{:S(2)}, u32[]{:S(2)}) %collective-permute-start.7) | collective-permute-done | bytes 262176 | tf_op jit(solution)/shard_map/ppermute | solution.py:19
  70.7 3.8 %collective-permute-done.8.refs_2_ = bf16[64,2048]{1,0:T(8,128)(2,1)S(1)} collective-permute-done((bf16[64,2048]{1,0:T(8,128)(2,1)S(1)}, bf16[64,2048]{1,0:T(8,128)(2,1)S(1)}, u32[]{:S(2)}, u32[]{:S(2)}) %collective-permute-start.8) | collective-permute-done | bytes 262176 | tf_op jit(solution)/shard_map/ppermute | solution.py:19
  74.5 2.0 collect.2.refs_0_
  78.2 2.8 collective-permute-done.16.refs_1_
  81.0 2.5 assemble.2.refs_2_.refs_0_
  84.0 4.1 %forward.4 = (bf16[256,1024]{1,0:T(8,128)(2,1)S(1)}, bf16[256,1024]{1,0:T(8,128)(2,1)S(1)}) custom-call(s32[2]{0:T(128)S(1)} %get-tuple-element.122.scalars_ref, bf16[1024,1024]{1,0:T(8,128)(2,1)S(1)} %get-tuple-element.64.refs_1_.refs_8_.refs_0_, bf16[1024,1024]{1,0:T(8,128)(2,1)} %collective-permute-done.4.refs_1_, ...), custom_call_target="tpu_custom_call" | custom-call | flops 2147483648 | bytes 6291456 | tf_op jit(solution)/shard_map/forward/pallas_call | solution.py:85
  90.2 2.7 collective-permute-done.2.refs_3_
  99.5 4.1 %forward.5 = (bf16[256,1024]{1,0:T(8,128)(2,1)S(1)}, bf16[256,1024]{1,0:T(8,128)(2,1)S(1)}) custom-call(s32[2]{0:T(128)S(1)} %get-tuple-element.123.scalars_ref, bf16[1024,1024]{1,0:T(8,128)(2,1)S(1)} %get-tuple-element.64.refs_1_.refs_8_.refs_0_, bf16[1024,1024]{1,0:T(8,128)(2,1)} %collective-permute-done.4.refs_1_, ...), custom_call_target="tpu_custom_call" | custom-call | flops 2147483648 | bytes 6291456 | tf_op jit(solution)/shard_map/forward/pallas_call | solution.py:85
  105.3 10.4 %collective-permute-done.17.refs_1_ = bf16[128,2048]{1,0:T(8,128)(2,1)S(1)} collective-permute-done((bf16[128,2048]{1,0:T(8,128)(2,1)S(1)}, bf16[128,2048]{1,0:T(8,128)(2,1)S(1)}, u32[]{:S(2)}, u32[]{:S(2)}) %collective-permute-start.17) | collective-permute-done | bytes 524320 | tf_op jit(solution)/shard_map/ppermute | solution.py:19
  115.7 10.1 %collective-permute-done.19.refs_3_ = bf16[128,2048]{1,0:T(8,128)(2,1)S(1)} collective-permute-done((bf16[128,2048]{1,0:T(8,128)(2,1)S(1)}, bf16[128,2048]{1,0:T(8,128)(2,1)S(1)}, u32[]{:S(2)}, u32[]{:S(2)}) %collective-permute-start.19) | collective-permute-done | bytes 524320 | tf_op jit(solution)/shard_map/ppermute | solution.py:19
  128.6 2.0 collective-permute-done.22.refs_1_
  131.5 4.1 %forward.6 = (bf16[256,1024]{1,0:T(8,128)(2,1)S(1)}, bf16[256,1024]{1,0:T(8,128)(2,1)S(1)}) custom-call(s32[2]{0:T(128)S(1)} %get-tuple-element.122.scalars_ref, bf16[1024,1024]{1,0:T(8,128)(2,1)S(1)} %get-tuple-element.64.refs_1_.refs_8_.refs_0_, bf16[1024,1024]{1,0:T(8,128)(2,1)} %collective-permute-done.4.refs_1_, ...), custom_call_target="tpu_custom_call" | custom-call | flops 2147483648 | bytes 6291456 | tf_op jit(solution)/shard_map/forward/pallas_call | solution.py:85
  143.7 1.7 collective-permute-start.28
  145.5 4.1 %forward.7 = (bf16[256,1024]{1,0:T(8,128)(2,1)S(1)}, bf16[256,1024]{1,0:T(8,128)(2,1)S(1)}) custom-call(s32[2]{0:T(128)S(1)} %get-tuple-element.123.scalars_ref, bf16[1024,1024]{1,0:T(8,128)(2,1)S(1)} %get-tuple-element.64.refs_1_.refs_8_.refs_0_, bf16[1024,1024]{1,0:T(8,128)(2,1)} %collective-permute-done.4.refs_1_, ...), custom_call_target="tpu_custom_call" | custom-call | flops 2147483648 | bytes 6291456 | tf_op jit(solution)/shard_map/forward/pallas_call | solution.py:85
  149.5 2.0 collective-permute-done.36.refs_3_
  156.0 4.1 %collective-permute-done.28 = bf16[128,640]{1,0:T(8,128)(2,1)S(1)} collective-permute-done((bf16[128,640]{1,0:T(8,128)(2,1)S(1)}, bf16[128,640]{1,0:T(8,128)(2,1)S(1)}, u32[]{:S(2)}, u32[]{:S(2)}) %collective-permute-start.28) | collective-permute-done | bytes 163872 | tf_op jit(solution)/shard_map/ppermute | solution.py:19
  160.8 2.9 %collective-permute-done.37.refs_1_ = bf16[128,1024]{1,0:T(8,128)(2,1)S(1)} collective-permute-done((bf16[128,1024]{1,0:T(8,128)(2,1)S(1)}, bf16[128,1024]{1,0:T(8,128)(2,1)S(1)}, u32[]{:S(2)}, u32[]{:S(2)}) %collective-permute-start.37) | collective-permute-done | bytes 262176 | tf_op jit(solution)/shard_map/ppermute | solution.py:19
  165.6 1.9 collective-permute-start.30
  172.4 3.5 %collective-permute-done.30 = bf16[128,640]{1,0:T(8,128)(2,1)S(1)} collective-permute-done((bf16[128,640]{1,0:T(8,128)(2,1)S(1)}, bf16[128,640]{1,0:T(8,128)(2,1)S(1)}, u32[]{:S(2)}, u32[]{:S(2)}) %collective-permute-start.30) | collective-permute-done | bytes 163872 | tf_op jit(solution)/shard_map/ppermute | solution.py:19
  179.5 3.0 %collective-permute-done.41 = bf16[128,640]{1,0:T(8,128)(2,1)S(1)} collective-permute-done((bf16[128,640]{1,0:T(8,128)(2,1)S(1)}, bf16[128,640]{1,0:T(8,128)(2,1)S(1)}, u32[]{:S(2)}, u32[]{:S(2)}) %collective-permute-start.41) | collective-permute-done | bytes 163872 | tf_op jit(solution)/shard_map/ppermute | solution.py:19
  182.6 3.7 %collective-permute-start.43 = (bf16[128,640]{1,0:T(8,128)(2,1)S(1)}, bf16[128,640]{1,0:T(8,128)(2,1)S(1)}, u32[]{:S(2)}, u32[]{:S(2)}) collective-permute-start(bf16[128,640]{1,0:T(8,128)(2,1)S(1)} %add_convert_fusion.2), channel_id=1, source_target_pairs={{0,1},{1,0},{2,3},{3,2},{4,5},{5,4},{6,7},{7,6},{8,9},{9,8},{10,11... | collective-permute-start | bytes 491528 | tf_op jit(solution)/shard_map/ppermute | solution.py:19
  186.5 3.1 %collective-permute-done.43 = bf16[128,640]{1,0:T(8,128)(2,1)S(1)} collective-permute-done((bf16[128,640]{1,0:T(8,128)(2,1)S(1)}, bf16[128,640]{1,0:T(8,128)(2,1)S(1)}, u32[]{:S(2)}, u32[]{:S(2)}) %collective-permute-start.43) | collective-permute-done | bytes 163872 | tf_op jit(solution)/shard_map/ppermute | solution.py:19
  191.0 6.7 %collective-permute-done.44 = bf16[128,640]{1,0:T(8,128)(2,1)S(1)} collective-permute-done((bf16[128,640]{1,0:T(8,128)(2,1)S(1)}, bf16[128,640]{1,0:T(8,128)(2,1)S(1)}, u32[]{:S(2)}, u32[]{:S(2)}) %collective-permute-start.44) | collective-permute-done | bytes 163872 | tf_op jit(solution)/shard_map/ppermute | solution.py:19
  201.4 2.4 out_grad_of.2.refs_4_
  208.4 2.4 out_grad_of.3
  213.0 2.5 collective-permute-done.50.refs_5_
  216.7 4.0 %collective-permute-done.52.refs_7_ = bf16[128,1024]{1,0:T(8,128)(2,1)S(1)} collective-permute-done((bf16[128,1024]{1,0:T(8,128)(2,1)S(1)}, bf16[128,1024]{1,0:T(8,128)(2,1)S(1)}, u32[]{:S(2)}, u32[]{:S(2)}) %collective-permute-start.52) | collective-permute-done | bytes 262176 | tf_op jit(solution)/shard_map/ppermute | solution.py:19
  226.4 10.8 %collective-permute-done.53.refs_2_ = bf16[256,1024]{1,0:T(8,128)(2,1)S(1)} collective-permute-done((bf16[256,1024]{1,0:T(8,128)(2,1)S(1)}, bf16[256,1024]{1,0:T(8,128)(2,1)S(1)}, u32[]{:S(2)}, u32[]{:S(2)}) %collective-permute-start.53) | collective-permute-done | bytes 524320 | tf_op jit(solution)/shard_map/ppermute | solution.py:19
  239.3 3.2 %weight_grad_of.3.refs_4_ = f32[1024,2048]{1,0:T(8,128)S(1)} custom-call(s32[2]{0:T(128)S(1)} %pad_add_fusion.scalars_ref, bf16[1024,1024]{1,0:T(8,128)(2,1)S(1)} %turn_columns.3.refs_3_.refs_0_, bf16[512,1024]{1,0:T(8,128)(2,1)S(1)} %get-tuple-element.111.refs_1_, bf16[512,1024]{1,0:T(8,128)(2,1)S(1)} %get-tuple-element.112.refs_2_), custom_call_target="tpu_custom_call" | custom-call | flops 2147483648 | bytes 4194304 | tf_op jit(solution)/shard_map/weight_grad_of/pallas_call | solution.py:85
  242.5 4.3 %collective-permute-done.57.refs_2_ = bf16[256,1024]{1,0:T(8,128)(2,1)S(1)} collective-permute-done((bf16[256,1024]{1,0:T(8,128)(2,1)S(1)}, bf16[256,1024]{1,0:T(8,128)(2,1)S(1)}, u32[]{:S(2)}, u32[]{:S(2)}) %collective-permute-start.57) | collective-permute-done | bytes 524320 | tf_op jit(solution)/shard_map/ppermute | solution.py:19
  248.6 3.2 %weight_grad_of.4 = (f32[1024,2048]{1,0:T(8,128)S(1)}, f32[16,128]{1,0:T(8,128)S(1)}) custom-call(s32[2]{0:T(128)S(1)} %pad_add_fusion.scalars_ref, bf16[1024,1024]{1,0:T(8,128)(2,1)S(1)} %turn_columns.2.refs_3_.refs_0_, bf16[512,1024]{1,0:T(8,128)(2,1)S(1)} %get-tuple-element.115.refs_1_, ...), custom_call_target="tpu_custom_call", output_to_operand_aliasing={{0}: (5, {})} | custom-call | flops 2147483648 | bytes 4194304 | tf_op jit(solution)/shard_map/weight_grad_of/pallas_call | solution.py:85
  252.3 5.1 %weight_grad_of.5 = (f32[1024,2048]{1,0:T(8,128)S(1)}, f32[16,128]{1,0:T(8,128)S(1)}) custom-call(s32[2]{0:T(128)S(1)} %pad_add_fusion.scalars_ref, bf16[1024,1024]{1,0:T(8,128)(2,1)S(1)} %turn_columns.3.refs_3_.refs_0_, bf16[512,1024]{1,0:T(8,128)(2,1)S(1)} %collective-permute-done.55.refs_1_, ...), custom_call_target="tpu_custom_call", output_to_operand_aliasing={{0}: (8, {})} | custom-call | flops 4294967296 | bytes 4194304 | tf_op jit(solution)/shard_map/weight_grad_of/pallas_call | solution.py:85
  257.3 3.9 %collective-permute-start.63 = (f32[16,128]{1,0:T(8,128)S(1)}, f32[16,128]{1,0:T(8,128)S(1)}, u32[]{:S(2)}, u32[]{:S(2)}) collective-permute-start(f32[16,128]{1,0:T(8,128)S(1)} %get-tuple-element.120), channel_id=1, source_target_pairs={{0,3},{1,2},{2,1},{3,0},{4,7},{5,6},{6,5},{7,4},{8,11},{9,10},{10,... | collective-permute-start | bytes 24584 | tf_op jit(solution)/shard_map/ppermute | solution.py:40
  262.9 2.9 %collective-permute-done.62 = f32[16,128]{1,0:T(8,128)S(1)} collective-permute-done((f32[16,128]{1,0:T(8,128)S(1)}, f32[16,128]{1,0:T(8,128)S(1)}, u32[]{:S(2)}, u32[]{:S(2)}) %collective-permute-start.62) | collective-permute-done | bytes 8224 | tf_op jit(solution)/shard_map/ppermute | solution.py:40
  271.1 2.2 collective-permute-done.67.refs_1_
  273.4 7.5 %update.1 = (f32[1024,2048]{1,0:T(8,128)}, f32[1024,2048]{1,0:T(8,128)}) custom-call(s32[1]{0:T(128)} %constant.21.clone.1.scalars_ref, f32[16,128]{1,0:T(8,128)S(1)} %add_add_fusion.refs_0_, f32[16,128]{1,0:T(8,128)S(1)} %collective-permute-done.67.refs_1_, f32[1024,2048]{1,0:T(8,128)S(1)} %bitcast.9, f32[1024,2048]{1,0:T(8,128)S(1)} %bitcast.11, ...), custom_call_target="tpu_custom_call" | custom-call | flops 8388608 | bytes 41943040 | tf_op jit(solution)/shard_map/update/pallas_call | solution.py:85
  (158 shorter events, 85.1 us)
Async XLA Ops:
  1.9 12.3 %collective-permute-start.10 = (bf16[64,2048]{1,0:T(8,128)(2,1)S(1)}, bf16[64,2048]{1,0:T(8,128)(2,1)}, u32[]{:S(2)}, u32[]{:S(2)}) collective-permute-start(bf16[64,2048]{1,0:T(8,128)(2,1)S(1)} %get-tuple-element.70.refs_0_), channel_id=1, source_target_pairs={{0,1},{1,2},{2,3},{3,0},{4,5},{5,6},{6,7},{7,4},{8,9},{9,10},{10,1... | collective-permute-start | bytes 786440 | tf_op jit(solution)/shard_map/ppermute | solution.py:171
  5.0 14.8 %collective-permute-start.3 = (bf16[64,2048]{1,0:T(8,128)(2,1)S(1)}, bf16[64,2048]{1,0:T(8,128)(2,1)S(1)}, u32[]{:S(2)}, u32[]{:S(2)}) collective-permute-start(bf16[64,2048]{1,0:T(8,128)(2,1)S(1)} %get-tuple-element.63.refs_0_), channel_id=1, source_target_pairs={{0,1},{1,2},{2,3},{3,0},{4,5},{5,6},{6,7},{7,4},{8,9},{9,10},{10,1... | collective-permute-start | bytes 786440 | tf_op jit(solution)/shard_map/ppermute | solution.py:171
  14.3 13.6 %collective-permute-start.11 = (bf16[64,2048]{1,0:T(8,128)(2,1)}, bf16[64,2048]{1,0:T(8,128)(2,1)}, u32[]{:S(2)}, u32[]{:S(2)}) collective-permute-start(bf16[64,2048]{1,0:T(8,128)(2,1)} %collective-permute-done.10.refs_1_), channel_id=1, source_target_pairs={{0,1},{1,2},{2,3},{3,0},{4,5},{5,6},{6,7},{7,4},{8,9},{9,10},{10,1... | collective-permute-start | bytes 786440 | tf_op jit(solution)/shard_map/ppermute | solution.py:171
  14.3 37.7 %collective-permute-start = (bf16[128,2048]{1,0:T(8,128)(2,1)S(1)}, bf16[128,2048]{1,0:T(8,128)(2,1)}, u32[]{:S(2)}, u32[]{:S(2)}) collective-permute-start(bf16[128,2048]{1,0:T(8,128)(2,1)S(1)} %get-tuple-element.62.refs_0_), channel_id=1, source_target_pairs={{0,1},{1,2},{2,3},{3,0},{4,5},{5,6},{6,7},{7,4},{8,9},{9,10},{10,1... | collective-permute-start | bytes 1572872 | tf_op jit(solution)/shard_map/ppermute | solution.py:171
  27.8 14.7 %collective-permute-start.5 = (bf16[64,2048]{1,0:T(8,128)(2,1)S(1)}, bf16[64,2048]{1,0:T(8,128)(2,1)}, u32[]{:S(2)}, u32[]{:S(2)}) collective-permute-start(bf16[64,2048]{1,0:T(8,128)(2,1)S(1)} %relay.1.refs_1_), channel_id=1, source_target_pairs={{0,1},{1,2},{2,3},{3,0},{4,5},{5,6},{6,7},{7,4},{8,9},{9,10},{10,1... | collective-permute-start | bytes 786440 | tf_op jit(solution)/shard_map/ppermute | solution.py:171
  27.9 20.1 %collective-permute-start.12 = (bf16[64,2048]{1,0:T(8,128)(2,1)}, bf16[64,2048]{1,0:T(8,128)(2,1)S(1)}, u32[]{:S(2)}, u32[]{:S(2)}) collective-permute-start(bf16[64,2048]{1,0:T(8,128)(2,1)} %collective-permute-done.11.refs_2_), channel_id=1, source_target_pairs={{0,1},{1,2},{2,3},{3,0},{4,5},{5,6},{6,7},{7,4},{8,9},{9,10},{10,1... | collective-permute-start | bytes 786440 | tf_op jit(solution)/shard_map/ppermute | solution.py:171
  42.5 11.3 %collective-permute-start.6 = (bf16[64,2048]{1,0:T(8,128)(2,1)}, bf16[64,2048]{1,0:T(8,128)(2,1)S(1)}, u32[]{:S(2)}, u32[]{:S(2)}) collective-permute-start(bf16[64,2048]{1,0:T(8,128)(2,1)} %collective-permute-done.5.refs_2_), channel_id=1, source_target_pairs={{0,1},{1,2},{2,3},{3,0},{4,5},{5,6},{6,7},{7,4},{8,9},{9,10},{10,1... | collective-permute-start | bytes 786440 | tf_op jit(solution)/shard_map/ppermute | solution.py:171
  50.2 9.3 %collective-permute-start.13 = (bf16[64,2048]{1,0:T(8,128)(2,1)S(1)}, bf16[64,2048]{1,0:T(8,128)(2,1)S(1)}, u32[]{:S(2)}, u32[]{:S(2)}) collective-permute-start(bf16[64,2048]{1,0:T(8,128)(2,1)S(1)} %get-tuple-element.72), channel_id=1, source_target_pairs={{0,8},{4,12},{8,0},{12,4},{16,24},{20,28},{24,16},{28,20},{1,9},{5... | collective-permute-start | bytes 786440 | tf_op jit(solution)/shard_map/ppermute | solution.py:19
  52.0 14.4 %collective-permute-start.1 = (bf16[128,2048]{1,0:T(8,128)(2,1)}, bf16[128,2048]{1,0:T(8,128)(2,1)S(1)}, u32[]{:S(2)}, u32[]{:S(2)}) collective-permute-start(bf16[128,2048]{1,0:T(8,128)(2,1)} %collective-permute-done.refs_1_), channel_id=1, source_target_pairs={{0,1},{1,2},{2,3},{3,0},{4,5},{5,6},{6,7},{7,4},{8,9},{9,10},{10,1... | collective-permute-start | bytes 1572872 | tf_op jit(solution)/shard_map/ppermute | solution.py:171
  52.0 11.9 %collective-permute-start.14 = (bf16[64,2048]{1,0:T(8,128)(2,1)S(1)}, bf16[64,2048]{1,0:T(8,128)(2,1)S(1)}, u32[]{:S(2)}, u32[]{:S(2)}) collective-permute-start(bf16[64,2048]{1,0:T(8,128)(2,1)S(1)} %get-tuple-element.73), channel_id=1, source_target_pairs={{0,16},{4,20},{8,24},{12,28},{16,0},{20,4},{24,8},{28,12},{1,17},{... | collective-permute-start | bytes 786440 | tf_op jit(solution)/shard_map/ppermute | solution.py:19
  53.5 12.9 %collective-permute-start.15 = (bf16[64,2048]{1,0:T(8,128)(2,1)S(1)}, bf16[64,2048]{1,0:T(8,128)(2,1)S(1)}, u32[]{:S(2)}, u32[]{:S(2)}) collective-permute-start(bf16[64,2048]{1,0:T(8,128)(2,1)S(1)} %get-tuple-element.74), channel_id=1, source_target_pairs={{0,24},{4,28},{8,16},{12,20},{16,8},{20,12},{24,0},{28,4},{1,25},{... | collective-permute-start | bytes 786440 | tf_op jit(solution)/shard_map/ppermute | solution.py:19
  55.8 14.9 %collective-permute-start.7 = (bf16[64,2048]{1,0:T(8,128)(2,1)S(1)}, bf16[64,2048]{1,0:T(8,128)(2,1)S(1)}, u32[]{:S(2)}, u32[]{:S(2)}) collective-permute-start(bf16[64,2048]{1,0:T(8,128)(2,1)S(1)} %get-tuple-element.67), channel_id=1, source_target_pairs={{0,8},{4,12},{8,0},{12,4},{16,24},{20,28},{24,16},{28,20},{1,9},{5... | collective-permute-start | bytes 786440 | tf_op jit(solution)/shard_map/ppermute | solution.py:19
  59.5 15.0 %collective-permute-start.8 = (bf16[64,2048]{1,0:T(8,128)(2,1)S(1)}, bf16[64,2048]{1,0:T(8,128)(2,1)S(1)}, u32[]{:S(2)}, u32[]{:S(2)}) collective-permute-start(bf16[64,2048]{1,0:T(8,128)(2,1)S(1)} %get-tuple-element.68), channel_id=1, source_target_pairs={{0,16},{4,20},{8,24},{12,28},{16,0},{20,4},{24,8},{28,12},{1,17},{... | collective-permute-start | bytes 786440 | tf_op jit(solution)/shard_map/ppermute | solution.py:19
  63.9 10.6 %collective-permute-start.9 = (bf16[64,2048]{1,0:T(8,128)(2,1)S(1)}, bf16[64,2048]{1,0:T(8,128)(2,1)S(1)}, u32[]{:S(2)}, u32[]{:S(2)}) collective-permute-start(bf16[64,2048]{1,0:T(8,128)(2,1)S(1)} %get-tuple-element.69), channel_id=1, source_target_pairs={{0,24},{4,28},{8,16},{12,20},{16,8},{20,12},{24,0},{28,4},{1,25},{... | collective-permute-start | bytes 786440 | tf_op jit(solution)/shard_map/ppermute | solution.py:19
  76.5 7.5 %collective-permute-start.4 = (bf16[1024,1024]{1,0:T(8,128)(2,1)}, bf16[1024,1024]{1,0:T(8,128)(2,1)}, u32[]{:S(2)}, u32[]{:S(2)}) collective-permute-start(bf16[1024,1024]{1,0:T(8,128)(2,1)} %get-tuple-element.65), channel_id=1, source_target_pairs={{0,4},{4,0},{8,12},{12,8},{16,20},{20,16},{24,28},{28,24},{1,5},{5... | collective-permute-start | bytes 6291464 | tf_op jit(solution)/shard_map/ppermute | solution.py:19
  77.0 15.9 %collective-permute-start.2 = (bf16[128,2048]{1,0:T(8,128)(2,1)S(1)}, bf16[128,2048]{1,0:T(8,128)(2,1)}, u32[]{:S(2)}, u32[]{:S(2)}) collective-permute-start(bf16[128,2048]{1,0:T(8,128)(2,1)S(1)} %collective-permute-done.1.refs_9_.refs_2_), channel_id=1, source_target_pairs={{0,1},{1,2},{2,3},{3,0},{4,5},{5,6},{6,7},{7,4},{8,9},{9,10},{10,1... | collective-permute-start | bytes 1572872 | tf_op jit(solution)/shard_map/ppermute | solution.py:171
  88.1 15.5 %collective-permute-start.21 = (bf16[256,1024]{1,0:T(8,128)(2,1)S(1)}, bf16[256,1024]{1,0:T(8,128)(2,1)S(1)}, u32[]{:S(2)}, u32[]{:S(2)}) collective-permute-start(bf16[256,1024]{1,0:T(8,128)(2,1)S(1)} %get-tuple-element.82), channel_id=1, source_target_pairs={{0,16},{4,20},{8,24},{12,28},{16,0},{20,4},{24,8},{28,12},{1,17},{... | collective-permute-start | bytes 1572872 | tf_op jit(solution)/shard_map/ppermute | solution.py:19
  89.7 14.8 %collective-permute-start.20 = (bf16[256,1024]{1,0:T(8,128)(2,1)S(1)}, bf16[256,1024]{1,0:T(8,128)(2,1)S(1)}, u32[]{:S(2)}, u32[]{:S(2)}) collective-permute-start(bf16[256,1024]{1,0:T(8,128)(2,1)S(1)} %get-tuple-element.75.refs_4_), channel_id=1, source_target_pairs={{0,8},{4,12},{8,0},{12,4},{16,24},{20,28},{24,16},{28,20},{1,9},{5... | collective-permute-start | bytes 1572872 | tf_op jit(solution)/shard_map/ppermute | solution.py:19
  94.6 21.1 %collective-permute-start.17 = (bf16[128,2048]{1,0:T(8,128)(2,1)S(1)}, bf16[128,2048]{1,0:T(8,128)(2,1)S(1)}, u32[]{:S(2)}, u32[]{:S(2)}) collective-permute-start(bf16[128,2048]{1,0:T(8,128)(2,1)S(1)} %get-tuple-element.77), channel_id=1, source_target_pairs={{0,8},{4,12},{8,0},{12,4},{16,24},{20,28},{24,16},{28,20},{1,9},{5... | collective-permute-start | bytes 1572872 | tf_op jit(solution)/shard_map/ppermute | solution.py:19
  95.7 20.0 %collective-permute-start.18 = (bf16[128,2048]{1,0:T(8,128)(2,1)S(1)}, bf16[128,2048]{1,0:T(8,128)(2,1)S(1)}, u32[]{:S(2)}, u32[]{:S(2)}) collective-permute-start(bf16[128,2048]{1,0:T(8,128)(2,1)S(1)} %get-tuple-element.78), channel_id=1, source_target_pairs={{0,16},{4,20},{8,24},{12,28},{16,0},{20,4},{24,8},{28,12},{1,17},{... | collective-permute-start | bytes 1572872 | tf_op jit(solution)/shard_map/ppermute | solution.py:19
  96.5 29.2 %collective-permute-start.19 = (bf16[128,2048]{1,0:T(8,128)(2,1)S(1)}, bf16[128,2048]{1,0:T(8,128)(2,1)S(1)}, u32[]{:S(2)}, u32[]{:S(2)}) collective-permute-start(bf16[128,2048]{1,0:T(8,128)(2,1)S(1)} %get-tuple-element.79), channel_id=1, source_target_pairs={{0,24},{4,28},{8,16},{12,20},{16,8},{20,12},{24,0},{28,4},{1,25},{... | collective-permute-start | bytes 1572872 | tf_op jit(solution)/shard_map/ppermute | solution.py:19
  126.5 9.0 %collective-permute-start.24 = (bf16[128,1024]{1,0:T(8,128)(2,1)S(1)}, bf16[128,1024]{1,0:T(8,128)(2,1)S(1)}, u32[]{:S(2)}, u32[]{:S(2)}) collective-permute-start(bf16[128,1024]{1,0:T(8,128)(2,1)S(1)} %get-tuple-element.86), channel_id=1, source_target_pairs={{0,8},{4,12},{8,0},{12,4},{16,24},{20,28},{24,16},{28,20},{1,9},{5... | collective-permute-start | bytes 786440 | tf_op jit(solution)/shard_map/ppermute | solution.py:19
  127.9 8.4 %collective-permute-start.23 = (bf16[128,1024]{1,0:T(8,128)(2,1)S(1)}, bf16[128,1024]{1,0:T(8,128)(2,1)S(1)}, u32[]{:S(2)}, u32[]{:S(2)}) collective-permute-start(bf16[128,1024]{1,0:T(8,128)(2,1)S(1)} %get-tuple-element.83.refs_4_), channel_id=1, source_target_pairs={{0,16},{4,20},{8,24},{12,28},{16,0},{20,4},{24,8},{28,12},{1,17},{... | collective-permute-start | bytes 786440 | tf_op jit(solution)/shard_map/ppermute | solution.py:19
  136.7 14.8 %collective-permute-start.36 = (bf16[256,1024]{1,0:T(8,128)(2,1)S(1)}, bf16[256,1024]{1,0:T(8,128)(2,1)S(1)}, u32[]{:S(2)}, u32[]{:S(2)}) collective-permute-start(bf16[256,1024]{1,0:T(8,128)(2,1)S(1)} %get-tuple-element.95), channel_id=1, source_target_pairs={{0,16},{4,20},{8,24},{12,28},{16,0},{20,4},{24,8},{28,12},{1,17},{... | collective-permute-start | bytes 1572872 | tf_op jit(solution)/shard_map/ppermute | solution.py:19
  137.7 14.8 %collective-permute-start.35 = (bf16[256,1024]{1,0:T(8,128)(2,1)S(1)}, bf16[256,1024]{1,0:T(8,128)(2,1)S(1)}, u32[]{:S(2)}, u32[]{:S(2)}) collective-permute-start(bf16[256,1024]{1,0:T(8,128)(2,1)S(1)} %get-tuple-element.87.refs_4_), channel_id=1, source_target_pairs={{0,8},{4,12},{8,0},{12,4},{16,24},{20,28},{24,16},{28,20},{1,9},{5... | collective-permute-start | bytes 1572872 | tf_op jit(solution)/shard_map/ppermute | solution.py:19
  141.9 14.1 %collective-permute-start.26 = (bf16[128,640]{1,0:T(8,128)(2,1)S(1)}, bf16[128,640]{1,0:T(8,128)(2,1)S(1)}, u32[]{:S(2)}, u32[]{:S(2)}) collective-permute-start(bf16[128,640]{1,0:T(8,128)(2,1)S(1)} %get-tuple-element.90), channel_id=1, source_target_pairs={{0,8},{4,12},{8,0},{12,4},{16,24},{20,28},{24,16},{28,20},{1,9},{5... | collective-permute-start | bytes 491528 | tf_op jit(solution)/shard_map/ppermute | solution.py:19
  142.6 13.4 %collective-permute-start.27 = (bf16[128,640]{1,0:T(8,128)(2,1)S(1)}, bf16[128,640]{1,0:T(8,128)(2,1)S(1)}, u32[]{:S(2)}, u32[]{:S(2)}) collective-permute-start(bf16[128,640]{1,0:T(8,128)(2,1)S(1)} %get-tuple-element.91), channel_id=1, source_target_pairs={{0,16},{4,20},{8,24},{12,28},{16,0},{20,4},{24,8},{28,12},{1,17},{... | collective-permute-start | bytes 491528 | tf_op jit(solution)/shard_map/ppermute | solution.py:19
  143.7 16.4 %collective-permute-start.28 = (bf16[128,640]{1,0:T(8,128)(2,1)S(1)}, bf16[128,640]{1,0:T(8,128)(2,1)S(1)}, u32[]{:S(2)}, u32[]{:S(2)}) collective-permute-start(bf16[128,640]{1,0:T(8,128)(2,1)S(1)} %get-tuple-element.92), channel_id=1, source_target_pairs={{0,24},{4,28},{8,16},{12,20},{16,8},{20,12},{24,0},{28,4},{1,25},{... | collective-permute-start | bytes 491528 | tf_op jit(solution)/shard_map/ppermute | solution.py:19
  153.3 10.4 %collective-permute-start.37 = (bf16[128,1024]{1,0:T(8,128)(2,1)S(1)}, bf16[128,1024]{1,0:T(8,128)(2,1)S(1)}, u32[]{:S(2)}, u32[]{:S(2)}) collective-permute-start(bf16[128,1024]{1,0:T(8,128)(2,1)S(1)} %get-tuple-element.97), channel_id=1, source_target_pairs={{0,16},{4,20},{8,24},{12,28},{16,0},{20,4},{24,8},{28,12},{1,17},{... | collective-permute-start | bytes 786440 | tf_op jit(solution)/shard_map/ppermute | solution.py:19
  154.4 9.9 %collective-permute-start.38 = (bf16[128,1024]{1,0:T(8,128)(2,1)S(1)}, bf16[128,1024]{1,0:T(8,128)(2,1)S(1)}, u32[]{:S(2)}, u32[]{:S(2)}) collective-permute-start(bf16[128,1024]{1,0:T(8,128)(2,1)S(1)} %get-tuple-element.99), channel_id=1, source_target_pairs={{0,8},{4,12},{8,0},{12,4},{16,24},{20,28},{24,16},{28,20},{1,9},{5... | collective-permute-start | bytes 786440 | tf_op jit(solution)/shard_map/ppermute | solution.py:19
  165.6 10.3 %collective-permute-start.30 = (bf16[128,640]{1,0:T(8,128)(2,1)S(1)}, bf16[128,640]{1,0:T(8,128)(2,1)S(1)}, u32[]{:S(2)}, u32[]{:S(2)}) collective-permute-start(bf16[128,640]{1,0:T(8,128)(2,1)S(1)} %add_convert_fusion.4), channel_id=1, source_target_pairs={{0,2},{1,3},{2,0},{3,1},{4,6},{5,7},{6,4},{7,5},{8,10},{9,11},{10,... | collective-permute-start | bytes 491528 | tf_op jit(solution)/shard_map/ppermute | solution.py:19
  168.8 10.1 %collective-permute-start.40 = (bf16[128,640]{1,0:T(8,128)(2,1)S(1)}, bf16[128,640]{1,0:T(8,128)(2,1)S(1)}, u32[]{:S(2)}, u32[]{:S(2)}) collective-permute-start(bf16[128,640]{1,0:T(8,128)(2,1)S(1)} %get-tuple-element.104), channel_id=1, source_target_pairs={{0,8},{4,12},{8,0},{12,4},{16,24},{20,28},{24,16},{28,20},{1,9},{5... | collective-permute-start | bytes 491528 | tf_op jit(solution)/shard_map/ppermute | solution.py:19
  170.2 12.3 %collective-permute-start.41 = (bf16[128,640]{1,0:T(8,128)(2,1)S(1)}, bf16[128,640]{1,0:T(8,128)(2,1)S(1)}, u32[]{:S(2)}, u32[]{:S(2)}) collective-permute-start(bf16[128,640]{1,0:T(8,128)(2,1)S(1)} %get-tuple-element.105), channel_id=1, source_target_pairs={{0,16},{4,20},{8,24},{12,28},{16,0},{20,4},{24,8},{28,12},{1,17},{... | collective-permute-start | bytes 491528 | tf_op jit(solution)/shard_map/ppermute | solution.py:19
  171.9 10.6 %collective-permute-start.42 = (bf16[128,640]{1,0:T(8,128)(2,1)S(1)}, bf16[128,640]{1,0:T(8,128)(2,1)S(1)}, u32[]{:S(2)}, u32[]{:S(2)}) collective-permute-start(bf16[128,640]{1,0:T(8,128)(2,1)S(1)} %get-tuple-element.106), channel_id=1, source_target_pairs={{0,24},{4,28},{8,16},{12,20},{16,8},{20,12},{24,0},{28,4},{1,25},{... | collective-permute-start | bytes 491528 | tf_op jit(solution)/shard_map/ppermute | solution.py:19
  175.9 10.3 %collective-permute-start.33 = (bf16[128,640]{1,0:T(8,128)(2,1)S(1)}, bf16[128,640]{1,0:T(8,128)(2,1)S(1)}, u32[]{:S(2)}, u32[]{:S(2)}) collective-permute-start(bf16[128,640]{1,0:T(8,128)(2,1)S(1)} %add_convert_fusion.3.refs_0_), channel_id=1, source_target_pairs={{0,24},{4,28},{8,16},{12,20},{16,8},{20,12},{24,0},{28,4},{1,25},{... | collective-permute-start | bytes 491528 | tf_op jit(solution)/shard_map/ppermute | solution.py:19
  177.4 9.0 %collective-permute-start.32 = (bf16[128,640]{1,0:T(8,128)(2,1)S(1)}, bf16[128,640]{1,0:T(8,128)(2,1)S(1)}, u32[]{:S(2)}, u32[]{:S(2)}) collective-permute-start(bf16[128,640]{1,0:T(8,128)(2,1)S(1)} %add_convert_fusion.3.refs_0_), channel_id=1, source_target_pairs={{0,16},{4,20},{8,24},{12,28},{16,0},{20,4},{24,8},{28,12},{1,17},{... | collective-permute-start | bytes 491528 | tf_op jit(solution)/shard_map/ppermute | solution.py:19
  186.4 15.0 %collective-permute-start.34 = (bf16[4,128,640]{2,1,0:T(8,128)(2,1)S(1)}, bf16[4,128,640]{2,1,0:T(8,128)(2,1)S(1)}, u32[]{:S(2)}, u32[]{:S(2)}) collective-permute-start(bf16[4,128,640]{2,1,0:T(8,128)(2,1)S(1)} %pile.2.refs_0_), channel_id=1, source_target_pairs={{0,4},{4,0},{8,12},{12,8},{16,20},{20,16},{24,28},{28,24},{1,5},{5... | collective-permute-start | bytes 1966088 | tf_op jit(solution)/shard_map/ppermute | solution.py:19
  189.6 8.2 %collective-permute-start.44 = (bf16[128,640]{1,0:T(8,128)(2,1)S(1)}, bf16[128,640]{1,0:T(8,128)(2,1)S(1)}, u32[]{:S(2)}, u32[]{:S(2)}) collective-permute-start(bf16[128,640]{1,0:T(8,128)(2,1)S(1)} %add_convert_fusion.1), channel_id=1, source_target_pairs={{0,2},{1,3},{2,0},{3,1},{4,6},{5,7},{6,4},{7,5},{8,10},{9,11},{10,... | collective-permute-start | bytes 491528 | tf_op jit(solution)/shard_map/ppermute | solution.py:19
  206.3 9.2 %collective-permute-start.50 = (bf16[128,1024]{1,0:T(8,128)(2,1)S(1)}, bf16[128,1024]{1,0:T(8,128)(2,1)S(1)}, u32[]{:S(2)}, u32[]{:S(2)}) collective-permute-start(bf16[128,1024]{1,0:T(8,128)(2,1)S(1)} %get-tuple-element.126.refs_1_), channel_id=1, source_target_pairs={{0,8},{4,12},{8,0},{12,4},{16,24},{20,28},{24,16},{28,20},{1,9},{5... | collective-permute-start | bytes 786440 | tf_op jit(solution)/shard_map/ppermute | solution.py:19
  207.6 9.1 %collective-permute-start.49 = (bf16[128,1024]{1,0:T(8,128)(2,1)S(1)}, bf16[128,1024]{1,0:T(8,128)(2,1)S(1)}, u32[]{:S(2)}, u32[]{:S(2)}) collective-permute-start(bf16[128,1024]{1,0:T(8,128)(2,1)S(1)} %get-tuple-element.127.refs_0_), channel_id=1, source_target_pairs={{0,16},{4,20},{8,24},{12,28},{16,0},{20,4},{24,8},{28,12},{1,17},{... | collective-permute-start | bytes 786440 | tf_op jit(solution)/shard_map/ppermute | solution.py:19
  210.8 9.8 %collective-permute-start.52 = (bf16[128,1024]{1,0:T(8,128)(2,1)S(1)}, bf16[128,1024]{1,0:T(8,128)(2,1)S(1)}, u32[]{:S(2)}, u32[]{:S(2)}) collective-permute-start(bf16[128,1024]{1,0:T(8,128)(2,1)S(1)} %get-tuple-element.124.refs_3_), channel_id=1, source_target_pairs={{0,8},{4,12},{8,0},{12,4},{16,24},{20,28},{24,16},{28,20},{1,9},{5... | collective-permute-start | bytes 786440 | tf_op jit(solution)/shard_map/ppermute | solution.py:19
  212.0 9.6 %collective-permute-start.51 = (bf16[128,1024]{1,0:T(8,128)(2,1)S(1)}, bf16[128,1024]{1,0:T(8,128)(2,1)S(1)}, u32[]{:S(2)}, u32[]{:S(2)}) collective-permute-start(bf16[128,1024]{1,0:T(8,128)(2,1)S(1)} %get-tuple-element.125.refs_2_), channel_id=1, source_target_pairs={{0,16},{4,20},{8,24},{12,28},{16,0},{20,4},{24,8},{28,12},{1,17},{... | collective-permute-start | bytes 786440 | tf_op jit(solution)/shard_map/ppermute | solution.py:19
  222.3 14.9 %collective-permute-start.53 = (bf16[256,1024]{1,0:T(8,128)(2,1)S(1)}, bf16[256,1024]{1,0:T(8,128)(2,1)S(1)}, u32[]{:S(2)}, u32[]{:S(2)}) collective-permute-start(bf16[256,1024]{1,0:T(8,128)(2,1)S(1)} %get-tuple-element.109.refs_0_), channel_id=1, source_target_pairs={{0,8},{4,12},{8,0},{12,4},{16,24},{20,28},{24,16},{28,20},{1,9},{5... | collective-permute-start | bytes 1572872 | tf_op jit(solution)/shard_map/ppermute | solution.py:19
  223.2 14.9 %collective-permute-start.54 = (bf16[256,1024]{1,0:T(8,128)(2,1)S(1)}, bf16[256,1024]{1,0:T(8,128)(2,1)S(1)}, u32[]{:S(2)}, u32[]{:S(2)}) collective-permute-start(bf16[256,1024]{1,0:T(8,128)(2,1)S(1)} %get-tuple-element.110.refs_1_), channel_id=1, source_target_pairs={{0,16},{4,20},{8,24},{12,28},{16,0},{20,4},{24,8},{28,12},{1,17},{... | collective-permute-start | bytes 1572872 | tf_op jit(solution)/shard_map/ppermute | solution.py:19
  224.1 22.7 %collective-permute-start.57 = (bf16[256,1024]{1,0:T(8,128)(2,1)S(1)}, bf16[256,1024]{1,0:T(8,128)(2,1)S(1)}, u32[]{:S(2)}, u32[]{:S(2)}) collective-permute-start(bf16[256,1024]{1,0:T(8,128)(2,1)S(1)} %get-tuple-element.113.refs_0_), channel_id=1, source_target_pairs={{0,8},{4,12},{8,0},{12,4},{16,24},{20,28},{24,16},{28,20},{1,9},{5... | collective-permute-start | bytes 1572872 | tf_op jit(solution)/shard_map/ppermute | solution.py:19
  225.2 22.1 %collective-permute-start.58 = (bf16[256,1024]{1,0:T(8,128)(2,1)S(1)}, bf16[256,1024]{1,0:T(8,128)(2,1)S(1)}, u32[]{:S(2)}, u32[]{:S(2)}) collective-permute-start(bf16[256,1024]{1,0:T(8,128)(2,1)S(1)} %get-tuple-element.114.refs_1_), channel_id=1, source_target_pairs={{0,16},{4,20},{8,24},{12,28},{16,0},{20,4},{24,8},{28,12},{1,17},{... | collective-permute-start | bytes 1572872 | tf_op jit(solution)/shard_map/ppermute | solution.py:19
  238.7 13.1 %collective-permute-start.55 = (bf16[512,1024]{1,0:T(8,128)(2,1)S(1)}, bf16[512,1024]{1,0:T(8,128)(2,1)S(1)}, u32[]{:S(2)}, u32[]{:S(2)}) collective-permute-start(bf16[512,1024]{1,0:T(8,128)(2,1)S(1)} %get-tuple-element.111.refs_1_), channel_id=1, source_target_pairs={{0,4},{4,0},{8,12},{12,8},{16,20},{20,16},{24,28},{28,24},{1,5},{5... | collective-permute-start | bytes 3145736 | tf_op jit(solution)/shard_map/ppermute | solution.py:19
  238.8 13.0 %collective-permute-start.56 = (bf16[512,1024]{1,0:T(8,128)(2,1)S(1)}, bf16[512,1024]{1,0:T(8,128)(2,1)S(1)}, u32[]{:S(2)}, u32[]{:S(2)}) collective-permute-start(bf16[512,1024]{1,0:T(8,128)(2,1)S(1)} %get-tuple-element.112.refs_2_), channel_id=1, source_target_pairs={{0,4},{4,0},{8,12},{12,8},{16,20},{20,16},{24,28},{28,24},{1,5},{5... | collective-permute-start | bytes 3145736 | tf_op jit(solution)/shard_map/ppermute | solution.py:19
  (30 other events, 238.7 us)

commit v13 on v12

--- a/solution.py
+++ b/solution.py
@@ -489,23 +489,39 @@
     n_sum = len(sums)
 
     def body(_, *refs):
-        weight_ref, velocity_ref, grad_ref, new_weight_ref, new_velocity_ref = refs[n_sum:]
+        weight_ref, velocity_ref, grad_ref = refs[n_sum : n_sum + 3]
+        outs, (slots_ref, sems) = refs[n_sum + 3 : n_sum + 5], refs[n_sum + 5 :]
         total = refs[0][...]
         for ref in refs[1:n_sum]:
             total += ref[...]
         grad_norm = jnp.sqrt(jnp.sum(total[:8], keepdims=True))
         weight_norm = jnp.sqrt(jnp.sum(total[8:], keepdims=True))
         trust = weight_norm / (grad_norm + NORM_EPSILON)
-        new_velocity = MOMENTUM * velocity_ref[...] + trust * grad_ref[...]
-        new_velocity_ref[...] = new_velocity
-        new_weight_ref[...] = weight_ref[...] - LEARN_RATE * new_velocity
-
-    tile = pl.BlockSpec((step, width), lambda i, s: (i, 0))
+        copies = []
+        for index in range(depth // step):
+            rows, slot = slice(index * step, (index + 1) * step), index % 2
+            for copy in copies[2 * (index - 2) : 2 * (index - 1)] if index > 1 else ():
+                copy.wait()
+            new_velocity = MOMENTUM * velocity_ref[rows, :] + trust * grad_ref[rows, :]
+            slots_ref[slot, 0] = weight_ref[rows, :] - LEARN_RATE * new_velocity
+            slots_ref[slot, 1] = new_velocity
+            for which, out_ref in enumerate(outs):
+                copies.append(
+                    pltpu.make_async_copy(
+                        slots_ref.at[slot, which], out_ref.at[rows, :], sems.at[slot, which]
+                    )
+                )
+                copies[-1].start()
+        for copy in copies[-4:]:
+            copy.wait()
+
     out = like((depth, width), F32)
+    hbm = pl.BlockSpec(memory_space=pl.ANY)
     return run(
         body, jnp.zeros((1,), jnp.int32), [*sums, weight, velocity, weight_grad],
-        [pl.BlockSpec(one.shape, lambda i, s: (0, 0)) for one in sums] + [tile] * 3, [out, out], [tile, tile],
-        grid=(depth // step,), flops=4 * depth * width, moved=20 * depth * width, limit=16, name="update",
+        [None] * (n_sum + 3), [out, out], [hbm, hbm],
+        scratch=[pltpu.VMEM((2, 2, step, width), F32), pltpu.SemaphoreType.DMA((2, 2))],
+        flops=4 * depth * width, moved=20 * depth * width, limit=10, name="update",
     )
 
 

time: 281 us -> 281 us (level)
  no operation moved by 1% of the time
where the time goes in v13:
time: 281 us
  waiting for transfers between devices  138 us (49%)
  starting transfers between devices  69.8 us (25%)
  Pallas kernels  64 us (23%)
  local copies, waits for them, and re-layouts  6.6 us (2%)
    ppermute x52, waiting for transfers between devices, swap(): lax.ppermute(value, axis, [(i, i ^ mask) for i in range(lax.axis_size(axi...  97.3 us
    pallas_call x33, Pallas kernels, run(): return call(scalars, *operands, *after)  64 us
    ppermute x52, starting transfers between devices, swap(): lax.ppermute(value, axis, [(i, i ^ mask) for i in range(lax.axis_size(axi...  52.8 us
    ppermute x9, waiting for transfers between devices, ring_step(): lax.ppermute(share, 'feat', [(i, (i + 1) % n_feat) for i in range(n_feat)])  32.8 us
    ppermute x9, starting transfers between devices, ring_step(): lax.ppermute(share, 'feat', [(i, (i + 1) % n_feat) for i in range(n_feat)])  9.07 us
    ppermute x7, waiting for transfers between devices, sum_everywhere(): lax.ppermute(value, axes, [(i, i ^ mask) for i in range(count)])  8.02 us
    ppermute x7, starting transfers between devices, sum_everywhere(): lax.ppermute(value, axes, [(i, i ^ mask) for i in range(count)])  7.92 us
    unnamed x20, local copies, waits for them, and re-layouts  6.53 us
  transfers between devices with their start and end apart: 68, of which 45 were waited for; matrix products, arithmetic and copies ran while one was open for 0% of the time, Pallas kernels for 17%

profile of v13, /device:TPU:0, one launch (start us, length us, event | category | flops | bytes accessed | tf_op | source)
XLA Modules:
  0.0 280.6 jit_solution(14871540931597366200)
XLA Ops:
  1.9 3.1 %collective-permute-start.10 = (bf16[64,2048]{1,0:T(8,128)(2,1)S(1)}, bf16[64,2048]{1,0:T(8,128)(2,1)}, u32[]{:S(2)}, u32[]{:S(2)}) collective-permute-start(bf16[64,2048]{1,0:T(8,128)(2,1)S(1)} %get-tuple-element.70.refs_0_), channel_id=1, source_target_pairs={{0,1},{1,2},{2,3},{3,0},{4,5},{5,6},{6,7},{7,4},{8,9},{9,10},{10,1... | collective-permute-start | bytes 786440 | tf_op jit(solution)/shard_map/ppermute | solution.py:171
  6.6 7.7 %collective-permute-done.10.refs_1_ = bf16[64,2048]{1,0:T(8,128)(2,1)} collective-permute-done((bf16[64,2048]{1,0:T(8,128)(2,1)S(1)}, bf16[64,2048]{1,0:T(8,128)(2,1)}, u32[]{:S(2)}, u32[]{:S(2)}) %collective-permute-start.10) | collective-permute-done | bytes 262176 | tf_op jit(solution)/shard_map/ppermute | solution.py:171
  15.9 3.9 %collective-permute-done.3.refs_1_.refs_0_ = bf16[64,2048]{1,0:T(8,128)(2,1)S(1)} collective-permute-done((bf16[64,2048]{1,0:T(8,128)(2,1)S(1)}, bf16[64,2048]{1,0:T(8,128)(2,1)S(1)}, u32[]{:S(2)}, u32[]{:S(2)}) %collective-permute-start.3) | collective-permute-done | bytes 262176 | tf_op jit(solution)/shard_map/ppermute | solution.py:171
  19.8 3.4 %copy-done = f32[1024,2048]{1,0:T(8,128)S(1)} copy-done((f32[1024,2048]{1,0:T(8,128)S(1)}, f32[1024,2048]{1,0:T(8,128)}, u32[]{:S(2)}) %copy-start) | copy-done | bytes 8388632
  23.2 4.6 %turn_weight.1 = (bf16[1024,1024]{1,0:T(8,128)(2,1)}, bf16[1024,1024]{1,0:T(8,128)(2,1)S(1)}, f32[16,128]{1,0:T(8,128)S(1)}) custom-call(s32[1]{0:T(128)} %bitcast.1.scalars_ref, f32[1024,2048]{1,0:T(8,128)S(1)} %copy-done, bf16[64,2048]{1,0:T(8,128)(2,1)S(1)} %collective-permute-done.3.refs_1_.refs_0_), custom_call_target="tpu_custom_call" | custom-call | flops 4194304 | bytes 12582912 | tf_op jit(solution)/shard_map/turn_weight/pallas_call | solution.py:85
  29.6 12.9 %collective-permute-done.5.refs_2_ = bf16[64,2048]{1,0:T(8,128)(2,1)} collective-permute-done((bf16[64,2048]{1,0:T(8,128)(2,1)S(1)}, bf16[64,2048]{1,0:T(8,128)(2,1)}, u32[]{:S(2)}, u32[]{:S(2)}) %collective-permute-start.5) | collective-permute-done | bytes 262176 | tf_op jit(solution)/shard_map/ppermute | solution.py:171
  42.5 5.5 %collective-permute-done.12.refs_3_ = bf16[64,2048]{1,0:T(8,128)(2,1)S(1)} collective-permute-done((bf16[64,2048]{1,0:T(8,128)(2,1)}, bf16[64,2048]{1,0:T(8,128)(2,1)S(1)}, u32[]{:S(2)}, u32[]{:S(2)}) %collective-permute-start.12) | collective-permute-done | bytes 262176 | tf_op jit(solution)/shard_map/ppermute | solution.py:171
  50.2 1.8 collective-permute-start.13
  55.8 1.8 collective-permute-start.7
  57.7 1.8 collective-permute-done.13.refs_5_
  59.5 1.8 collective-permute-start.8
  61.3 2.7 collective-permute-done.14.refs_6_
  66.4 4.3 %collective-permute-done.7.refs_1_ = bf16[64,2048]{1,0:T(8,128)(2,1)S(1)} collective-permute-done((bf16[64,2048]{1,0:T(8,128)(2,1)S(1)}, bf16[64,2048]{1,0:T(8,128)(2,1)S(1)}, u32[]{:S(2)}, u32[]{:S(2)}) %collective-permute-start.7) | collective-permute-done | bytes 262176 | tf_op jit(solution)/shard_map/ppermute | solution.py:19
  70.7 3.8 %collective-permute-done.8.refs_2_ = bf16[64,2048]{1,0:T(8,128)(2,1)S(1)} collective-permute-done((bf16[64,2048]{1,0:T(8,128)(2,1)S(1)}, bf16[64,2048]{1,0:T(8,128)(2,1)S(1)}, u32[]{:S(2)}, u32[]{:S(2)}) %collective-permute-start.8) | collective-permute-done | bytes 262176 | tf_op jit(solution)/shard_map/ppermute | solution.py:19
  74.5 2.0 collect.2.refs_0_
  78.2 2.8 collective-permute-done.16.refs_1_
  81.0 2.5 assemble.2.refs_2_.refs_0_
  84.0 4.1 %forward.4 = (bf16[256,1024]{1,0:T(8,128)(2,1)S(1)}, bf16[256,1024]{1,0:T(8,128)(2,1)S(1)}) custom-call(s32[2]{0:T(128)S(1)} %get-tuple-element.122.scalars_ref, bf16[1024,1024]{1,0:T(8,128)(2,1)S(1)} %get-tuple-element.64.refs_1_.refs_8_.refs_0_, bf16[1024,1024]{1,0:T(8,128)(2,1)} %collective-permute-done.4.refs_1_, ...), custom_call_target="tpu_custom_call" | custom-call | flops 2147483648 | bytes 6291456 | tf_op jit(solution)/shard_map/forward/pallas_call | solution.py:85
  90.2 2.7 collective-permute-done.2.refs_3_
  99.5 4.1 %forward.5 = (bf16[256,1024]{1,0:T(8,128)(2,1)S(1)}, bf16[256,1024]{1,0:T(8,128)(2,1)S(1)}) custom-call(s32[2]{0:T(128)S(1)} %get-tuple-element.123.scalars_ref, bf16[1024,1024]{1,0:T(8,128)(2,1)S(1)} %get-tuple-element.64.refs_1_.refs_8_.refs_0_, bf16[1024,1024]{1,0:T(8,128)(2,1)} %collective-permute-done.4.refs_1_, ...), custom_call_target="tpu_custom_call" | custom-call | flops 2147483648 | bytes 6291456 | tf_op jit(solution)/shard_map/forward/pallas_call | solution.py:85
  105.3 10.4 %collective-permute-done.17.refs_1_ = bf16[128,2048]{1,0:T(8,128)(2,1)S(1)} collective-permute-done((bf16[128,2048]{1,0:T(8,128)(2,1)S(1)}, bf16[128,2048]{1,0:T(8,128)(2,1)S(1)}, u32[]{:S(2)}, u32[]{:S(2)}) %collective-permute-start.17) | collective-permute-done | bytes 524320 | tf_op jit(solution)/shard_map/ppermute | solution.py:19
  115.7 10.1 %collective-permute-done.19.refs_3_ = bf16[128,2048]{1,0:T(8,128)(2,1)S(1)} collective-permute-done((bf16[128,2048]{1,0:T(8,128)(2,1)S(1)}, bf16[128,2048]{1,0:T(8,128)(2,1)S(1)}, u32[]{:S(2)}, u32[]{:S(2)}) %collective-permute-start.19) | collective-permute-done | bytes 524320 | tf_op jit(solution)/shard_map/ppermute | solution.py:19
  128.6 2.0 collective-permute-done.22.refs_1_
  131.5 4.1 %forward.6 = (bf16[256,1024]{1,0:T(8,128)(2,1)S(1)}, bf16[256,1024]{1,0:T(8,128)(2,1)S(1)}) custom-call(s32[2]{0:T(128)S(1)} %get-tuple-element.122.scalars_ref, bf16[1024,1024]{1,0:T(8,128)(2,1)S(1)} %get-tuple-element.64.refs_1_.refs_8_.refs_0_, bf16[1024,1024]{1,0:T(8,128)(2,1)} %collective-permute-done.4.refs_1_, ...), custom_call_target="tpu_custom_call" | custom-call | flops 2147483648 | bytes 6291456 | tf_op jit(solution)/shard_map/forward/pallas_call | solution.py:85
  143.7 1.7 collective-permute-start.28
  145.5 4.1 %forward.7 = (bf16[256,1024]{1,0:T(8,128)(2,1)S(1)}, bf16[256,1024]{1,0:T(8,128)(2,1)S(1)}) custom-call(s32[2]{0:T(128)S(1)} %get-tuple-element.123.scalars_ref, bf16[1024,1024]{1,0:T(8,128)(2,1)S(1)} %get-tuple-element.64.refs_1_.refs_8_.refs_0_, bf16[1024,1024]{1,0:T(8,128)(2,1)} %collective-permute-done.4.refs_1_, ...), custom_call_target="tpu_custom_call" | custom-call | flops 2147483648 | bytes 6291456 | tf_op jit(solution)/shard_map/forward/pallas_call | solution.py:85
  149.5 2.0 collective-permute-done.36.refs_3_
  156.0 4.1 %collective-permute-done.28 = bf16[128,640]{1,0:T(8,128)(2,1)S(1)} collective-permute-done((bf16[128,640]{1,0:T(8,128)(2,1)S(1)}, bf16[128,640]{1,0:T(8,128)(2,1)S(1)}, u32[]{:S(2)}, u32[]{:S(2)}) %collective-permute-start.28) | collective-permute-done | bytes 163872 | tf_op jit(solution)/shard_map/ppermute | solution.py:19
  160.8 2.9 %collective-permute-done.37.refs_1_ = bf16[128,1024]{1,0:T(8,128)(2,1)S(1)} collective-permute-done((bf16[128,1024]{1,0:T(8,128)(2,1)S(1)}, bf16[128,1024]{1,0:T(8,128)(2,1)S(1)}, u32[]{:S(2)}, u32[]{:S(2)}) %collective-permute-start.37) | collective-permute-done | bytes 262176 | tf_op jit(solution)/shard_map/ppermute | solution.py:19
  165.6 1.9 collective-permute-start.30
  172.4 3.5 %collective-permute-done.30 = bf16[128,640]{1,0:T(8,128)(2,1)S(1)} collective-permute-done((bf16[128,640]{1,0:T(8,128)(2,1)S(1)}, bf16[128,640]{1,0:T(8,128)(2,1)S(1)}, u32[]{:S(2)}, u32[]{:S(2)}) %collective-permute-start.30) | collective-permute-done | bytes 163872 | tf_op jit(solution)/shard_map/ppermute | solution.py:19
  179.5 3.0 %collective-permute-done.41 = bf16[128,640]{1,0:T(8,128)(2,1)S(1)} collective-permute-done((bf16[128,640]{1,0:T(8,128)(2,1)S(1)}, bf16[128,640]{1,0:T(8,128)(2,1)S(1)}, u32[]{:S(2)}, u32[]{:S(2)}) %collective-permute-start.41) | collective-permute-done | bytes 163872 | tf_op jit(solution)/shard_map/ppermute | solution.py:19
  182.6 3.7 %collective-permute-start.43 = (bf16[128,640]{1,0:T(8,128)(2,1)S(1)}, bf16[128,640]{1,0:T(8,128)(2,1)S(1)}, u32[]{:S(2)}, u32[]{:S(2)}) collective-permute-start(bf16[128,640]{1,0:T(8,128)(2,1)S(1)} %add_convert_fusion.2), channel_id=1, source_target_pairs={{0,1},{1,0},{2,3},{3,2},{4,5},{5,4},{6,7},{7,6},{8,9},{9,8},{10,11... | collective-permute-start | bytes 491528 | tf_op jit(solution)/shard_map/ppermute | solution.py:19
  186.5 3.1 %collective-permute-done.43 = bf16[128,640]{1,0:T(8,128)(2,1)S(1)} collective-permute-done((bf16[128,640]{1,0:T(8,128)(2,1)S(1)}, bf16[128,640]{1,0:T(8,128)(2,1)S(1)}, u32[]{:S(2)}, u32[]{:S(2)}) %collective-permute-start.43) | collective-permute-done | bytes 163872 | tf_op jit(solution)/shard_map/ppermute | solution.py:19
  191.0 6.7 %collective-permute-done.44 = bf16[128,640]{1,0:T(8,128)(2,1)S(1)} collective-permute-done((bf16[128,640]{1,0:T(8,128)(2,1)S(1)}, bf16[128,640]{1,0:T(8,128)(2,1)S(1)}, u32[]{:S(2)}, u32[]{:S(2)}) %collective-permute-start.44) | collective-permute-done | bytes 163872 | tf_op jit(solution)/shard_map/ppermute | solution.py:19
  201.4 2.4 out_grad_of.2.refs_4_
  208.4 2.4 out_grad_of.3
  213.0 2.5 collective-permute-done.50.refs_5_
  216.7 4.0 %collective-permute-done.52.refs_7_ = bf16[128,1024]{1,0:T(8,128)(2,1)S(1)} collective-permute-done((bf16[128,1024]{1,0:T(8,128)(2,1)S(1)}, bf16[128,1024]{1,0:T(8,128)(2,1)S(1)}, u32[]{:S(2)}, u32[]{:S(2)}) %collective-permute-start.52) | collective-permute-done | bytes 262176 | tf_op jit(solution)/shard_map/ppermute | solution.py:19
  226.4 10.8 %collective-permute-done.53.refs_2_ = bf16[256,1024]{1,0:T(8,128)(2,1)S(1)} collective-permute-done((bf16[256,1024]{1,0:T(8,128)(2,1)S(1)}, bf16[256,1024]{1,0:T(8,128)(2,1)S(1)}, u32[]{:S(2)}, u32[]{:S(2)}) %collective-permute-start.53) | collective-permute-done | bytes 524320 | tf_op jit(solution)/shard_map/ppermute | solution.py:19
  239.3 3.2 %weight_grad_of.3.refs_4_ = f32[1024,2048]{1,0:T(8,128)S(1)} custom-call(s32[2]{0:T(128)S(1)} %pad_add_fusion.scalars_ref, bf16[1024,1024]{1,0:T(8,128)(2,1)S(1)} %turn_columns.3.refs_3_.refs_0_, bf16[512,1024]{1,0:T(8,128)(2,1)S(1)} %get-tuple-element.111.refs_1_, bf16[512,1024]{1,0:T(8,128)(2,1)S(1)} %get-tuple-element.112.refs_2_), custom_call_target="tpu_custom_call" | custom-call | flops 2147483648 | bytes 4194304 | tf_op jit(solution)/shard_map/weight_grad_of/pallas_call | solution.py:85
  242.5 4.3 %collective-permute-done.57.refs_2_ = bf16[256,1024]{1,0:T(8,128)(2,1)S(1)} collective-permute-done((bf16[256,1024]{1,0:T(8,128)(2,1)S(1)}, bf16[256,1024]{1,0:T(8,128)(2,1)S(1)}, u32[]{:S(2)}, u32[]{:S(2)}) %collective-permute-start.57) | collective-permute-done | bytes 524320 | tf_op jit(solution)/shard_map/ppermute | solution.py:19
  248.6 3.2 %weight_grad_of.4 = (f32[1024,2048]{1,0:T(8,128)S(1)}, f32[16,128]{1,0:T(8,128)S(1)}) custom-call(s32[2]{0:T(128)S(1)} %pad_add_fusion.scalars_ref, bf16[1024,1024]{1,0:T(8,128)(2,1)S(1)} %turn_columns.2.refs_3_.refs_0_, bf16[512,1024]{1,0:T(8,128)(2,1)S(1)} %get-tuple-element.115.refs_1_, ...), custom_call_target="tpu_custom_call", output_to_operand_aliasing={{0}: (5, {})} | custom-call | flops 2147483648 | bytes 4194304 | tf_op jit(solution)/shard_map/weight_grad_of/pallas_call | solution.py:85
  252.3 5.1 %weight_grad_of.5 = (f32[1024,2048]{1,0:T(8,128)S(1)}, f32[16,128]{1,0:T(8,128)S(1)}) custom-call(s32[2]{0:T(128)S(1)} %pad_add_fusion.scalars_ref, bf16[1024,1024]{1,0:T(8,128)(2,1)S(1)} %turn_columns.3.refs_3_.refs_0_, bf16[512,1024]{1,0:T(8,128)(2,1)S(1)} %collective-permute-done.55.refs_1_, ...), custom_call_target="tpu_custom_call", output_to_operand_aliasing={{0}: (8, {})} | custom-call | flops 4294967296 | bytes 4194304 | tf_op jit(solution)/shard_map/weight_grad_of/pallas_call | solution.py:85
  257.3 3.9 %collective-permute-start.63 = (f32[16,128]{1,0:T(8,128)S(1)}, f32[16,128]{1,0:T(8,128)S(1)}, u32[]{:S(2)}, u32[]{:S(2)}) collective-permute-start(f32[16,128]{1,0:T(8,128)S(1)} %get-tuple-element.120), channel_id=1, source_target_pairs={{0,3},{1,2},{2,1},{3,0},{4,7},{5,6},{6,5},{7,4},{8,11},{9,10},{10,... | collective-permute-start | bytes 24584 | tf_op jit(solution)/shard_map/ppermute | solution.py:40
  262.9 2.9 %collective-permute-done.62 = f32[16,128]{1,0:T(8,128)S(1)} collective-permute-done((f32[16,128]{1,0:T(8,128)S(1)}, f32[16,128]{1,0:T(8,128)S(1)}, u32[]{:S(2)}, u32[]{:S(2)}) %collective-permute-start.62) | collective-permute-done | bytes 8224 | tf_op jit(solution)/shard_map/ppermute | solution.py:40
  271.1 2.2 collective-permute-done.67.refs_1_
  273.3 7.0 %update.1 = (f32[1024,2048]{1,0:T(8,128)}, f32[1024,2048]{1,0:T(8,128)}) custom-call(s32[1]{0:T(128)} %constant.21.clone.1.scalars_ref, f32[16,128]{1,0:T(8,128)S(1)} %add_add_fusion.refs_0_, f32[16,128]{1,0:T(8,128)S(1)} %collective-permute-done.67.refs_1_, f32[1024,2048]{1,0:T(8,128)S(1)} %bitcast.9, f32[1024,2048]{1,0:T(8,128)S(1)} %bitcast.11, ...), custom_call_target="tpu_custom_call" | custom-call | flops 8388608 | bytes 41943040 | tf_op jit(solution)/shard_map/update/pallas_call | solution.py:85
  (158 shorter events, 85.1 us)
Async XLA Ops:
  1.9 12.3 %collective-permute-start.10 = (bf16[64,2048]{1,0:T(8,128)(2,1)S(1)}, bf16[64,2048]{1,0:T(8,128)(2,1)}, u32[]{:S(2)}, u32[]{:S(2)}) collective-permute-start(bf16[64,2048]{1,0:T(8,128)(2,1)S(1)} %get-tuple-element.70.refs_0_), channel_id=1, source_target_pairs={{0,1},{1,2},{2,3},{3,0},{4,5},{5,6},{6,7},{7,4},{8,9},{9,10},{10,1... | collective-permute-start | bytes 786440 | tf_op jit(solution)/shard_map/ppermute | solution.py:171
  5.0 14.8 %collective-permute-start.3 = (bf16[64,2048]{1,0:T(8,128)(2,1)S(1)}, bf16[64,2048]{1,0:T(8,128)(2,1)S(1)}, u32[]{:S(2)}, u32[]{:S(2)}) collective-permute-start(bf16[64,2048]{1,0:T(8,128)(2,1)S(1)} %get-tuple-element.63.refs_0_), channel_id=1, source_target_pairs={{0,1},{1,2},{2,3},{3,0},{4,5},{5,6},{6,7},{7,4},{8,9},{9,10},{10,1... | collective-permute-start | bytes 786440 | tf_op jit(solution)/shard_map/ppermute | solution.py:171
  14.3 13.6 %collective-permute-start.11 = (bf16[64,2048]{1,0:T(8,128)(2,1)}, bf16[64,2048]{1,0:T(8,128)(2,1)}, u32[]{:S(2)}, u32[]{:S(2)}) collective-permute-start(bf16[64,2048]{1,0:T(8,128)(2,1)} %collective-permute-done.10.refs_1_), channel_id=1, source_target_pairs={{0,1},{1,2},{2,3},{3,0},{4,5},{5,6},{6,7},{7,4},{8,9},{9,10},{10,1... | collective-permute-start | bytes 786440 | tf_op jit(solution)/shard_map/ppermute | solution.py:171
  14.3 37.7 %collective-permute-start = (bf16[128,2048]{1,0:T(8,128)(2,1)S(1)}, bf16[128,2048]{1,0:T(8,128)(2,1)}, u32[]{:S(2)}, u32[]{:S(2)}) collective-permute-start(bf16[128,2048]{1,0:T(8,128)(2,1)S(1)} %get-tuple-element.62.refs_0_), channel_id=1, source_target_pairs={{0,1},{1,2},{2,3},{3,0},{4,5},{5,6},{6,7},{7,4},{8,9},{9,10},{10,1... | collective-permute-start | bytes 1572872 | tf_op jit(solution)/shard_map/ppermute | solution.py:171
  27.8 14.7 %collective-permute-start.5 = (bf16[64,2048]{1,0:T(8,128)(2,1)S(1)}, bf16[64,2048]{1,0:T(8,128)(2,1)}, u32[]{:S(2)}, u32[]{:S(2)}) collective-permute-start(bf16[64,2048]{1,0:T(8,128)(2,1)S(1)} %relay.1.refs_1_), channel_id=1, source_target_pairs={{0,1},{1,2},{2,3},{3,0},{4,5},{5,6},{6,7},{7,4},{8,9},{9,10},{10,1... | collective-permute-start | bytes 786440 | tf_op jit(solution)/shard_map/ppermute | solution.py:171
  27.9 20.1 %collective-permute-start.12 = (bf16[64,2048]{1,0:T(8,128)(2,1)}, bf16[64,2048]{1,0:T(8,128)(2,1)S(1)}, u32[]{:S(2)}, u32[]{:S(2)}) collective-permute-start(bf16[64,2048]{1,0:T(8,128)(2,1)} %collective-permute-done.11.refs_2_), channel_id=1, source_target_pairs={{0,1},{1,2},{2,3},{3,0},{4,5},{5,6},{6,7},{7,4},{8,9},{9,10},{10,1... | collective-permute-start | bytes 786440 | tf_op jit(solution)/shard_map/ppermute | solution.py:171
  42.5 11.3 %collective-permute-start.6 = (bf16[64,2048]{1,0:T(8,128)(2,1)}, bf16[64,2048]{1,0:T(8,128)(2,1)S(1)}, u32[]{:S(2)}, u32[]{:S(2)}) collective-permute-start(bf16[64,2048]{1,0:T(8,128)(2,1)} %collective-permute-done.5.refs_2_), channel_id=1, source_target_pairs={{0,1},{1,2},{2,3},{3,0},{4,5},{5,6},{6,7},{7,4},{8,9},{9,10},{10,1... | collective-permute-start | bytes 786440 | tf_op jit(solution)/shard_map/ppermute | solution.py:171
  50.2 9.3 %collective-permute-start.13 = (bf16[64,2048]{1,0:T(8,128)(2,1)S(1)}, bf16[64,2048]{1,0:T(8,128)(2,1)S(1)}, u32[]{:S(2)}, u32[]{:S(2)}) collective-permute-start(bf16[64,2048]{1,0:T(8,128)(2,1)S(1)} %get-tuple-element.72), channel_id=1, source_target_pairs={{0,8},{4,12},{8,0},{12,4},{16,24},{20,28},{24,16},{28,20},{1,9},{5... | collective-permute-start | bytes 786440 | tf_op jit(solution)/shard_map/ppermute | solution.py:19
  52.0 14.4 %collective-permute-start.1 = (bf16[128,2048]{1,0:T(8,128)(2,1)}, bf16[128,2048]{1,0:T(8,128)(2,1)S(1)}, u32[]{:S(2)}, u32[]{:S(2)}) collective-permute-start(bf16[128,2048]{1,0:T(8,128)(2,1)} %collective-permute-done.refs_1_), channel_id=1, source_target_pairs={{0,1},{1,2},{2,3},{3,0},{4,5},{5,6},{6,7},{7,4},{8,9},{9,10},{10,1... | collective-permute-start | bytes 1572872 | tf_op jit(solution)/shard_map/ppermute | solution.py:171
  52.0 11.9 %collective-permute-start.14 = (bf16[64,2048]{1,0:T(8,128)(2,1)S(1)}, bf16[64,2048]{1,0:T(8,128)(2,1)S(1)}, u32[]{:S(2)}, u32[]{:S(2)}) collective-permute-start(bf16[64,2048]{1,0:T(8,128)(2,1)S(1)} %get-tuple-element.73), channel_id=1, source_target_pairs={{0,16},{4,20},{8,24},{12,28},{16,0},{20,4},{24,8},{28,12},{1,17},{... | collective-permute-start | bytes 786440 | tf_op jit(solution)/shard_map/ppermute | solution.py:19
  53.5 12.9 %collective-permute-start.15 = (bf16[64,2048]{1,0:T(8,128)(2,1)S(1)}, bf16[64,2048]{1,0:T(8,128)(2,1)S(1)}, u32[]{:S(2)}, u32[]{:S(2)}) collective-permute-start(bf16[64,2048]{1,0:T(8,128)(2,1)S(1)} %get-tuple-element.74), channel_id=1, source_target_pairs={{0,24},{4,28},{8,16},{12,20},{16,8},{20,12},{24,0},{28,4},{1,25},{... | collective-permute-start | bytes 786440 | tf_op jit(solution)/shard_map/ppermute | solution.py:19
  55.8 14.9 %collective-permute-start.7 = (bf16[64,2048]{1,0:T(8,128)(2,1)S(1)}, bf16[64,2048]{1,0:T(8,128)(2,1)S(1)}, u32[]{:S(2)}, u32[]{:S(2)}) collective-permute-start(bf16[64,2048]{1,0:T(8,128)(2,1)S(1)} %get-tuple-element.67), channel_id=1, source_target_pairs={{0,8},{4,12},{8,0},{12,4},{16,24},{20,28},{24,16},{28,20},{1,9},{5... | collective-permute-start | bytes 786440 | tf_op jit(solution)/shard_map/ppermute | solution.py:19
  59.5 15.0 %collective-permute-start.8 = (bf16[64,2048]{1,0:T(8,128)(2,1)S(1)}, bf16[64,2048]{1,0:T(8,128)(2,1)S(1)}, u32[]{:S(2)}, u32[]{:S(2)}) collective-permute-start(bf16[64,2048]{1,0:T(8,128)(2,1)S(1)} %get-tuple-element.68), channel_id=1, source_target_pairs={{0,16},{4,20},{8,24},{12,28},{16,0},{20,4},{24,8},{28,12},{1,17},{... | collective-permute-start | bytes 786440 | tf_op jit(solution)/shard_map/ppermute | solution.py:19
  63.9 10.6 %collective-permute-start.9 = (bf16[64,2048]{1,0:T(8,128)(2,1)S(1)}, bf16[64,2048]{1,0:T(8,128)(2,1)S(1)}, u32[]{:S(2)}, u32[]{:S(2)}) collective-permute-start(bf16[64,2048]{1,0:T(8,128)(2,1)S(1)} %get-tuple-element.69), channel_id=1, source_target_pairs={{0,24},{4,28},{8,16},{12,20},{16,8},{20,12},{24,0},{28,4},{1,25},{... | collective-permute-start | bytes 786440 | tf_op jit(solution)/shard_map/ppermute | solution.py:19
  76.5 7.5 %collective-permute-start.4 = (bf16[1024,1024]{1,0:T(8,128)(2,1)}, bf16[1024,1024]{1,0:T(8,128)(2,1)}, u32[]{:S(2)}, u32[]{:S(2)}) collective-permute-start(bf16[1024,1024]{1,0:T(8,128)(2,1)} %get-tuple-element.65), channel_id=1, source_target_pairs={{0,4},{4,0},{8,12},{12,8},{16,20},{20,16},{24,28},{28,24},{1,5},{5... | collective-permute-start | bytes 6291464 | tf_op jit(solution)/shard_map/ppermute | solution.py:19
  77.0 15.9 %collective-permute-start.2 = (bf16[128,2048]{1,0:T(8,128)(2,1)S(1)}, bf16[128,2048]{1,0:T(8,128)(2,1)}, u32[]{:S(2)}, u32[]{:S(2)}) collective-permute-start(bf16[128,2048]{1,0:T(8,128)(2,1)S(1)} %collective-permute-done.1.refs_9_.refs_2_), channel_id=1, source_target_pairs={{0,1},{1,2},{2,3},{3,0},{4,5},{5,6},{6,7},{7,4},{8,9},{9,10},{10,1... | collective-permute-start | bytes 1572872 | tf_op jit(solution)/shard_map/ppermute | solution.py:171
  88.1 15.5 %collective-permute-start.21 = (bf16[256,1024]{1,0:T(8,128)(2,1)S(1)}, bf16[256,1024]{1,0:T(8,128)(2,1)S(1)}, u32[]{:S(2)}, u32[]{:S(2)}) collective-permute-start(bf16[256,1024]{1,0:T(8,128)(2,1)S(1)} %get-tuple-element.82), channel_id=1, source_target_pairs={{0,16},{4,20},{8,24},{12,28},{16,0},{20,4},{24,8},{28,12},{1,17},{... | collective-permute-start | bytes 1572872 | tf_op jit(solution)/shard_map/ppermute | solution.py:19
  89.7 14.8 %collective-permute-start.20 = (bf16[256,1024]{1,0:T(8,128)(2,1)S(1)}, bf16[256,1024]{1,0:T(8,128)(2,1)S(1)}, u32[]{:S(2)}, u32[]{:S(2)}) collective-permute-start(bf16[256,1024]{1,0:T(8,128)(2,1)S(1)} %get-tuple-element.75.refs_4_), channel_id=1, source_target_pairs={{0,8},{4,12},{8,0},{12,4},{16,24},{20,28},{24,16},{28,20},{1,9},{5... | collective-permute-start | bytes 1572872 | tf_op jit(solution)/shard_map/ppermute | solution.py:19
  94.6 21.1 %collective-permute-start.17 = (bf16[128,2048]{1,0:T(8,128)(2,1)S(1)}, bf16[128,2048]{1,0:T(8,128)(2,1)S(1)}, u32[]{:S(2)}, u32[]{:S(2)}) collective-permute-start(bf16[128,2048]{1,0:T(8,128)(2,1)S(1)} %get-tuple-element.77), channel_id=1, source_target_pairs={{0,8},{4,12},{8,0},{12,4},{16,24},{20,28},{24,16},{28,20},{1,9},{5... | collective-permute-start | bytes 1572872 | tf_op jit(solution)/shard_map/ppermute | solution.py:19
  95.7 20.0 %collective-permute-start.18 = (bf16[128,2048]{1,0:T(8,128)(2,1)S(1)}, bf16[128,2048]{1,0:T(8,128)(2,1)S(1)}, u32[]{:S(2)}, u32[]{:S(2)}) collective-permute-start(bf16[128,2048]{1,0:T(8,128)(2,1)S(1)} %get-tuple-element.78), channel_id=1, source_target_pairs={{0,16},{4,20},{8,24},{12,28},{16,0},{20,4},{24,8},{28,12},{1,17},{... | collective-permute-start | bytes 1572872 | tf_op jit(solution)/shard_map/ppermute | solution.py:19
  96.5 29.2 %collective-permute-start.19 = (bf16[128,2048]{1,0:T(8,128)(2,1)S(1)}, bf16[128,2048]{1,0:T(8,128)(2,1)S(1)}, u32[]{:S(2)}, u32[]{:S(2)}) collective-permute-start(bf16[128,2048]{1,0:T(8,128)(2,1)S(1)} %get-tuple-element.79), channel_id=1, source_target_pairs={{0,24},{4,28},{8,16},{12,20},{16,8},{20,12},{24,0},{28,4},{1,25},{... | collective-permute-start | bytes 1572872 | tf_op jit(solution)/shard_map/ppermute | solution.py:19
  126.5 9.0 %collective-permute-start.24 = (bf16[128,1024]{1,0:T(8,128)(2,1)S(1)}, bf16[128,1024]{1,0:T(8,128)(2,1)S(1)}, u32[]{:S(2)}, u32[]{:S(2)}) collective-permute-start(bf16[128,1024]{1,0:T(8,128)(2,1)S(1)} %get-tuple-element.86), channel_id=1, source_target_pairs={{0,8},{4,12},{8,0},{12,4},{16,24},{20,28},{24,16},{28,20},{1,9},{5... | collective-permute-start | bytes 786440 | tf_op jit(solution)/shard_map/ppermute | solution.py:19
  127.9 8.4 %collective-permute-start.23 = (bf16[128,1024]{1,0:T(8,128)(2,1)S(1)}, bf16[128,1024]{1,0:T(8,128)(2,1)S(1)}, u32[]{:S(2)}, u32[]{:S(2)}) collective-permute-start(bf16[128,1024]{1,0:T(8,128)(2,1)S(1)} %get-tuple-element.83.refs_4_), channel_id=1, source_target_pairs={{0,16},{4,20},{8,24},{12,28},{16,0},{20,4},{24,8},{28,12},{1,17},{... | collective-permute-start | bytes 786440 | tf_op jit(solution)/shard_map/ppermute | solution.py:19
  136.7 14.8 %collective-permute-start.36 = (bf16[256,1024]{1,0:T(8,128)(2,1)S(1)}, bf16[256,1024]{1,0:T(8,128)(2,1)S(1)}, u32[]{:S(2)}, u32[]{:S(2)}) collective-permute-start(bf16[256,1024]{1,0:T(8,128)(2,1)S(1)} %get-tuple-element.95), channel_id=1, source_target_pairs={{0,16},{4,20},{8,24},{12,28},{16,0},{20,4},{24,8},{28,12},{1,17},{... | collective-permute-start | bytes 1572872 | tf_op jit(solution)/shard_map/ppermute | solution.py:19
  137.7 14.8 %collective-permute-start.35 = (bf16[256,1024]{1,0:T(8,128)(2,1)S(1)}, bf16[256,1024]{1,0:T(8,128)(2,1)S(1)}, u32[]{:S(2)}, u32[]{:S(2)}) collective-permute-start(bf16[256,1024]{1,0:T(8,128)(2,1)S(1)} %get-tuple-element.87.refs_4_), channel_id=1, source_target_pairs={{0,8},{4,12},{8,0},{12,4},{16,24},{20,28},{24,16},{28,20},{1,9},{5... | collective-permute-start | bytes 1572872 | tf_op jit(solution)/shard_map/ppermute | solution.py:19
  141.9 14.1 %collective-permute-start.26 = (bf16[128,640]{1,0:T(8,128)(2,1)S(1)}, bf16[128,640]{1,0:T(8,128)(2,1)S(1)}, u32[]{:S(2)}, u32[]{:S(2)}) collective-permute-start(bf16[128,640]{1,0:T(8,128)(2,1)S(1)} %get-tuple-element.90), channel_id=1, source_target_pairs={{0,8},{4,12},{8,0},{12,4},{16,24},{20,28},{24,16},{28,20},{1,9},{5... | collective-permute-start | bytes 491528 | tf_op jit(solution)/shard_map/ppermute | solution.py:19
  142.6 13.4 %collective-permute-start.27 = (bf16[128,640]{1,0:T(8,128)(2,1)S(1)}, bf16[128,640]{1,0:T(8,128)(2,1)S(1)}, u32[]{:S(2)}, u32[]{:S(2)}) collective-permute-start(bf16[128,640]{1,0:T(8,128)(2,1)S(1)} %get-tuple-element.91), channel_id=1, source_target_pairs={{0,16},{4,20},{8,24},{12,28},{16,0},{20,4},{24,8},{28,12},{1,17},{... | collective-permute-start | bytes 491528 | tf_op jit(solution)/shard_map/ppermute | solution.py:19
  143.7 16.4 %collective-permute-start.28 = (bf16[128,640]{1,0:T(8,128)(2,1)S(1)}, bf16[128,640]{1,0:T(8,128)(2,1)S(1)}, u32[]{:S(2)}, u32[]{:S(2)}) collective-permute-start(bf16[128,640]{1,0:T(8,128)(2,1)S(1)} %get-tuple-element.92), channel_id=1, source_target_pairs={{0,24},{4,28},{8,16},{12,20},{16,8},{20,12},{24,0},{28,4},{1,25},{... | collective-permute-start | bytes 491528 | tf_op jit(solution)/shard_map/ppermute | solution.py:19
  153.3 10.4 %collective-permute-start.37 = (bf16[128,1024]{1,0:T(8,128)(2,1)S(1)}, bf16[128,1024]{1,0:T(8,128)(2,1)S(1)}, u32[]{:S(2)}, u32[]{:S(2)}) collective-permute-start(bf16[128,1024]{1,0:T(8,128)(2,1)S(1)} %get-tuple-element.97), channel_id=1, source_target_pairs={{0,16},{4,20},{8,24},{12,28},{16,0},{20,4},{24,8},{28,12},{1,17},{... | collective-permute-start | bytes 786440 | tf_op jit(solution)/shard_map/ppermute | solution.py:19
  154.4 9.9 %collective-permute-start.38 = (bf16[128,1024]{1,0:T(8,128)(2,1)S(1)}, bf16[128,1024]{1,0:T(8,128)(2,1)S(1)}, u32[]{:S(2)}, u32[]{:S(2)}) collective-permute-start(bf16[128,1024]{1,0:T(8,128)(2,1)S(1)} %get-tuple-element.99), channel_id=1, source_target_pairs={{0,8},{4,12},{8,0},{12,4},{16,24},{20,28},{24,16},{28,20},{1,9},{5... | collective-permute-start | bytes 786440 | tf_op jit(solution)/shard_map/ppermute | solution.py:19
  165.6 10.3 %collective-permute-start.30 = (bf16[128,640]{1,0:T(8,128)(2,1)S(1)}, bf16[128,640]{1,0:T(8,128)(2,1)S(1)}, u32[]{:S(2)}, u32[]{:S(2)}) collective-permute-start(bf16[128,640]{1,0:T(8,128)(2,1)S(1)} %add_convert_fusion.4), channel_id=1, source_target_pairs={{0,2},{1,3},{2,0},{3,1},{4,6},{5,7},{6,4},{7,5},{8,10},{9,11},{10,... | collective-permute-start | bytes 491528 | tf_op jit(solution)/shard_map/ppermute | solution.py:19
  168.8 10.1 %collective-permute-start.40 = (bf16[128,640]{1,0:T(8,128)(2,1)S(1)}, bf16[128,640]{1,0:T(8,128)(2,1)S(1)}, u32[]{:S(2)}, u32[]{:S(2)}) collective-permute-start(bf16[128,640]{1,0:T(8,128)(2,1)S(1)} %get-tuple-element.104), channel_id=1, source_target_pairs={{0,8},{4,12},{8,0},{12,4},{16,24},{20,28},{24,16},{28,20},{1,9},{5... | collective-permute-start | bytes 491528 | tf_op jit(solution)/shard_map/ppermute | solution.py:19
  170.2 12.3 %collective-permute-start.41 = (bf16[128,640]{1,0:T(8,128)(2,1)S(1)}, bf16[128,640]{1,0:T(8,128)(2,1)S(1)}, u32[]{:S(2)}, u32[]{:S(2)}) collective-permute-start(bf16[128,640]{1,0:T(8,128)(2,1)S(1)} %get-tuple-element.105), channel_id=1, source_target_pairs={{0,16},{4,20},{8,24},{12,28},{16,0},{20,4},{24,8},{28,12},{1,17},{... | collective-permute-start | bytes 491528 | tf_op jit(solution)/shard_map/ppermute | solution.py:19
  171.9 10.6 %collective-permute-start.42 = (bf16[128,640]{1,0:T(8,128)(2,1)S(1)}, bf16[128,640]{1,0:T(8,128)(2,1)S(1)}, u32[]{:S(2)}, u32[]{:S(2)}) collective-permute-start(bf16[128,640]{1,0:T(8,128)(2,1)S(1)} %get-tuple-element.106), channel_id=1, source_target_pairs={{0,24},{4,28},{8,16},{12,20},{16,8},{20,12},{24,0},{28,4},{1,25},{... | collective-permute-start | bytes 491528 | tf_op jit(solution)/shard_map/ppermute | solution.py:19
  175.9 10.3 %collective-permute-start.33 = (bf16[128,640]{1,0:T(8,128)(2,1)S(1)}, bf16[128,640]{1,0:T(8,128)(2,1)S(1)}, u32[]{:S(2)}, u32[]{:S(2)}) collective-permute-start(bf16[128,640]{1,0:T(8,128)(2,1)S(1)} %add_convert_fusion.3.refs_0_), channel_id=1, source_target_pairs={{0,24},{4,28},{8,16},{12,20},{16,8},{20,12},{24,0},{28,4},{1,25},{... | collective-permute-start | bytes 491528 | tf_op jit(solution)/shard_map/ppermute | solution.py:19
  177.4 9.0 %collective-permute-start.32 = (bf16[128,640]{1,0:T(8,128)(2,1)S(1)}, bf16[128,640]{1,0:T(8,128)(2,1)S(1)}, u32[]{:S(2)}, u32[]{:S(2)}) collective-permute-start(bf16[128,640]{1,0:T(8,128)(2,1)S(1)} %add_convert_fusion.3.refs_0_), channel_id=1, source_target_pairs={{0,16},{4,20},{8,24},{12,28},{16,0},{20,4},{24,8},{28,12},{1,17},{... | collective-permute-start | bytes 491528 | tf_op jit(solution)/shard_map/ppermute | solution.py:19
  186.4 15.0 %collective-permute-start.34 = (bf16[4,128,640]{2,1,0:T(8,128)(2,1)S(1)}, bf16[4,128,640]{2,1,0:T(8,128)(2,1)S(1)}, u32[]{:S(2)}, u32[]{:S(2)}) collective-permute-start(bf16[4,128,640]{2,1,0:T(8,128)(2,1)S(1)} %pile.2.refs_0_), channel_id=1, source_target_pairs={{0,4},{4,0},{8,12},{12,8},{16,20},{20,16},{24,28},{28,24},{1,5},{5... | collective-permute-start | bytes 1966088 | tf_op jit(solution)/shard_map/ppermute | solution.py:19
  189.6 8.2 %collective-permute-start.44 = (bf16[128,640]{1,0:T(8,128)(2,1)S(1)}, bf16[128,640]{1,0:T(8,128)(2,1)S(1)}, u32[]{:S(2)}, u32[]{:S(2)}) collective-permute-start(bf16[128,640]{1,0:T(8,128)(2,1)S(1)} %add_convert_fusion.1), channel_id=1, source_target_pairs={{0,2},{1,3},{2,0},{3,1},{4,6},{5,7},{6,4},{7,5},{8,10},{9,11},{10,... | collective-permute-start | bytes 491528 | tf_op jit(solution)/shard_map/ppermute | solution.py:19
  206.3 9.2 %collective-permute-start.50 = (bf16[128,1024]{1,0:T(8,128)(2,1)S(1)}, bf16[128,1024]{1,0:T(8,128)(2,1)S(1)}, u32[]{:S(2)}, u32[]{:S(2)}) collective-permute-start(bf16[128,1024]{1,0:T(8,128)(2,1)S(1)} %get-tuple-element.126.refs_1_), channel_id=1, source_target_pairs={{0,8},{4,12},{8,0},{12,4},{16,24},{20,28},{24,16},{28,20},{1,9},{5... | collective-permute-start | bytes 786440 | tf_op jit(solution)/shard_map/ppermute | solution.py:19
  207.6 9.1 %collective-permute-start.49 = (bf16[128,1024]{1,0:T(8,128)(2,1)S(1)}, bf16[128,1024]{1,0:T(8,128)(2,1)S(1)}, u32[]{:S(2)}, u32[]{:S(2)}) collective-permute-start(bf16[128,1024]{1,0:T(8,128)(2,1)S(1)} %get-tuple-element.127.refs_0_), channel_id=1, source_target_pairs={{0,16},{4,20},{8,24},{12,28},{16,0},{20,4},{24,8},{28,12},{1,17},{... | collective-permute-start | bytes 786440 | tf_op jit(solution)/shard_map/ppermute | solution.py:19
  210.8 9.8 %collective-permute-start.52 = (bf16[128,1024]{1,0:T(8,128)(2,1)S(1)}, bf16[128,1024]{1,0:T(8,128)(2,1)S(1)}, u32[]{:S(2)}, u32[]{:S(2)}) collective-permute-start(bf16[128,1024]{1,0:T(8,128)(2,1)S(1)} %get-tuple-element.124.refs_3_), channel_id=1, source_target_pairs={{0,8},{4,12},{8,0},{12,4},{16,24},{20,28},{24,16},{28,20},{1,9},{5... | collective-permute-start | bytes 786440 | tf_op jit(solution)/shard_map/ppermute | solution.py:19
  212.0 9.6 %collective-permute-start.51 = (bf16[128,1024]{1,0:T(8,128)(2,1)S(1)}, bf16[128,1024]{1,0:T(8,128)(2,1)S(1)}, u32[]{:S(2)}, u32[]{:S(2)}) collective-permute-start(bf16[128,1024]{1,0:T(8,128)(2,1)S(1)} %get-tuple-element.125.refs_2_), channel_id=1, source_target_pairs={{0,16},{4,20},{8,24},{12,28},{16,0},{20,4},{24,8},{28,12},{1,17},{... | collective-permute-start | bytes 786440 | tf_op jit(solution)/shard_map/ppermute | solution.py:19
  222.3 14.9 %collective-permute-start.53 = (bf16[256,1024]{1,0:T(8,128)(2,1)S(1)}, bf16[256,1024]{1,0:T(8,128)(2,1)S(1)}, u32[]{:S(2)}, u32[]{:S(2)}) collective-permute-start(bf16[256,1024]{1,0:T(8,128)(2,1)S(1)} %get-tuple-element.109.refs_0_), channel_id=1, source_target_pairs={{0,8},{4,12},{8,0},{12,4},{16,24},{20,28},{24,16},{28,20},{1,9},{5... | collective-permute-start | bytes 1572872 | tf_op jit(solution)/shard_map/ppermute | solution.py:19
  223.2 14.9 %collective-permute-start.54 = (bf16[256,1024]{1,0:T(8,128)(2,1)S(1)}, bf16[256,1024]{1,0:T(8,128)(2,1)S(1)}, u32[]{:S(2)}, u32[]{:S(2)}) collective-permute-start(bf16[256,1024]{1,0:T(8,128)(2,1)S(1)} %get-tuple-element.110.refs_1_), channel_id=1, source_target_pairs={{0,16},{4,20},{8,24},{12,28},{16,0},{20,4},{24,8},{28,12},{1,17},{... | collective-permute-start | bytes 1572872 | tf_op jit(solution)/shard_map/ppermute | solution.py:19
  224.1 22.7 %collective-permute-start.57 = (bf16[256,1024]{1,0:T(8,128)(2,1)S(1)}, bf16[256,1024]{1,0:T(8,128)(2,1)S(1)}, u32[]{:S(2)}, u32[]{:S(2)}) collective-permute-start(bf16[256,1024]{1,0:T(8,128)(2,1)S(1)} %get-tuple-element.113.refs_0_), channel_id=1, source_target_pairs={{0,8},{4,12},{8,0},{12,4},{16,24},{20,28},{24,16},{28,20},{1,9},{5... | collective-permute-start | bytes 1572872 | tf_op jit(solution)/shard_map/ppermute | solution.py:19
  225.2 22.1 %collective-permute-start.58 = (bf16[256,1024]{1,0:T(8,128)(2,1)S(1)}, bf16[256,1024]{1,0:T(8,128)(2,1)S(1)}, u32[]{:S(2)}, u32[]{:S(2)}) collective-permute-start(bf16[256,1024]{1,0:T(8,128)(2,1)S(1)} %get-tuple-element.114.refs_1_), channel_id=1, source_target_pairs={{0,16},{4,20},{8,24},{12,28},{16,0},{20,4},{24,8},{28,12},{1,17},{... | collective-permute-start | bytes 1572872 | tf_op jit(solution)/shard_map/ppermute | solution.py:19
  238.7 13.1 %collective-permute-start.55 = (bf16[512,1024]{1,0:T(8,128)(2,1)S(1)}, bf16[512,1024]{1,0:T(8,128)(2,1)S(1)}, u32[]{:S(2)}, u32[]{:S(2)}) collective-permute-start(bf16[512,1024]{1,0:T(8,128)(2,1)S(1)} %get-tuple-element.111.refs_1_), channel_id=1, source_target_pairs={{0,4},{4,0},{8,12},{12,8},{16,20},{20,16},{24,28},{28,24},{1,5},{5... | collective-permute-start | bytes 3145736 | tf_op jit(solution)/shard_map/ppermute | solution.py:19
  238.8 13.0 %collective-permute-start.56 = (bf16[512,1024]{1,0:T(8,128)(2,1)S(1)}, bf16[512,1024]{1,0:T(8,128)(2,1)S(1)}, u32[]{:S(2)}, u32[]{:S(2)}) collective-permute-start(bf16[512,1024]{1,0:T(8,128)(2,1)S(1)} %get-tuple-element.112.refs_2_), channel_id=1, source_target_pairs={{0,4},{4,0},{8,12},{12,8},{16,20},{20,16},{24,28},{28,24},{1,5},{5... | collective-permute-start | bytes 3145736 | tf_op jit(solution)/shard_map/ppermute | solution.py:19
  (30 other events, 238.7 us)
